TPU v7x, 32 devices: a whole 2x2x4 slice. The times are simulated.
32 devices in a mesh: blk: 16 (over z, x, core), rep: 2 (over y).
Axes of the slice: x: 2, y: 2, z: 4, core: 2. Of those that a mesh axis runs over, the one named last changes fastest.
Arguments:
- features: bfloat16 [16384, 256], P(('blk', 'rep')), may hold values from -6 to 6
- out_grad: bfloat16 [16384, 256], P('blk'), may hold values from -4 to 4
- weight: bfloat16 [256, 256], replicated, may hold values from -0.375 to 0.375
- block_words: int32 [16, 16, 8, 16, 128], P('blk', 'rep'), may hold values from 0 to 255
- block_coords: int32 [16, 16, 2, 8], P('blk', 'rep'), may hold values from 0 to 7, as said below
- block_counts: int32 [16, 16], P('blk', 'rep'), may hold values from 1 to 8, as said below
- degrees: int32 [16384], P('blk'), may hold values from 1 to 127
Outputs:
- input_grad: bfloat16 [16384, 256], P(('blk', 'rep'))
- weight_grad: float32 [256, 256], replicated
Inputs may be any that keep to these rules, and one draw needn't show every extreme that they name: `block_coords`: within one slab pair the 8 slots name distinct pairs of row block and column block. `block_counts`: the 8 slab pairs of one device include one in which all 8 slots are live.
All inputs are finite; a program needn't handle non-finite values.
Results may differ from a plain program's by a relative error of at most 0.015.
Values may be sent and summed in bfloat16 or wider, within the bound.
No kernel may reach another device: no remote copies, remote signals or barrier semaphores. Data moves between devices by JAX's collectives and lax.ppermute only.
A program may use at most 64 MiB of HBM per device.

v0:
```python
import math

import jax
import jax.numpy as jnp
from jax import lax
from jax.sharding import PartitionSpec as P


def from_behind(block, axis, distance):
    devices = range(lax.axis_size(axis))
    route = [((i - distance) % len(devices), i) for i in devices]
    return lax.ppermute(block, axis, route)


def unpack_block(slot_words):
    shifts = jnp.arange(8, dtype=jnp.int32)
    bit_values = jnp.bitwise_and(
        jnp.right_shift(slot_words[:, :, None, :], shifts[None, None, :, None]), 1
    )
    return bit_values.reshape(slot_words.shape[0], 128, 128).astype(jnp.bfloat16)


def per_device(features, out_grad, weight, block_words, block_coords, block_counts, degrees):
    slab_rows, width = out_grad.shape
    row_blocks = slab_rows // 128
    group_size = lax.axis_size("rep")
    step_count = lax.axis_size("blk") // group_size
    rep_index = lax.axis_index("rep")
    inverse_root = lax.rsqrt(degrees.astype(jnp.float32))
    scaled = (out_grad.astype(jnp.float32) * inverse_root[:, None]).astype(jnp.bfloat16)
    column_ids = jnp.arange(row_blocks, dtype=jnp.int32)
    slot_total = block_words.shape[2]
    slot_ids = jnp.arange(slot_total, dtype=jnp.int32)

    def add_slot(accumulated, source_slab, slot_index):
        slot_words = lax.dynamic_index_in_dim(block_words[0], slot_index, 0, keepdims=False)
        coords = lax.dynamic_index_in_dim(block_coords[0], slot_index, 0, keepdims=False)
        live_count = lax.dynamic_index_in_dim(block_counts[0], slot_index, 0, keepdims=False)
        picked = jnp.take(source_slab.reshape(row_blocks, 128, width), coords[0], axis=0)
        transposed = unpack_block(slot_words)
        contrib = jnp.einsum("bvu,buf->bvf", transposed, picked, preferred_element_type=jnp.float32)
        live_slots = slot_ids < live_count
        placement = ((coords[1][:, None] == column_ids[None, :]) & live_slots[:, None]).astype(
            jnp.float32
        )
        return accumulated + jnp.einsum("bc,bvf->cvf", placement, contrib)

    empty = jnp.zeros((row_blocks, 128, width), jnp.float32)
    current = scaled
    for bit in range(group_size.bit_length() - 1):
        shifted = from_behind(current, "blk", -(1 << bit) * step_count)
        current = jnp.where(
            jnp.bitwise_and(jnp.right_shift(rep_index, bit), 1) == 1, shifted, current
        )
    accumulated = add_slot(empty, current, 0)

    def advance(step_index, state_tuple):
        current, accumulated = state_tuple
        current = from_behind(current, "blk", -1)
        return (current, add_slot(accumulated, current, step_index))

    current, accumulated = lax.fori_loop(1, step_count, advance, (current, accumulated))
    partial_sums = accumulated.reshape(slab_rows, width)
    share_rows = slab_rows // group_size
    share_root = lax.dynamic_slice_in_dim(inverse_root, rep_index * share_rows, share_rows, 0)
    whole_sums = lax.psum(partial_sums, "rep")
    own_sums = lax.dynamic_slice_in_dim(whole_sums, rep_index * share_rows, share_rows, 0)
    aggregated = (own_sums * share_root[:, None]).astype(jnp.bfloat16)
    input_grad = lax.dot_general(
        aggregated, weight, (((1,), (1,)), ((), ())), preferred_element_type=jnp.float32
    ).astype(jnp.bfloat16)
    weight_term = lax.dot_general(
        features, aggregated, (((0,), (0,)), ((), ())), preferred_element_type=jnp.float32
    )
    node_total = slab_rows * lax.axis_size("blk")
    weight_grad = lax.psum(weight_term, ("blk", "rep")) * (1.0 / math.sqrt(node_total))
    return (input_grad, weight_grad)


def solution(mesh):
    return jax.shard_map(
        per_device,
        mesh=mesh,
        in_specs=(
            P(("blk", "rep"), None),
            P("blk", None),
            P(),
            P("blk", "rep", None, None, None),
            P("blk", "rep", None, None),
            P("blk", "rep"),
            P("blk"),
        ),
        out_specs=(P(("blk", "rep"), None), P()),
        check_vma=False,
    )
```

profile of v0, /device:TPU:0, one launch (start us, length us, event | category | flops | bytes accessed | tf_op | source)
XLA Modules:
  0.0 310.9 jit_solution(16028933882926463965)
XLA Ops:
  7.2 0.7 convert_rsqrt_fusion
  8.0 1.3 multiply_convert_fusion
  9.3 4.1 %collective-permute-start.1 = (bf16[1024,256]{1,0:T(8,128)(2,1)S(1)}, bf16[1024,256]{1,0:T(8,128)(2,1)S(1)}, u32[]{:S(2)}, u32[]{:S(2)}) collective-permute-start(bf16[1024,256]{1,0:T(8,128)(2,1)S(1)} %multiply_convert_fusion), channel_id=1, source_target_pairs={{16,0},{18,2},{20,4},{22,6},{24,8},{26,10},{28,12},{30,14},{0,16},... | collective-permute-start | bytes 1572872 | tf_op jit(solution)/shard_map/ppermute | solution.py:12
  13.4 0.7 compare_and_fusion.1
  14.2 0.6 copy-done.4
  14.9 0.7 slice_bitcast_fusion.2
  15.6 0.8 slice_bitcast_fusion.1
  16.4 20.1 %collective-permute-done.1 = bf16[1024,256]{1,0:T(8,128)(2,1)S(1)} collective-permute-done((bf16[1024,256]{1,0:T(8,128)(2,1)S(1)}, bf16[1024,256]{1,0:T(8,128)(2,1)S(1)}, u32[]{:S(2)}, u32[]{:S(2)}) %collective-permute-start.1) | collective-permute-done | bytes 524320 | tf_op jit(solution)/shard_map/ppermute | solution.py:12
  36.8 0.6 gather_fusion.1
  38.2 89.1 %while.20 = (s32[]{:T(128)}, bf16[1024,256]{1,0:T(8,128)(2,1)S(1)}, f32[8,128,256]{2,0,1:T(8,128)S(1)}, s32[1,8,2,8]{3,2,1,0:T(2,128)}, s32[1,8]{1,0:T(1,128)S(1...) while((s32[]{:T(128)}, bf16[1024,256]{1,0:T(8,128)(2,1)S(1)}, ...), condition=%wide.region_1.3_spmd.clone.clone, body=%wide.region_0.2_spmd.clone.clone.sunk | while | flops 72221880 | bytes 8067647 | solution.py:62
  38.2 4.1 %collective-permute-start = (bf16[1024,256]{1,0:T(8,128)(2,1)S(1)}, bf16[1024,256]{1,0:T(8,128)(2,1)S(1)}, u32[]{:S(2)}, u32[]{:S(2)}) collective-permute-start(bf16[1024,256]{1,0:T(8,128)(2,1)S(1)} %get-tuple-element.308), channel_id=1, source_target_pairs={{2,0},{4,2},{6,4},{8,6},{10,8},{12,10},{14,12},{16,14},{18,16},{20... | collective-permute-start | bytes 1572872 | tf_op jit(solution)/shard_map/while/body/eval_jaxpr/ppermute | solution.py:12
  42.3 0.6 constant_dynamic-slice_fusion.5
  42.9 0.7 constant_dynamic-slice_fusion.4
  43.7 0.7 iota_compare_fusion.5
  44.4 0.9 dynamic-slice_bitcast_fusion.2
  45.2 3.8 %collective-permute-done = bf16[1024,256]{1,0:T(8,128)(2,1)S(1)} collective-permute-done((bf16[1024,256]{1,0:T(8,128)(2,1)S(1)}, bf16[1024,256]{1,0:T(8,128)(2,1)S(1)}, u32[]{:S(2)}, u32[]{:S(2)}) %collective-permute-start) | collective-permute-done | bytes 524320 | tf_op jit(solution)/shard_map/while/body/eval_jaxpr/ppermute | solution.py:12
  49.0 0.6 gather_fusion
  50.5 4.7 %collective-permute-start = (bf16[1024,256]{1,0:T(8,128)(2,1)S(1)}, bf16[1024,256]{1,0:T(8,128)(2,1)S(1)}, u32[]{:S(2)}, u32[]{:S(2)}) collective-permute-start(bf16[1024,256]{1,0:T(8,128)(2,1)S(1)} %get-tuple-element.308), channel_id=1, source_target_pairs={{2,0},{4,2},{6,4},{8,6},{10,8},{12,10},{14,12},{16,14},{18,16},{20... | collective-permute-start | bytes 1572872 | tf_op jit(solution)/shard_map/while/body/eval_jaxpr/ppermute | solution.py:12
  55.2 0.6 constant_dynamic-slice_fusion.5
  55.7 0.7 constant_dynamic-slice_fusion.4
  56.5 0.7 iota_compare_fusion.5
  57.2 0.9 dynamic-slice_bitcast_fusion.2
  58.0 3.8 %collective-permute-done = bf16[1024,256]{1,0:T(8,128)(2,1)S(1)} collective-permute-done((bf16[1024,256]{1,0:T(8,128)(2,1)S(1)}, bf16[1024,256]{1,0:T(8,128)(2,1)S(1)}, u32[]{:S(2)}, u32[]{:S(2)}) %collective-permute-start) | collective-permute-done | bytes 524320 | tf_op jit(solution)/shard_map/while/body/eval_jaxpr/ppermute | solution.py:12
  61.9 0.6 gather_fusion
  63.3 4.7 %collective-permute-start = (bf16[1024,256]{1,0:T(8,128)(2,1)S(1)}, bf16[1024,256]{1,0:T(8,128)(2,1)S(1)}, u32[]{:S(2)}, u32[]{:S(2)}) collective-permute-start(bf16[1024,256]{1,0:T(8,128)(2,1)S(1)} %get-tuple-element.308), channel_id=1, source_target_pairs={{2,0},{4,2},{6,4},{8,6},{10,8},{12,10},{14,12},{16,14},{18,16},{20... | collective-permute-start | bytes 1572872 | tf_op jit(solution)/shard_map/while/body/eval_jaxpr/ppermute | solution.py:12
  68.0 0.6 constant_dynamic-slice_fusion.5
  68.5 0.7 constant_dynamic-slice_fusion.4
  69.3 0.7 iota_compare_fusion.5
  70.0 0.9 dynamic-slice_bitcast_fusion.2
  70.9 3.8 %collective-permute-done = bf16[1024,256]{1,0:T(8,128)(2,1)S(1)} collective-permute-done((bf16[1024,256]{1,0:T(8,128)(2,1)S(1)}, bf16[1024,256]{1,0:T(8,128)(2,1)S(1)}, u32[]{:S(2)}, u32[]{:S(2)}) %collective-permute-start) | collective-permute-done | bytes 524320 | tf_op jit(solution)/shard_map/while/body/eval_jaxpr/ppermute | solution.py:12
  74.7 0.6 gather_fusion
  76.1 4.7 %collective-permute-start = (bf16[1024,256]{1,0:T(8,128)(2,1)S(1)}, bf16[1024,256]{1,0:T(8,128)(2,1)S(1)}, u32[]{:S(2)}, u32[]{:S(2)}) collective-permute-start(bf16[1024,256]{1,0:T(8,128)(2,1)S(1)} %get-tuple-element.308), channel_id=1, source_target_pairs={{2,0},{4,2},{6,4},{8,6},{10,8},{12,10},{14,12},{16,14},{18,16},{20... | collective-permute-start | bytes 1572872 | tf_op jit(solution)/shard_map/while/body/eval_jaxpr/ppermute | solution.py:12
  80.8 0.6 constant_dynamic-slice_fusion.5
  81.4 0.7 constant_dynamic-slice_fusion.4
  82.1 0.7 iota_compare_fusion.5
  82.8 0.9 dynamic-slice_bitcast_fusion.2
  83.7 3.8 %collective-permute-done = bf16[1024,256]{1,0:T(8,128)(2,1)S(1)} collective-permute-done((bf16[1024,256]{1,0:T(8,128)(2,1)S(1)}, bf16[1024,256]{1,0:T(8,128)(2,1)S(1)}, u32[]{:S(2)}, u32[]{:S(2)}) %collective-permute-start) | collective-permute-done | bytes 524320 | tf_op jit(solution)/shard_map/while/body/eval_jaxpr/ppermute | solution.py:12
  87.5 0.6 gather_fusion
  88.9 4.7 %collective-permute-start = (bf16[1024,256]{1,0:T(8,128)(2,1)S(1)}, bf16[1024,256]{1,0:T(8,128)(2,1)S(1)}, u32[]{:S(2)}, u32[]{:S(2)}) collective-permute-start(bf16[1024,256]{1,0:T(8,128)(2,1)S(1)} %get-tuple-element.308), channel_id=1, source_target_pairs={{2,0},{4,2},{6,4},{8,6},{10,8},{12,10},{14,12},{16,14},{18,16},{20... | collective-permute-start | bytes 1572872 | tf_op jit(solution)/shard_map/while/body/eval_jaxpr/ppermute | solution.py:12
  93.6 0.6 constant_dynamic-slice_fusion.5
  94.2 0.7 constant_dynamic-slice_fusion.4
  94.9 0.7 iota_compare_fusion.5
  95.6 0.9 dynamic-slice_bitcast_fusion.2
  96.5 3.8 %collective-permute-done = bf16[1024,256]{1,0:T(8,128)(2,1)S(1)} collective-permute-done((bf16[1024,256]{1,0:T(8,128)(2,1)S(1)}, bf16[1024,256]{1,0:T(8,128)(2,1)S(1)}, u32[]{:S(2)}, u32[]{:S(2)}) %collective-permute-start) | collective-permute-done | bytes 524320 | tf_op jit(solution)/shard_map/while/body/eval_jaxpr/ppermute | solution.py:12
  101.7 4.7 %collective-permute-start = (bf16[1024,256]{1,0:T(8,128)(2,1)S(1)}, bf16[1024,256]{1,0:T(8,128)(2,1)S(1)}, u32[]{:S(2)}, u32[]{:S(2)}) collective-permute-start(bf16[1024,256]{1,0:T(8,128)(2,1)S(1)} %get-tuple-element.308), channel_id=1, source_target_pairs={{2,0},{4,2},{6,4},{8,6},{10,8},{12,10},{14,12},{16,14},{18,16},{20... | collective-permute-start | bytes 1572872 | tf_op jit(solution)/shard_map/while/body/eval_jaxpr/ppermute | solution.py:12
  106.4 0.6 constant_dynamic-slice_fusion.5
  107.0 0.7 constant_dynamic-slice_fusion.4
  107.8 0.7 iota_compare_fusion.5
  108.4 0.9 dynamic-slice_bitcast_fusion.2
  109.3 3.8 %collective-permute-done = bf16[1024,256]{1,0:T(8,128)(2,1)S(1)} collective-permute-done((bf16[1024,256]{1,0:T(8,128)(2,1)S(1)}, bf16[1024,256]{1,0:T(8,128)(2,1)S(1)}, u32[]{:S(2)}, u32[]{:S(2)}) %collective-permute-start) | collective-permute-done | bytes 524320 | tf_op jit(solution)/shard_map/while/body/eval_jaxpr/ppermute | solution.py:12
  114.5 4.7 %collective-permute-start = (bf16[1024,256]{1,0:T(8,128)(2,1)S(1)}, bf16[1024,256]{1,0:T(8,128)(2,1)S(1)}, u32[]{:S(2)}, u32[]{:S(2)}) collective-permute-start(bf16[1024,256]{1,0:T(8,128)(2,1)S(1)} %get-tuple-element.308), channel_id=1, source_target_pairs={{2,0},{4,2},{6,4},{8,6},{10,8},{12,10},{14,12},{16,14},{18,16},{20... | collective-permute-start | bytes 1572872 | tf_op jit(solution)/shard_map/while/body/eval_jaxpr/ppermute | solution.py:12
  119.2 0.6 constant_dynamic-slice_fusion.5
  119.8 0.7 constant_dynamic-slice_fusion.4
  120.6 0.7 iota_compare_fusion.5
  121.2 0.9 dynamic-slice_bitcast_fusion.2
  122.1 3.8 %collective-permute-done = bf16[1024,256]{1,0:T(8,128)(2,1)S(1)} collective-permute-done((bf16[1024,256]{1,0:T(8,128)(2,1)S(1)}, bf16[1024,256]{1,0:T(8,128)(2,1)S(1)}, u32[]{:S(2)}, u32[]{:S(2)}) %collective-permute-start) | collective-permute-done | bytes 524320 | tf_op jit(solution)/shard_map/while/body/eval_jaxpr/ppermute | solution.py:12
  127.3 1.3 copy.10
  128.8 41.4 %all-reduce.3.cloned.1.call-done = f32[1024,256]{1,0:T(8,128)} async-done(((f32[1024,256]{1,0:T(8,128)}), f32[1024,256]{1,0:T(8,128)}) %all-reduce.3.cloned.1.call-update) | async-done | bytes 1048592 | tf_op jit(solution)/shard_map/psum | solution.py:66
  170.3 2.2 convolution_bitcast_fusion
  172.5 0.9 copy-done.3
  173.4 1.0 convolution_convert_fusion
  174.4 127.9 %all-reduce.5.cloned.1.call-done = f32[256,256]{0,1:T(8,128)} async-done(((f32[256,256]{0,1:T(8,128)}), f32[256,256]{0,1:T(8,128)}) %all-reduce.5.cloned.1.call-update) | async-done | bytes 262160 | tf_op jit(solution)/shard_map/psum | solution.py:76
  302.3 1.0 broadcast_multiply_fusion
  303.2 0.8 copy.11
  (79 shorter events, 9.7 us)
Async XLA Ops:
  7.2 163.1 %copy-start = (bf16[512,256]{1,0:T(8,128)(2,1)S(1)}, bf16[512,256]{1,0:T(8,128)(2,1)}, u32[]{:S(2)}) copy-start(bf16[512,256]{1,0:T(8,128)(2,1)} %param.11) | copy-start | bytes 786436
  7.2 163.1 %all-reduce.3.cloned.1.call-start = ((), (), s32[]{:S(2)}) async-start(), calls=%async_computation | async-start | bytes 2097152 | tf_op jit(solution)/shard_map/psum | solution.py:66
  7.9 28.6 %copy-start.1 = (bf16[1024,256]{1,0:T(8,128)(2,1)S(1)}, bf16[1024,256]{1,0:T(8,128)(2,1)}, u32[]{:S(2)}) copy-start(bf16[1024,256]{1,0:T(8,128)(2,1)} %param.12) | copy-start | bytes 1572868
  9.3 27.3 %collective-permute-start.1 = (bf16[1024,256]{1,0:T(8,128)(2,1)S(1)}, bf16[1024,256]{1,0:T(8,128)(2,1)S(1)}, u32[]{:S(2)}, u32[]{:S(2)}) collective-permute-start(bf16[1024,256]{1,0:T(8,128)(2,1)S(1)} %multiply_convert_fusion), channel_id=1, source_target_pairs={{16,0},{18,2},{20,4},{22,6},{24,8},{26,10},{28,12},{30,14},{0,16},... | collective-permute-start | bytes 1572872 | tf_op jit(solution)/shard_map/ppermute | solution.py:12
  14.2 0.7 copy-start.4
  38.2 10.8 %collective-permute-start = (bf16[1024,256]{1,0:T(8,128)(2,1)S(1)}, bf16[1024,256]{1,0:T(8,128)(2,1)S(1)}, u32[]{:S(2)}, u32[]{:S(2)}) collective-permute-start(bf16[1024,256]{1,0:T(8,128)(2,1)S(1)} %get-tuple-element.308), channel_id=1, source_target_pairs={{2,0},{4,2},{6,4},{8,6},{10,8},{12,10},{14,12},{16,14},{18,16},{20... | collective-permute-start | bytes 1572872 | tf_op jit(solution)/shard_map/while/body/eval_jaxpr/ppermute | solution.py:12
  50.5 11.4 %collective-permute-start = (bf16[1024,256]{1,0:T(8,128)(2,1)S(1)}, bf16[1024,256]{1,0:T(8,128)(2,1)S(1)}, u32[]{:S(2)}, u32[]{:S(2)}) collective-permute-start(bf16[1024,256]{1,0:T(8,128)(2,1)S(1)} %get-tuple-element.308), channel_id=1, source_target_pairs={{2,0},{4,2},{6,4},{8,6},{10,8},{12,10},{14,12},{16,14},{18,16},{20... | collective-permute-start | bytes 1572872 | tf_op jit(solution)/shard_map/while/body/eval_jaxpr/ppermute | solution.py:12
  63.3 11.4 %collective-permute-start = (bf16[1024,256]{1,0:T(8,128)(2,1)S(1)}, bf16[1024,256]{1,0:T(8,128)(2,1)S(1)}, u32[]{:S(2)}, u32[]{:S(2)}) collective-permute-start(bf16[1024,256]{1,0:T(8,128)(2,1)S(1)} %get-tuple-element.308), channel_id=1, source_target_pairs={{2,0},{4,2},{6,4},{8,6},{10,8},{12,10},{14,12},{16,14},{18,16},{20... | collective-permute-start | bytes 1572872 | tf_op jit(solution)/shard_map/while/body/eval_jaxpr/ppermute | solution.py:12
  76.1 11.4 %collective-permute-start = (bf16[1024,256]{1,0:T(8,128)(2,1)S(1)}, bf16[1024,256]{1,0:T(8,128)(2,1)S(1)}, u32[]{:S(2)}, u32[]{:S(2)}) collective-permute-start(bf16[1024,256]{1,0:T(8,128)(2,1)S(1)} %get-tuple-element.308), channel_id=1, source_target_pairs={{2,0},{4,2},{6,4},{8,6},{10,8},{12,10},{14,12},{16,14},{18,16},{20... | collective-permute-start | bytes 1572872 | tf_op jit(solution)/shard_map/while/body/eval_jaxpr/ppermute | solution.py:12
  88.9 11.4 %collective-permute-start = (bf16[1024,256]{1,0:T(8,128)(2,1)S(1)}, bf16[1024,256]{1,0:T(8,128)(2,1)S(1)}, u32[]{:S(2)}, u32[]{:S(2)}) collective-permute-start(bf16[1024,256]{1,0:T(8,128)(2,1)S(1)} %get-tuple-element.308), channel_id=1, source_target_pairs={{2,0},{4,2},{6,4},{8,6},{10,8},{12,10},{14,12},{16,14},{18,16},{20... | collective-permute-start | bytes 1572872 | tf_op jit(solution)/shard_map/while/body/eval_jaxpr/ppermute | solution.py:12
  101.7 11.4 %collective-permute-start = (bf16[1024,256]{1,0:T(8,128)(2,1)S(1)}, bf16[1024,256]{1,0:T(8,128)(2,1)S(1)}, u32[]{:S(2)}, u32[]{:S(2)}) collective-permute-start(bf16[1024,256]{1,0:T(8,128)(2,1)S(1)} %get-tuple-element.308), channel_id=1, source_target_pairs={{2,0},{4,2},{6,4},{8,6},{10,8},{12,10},{14,12},{16,14},{18,16},{20... | collective-permute-start | bytes 1572872 | tf_op jit(solution)/shard_map/while/body/eval_jaxpr/ppermute | solution.py:12
  114.5 11.4 %collective-permute-start = (bf16[1024,256]{1,0:T(8,128)(2,1)S(1)}, bf16[1024,256]{1,0:T(8,128)(2,1)S(1)}, u32[]{:S(2)}, u32[]{:S(2)}) collective-permute-start(bf16[1024,256]{1,0:T(8,128)(2,1)S(1)} %get-tuple-element.308), channel_id=1, source_target_pairs={{2,0},{4,2},{6,4},{8,6},{10,8},{12,10},{14,12},{16,14},{18,16},{20... | collective-permute-start | bytes 1572872 | tf_op jit(solution)/shard_map/while/body/eval_jaxpr/ppermute | solution.py:12
  128.7 173.6 %all-reduce.5.cloned.1.call-start = ((), (), s32[]{:S(2)}) async-start(), calls=%async_computation.1 | async-start | bytes 524288 | tf_op jit(solution)/shard_map/psum | solution.py:76
  170.3 2.2 copy-start.2
  172.5 0.9 copy-start.3
Sparse Core Ops, SparseCore 0:
  128.8 41.4 all-reduce.2
  177.3 124.9 all-reduce.4
where the time goes:
time: 312 us; the launch traced here: 311 us
  waiting for transfers between devices  216 us (69%)
  starting transfers between devices  36.3 us (12%)
  local copies, waits for them, and re-layouts  25.7 us (8%)
  between operations  14.1 us (5%)
  matrix products  9.53 us (3%)
  other arithmetic  8.72 us (3%)
    psum x1, waiting for transfers between devices, per_device(): lax.psum(weight_term, ('blk', 'rep')) * (1.0 / math.sqrt(node_total))  128 us
    ppermute x8, waiting for transfers between devices, from_behind(): return lax.ppermute(block, axis, route)  46.8 us
    psum x1, waiting for transfers between devices, per_device(): whole_sums = lax.psum(partial_sums, 'rep')  41.4 us
    ppermute x8, starting transfers between devices, from_behind(): return lax.ppermute(block, axis, route)  36.2 us
    shift_right_arithmetic x24, local copies, waits for them, and re-layouts, unpack_block(): jnp.right_shift(slot_words[:, :, None, :], shifts[None, None, :, None])  7.51 us
  transfers between devices with their start and end apart: 10, of which 10 were waited for; matrix products, arithmetic and copies ran while one was open for 8% of the time, Pallas kernels for 0%

commit v1 on v0

v1 whole, which is shorter than its diff:
```python
import functools
import math

import jax
import jax.numpy as jnp
from jax import lax
from jax.experimental import pallas as pl
from jax.experimental.pallas import tpu as pltpu
from jax.sharding import PartitionSpec as P

CORES = 2
COLUMNS = 2


def device_of(row, column, core):
    return (row * COLUMNS + column) * CORES + core


def places(blk_size):
    rows = blk_size // (COLUMNS * CORES)
    return [(z, x, c) for z in range(rows) for x in range(COLUMNS) for c in range(CORES)]


def ring_order(rows):
    return [(z, 0) for z in range(rows)] + [(z, 1) for z in reversed(range(rows))]


def along_ring(block, distance):
    rows = lax.axis_size("blk") // (COLUMNS * CORES)
    order = ring_order(rows)
    route = []
    for place, (z, x) in enumerate(order):
        to_z, to_x = order[(place + distance) % len(order)]
        route += [(device_of(z, x, c), device_of(to_z, to_x, c)) for c in range(CORES)]
    return lax.ppermute(block, "blk", route)


def along_rows(block, distance):
    rows = lax.axis_size("blk") // (COLUMNS * CORES)
    route = [
        (device_of(z, x, c), device_of((z + distance) % rows, x, c))
        for z, x, c in places(lax.axis_size("blk"))
    ]
    return lax.ppermute(block, "blk", route)


def across_columns(block):
    route = [
        (device_of(z, x, c), device_of(z, 1 - x, c)) for z, x, c in places(lax.axis_size("blk"))
    ]
    return lax.ppermute(block, "blk", route)


def across_cores(block):
    route = [
        (device_of(z, x, c), device_of(z, x, 1 - c)) for z, x, c in places(lax.axis_size("blk"))
    ]
    return lax.ppermute(block, "blk", route)


def along_rep(block, distance):
    size = lax.axis_size("rep")
    return lax.ppermute(block, "rep", [(i, (i + distance) % size) for i in range(size)])


def from_all_reps(block):
    return [block] + [along_rep(block, d) for d in range(1, lax.axis_size("rep"))]


def tree_sum(terms):
    while len(terms) > 1:
        half = len(terms) // 2
        terms = [terms[d] + terms[d + half] for d in range(half)]
    return terms[0]


def add_pairs(index_ref, facts, words, slabs, sums_ref, slot_total):
    bit_ids = lax.broadcasted_iota(jnp.int32, (16, 8, 128), 1)
    fact_width = 1 + 2 * slot_total
    for slab_id, slab_ref in enumerate(slabs):
        for target in range(2):
            pair = index_ref[slab_id * 2 + target]
            base = pair * fact_width
            live_count = facts[target][base]
            for slot in range(slot_total):
                row_block = facts[target][base + 1 + slot]
                column_block = facts[target][base + 1 + slot_total + slot]
                live = jnp.where(slot < live_count, 255, 0)
                slot_words = jnp.bitwise_and(words[target][pair, slot].astype(jnp.int32), live)
                bits = jnp.bitwise_and(jnp.right_shift(slot_words[:, None, :], bit_ids), 1)
                transposed = bits.reshape(128, 128).astype(jnp.float32).astype(jnp.bfloat16)
                rows = pl.ds(pl.multiple_of(row_block * 128, 128), 128)
                columns = pl.ds(pl.multiple_of(column_block * 128, 128), 128)
                sums_ref[target, columns, :] += jnp.dot(
                    transposed, slab_ref[rows, :], preferred_element_type=jnp.float32
                )


def step_kernel(slab_total, slot_total, first, index_ref, fact_a, fact_b, words_a, words_b, *refs):
    slabs = refs[:slab_total]
    sums_ref = refs[-1]
    if first:
        sums_ref[...] = jnp.zeros_like(sums_ref)
    else:
        sums_ref[...] = refs[slab_total][...]
    add_pairs(index_ref, (fact_a, fact_b), (words_a, words_b), slabs, sums_ref, slot_total)


def last_kernel(
    slot_total, rep_size, index_ref, order_ref, fact_a, fact_b, words_a, words_b, slab_ref, sums_in,
    features_ref, roots_ref, own_ref, other_ref, term_ref, sums_ref,
):
    sums_ref[...] = sums_in[...]
    add_pairs(index_ref, (fact_a, fact_b), (words_a, words_b), [slab_ref], sums_ref, slot_total)
    own_ref[...] = sums_ref[0]
    other_ref[...] = sums_ref[1]
    share = sums_ref.shape[1] // rep_size
    term = jnp.zeros(term_ref.shape, jnp.float32)
    for target in range(2):
        for d in range(rep_size):
            rows = pl.ds(pl.multiple_of(order_ref[d] * share, share), share)
            part = (sums_ref[target, rows, :] * roots_ref[target, rows, :]).astype(jnp.bfloat16)
            term += jnp.dot(features_ref[d, target], part, preferred_element_type=jnp.float32)
    term_ref[...] = term.astype(term_ref.dtype)


SMEM = pl.BlockSpec(memory_space=pltpu.SMEM)
VMEM = pl.BlockSpec(memory_space=pltpu.VMEM)
PARAMS = pltpu.CompilerParams(vmem_limit_bytes=48 * 1024 * 1024)


def per_device(features, out_grad, weight, block_words, block_coords, block_counts, degrees):
    slab_rows, width = out_grad.shape
    rep_size = lax.axis_size("rep")
    blk_size = lax.axis_size("blk")
    chips = blk_size // CORES
    rows_of_chips = chips // COLUMNS
    rep_index = lax.axis_index("rep")
    blk_index = lax.axis_index("blk")
    core = blk_index % CORES
    chip = blk_index // CORES
    share_width = width // rep_size
    share_rows = slab_rows // rep_size
    slot_total = block_words.shape[2]
    half_steps = block_words.shape[1] // 2

    inverse_root = lax.rsqrt(degrees.astype(jnp.float32))
    own_columns = lax.dynamic_slice_in_dim(out_grad, rep_index * share_width, share_width, 1)
    scaled = (own_columns.astype(jnp.float32) * inverse_root[:, None]).astype(jnp.bfloat16)

    words = block_words[0].astype(jnp.int16).reshape(half_steps, 2, slot_total, 16, 128)
    facts = jnp.concatenate(
        [block_counts[0][:, None], block_coords[0].reshape(2 * half_steps, 2 * slot_total)], axis=1
    ).reshape(half_steps, 2, 1 + 2 * slot_total)
    words = jnp.stack([words[:, 0], across_cores(words[:, 1])])
    facts = jnp.stack([facts[:, 0], across_cores(facts[:, 1])])
    words = jnp.concatenate(from_all_reps(words), axis=1)
    facts = jnp.concatenate(from_all_reps(facts), axis=1)
    words_a, words_b = words[0], words[1]
    fact_a, fact_b = facts[0].reshape(-1), facts[1].reshape(-1)

    turned = features.T
    turned = jnp.stack([turned, across_cores(turned)])
    turned = jnp.stack(from_all_reps(turned))
    roots = jnp.stack([inverse_root, across_cores(inverse_root)])
    roots = jnp.broadcast_to(roots[:, :, None], (2, slab_rows, share_width))

    ring_row = chip // COLUMNS
    place = jnp.where(chip % COLUMNS == 0, ring_row, chips - 1 - ring_row)

    def pair_indices(distances):
        entries = []
        for distance in distances:
            at = (place + distance) % chips
            source = jnp.where(
                at < rows_of_chips, at * COLUMNS, (chips - 1 - at) * COLUMNS + 1
            )
            for target in range(2):
                offset = (source - chip - jnp.where(core == 0, target, 0)) % chips
                behind = (rep_index - offset // half_steps) % rep_size
                entries.append(behind * half_steps + offset % half_steps)
        return jnp.stack(entries).astype(jnp.int32)

    pair_cost = 2 * slot_total * 128 * 128 * share_width * 2
    sums_shape = jax.ShapeDtypeStruct((2, slab_rows, share_width), jnp.float32)

    def add_step(distances, slabs, sums):
        first = sums is None
        operands = [pair_indices(distances), fact_a, fact_b, words_a, words_b, *slabs]
        specs = [SMEM] * 3 + [VMEM] * (2 + len(slabs))
        aliases = {}
        if not first:
            aliases = {len(operands): 0}
            operands.append(sums)
            specs.append(VMEM)
        return pl.pallas_call(
            functools.partial(step_kernel, len(slabs), slot_total, first),
            out_shape=sums_shape,
            in_specs=specs,
            out_specs=VMEM,
            input_output_aliases=aliases,
            compiler_params=PARAMS,
            cost_estimate=pl.CostEstimate(
                flops=pair_cost * len(slabs), bytes_accessed=4 << 20, transcendentals=0
            ),
            name="add_step",
        )(*operands)

    sums = add_step([0], [scaled], None)
    forward = backward = scaled
    for step in range(1, chips // 2):
        forward, backward = along_ring(forward, 1), along_ring(backward, -1)
        sums = add_step([-step, step], [forward, backward], sums)
    forward = along_ring(forward, 1)

    order = ((rep_index - jnp.arange(rep_size, dtype=jnp.int32)) % rep_size).astype(jnp.int32)
    slab_shape = jax.ShapeDtypeStruct((slab_rows, share_width), jnp.float32)
    own_sums, other_sums, term = pl.pallas_call(
        functools.partial(last_kernel, slot_total, rep_size),
        out_shape=(slab_shape, slab_shape, jax.ShapeDtypeStruct((width, share_width), jnp.bfloat16)),
        in_specs=[SMEM] * 4 + [VMEM] * 6,
        out_specs=(VMEM,) * 3,
        scratch_shapes=[pltpu.VMEM(sums_shape.shape, jnp.float32)],
        compiler_params=PARAMS,
        name="last_step",
    )(
        pair_indices([chips // 2]), order, fact_a, fact_b, words_a, words_b, forward, sums,
        turned, roots,
    )

    total = tree_sum(
        [t.astype(jnp.float32) for t in [term] + [along_rows(term, d) for d in range(1, rows_of_chips)]]
    ).astype(jnp.bfloat16)
    total = total.astype(jnp.float32) + across_columns(total).astype(jnp.float32)
    total = total + across_cores(total)
    total = total * (1.0 / math.sqrt(slab_rows * blk_size))
    weight_grad = jnp.zeros((width, width), jnp.float32)
    for d, columns in enumerate(from_all_reps(total)):
        at = ((rep_index - d) % rep_size) * share_width
        weight_grad = lax.dynamic_update_slice_in_dim(weight_grad, columns, at, 1)

    own_sums = own_sums + across_cores(other_sums)
    aggregated = (own_sums * inverse_root[:, None]).astype(jnp.bfloat16)
    result = jnp.zeros((share_rows, width), jnp.float32)
    for d in range(rep_size):
        rows_to = ((rep_index + d) % rep_size) * share_rows
        part = lax.dynamic_slice_in_dim(aggregated, rows_to, share_rows, 0)
        if d:
            part = along_rep(part, d)
        columns_at = ((rep_index - d) % rep_size) * share_width
        side = lax.dynamic_slice_in_dim(weight, columns_at, share_width, 1)
        result = result + lax.dot_general(
            part, side, (((1,), (1,)), ((), ())), preferred_element_type=jnp.float32
        )
    return (result.astype(jnp.bfloat16), weight_grad)


def solution(mesh):
    return jax.shard_map(
        per_device,
        mesh=mesh,
        in_specs=(
            P(("blk", "rep"), None),
            P("blk", None),
            P(),
            P("blk", "rep", None, None, None),
            P("blk", "rep", None, None),
            P("blk", "rep"),
            P("blk"),
        ),
        out_specs=(P(("blk", "rep"), None), P()),
        check_vma=False,
    )
```

time: 312 us -> 64.1 us (0.21)
  waiting for transfers between devices: 216 us -> 22.9 us
  local copies, waits for them, and re-layouts: 25.7 us -> 1.46 us
  between operations: 14.1 us -> 2.3 us
  starting transfers between devices: 36.3 us -> 25.7 us
  matrix products: 9.53 us -> 1.17 us
  Pallas kernels: 0 us -> 6.78 us
  other arithmetic: 8.72 us -> 3.6 us
    psum x2 -> x0, waiting for transfers between devices: 169 us -> none  [the longest x1 128 us: per_device(): lax.psum(weight_term, ('blk', 'rep')) * (1.0 / math.sqrt(node_total))]
    ppermute x8 -> x22, waiting for transfers between devices: 46.8 us -> 22.9 us  [the longest x7 8.59 us: along_ring(): return lax.ppermute(block, 'blk', route)]
    ppermute x8 -> x22, starting transfers between devices: 36.2 us -> 25.7 us  [the longest x7 9.69 us: along_ring(): return lax.ppermute(block, 'blk', route)]
    dynamic_slice x15 -> x1, local copies, waits for them, and re-layouts: 8.9 us -> 0.02 us  [per_device(): part = lax.dynamic_slice_in_dim(aggregated, rows_to, share_rows, 0)]
    dot_general x18 -> x2, matrix products: 9.53 us -> 1.17 us  [per_device(): lax.dot_general(part, side, (((1,), (1,)), ((), ())), preferred_element_t...]
    shift_right_arithmetic x24 -> x0, local copies, waits for them, and re-layouts: 7.51 us -> none  [unpack_block(): jnp.right_shift(slot_words[:, :, None, :], shifts[None, None, :, None])]
    pallas_call x0 -> x5, Pallas kernels: none -> 6.78 us  [the longest x4 5.29 us: add_step(): pl.pallas_call(functools.partial(step_kernel, len(slabs), slot_total, fir...]
    gather x8 -> x0, local copies, waits for them, and re-layouts: 4.63 us -> none  [add_slot(): jnp.take(source_slab.reshape(row_blocks, 128, width), coords[0], axis=0)]
  transfers between devices with their start and end apart: 10 -> 22, of which waited for: 10 -> 11; matrix products, arithmetic and copies ran while one was open for 8% -> 4% of each run, Pallas kernels for 0% -> 8%
where the time goes in v1:
time: 64.1 us; the launch traced here: 63.9 us
  starting transfers between devices  25.7 us (40%)
  waiting for transfers between devices  22.9 us (36%)
  Pallas kernels  6.78 us (11%)
  other arithmetic  3.6 us (6%)
  between operations  2.3 us (4%)
  local copies, waits for them, and re-layouts  1.46 us (2%)
  matrix products  1.17 us (2%)
    ppermute x7, starting transfers between devices, along_ring(): return lax.ppermute(block, 'blk', route)  9.69 us
    ppermute x7, waiting for transfers between devices, along_ring(): return lax.ppermute(block, 'blk', route)  8.59 us
    ppermute x5, waiting for transfers between devices, along_rep(): lax.ppermute(block, 'rep', [(i, (i + distance) % size) for i in range(siz...  7.51 us
    ppermute x5, starting transfers between devices, along_rep(): lax.ppermute(block, 'rep', [(i, (i + distance) % size) for i in range(siz...  7.36 us
    ppermute x3, starting transfers between devices, along_rows(): return lax.ppermute(block, 'blk', route)  6.48 us
    pallas_call x4, Pallas kernels, add_step(): pl.pallas_call(functools.partial(step_kernel, len(slabs), slot_total, fir...  5.29 us
    ppermute x1, waiting for transfers between devices, across_columns(): return lax.ppermute(block, 'blk', route)  2.81 us
    ppermute x3, waiting for transfers between devices, along_rows(): return lax.ppermute(block, 'blk', route)  2.63 us
  transfers between devices with their start and end apart: 22, of which 11 were waited for; matrix products, arithmetic and copies ran while one was open for 4% of the time, Pallas kernels for 8%

profile of v1, /device:TPU:0, one launch (start us, length us, event | category | flops | bytes accessed | tf_op | source)
XLA Modules:
  0.0 63.9 jit_solution(12178408663913820097)
XLA Ops:
  0.6 0.0 copy-start
  0.7 0.8 %convert_rsqrt_fusion = f32[1024]{0:T(1024)S(1)} fusion(s32[1024]{0:T(1024)} %param.13), kind=kLoop, calls=%fused_computation.24 | loop fusion | flops 1024 | bytes 8192 | tf_op jit(solution)/shard_map/rsqrt | solution.py:147
  1.4 1.2 %multiply_convert_fusion.1.refs_0_ = bf16[1024,128]{1,0:T(8,128)(2,1)S(1)} fusion(f32[1024]{0:T(1024)S(1)} %convert_rsqrt_fusion, bf16[1024,256]{1,0:T(8,128)(2,1)} %param.8, s32[]{:T(128)S(6)} %select_n.394), kind=kLoop, calls=%fused_computation.6 | loop fusion | flops 393216 | bytes 528388 | tf_op jit(solution)/shard_map/convert_element_type | solution.py:149
  2.6 3.1 %collective-permute-start.4 = (bf16[1024,128]{1,0:T(8,128)(2,1)S(1)}, bf16[1024,128]{1,0:T(8,128)(2,1)S(1)}, u32[]{:S(2)}, u32[]{:S(2)}) collective-permute-start(bf16[1024,128]{1,0:T(8,128)(2,1)S(1)} %multiply_convert_fusion.1.refs_0_), channel_id=1, source_target_pairs={{0,8},{2,10},{8,16},{10,18},{16,24},{18,26},{24,28},{26,30},{28,20... | collective-permute-start | bytes 786440 | tf_op jit(solution)/shard_map/ppermute | solution.py:35
  5.6 0.0 collective-permute-start.8
  5.7 0.0 collective-permute-start.13
  5.7 0.0 copy-start.5
  5.7 0.0 copy-start.4
  5.8 0.6 collective-permute-start.2
  6.3 0.5 broadcast.92
  6.8 0.7 %reduce.3 = s32[8]{0:T(128)S(1)} reduce(s32[1,8]{1,0:T(1,128)S(1)} %copy-done.5, s32[]{:T(128)} %broadcast.92), dimensions={0}, to_apply=%param.12.reduce_sub_computation.3 | reduce | bytes 68 | tf_op args[5]
  7.5 0.1 concatenate.19
  7.6 0.1 concatenate.15
  7.7 0.1 fusion.5
  7.8 0.0 collective-permute-start
  8.7 0.0 copy-start.2
  9.1 0.1 pad_add_fusion.9.index_ref
  9.2 0.1 and_select_fusion
  9.3 0.1 pad_add_fusion.8.index_ref
  9.4 0.1 pad_add_fusion.7.index_ref
  9.5 0.0 collective-permute-done
  9.5 2.0 %collective-permute-start.1 = (s32[2,4,17]{2,1,0:T(4,128)S(1)}, s32[2,4,17]{2,1,0:T(4,128)S(1)}, u32[]{:S(2)}, u32[]{:S(2)}) collective-permute-start(s32[2,4,17]{2,1,0:T(4,128)S(1)} %pad_add_fusion.3), channel_id=1, source_target_pairs={{0,1},{1,0},{2,3},{3,2},{4,5},{5,4},{6,7},{7,6},{8,9},{9,8},{10,11... | collective-permute-start | bytes 1640 | tf_op jit(solution)/shard_map/ppermute | solution.py:63
  11.5 0.1 pad_add_fusion.6.index_ref
  11.6 0.1 copy.17
  11.7 1.4 %collective-permute-done.1 = s32[2,4,17]{2,1,0:T(4,128)S(1)} collective-permute-done((s32[2,4,17]{2,1,0:T(4,128)S(1)}, s32[2,4,17]{2,1,0:T(4,128)S(1)}, u32[]{:S(2)}, u32[]{:S(2)}) %collective-permute-start.1) | collective-permute-done | bytes 576 | tf_op jit(solution)/shard_map/ppermute | solution.py:63
  13.2 0.0 collective-permute-start.11
  13.2 2.1 %collective-permute-start.5 = (bf16[1024,128]{1,0:T(8,128)(2,1)S(1)}, bf16[1024,128]{1,0:T(8,128)(2,1)S(1)}, u32[]{:S(2)}, u32[]{:S(2)}) collective-permute-start(bf16[1024,128]{1,0:T(8,128)(2,1)S(1)} %collective-permute-done.4.refs_0_), channel_id=1, source_target_pairs={{0,8},{2,10},{8,16},{10,18},{16,24},{18,26},{24,28},{26,30},{28,20... | collective-permute-start | bytes 786440 | tf_op jit(solution)/shard_map/ppermute | solution.py:35
  15.3 1.6 %collective-permute-start.3 = (s16[2,4,8,16,128]{4,3,2,1,0:T(8,128)(2,1)S(1)}, s16[2,4,8,16,128]{4,3,2,1,0:T(8,128)(2,1)S(1)}, u32[]{:S(2)}, u32[]{:S(2)}) collective-permute-start(s16[2,4,8,16,128]{4,3,2,1,0:T(8,128)(2,1)S(1)} %pad_add_fusion.1), channel_id=1, source_target_pairs={{0,1},{1,0},{2,3},{3,2},{4,5},{5,4},{6,7},{7,6},{8,9},{9,8},{10,11... | collective-permute-start | bytes 786440 | tf_op jit(solution)/shard_map/ppermute | solution.py:63
  16.9 0.1 reshape_squeeze.7.fact_a
  16.9 0.1 reshape_squeeze.8.fact_b
  17.0 0.5 collective-permute-start.9
  17.5 4.6 %collective-permute-done.5.refs_0_ = bf16[1024,128]{1,0:T(8,128)(2,1)S(1)} collective-permute-done((bf16[1024,128]{1,0:T(8,128)(2,1)S(1)}, bf16[1024,128]{1,0:T(8,128)(2,1)S(1)}, u32[]{:S(2)}, u32[]{:S(2)}) %collective-permute-start.5) | collective-permute-done | bytes 262176 | tf_op jit(solution)/shard_map/ppermute | solution.py:35
  22.1 1.8 %collective-permute-start.6 = (bf16[1024,128]{1,0:T(8,128)(2,1)S(1)}, bf16[1024,128]{1,0:T(8,128)(2,1)S(1)}, u32[]{:S(2)}, u32[]{:S(2)}) collective-permute-start(bf16[1024,128]{1,0:T(8,128)(2,1)S(1)} %collective-permute-done.5.refs_0_), channel_id=1, source_target_pairs={{0,8},{2,10},{8,16},{10,18},{16,24},{18,26},{24,28},{26,30},{28,20... | collective-permute-start | bytes 786440 | tf_op jit(solution)/shard_map/ppermute | solution.py:35
  24.0 0.1 fusion.9
  24.0 1.6 %collective-permute-start.12 = (bf16[2,256,512]{2,1,0:T(8,128)(2,1)S(1)}, bf16[2,256,512]{2,1,0:T(8,128)(2,1)S(1)}, u32[]{:S(2)}, u32[]{:S(2)}) collective-permute-start(bf16[2,256,512]{2,1,0:T(8,128)(2,1)S(1)} %get-tuple-element.11), channel_id=1, source_target_pairs={{0,1},{1,0},{2,3},{3,2},{4,5},{5,4},{6,7},{7,6},{8,9},{9,8},{10,11... | collective-permute-start | bytes 1572872 | tf_op jit(solution)/shard_map/ppermute | solution.py:63
  25.7 0.5 collective-permute-start.10
  26.2 4.0 %collective-permute-done.6.refs_0_ = bf16[1024,128]{1,0:T(8,128)(2,1)S(1)} collective-permute-done((bf16[1024,128]{1,0:T(8,128)(2,1)S(1)}, bf16[1024,128]{1,0:T(8,128)(2,1)S(1)}, u32[]{:S(2)}, u32[]{:S(2)}) %collective-permute-start.6) | collective-permute-done | bytes 262176 | tf_op jit(solution)/shard_map/ppermute | solution.py:35
  30.2 1.7 %collective-permute-start.7 = (bf16[1024,128]{1,0:T(8,128)(2,1)S(1)}, bf16[1024,128]{1,0:T(8,128)(2,1)S(1)}, u32[]{:S(2)}, u32[]{:S(2)}) collective-permute-start(bf16[1024,128]{1,0:T(8,128)(2,1)S(1)} %collective-permute-done.6.refs_0_), channel_id=1, source_target_pairs={{0,8},{2,10},{8,16},{10,18},{16,24},{18,26},{24,28},{26,30},{28,20... | collective-permute-start | bytes 786440 | tf_op jit(solution)/shard_map/ppermute | solution.py:35
  31.9 1.0 %add_step.4.refs_2_ = f32[2,1024,128]{2,1,0:T(8,128)S(1)} custom-call(s32[2]{0:T(128)S(1)} %pad_add_fusion.9.index_ref, s32[136]{0:T(256)S(1)} %reshape_squeeze.7.fact_a, s32[136]{0:T(256)S(1)} %reshape_squeeze.8.fact_b, s16[8,8,16,128]{3,2,1,0:T(8,128)(2,1)S(1)} %get-tuple-element.13.words_a, s16[8,8,16,128]{3,2,1,0:T(8,128)(2,1)S(1)} %get-tuple-element.12.words_b, ...), custom_call_target="tpu_custom_call" | custom-call | flops 67108864 | bytes 4194304 | tf_op jit(solution)/shard_map/add_step/pallas_call | solution.py:196
  33.0 1.4 %add_step.5.refs_2_ = f32[2,1024,128]{2,1,0:T(8,128)S(1)} custom-call(s32[4]{0:T(128)S(1)} %pad_add_fusion.8.index_ref, s32[136]{0:T(256)S(1)} %reshape_squeeze.7.fact_a, s32[136]{0:T(256)S(1)} %reshape_squeeze.8.fact_b, s16[8,8,16,128]{3,2,1,0:T(8,128)(2,1)S(1)} %get-tuple-element.13.words_a, ...), custom_call_target="tpu_custom_call", output_to_operand_aliasing={{}: (7, {})} | custom-call | flops 134217728 | bytes 4194304 | tf_op jit(solution)/shard_map/add_step/pallas_call | solution.py:196
  34.4 1.4 %add_step.6.refs_2_ = f32[2,1024,128]{2,1,0:T(8,128)S(1)} custom-call(s32[4]{0:T(128)S(1)} %pad_add_fusion.7.index_ref, s32[136]{0:T(256)S(1)} %reshape_squeeze.7.fact_a, s32[136]{0:T(256)S(1)} %reshape_squeeze.8.fact_b, s16[8,8,16,128]{3,2,1,0:T(8,128)(2,1)S(1)} %get-tuple-element.13.words_a, ...), custom_call_target="tpu_custom_call", output_to_operand_aliasing={{}: (7, {})} | custom-call | flops 134217728 | bytes 4194304 | tf_op jit(solution)/shard_map/add_step/pallas_call | solution.py:196
  35.8 1.4 %add_step.7.sums_in = f32[2,1024,128]{2,1,0:T(8,128)S(1)} custom-call(s32[4]{0:T(128)S(1)} %pad_add_fusion.6.index_ref, s32[136]{0:T(256)S(1)} %reshape_squeeze.7.fact_a, s32[136]{0:T(256)S(1)} %reshape_squeeze.8.fact_b, s16[8,8,16,128]{3,2,1,0:T(8,128)(2,1)S(1)} %get-tuple-element.13.words_a, ...), custom_call_target="tpu_custom_call", output_to_operand_aliasing={{}: (7, {})} | custom-call | flops 134217728 | bytes 4194304 | tf_op jit(solution)/shard_map/add_step/pallas_call | solution.py:196
  37.3 0.1 collective-permute-done.12
  37.4 0.1 pad_maximum_fusion.features_ref
  37.5 0.3 broadcast_in_dim.4.roots_ref
  37.8 1.5 %last_step.1 = (f32[1024,128]{1,0:T(8,128)S(1)}, f32[1024,128]{1,0:T(8,128)S(1)}, bf16[256,128]{1,0:T(8,128)(2,1)S(1)}) custom-call(s32[2]{0:T(128)S(1)} %get-tuple-element.21.index_ref, s32[2]{0:T(128)S(1)} %get-tuple-element.20.order_ref, s32[136]{0:T(256)S(1)} %reshape_squeeze.7.fact_a, s32[136]{0:T(256)S(1)} %reshape_squeeze.8.fact_b, ...), custom_call_target="tpu_custom_call" | custom-call | tf_op jit(solution)/shard_map/last_step/pallas_call | solution.py:218
  39.3 2.7 %collective-permute-start.16 = (bf16[256,128]{1,0:T(8,128)(2,1)S(1)}, bf16[256,128]{1,0:T(8,128)(2,1)S(1)}, u32[]{:S(2)}, u32[]{:S(2)}) collective-permute-start(bf16[256,128]{1,0:T(8,128)(2,1)S(1)} %get-tuple-element.7), channel_id=1, source_target_pairs={{0,16},{2,18},{4,20},{6,22},{8,24},{10,26},{12,28},{14,30},{16,0},... | collective-permute-start | bytes 196616 | tf_op jit(solution)/shard_map/ppermute | solution.py:44
  42.0 1.5 %collective-permute-start.17 = (bf16[256,128]{1,0:T(8,128)(2,1)S(1)}, bf16[256,128]{1,0:T(8,128)(2,1)S(1)}, u32[]{:S(2)}, u32[]{:S(2)}) collective-permute-start(bf16[256,128]{1,0:T(8,128)(2,1)S(1)} %get-tuple-element.7), channel_id=1, source_target_pairs={{0,8},{2,10},{4,12},{6,14},{8,16},{10,18},{12,20},{14,22},{16,24},... | collective-permute-start | bytes 196616 | tf_op jit(solution)/shard_map/ppermute | solution.py:44
  43.5 2.3 %collective-permute-start.18 = (bf16[256,128]{1,0:T(8,128)(2,1)S(1)}, bf16[256,128]{1,0:T(8,128)(2,1)S(1)}, u32[]{:S(2)}, u32[]{:S(2)}) collective-permute-start(bf16[256,128]{1,0:T(8,128)(2,1)S(1)} %get-tuple-element.7), channel_id=1, source_target_pairs={{0,24},{2,26},{4,28},{6,30},{8,0},{10,2},{12,4},{14,6},{16,8},{18,... | collective-permute-start | bytes 196616 | tf_op jit(solution)/shard_map/ppermute | solution.py:44
  45.8 0.8 %collective-permute-done.16 = bf16[256,128]{1,0:T(8,128)(2,1)S(1)} collective-permute-done((bf16[256,128]{1,0:T(8,128)(2,1)S(1)}, bf16[256,128]{1,0:T(8,128)(2,1)S(1)}, u32[]{:S(2)}, u32[]{:S(2)}) %collective-permute-start.16) | collective-permute-done | bytes 65568 | tf_op jit(solution)/shard_map/ppermute | solution.py:44
  46.5 1.6 %collective-permute-done.17 = bf16[256,128]{1,0:T(8,128)(2,1)S(1)} collective-permute-done((bf16[256,128]{1,0:T(8,128)(2,1)S(1)}, bf16[256,128]{1,0:T(8,128)(2,1)S(1)}, u32[]{:S(2)}, u32[]{:S(2)}) %collective-permute-start.17) | collective-permute-done | bytes 65568 | tf_op jit(solution)/shard_map/ppermute | solution.py:44
  48.1 0.3 collective-permute-done.18
  48.5 1.5 %collective-permute-start.19 = (bf16[256,128]{1,0:T(8,128)(2,1)S(1)}, bf16[256,128]{1,0:T(8,128)(2,1)S(1)}, u32[]{:S(2)}, u32[]{:S(2)}) collective-permute-start(bf16[256,128]{1,0:T(8,128)(2,1)S(1)} %add_convert_fusion), channel_id=1, source_target_pairs={{0,4},{2,6},{4,0},{6,2},{8,12},{10,14},{12,8},{14,10},{16,20},{18,... | collective-permute-start | bytes 196616 | tf_op jit(solution)/shard_map/ppermute | solution.py:51
  50.0 2.8 %collective-permute-done.19 = bf16[256,128]{1,0:T(8,128)(2,1)S(1)} collective-permute-done((bf16[256,128]{1,0:T(8,128)(2,1)S(1)}, bf16[256,128]{1,0:T(8,128)(2,1)S(1)}, u32[]{:S(2)}, u32[]{:S(2)}) %collective-permute-start.19) | collective-permute-done | bytes 65568 | tf_op jit(solution)/shard_map/ppermute | solution.py:51
  52.8 0.1 collective-permute-start.20
  52.9 1.3 %collective-permute-done.20 = f32[256,128]{1,0:T(8,128)S(1)} collective-permute-done((f32[256,128]{1,0:T(8,128)S(1)}, f32[256,128]{1,0:T(8,128)S(1)}, u32[]{:S(2)}, u32[]{:S(2)}) %collective-permute-start.20) | collective-permute-done | bytes 131104 | tf_op jit(solution)/shard_map/ppermute | solution.py:58
  54.3 1.6 %collective-permute-start.21 = (f32[256,128]{1,0:T(8,128)S(1)}, f32[256,128]{1,0:T(8,128)S(1)}, u32[]{:S(2)}, u32[]{:S(2)}) collective-permute-start(f32[256,128]{1,0:T(8,128)S(1)} %get-tuple-element.9), channel_id=1, source_target_pairs={{0,1},{1,0},{2,3},{3,2},{4,5},{5,4},{6,7},{7,6},{8,9},{9,8},{10,11... | collective-permute-start | bytes 393224 | tf_op jit(solution)/shard_map/ppermute | solution.py:63
  55.9 0.2 multiply_convert_fusion
  56.1 0.6 collective-permute-start.15
  56.7 4.0 %collective-permute-done.21 = f32[256,128]{1,0:T(8,128)S(1)} collective-permute-done((f32[256,128]{1,0:T(8,128)S(1)}, f32[256,128]{1,0:T(8,128)S(1)}, u32[]{:S(2)}, u32[]{:S(2)}) %collective-permute-start.21) | collective-permute-done | bytes 131104 | tf_op jit(solution)/shard_map/ppermute | solution.py:63
  60.7 0.0 copy-start.3
  60.7 2.0 %collective-permute-done.15 = bf16[512,128]{1,0:T(8,128)(2,1)S(1)} collective-permute-done((bf16[512,128]{1,0:T(8,128)(2,1)S(1)}, bf16[512,128]{1,0:T(8,128)(2,1)S(1)}, u32[]{:S(2)}, u32[]{:S(2)}) %collective-permute-start.15) | collective-permute-done | bytes 131104 | tf_op jit(solution)/shard_map/ppermute | solution.py:63
  62.7 0.2 fusion.2
  63.0 0.9 %fusion = bf16[512,256]{1,0:T(8,128)(2,1)} fusion(f32[512,256]{1,0:T(8,128)S(1)} %fusion.2, bf16[1024,128]{1,0:T(8,128)(2,1)S(1)} %multiply_convert_fusion, s32[]{:T(128)S(6)} %select_n.466, bf16[256,256]{1,0:T(8,128)(2,1)S(1)} %copy-done, s32[]{:T(128)S(6)} %select_n.467), kind=kOutput, calls=%fused_computation.1 | convolution fusion | flops 33816576 | bytes 983048 | tf_op jit(solution)/shard_map/dot_general | solution.py:252
  (33 shorter events, 0.4 us)
Async XLA Ops:
  0.6 62.1 %copy-start = (bf16[256,256]{1,0:T(8,128)(2,1)S(1)}, bf16[256,256]{1,0:T(8,128)(2,1)}, u32[]{:S(2)}) copy-start(bf16[256,256]{1,0:T(8,128)(2,1)} %param.9) | copy-start | bytes 393220
  0.6 5.0 %copy-start.1 = (s32[1,8,8,16,128]{4,3,2,1,0:T(8,128)S(1)}, s32[1,8,8,16,128]{4,3,2,1,0:T(8,128)}, u32[]{:S(2)}) copy-start(s32[1,8,8,16,128]{4,3,2,1,0:T(8,128)} %param.10) | copy-start | bytes 1572868
  2.6 10.6 %collective-permute-start.4 = (bf16[1024,128]{1,0:T(8,128)(2,1)S(1)}, bf16[1024,128]{1,0:T(8,128)(2,1)S(1)}, u32[]{:S(2)}, u32[]{:S(2)}) collective-permute-start(bf16[1024,128]{1,0:T(8,128)(2,1)S(1)} %multiply_convert_fusion.1.refs_0_), channel_id=1, source_target_pairs={{0,8},{2,10},{8,16},{10,18},{16,24},{18,26},{24,28},{26,30},{28,20... | collective-permute-start | bytes 786440 | tf_op jit(solution)/shard_map/ppermute | solution.py:35
  5.6 11.4 %collective-permute-start.8 = (bf16[1024,128]{1,0:T(8,128)(2,1)S(1)}, bf16[1024,128]{1,0:T(8,128)(2,1)S(1)}, u32[]{:S(2)}, u32[]{:S(2)}) collective-permute-start(bf16[1024,128]{1,0:T(8,128)(2,1)S(1)} %multiply_convert_fusion.1.refs_0_), channel_id=1, source_target_pairs={{0,4},{2,6},{8,0},{10,2},{16,8},{18,10},{24,16},{26,18},{28,24},{3... | collective-permute-start | bytes 786440 | tf_op jit(solution)/shard_map/ppermute | solution.py:35
  5.7 20.0 %collective-permute-start.13 = (f32[1024]{0:T(1024)S(1)}, f32[1024]{0:T(1024)S(1)}, u32[]{:S(2)}, u32[]{:S(2)}) collective-permute-start(f32[1024]{0:T(1024)S(1)} %convert_rsqrt_fusion), channel_id=1, source_target_pairs={{0,2},{2,0},{4,6},{6,4},{8,10},{10,8},{12,14},{14,12},{16,18},{18,... | collective-permute-start | bytes 12296 | tf_op jit(solution)/shard_map/ppermute | solution.py:58
  5.7 1.1 %copy-start.5 = (s32[1,8]{1,0:T(1,128)S(1)}, s32[1,8]{1,0:T(1,128)}, u32[]{:S(2)}) copy-start(s32[1,8]{1,0:T(1,128)} %param.12) | copy-start | bytes 100
  5.7 1.8 %copy-start.4 = (s32[1,8,2,8]{3,2,1,0:T(2,128)S(1)}, s32[1,8,2,8]{3,2,1,0:T(2,128)}, u32[]{:S(2)}) copy-start(s32[1,8,2,8]{3,2,1,0:T(2,128)} %param.11) | copy-start | bytes 1540
  5.8 9.5 %collective-permute-start.2 = (s16[4,8,16,128]{3,2,1,0:T(8,128)(2,1)S(1)}, s16[4,8,16,128]{3,2,1,0:T(8,128)(2,1)S(1)}, u32[]{:S(2)}, u32[]{:S(2)}) collective-permute-start(s16[4,8,16,128]{3,2,1,0:T(8,128)(2,1)S(1)} %get-tuple-element.15), channel_id=1, source_target_pairs={{0,2},{2,0},{4,6},{6,4},{8,10},{10,8},{12,14},{14,12},{16,18},{18,... | collective-permute-start | bytes 393224 | tf_op jit(solution)/shard_map/ppermute | solution.py:58
  7.8 1.7 %collective-permute-start = (s32[4,17]{1,0:T(4,128)S(1)}, s32[4,17]{1,0:T(4,128)S(1)}, u32[]{:S(2)}, u32[]{:S(2)}) collective-permute-start(s32[4,17]{1,0:T(4,128)S(1)} %bitcast.56), channel_id=1, source_target_pairs={{0,2},{2,0},{4,6},{6,4},{8,10},{10,8},{12,14},{14,12},{16,18},{18,... | collective-permute-start | bytes 824 | tf_op jit(solution)/shard_map/ppermute | solution.py:58
  8.7 2.9 %copy-start.2 = (bf16[512,256]{1,0:T(8,128)(2,1)S(1)}, bf16[512,256]{1,0:T(8,128)(2,1)}, u32[]{:S(2)}) copy-start(bf16[512,256]{1,0:T(8,128)(2,1)} %param.7) | copy-start | bytes 786436
  9.5 3.7 %collective-permute-start.1 = (s32[2,4,17]{2,1,0:T(4,128)S(1)}, s32[2,4,17]{2,1,0:T(4,128)S(1)}, u32[]{:S(2)}, u32[]{:S(2)}) collective-permute-start(s32[2,4,17]{2,1,0:T(4,128)S(1)} %pad_add_fusion.3), channel_id=1, source_target_pairs={{0,1},{1,0},{2,3},{3,2},{4,5},{5,4},{6,7},{7,6},{8,9},{9,8},{10,11... | collective-permute-start | bytes 1640 | tf_op jit(solution)/shard_map/ppermute | solution.py:63
  13.2 10.8 %collective-permute-start.11 = (bf16[256,512]{1,0:T(8,128)(2,1)S(1)}, bf16[256,512]{1,0:T(8,128)(2,1)S(1)}, u32[]{:S(2)}, u32[]{:S(2)}) collective-permute-start(bf16[256,512]{1,0:T(8,128)(2,1)S(1)} %bitcast.44), channel_id=1, source_target_pairs={{0,2},{2,0},{4,6},{6,4},{8,10},{10,8},{12,14},{14,12},{16,18},{18,... | collective-permute-start | bytes 786440 | tf_op jit(solution)/shard_map/ppermute | solution.py:58
  13.2 9.0 %collective-permute-start.5 = (bf16[1024,128]{1,0:T(8,128)(2,1)S(1)}, bf16[1024,128]{1,0:T(8,128)(2,1)S(1)}, u32[]{:S(2)}, u32[]{:S(2)}) collective-permute-start(bf16[1024,128]{1,0:T(8,128)(2,1)S(1)} %collective-permute-done.4.refs_0_), channel_id=1, source_target_pairs={{0,8},{2,10},{8,16},{10,18},{16,24},{18,26},{24,28},{26,30},{28,20... | collective-permute-start | bytes 786440 | tf_op jit(solution)/shard_map/ppermute | solution.py:35
  15.3 10.4 %collective-permute-start.3 = (s16[2,4,8,16,128]{4,3,2,1,0:T(8,128)(2,1)S(1)}, s16[2,4,8,16,128]{4,3,2,1,0:T(8,128)(2,1)S(1)}, u32[]{:S(2)}, u32[]{:S(2)}) collective-permute-start(s16[2,4,8,16,128]{4,3,2,1,0:T(8,128)(2,1)S(1)} %pad_add_fusion.1), channel_id=1, source_target_pairs={{0,1},{1,0},{2,3},{3,2},{4,5},{5,4},{6,7},{7,6},{8,9},{9,8},{10,11... | collective-permute-start | bytes 786440 | tf_op jit(solution)/shard_map/ppermute | solution.py:63
  17.0 8.7 %collective-permute-start.9 = (bf16[1024,128]{1,0:T(8,128)(2,1)S(1)}, bf16[1024,128]{1,0:T(8,128)(2,1)S(1)}, u32[]{:S(2)}, u32[]{:S(2)}) collective-permute-start(bf16[1024,128]{1,0:T(8,128)(2,1)S(1)} %collective-permute-done.8.refs_1_), channel_id=1, source_target_pairs={{0,4},{2,6},{8,0},{10,2},{16,8},{18,10},{24,16},{26,18},{28,24},{3... | collective-permute-start | bytes 786440 | tf_op jit(solution)/shard_map/ppermute | solution.py:35
  22.1 8.1 %collective-permute-start.6 = (bf16[1024,128]{1,0:T(8,128)(2,1)S(1)}, bf16[1024,128]{1,0:T(8,128)(2,1)S(1)}, u32[]{:S(2)}, u32[]{:S(2)}) collective-permute-start(bf16[1024,128]{1,0:T(8,128)(2,1)S(1)} %collective-permute-done.5.refs_0_), channel_id=1, source_target_pairs={{0,8},{2,10},{8,16},{10,18},{16,24},{18,26},{24,28},{26,30},{28,20... | collective-permute-start | bytes 786440 | tf_op jit(solution)/shard_map/ppermute | solution.py:35
  24.0 13.3 %collective-permute-start.12 = (bf16[2,256,512]{2,1,0:T(8,128)(2,1)S(1)}, bf16[2,256,512]{2,1,0:T(8,128)(2,1)S(1)}, u32[]{:S(2)}, u32[]{:S(2)}) collective-permute-start(bf16[2,256,512]{2,1,0:T(8,128)(2,1)S(1)} %get-tuple-element.11), channel_id=1, source_target_pairs={{0,1},{1,0},{2,3},{3,2},{4,5},{5,4},{6,7},{7,6},{8,9},{9,8},{10,11... | collective-permute-start | bytes 1572872 | tf_op jit(solution)/shard_map/ppermute | solution.py:63
  25.7 10.1 %collective-permute-start.10 = (bf16[1024,128]{1,0:T(8,128)(2,1)S(1)}, bf16[1024,128]{1,0:T(8,128)(2,1)S(1)}, u32[]{:S(2)}, u32[]{:S(2)}) collective-permute-start(bf16[1024,128]{1,0:T(8,128)(2,1)S(1)} %collective-permute-done.9.refs_1_), channel_id=1, source_target_pairs={{0,4},{2,6},{8,0},{10,2},{16,8},{18,10},{24,16},{26,18},{28,24},{3... | collective-permute-start | bytes 786440 | tf_op jit(solution)/shard_map/ppermute | solution.py:35
  30.2 7.3 %collective-permute-start.7 = (bf16[1024,128]{1,0:T(8,128)(2,1)S(1)}, bf16[1024,128]{1,0:T(8,128)(2,1)S(1)}, u32[]{:S(2)}, u32[]{:S(2)}) collective-permute-start(bf16[1024,128]{1,0:T(8,128)(2,1)S(1)} %collective-permute-done.6.refs_0_), channel_id=1, source_target_pairs={{0,8},{2,10},{8,16},{10,18},{16,24},{18,26},{24,28},{26,30},{28,20... | collective-permute-start | bytes 786440 | tf_op jit(solution)/shard_map/ppermute | solution.py:35
  39.3 7.2 %collective-permute-start.16 = (bf16[256,128]{1,0:T(8,128)(2,1)S(1)}, bf16[256,128]{1,0:T(8,128)(2,1)S(1)}, u32[]{:S(2)}, u32[]{:S(2)}) collective-permute-start(bf16[256,128]{1,0:T(8,128)(2,1)S(1)} %get-tuple-element.7), channel_id=1, source_target_pairs={{0,16},{2,18},{4,20},{6,22},{8,24},{10,26},{12,28},{14,30},{16,0},... | collective-permute-start | bytes 196616 | tf_op jit(solution)/shard_map/ppermute | solution.py:44
  42.0 6.2 %collective-permute-start.17 = (bf16[256,128]{1,0:T(8,128)(2,1)S(1)}, bf16[256,128]{1,0:T(8,128)(2,1)S(1)}, u32[]{:S(2)}, u32[]{:S(2)}) collective-permute-start(bf16[256,128]{1,0:T(8,128)(2,1)S(1)} %get-tuple-element.7), channel_id=1, source_target_pairs={{0,8},{2,10},{4,12},{6,14},{8,16},{10,18},{12,20},{14,22},{16,24},... | collective-permute-start | bytes 196616 | tf_op jit(solution)/shard_map/ppermute | solution.py:44
  43.5 5.0 %collective-permute-start.18 = (bf16[256,128]{1,0:T(8,128)(2,1)S(1)}, bf16[256,128]{1,0:T(8,128)(2,1)S(1)}, u32[]{:S(2)}, u32[]{:S(2)}) collective-permute-start(bf16[256,128]{1,0:T(8,128)(2,1)S(1)} %get-tuple-element.7), channel_id=1, source_target_pairs={{0,24},{2,26},{4,28},{6,30},{8,0},{10,2},{12,4},{14,6},{16,8},{18,... | collective-permute-start | bytes 196616 | tf_op jit(solution)/shard_map/ppermute | solution.py:44
  48.5 4.3 %collective-permute-start.19 = (bf16[256,128]{1,0:T(8,128)(2,1)S(1)}, bf16[256,128]{1,0:T(8,128)(2,1)S(1)}, u32[]{:S(2)}, u32[]{:S(2)}) collective-permute-start(bf16[256,128]{1,0:T(8,128)(2,1)S(1)} %add_convert_fusion), channel_id=1, source_target_pairs={{0,4},{2,6},{4,0},{6,2},{8,12},{10,14},{12,8},{14,10},{16,20},{18,... | collective-permute-start | bytes 196616 | tf_op jit(solution)/shard_map/ppermute | solution.py:51
  50.0 5.9 %collective-permute-start.14 = (f32[1024,128]{1,0:T(8,128)S(1)}, f32[1024,128]{1,0:T(8,128)S(1)}, u32[]{:S(2)}, u32[]{:S(2)}) collective-permute-start(f32[1024,128]{1,0:T(8,128)S(1)} %get-tuple-element.6), channel_id=1, source_target_pairs={{0,2},{2,0},{4,6},{6,4},{8,10},{10,8},{12,14},{14,12},{16,18},{18,... | collective-permute-start | bytes 1572872 | tf_op jit(solution)/shard_map/ppermute | solution.py:58
  52.8 1.4 %collective-permute-start.20 = (f32[256,128]{1,0:T(8,128)S(1)}, f32[256,128]{1,0:T(8,128)S(1)}, u32[]{:S(2)}, u32[]{:S(2)}) collective-permute-start(f32[256,128]{1,0:T(8,128)S(1)} %convert_add_fusion), channel_id=1, source_target_pairs={{0,2},{2,0},{4,6},{6,4},{8,10},{10,8},{12,14},{14,12},{16,18},{18,... | collective-permute-start | bytes 393224 | tf_op jit(solution)/shard_map/ppermute | solution.py:58
  54.3 6.4 %collective-permute-start.21 = (f32[256,128]{1,0:T(8,128)S(1)}, f32[256,128]{1,0:T(8,128)S(1)}, u32[]{:S(2)}, u32[]{:S(2)}) collective-permute-start(f32[256,128]{1,0:T(8,128)S(1)} %get-tuple-element.9), channel_id=1, source_target_pairs={{0,1},{1,0},{2,3},{3,2},{4,5},{5,4},{6,7},{7,6},{8,9},{9,8},{10,11... | collective-permute-start | bytes 393224 | tf_op jit(solution)/shard_map/ppermute | solution.py:63
  56.1 6.6 %collective-permute-start.15 = (bf16[512,128]{1,0:T(8,128)(2,1)S(1)}, bf16[512,128]{1,0:T(8,128)(2,1)S(1)}, u32[]{:S(2)}, u32[]{:S(2)}) collective-permute-start(bf16[512,128]{1,0:T(8,128)(2,1)S(1)} %constant_dynamic-slice_fusion), channel_id=1, source_target_pairs={{0,1},{1,0},{2,3},{3,2},{4,5},{5,4},{6,7},{7,6},{8,9},{9,8},{10,11... | collective-permute-start | bytes 393224 | tf_op jit(solution)/shard_map/ppermute | solution.py:63
  60.7 2.2 %copy-start.3 = (f32[256,256]{1,0:T(8,128)}, f32[256,256]{1,0:T(8,128)S(1)}, u32[]{:S(2)}) copy-start(f32[256,256]{1,0:T(8,128)S(1)} %constant_dynamic-update-slice_fusion) | copy-start | bytes 786436

commit v2 on v1

--- a/solution.py
+++ b/solution.py
@@ -35,10 +35,9 @@
     return lax.ppermute(block, "blk", route)
 
 
-def along_rows(block, distance):
-    rows = lax.axis_size("blk") // (COLUMNS * CORES)
+def across_rows(block, distance):
     route = [
-        (device_of(z, x, c), device_of((z + distance) % rows, x, c))
+        (device_of(z, x, c), device_of(z ^ distance, x, c))
         for z, x, c in places(lax.axis_size("blk"))
     ]
     return lax.ppermute(block, "blk", route)
@@ -63,15 +62,18 @@
     return lax.ppermute(block, "rep", [(i, (i + distance) % size) for i in range(size)])
 
 
+def across_columns_and_rep(block, distance):
+    size = lax.axis_size("rep")
+    route = [
+        (device_of(z, x, c) * size + r, device_of(z, 1 - x, c) * size + (r + distance) % size)
+        for z, x, c in places(lax.axis_size("blk"))
+        for r in range(size)
+    ]
+    return lax.ppermute(block, ("blk", "rep"), route)
+
+
 def from_all_reps(block):
     return [block] + [along_rep(block, d) for d in range(1, lax.axis_size("rep"))]
-
-
-def tree_sum(terms):
-    while len(terms) > 1:
-        half = len(terms) // 2
-        terms = [terms[d] + terms[d + half] for d in range(half)]
-    return terms[0]
 
 
 def add_pairs(index_ref, facts, words, slabs, sums_ref, slot_total):
@@ -86,7 +88,8 @@
                 row_block = facts[target][base + 1 + slot]
                 column_block = facts[target][base + 1 + slot_total + slot]
                 live = jnp.where(slot < live_count, 255, 0)
-                slot_words = jnp.bitwise_and(words[target][pair, slot].astype(jnp.int32), live)
+                slot_words = words[target][pair, slot * 16 : slot * 16 + 16, :].astype(jnp.int32)
+                slot_words = jnp.bitwise_and(slot_words, live)
                 bits = jnp.bitwise_and(jnp.right_shift(slot_words[:, None, :], bit_ids), 1)
                 transposed = bits.reshape(128, 128).astype(jnp.float32).astype(jnp.bfloat16)
                 rows = pl.ds(pl.multiple_of(row_block * 128, 128), 128)
@@ -96,32 +99,46 @@
                 )
 
 
-def step_kernel(slab_total, slot_total, first, index_ref, fact_a, fact_b, words_a, words_b, *refs):
-    slabs = refs[:slab_total]
-    sums_ref = refs[-1]
+def fill(slab_buffer, halves):
+    half = slab_buffer.shape[1] // 2
+    for slab_id in range(len(halves) // 2):
+        slab_buffer[slab_id, :half, :] = halves[2 * slab_id][...]
+        slab_buffer[slab_id, half:, :] = halves[2 * slab_id + 1][...]
+    return [slab_buffer.at[slab_id] for slab_id in range(len(halves) // 2)]
+
+
+def step_kernel(half_total, slot_total, first, index_ref, fact_a, fact_b, words_a, words_b, *refs):
+    halves, sums_ref, slab_buffer = refs[:half_total], refs[-2], refs[-1]
     if first:
         sums_ref[...] = jnp.zeros_like(sums_ref)
     else:
-        sums_ref[...] = refs[slab_total][...]
+        sums_ref[...] = refs[half_total][...]
+    slabs = fill(slab_buffer, halves)
     add_pairs(index_ref, (fact_a, fact_b), (words_a, words_b), slabs, sums_ref, slot_total)
 
 
 def last_kernel(
-    slot_total, rep_size, index_ref, order_ref, fact_a, fact_b, words_a, words_b, slab_ref, sums_in,
-    features_ref, roots_ref, own_ref, other_ref, term_ref, sums_ref,
+    slot_total, rep_size, index_ref, order_ref, fact_a, fact_b, words_a, words_b, low_ref, high_ref,
+    sums_in, own_features, other_features, own_ref, other_ref, keep_ref, send_ref,
+    sums_ref, term_ref, slab_buffer,
 ):
     sums_ref[...] = sums_in[...]
-    add_pairs(index_ref, (fact_a, fact_b), (words_a, words_b), [slab_ref], sums_ref, slot_total)
+    slabs = fill(slab_buffer, [low_ref, high_ref])
+    add_pairs(index_ref, (fact_a, fact_b), (words_a, words_b), slabs, sums_ref, slot_total)
     own_ref[...] = sums_ref[0]
     other_ref[...] = sums_ref[1]
     share = sums_ref.shape[1] // rep_size
     term = jnp.zeros(term_ref.shape, jnp.float32)
-    for target in range(2):
+    for target, features_ref in enumerate((own_features, other_features)):
         for d in range(rep_size):
             rows = pl.ds(pl.multiple_of(order_ref[d] * share, share), share)
-            part = (sums_ref[target, rows, :] * roots_ref[target, rows, :]).astype(jnp.bfloat16)
-            term += jnp.dot(features_ref[d, target], part, preferred_element_type=jnp.float32)
-    term_ref[...] = term.astype(term_ref.dtype)
+            part = sums_ref[target, rows, :].astype(jnp.bfloat16)
+            term += jnp.dot(features_ref[d], part, preferred_element_type=jnp.float32)
+    term_ref[...] = term
+    half = term_ref.shape[0] // 2
+    core = order_ref[rep_size]
+    keep_ref[...] = term_ref[pl.ds(pl.multiple_of(core * half, half), half), :]
+    send_ref[...] = term_ref[pl.ds(pl.multiple_of((1 - core) * half, half), half), :]
 
 
 SMEM = pl.BlockSpec(memory_space=pltpu.SMEM)
@@ -148,22 +165,27 @@
     own_columns = lax.dynamic_slice_in_dim(out_grad, rep_index * share_width, share_width, 1)
     scaled = (own_columns.astype(jnp.float32) * inverse_root[:, None]).astype(jnp.bfloat16)
 
-    words = block_words[0].astype(jnp.int16).reshape(half_steps, 2, slot_total, 16, 128)
+    step_total = 2 * half_steps
     facts = jnp.concatenate(
-        [block_counts[0][:, None], block_coords[0].reshape(2 * half_steps, 2 * slot_total)], axis=1
-    ).reshape(half_steps, 2, 1 + 2 * slot_total)
-    words = jnp.stack([words[:, 0], across_cores(words[:, 1])])
-    facts = jnp.stack([facts[:, 0], across_cores(facts[:, 1])])
-    words = jnp.concatenate(from_all_reps(words), axis=1)
-    facts = jnp.concatenate(from_all_reps(facts), axis=1)
-    words_a, words_b = words[0], words[1]
-    fact_a, fact_b = facts[0].reshape(-1), facts[1].reshape(-1)
-
-    turned = features.T
-    turned = jnp.stack([turned, across_cores(turned)])
-    turned = jnp.stack(from_all_reps(turned))
-    roots = jnp.stack([inverse_root, across_cores(inverse_root)])
-    roots = jnp.broadcast_to(roots[:, :, None], (2, slab_rows, share_width))
+        [block_counts[0][:, None], block_coords[0].reshape(step_total, 2 * slot_total)], axis=1
+    )
+    facts = jnp.pad(facts, ((0, 0), (0, 2048 - facts.shape[1]))).reshape(step_total, 16, 128)
+    words = jnp.concatenate([block_words[0].reshape(step_total, slot_total * 16, 128), facts], axis=1)
+    words = jnp.stack(from_all_reps(words.astype(jnp.int16)))
+    words = words.reshape(rep_size, half_steps, 2, slot_total * 16 + 16, 128)
+    words_a = words[:, :, 0].reshape(rep_size * half_steps, slot_total * 16 + 16, 128)
+    words_b = across_cores(words[:, :, 1].reshape(rep_size * half_steps, slot_total * 16 + 16, 128))
+
+    def facts_of(words):
+        facts = words[:, slot_total * 16 :].reshape(-1, 2048)[:, : 1 + 2 * slot_total]
+        return facts.astype(jnp.int32).reshape(-1)
+
+    fact_a, fact_b = facts_of(words_a), facts_of(words_b)
+
+    share_root = lax.dynamic_slice_in_dim(inverse_root, rep_index * share_rows, share_rows, 0)
+    turned = (features.T.astype(jnp.float32) * share_root[None, :]).astype(jnp.bfloat16)
+    own_features = jnp.stack(from_all_reps(turned))
+    other_features = across_cores(own_features)
 
     ring_row = chip // COLUMNS
     place = jnp.where(chip % COLUMNS == 0, ring_row, chips - 1 - ring_row)
@@ -184,60 +206,81 @@
     pair_cost = 2 * slot_total * 128 * 128 * share_width * 2
     sums_shape = jax.ShapeDtypeStruct((2, slab_rows, share_width), jnp.float32)
 
-    def add_step(distances, slabs, sums):
+    def add_step(distances, halves, sums):
         first = sums is None
-        operands = [pair_indices(distances), fact_a, fact_b, words_a, words_b, *slabs]
-        specs = [SMEM] * 3 + [VMEM] * (2 + len(slabs))
+        operands = [pair_indices(distances), fact_a, fact_b, words_a, words_b, *halves]
+        specs = [SMEM] * 3 + [VMEM] * (2 + len(halves))
         aliases = {}
         if not first:
             aliases = {len(operands): 0}
             operands.append(sums)
             specs.append(VMEM)
+        slab_total = len(halves) // 2
         return pl.pallas_call(
-            functools.partial(step_kernel, len(slabs), slot_total, first),
+            functools.partial(step_kernel, len(halves), slot_total, first),
             out_shape=sums_shape,
             in_specs=specs,
             out_specs=VMEM,
             input_output_aliases=aliases,
+            scratch_shapes=[pltpu.VMEM((slab_total, slab_rows, share_width), jnp.bfloat16)],
             compiler_params=PARAMS,
             cost_estimate=pl.CostEstimate(
-                flops=pair_cost * len(slabs), bytes_accessed=4 << 20, transcendentals=0
+                flops=pair_cost * slab_total, bytes_accessed=4 << 20, transcendentals=0
             ),
             name="add_step",
         )(*operands)
 
-    sums = add_step([0], [scaled], None)
-    forward = backward = scaled
+    low, high = scaled[: slab_rows // 2], scaled[slab_rows // 2 :]
+    sums = add_step([0], [low, high], None)
+    low_up = low_down = low
+    high_up = high_down = high
     for step in range(1, chips // 2):
-        forward, backward = along_ring(forward, 1), along_ring(backward, -1)
-        sums = add_step([-step, step], [forward, backward], sums)
-    forward = along_ring(forward, 1)
-
-    order = ((rep_index - jnp.arange(rep_size, dtype=jnp.int32)) % rep_size).astype(jnp.int32)
+        low_up, high_down = along_ring(low_up, 1), along_ring(high_down, -1)
+        high_up, low_down = along_ring(high_up, 1), along_ring(low_down, -1)
+        sums = add_step([-step, step], [low_up, high_up, low_down, high_down], sums)
+    low_up, high_down = along_ring(low_up, 1), along_ring(high_down, -1)
+
+    order = (rep_index - jnp.arange(rep_size, dtype=jnp.int32)) % rep_size
+    order = jnp.concatenate([order, core[None]]).astype(jnp.int32)
     slab_shape = jax.ShapeDtypeStruct((slab_rows, share_width), jnp.float32)
-    own_sums, other_sums, term = pl.pallas_call(
+    half_term = jax.ShapeDtypeStruct((width // 2, share_width), jnp.float32)
+    own_sums, other_sums, keep, send = pl.pallas_call(
         functools.partial(last_kernel, slot_total, rep_size),
-        out_shape=(slab_shape, slab_shape, jax.ShapeDtypeStruct((width, share_width), jnp.bfloat16)),
-        in_specs=[SMEM] * 4 + [VMEM] * 6,
-        out_specs=(VMEM,) * 3,
-        scratch_shapes=[pltpu.VMEM(sums_shape.shape, jnp.float32)],
+        out_shape=(slab_shape, slab_shape, half_term, half_term),
+        in_specs=[SMEM] * 4 + [VMEM] * 7,
+        out_specs=(VMEM,) * 4,
+        scratch_shapes=[
+            pltpu.VMEM(sums_shape.shape, jnp.float32),
+            pltpu.VMEM((width, share_width), jnp.float32),
+            pltpu.VMEM((1, slab_rows, share_width), jnp.bfloat16),
+        ],
         compiler_params=PARAMS,
         name="last_step",
     )(
-        pair_indices([chips // 2]), order, fact_a, fact_b, words_a, words_b, forward, sums,
-        turned, roots,
+        pair_indices([chips // 2]), order, fact_a, fact_b, words_a, words_b, low_up, high_down, sums,
+        own_features, other_features,
     )
 
-    total = tree_sum(
-        [t.astype(jnp.float32) for t in [term] + [along_rows(term, d) for d in range(1, rows_of_chips)]]
-    ).astype(jnp.bfloat16)
-    total = total.astype(jnp.float32) + across_columns(total).astype(jnp.float32)
-    total = total + across_cores(total)
-    total = total * (1.0 / math.sqrt(slab_rows * blk_size))
-    weight_grad = jnp.zeros((width, width), jnp.float32)
-    for d, columns in enumerate(from_all_reps(total)):
+    total = keep + across_cores(send)
+    distance = 1
+    while distance < rows_of_chips:
+        total = total.astype(jnp.bfloat16)
+        total = total.astype(jnp.float32) + across_rows(total, distance).astype(jnp.float32)
+        distance *= 2
+    total = total.astype(jnp.bfloat16)
+    weight_half = jnp.zeros((width // 2, width), jnp.float32)
+    for d in range(rep_size):
+        near, far = total, across_columns(total)
+        if d:
+            near, far = along_rep(total, d), across_columns_and_rep(total, d)
+        columns = near.astype(jnp.float32) + far.astype(jnp.float32)
         at = ((rep_index - d) % rep_size) * share_width
-        weight_grad = lax.dynamic_update_slice_in_dim(weight_grad, columns, at, 1)
+        weight_half = lax.dynamic_update_slice_in_dim(weight_half, columns, at, 1)
+    weight_half = weight_half * (1.0 / math.sqrt(slab_rows * blk_size))
+    other_half = across_cores(weight_half)
+    weight_grad = jnp.concatenate(
+        [jnp.where(core == 0, weight_half, other_half), jnp.where(core == 0, other_half, weight_half)]
+    )
 
     own_sums = own_sums + across_cores(other_sums)
     aggregated = (own_sums * inverse_root[:, None]).astype(jnp.bfloat16)

time: 64.1 us -> 66.7 us (1.041)
  starting transfers between devices: 25.7 us -> 27.1 us
  local copies, waits for them, and re-layouts: 1.46 us -> 2.78 us
  Pallas kernels: 6.78 us -> 7.56 us
  other arithmetic: 3.6 us -> 2.93 us
    ppermute x7 -> x14, starting transfers between devices: 9.69 us -> 16.6 us  [along_ring(): return lax.ppermute(block, 'blk', route)]
    ppermute x3, waiting for transfers between devices: 2.63 us -> 9.38 us  [the longest x2 6.96 us: across_rows(): return lax.ppermute(block, 'blk', route)]
    ppermute x7 -> x14, waiting for transfers between devices: 8.59 us -> 4.06 us  [along_ring(): return lax.ppermute(block, 'blk', route)]
    ppermute x3, starting transfers between devices: 6.48 us -> 2.87 us  [the longest x2 2.19 us: across_rows(): return lax.ppermute(block, 'blk', route)]
    ppermute x1, waiting for transfers between devices: 2.81 us -> 0.42 us  [across_columns(): return lax.ppermute(block, 'blk', route)]
    ppermute x5 -> x4, starting transfers between devices: 7.36 us -> 5.58 us  [along_rep(): lax.ppermute(block, 'rep', [(i, (i + distance) % size) for i in range(siz...]
    unnamed x14 -> x18, local copies, waits for them, and re-layouts: 0.69 us -> 1.57 us
    slice x1 -> x2, local copies, waits for them, and re-layouts: 0.01 us -> 0.78 us  [the longest x1 0.76 us: per_device(): words[:, :, 1].reshape(rep_size * half_steps, slot_total * 16 + 16, 128)]
  transfers between devices with their start and end apart: 22 -> 27, of which waited for: 11 -> 11; matrix products, arithmetic and copies ran while one was open for 4% -> 5% of each run, Pallas kernels for 8% -> 9%
where the time goes in v2:
time: 66.7 us; the launch traced here: 66.5 us
  starting transfers between devices  27.1 us (41%)
  waiting for transfers between devices  23.2 us (35%)
  Pallas kernels  7.56 us (11%)
  other arithmetic  2.93 us (4%)
  local copies, waits for them, and re-layouts  2.78 us (4%)
  between operations  1.71 us (3%)
  matrix products  1.16 us (2%)
    ppermute x14, starting transfers between devices, along_ring(): return lax.ppermute(block, 'blk', route)  16.6 us
    ppermute x4, waiting for transfers between devices, along_rep(): lax.ppermute(block, 'rep', [(i, (i + distance) % size) for i in range(siz...  7.59 us
    ppermute x2, waiting for transfers between devices, across_rows(): return lax.ppermute(block, 'blk', route)  6.96 us
    pallas_call x4, Pallas kernels, add_step(): pl.pallas_call(functools.partial(step_kernel, len(halves), slot_total, fi...  5.73 us
    ppermute x4, starting transfers between devices, along_rep(): lax.ppermute(block, 'rep', [(i, (i + distance) % size) for i in range(siz...  5.58 us
    ppermute x14, waiting for transfers between devices, along_ring(): return lax.ppermute(block, 'blk', route)  4.06 us
    ppermute x1, waiting for transfers between devices, across_columns_and_rep(): return lax.ppermute(block, ('blk', 'rep'), route)  2.42 us
    ppermute x2, starting transfers between devices, across_rows(): return lax.ppermute(block, 'blk', route)  2.19 us
  transfers between devices with their start and end apart: 27, of which 11 were waited for; matrix products, arithmetic and copies ran while one was open for 5% of the time, Pallas kernels for 9%

profile of v2, /device:TPU:0, one launch (start us, length us, event | category | flops | bytes accessed | tf_op | source)
XLA Modules:
  0.0 66.5 jit_solution(4880378465551016642)
XLA Ops:
  0.7 0.7 %copy-done.4 = s32[1024]{0:T(1024)S(1)} copy-done((s32[1024]{0:T(1024)S(1)}, s32[1024]{0:T(1024)}, u32[]{:S(2)}) %copy-start.4) | copy-done | bytes 4120
  1.4 1.2 %multiply_convert_fusion.2 = bf16[1024,128]{1,0:T(8,128)(2,1)S(1)} fusion(f32[1024]{0:T(1024)S(1)} %convert_rsqrt_fusion, bf16[1024,256]{1,0:T(8,128)(2,1)} %param.8, s32[]{:T(128)S(6)} %select_n.409), kind=kLoop, calls=%fused_computation.6 | loop fusion | flops 393216 | bytes 528388 | tf_op jit(solution)/shard_map/convert_element_type | solution.py:166
  2.6 3.0 %collective-permute-start.13 = (bf16[512,128]{1,0:T(8,128)(2,1)S(1)}, bf16[512,128]{1,0:T(8,128)(2,1)S(1)}, u32[]{:S(2)}, u32[]{:S(2)}) collective-permute-start(bf16[512,128]{1,0:T(8,128)(2,1)S(1)} %get-tuple-element.17.refs_0_), channel_id=1, source_target_pairs={{0,4},{2,6},{8,0},{10,2},{16,8},{18,10},{24,16},{26,18},{28,24},{3... | collective-permute-start | bytes 393224 | tf_op jit(solution)/shard_map/ppermute | solution.py:35
  5.6 0.2 collective-permute-start.2
  5.7 2.0 %collective-permute-start.10 = (bf16[512,128]{1,0:T(8,128)(2,1)S(1)}, bf16[512,128]{1,0:T(8,128)(2,1)S(1)}, u32[]{:S(2)}, u32[]{:S(2)}) collective-permute-start(bf16[512,128]{1,0:T(8,128)(2,1)S(1)} %get-tuple-element.16.refs_1_), channel_id=1, source_target_pairs={{0,8},{2,10},{8,16},{10,18},{16,24},{18,26},{24,28},{26,30},{28,20... | collective-permute-start | bytes 393224 | tf_op jit(solution)/shard_map/ppermute | solution.py:35
  7.7 0.1 collective-permute-start.6
  7.7 0.1 dynamic_slice.19
  7.8 0.1 copy.19
  8.0 0.1 fusion.1
  8.0 2.0 %collective-permute-start.16 = (bf16[256,512]{1,0:T(8,128)(2,1)S(1)}, bf16[256,512]{1,0:T(8,128)(2,1)S(1)}, u32[]{:S(2)}, u32[]{:S(2)}) collective-permute-start(bf16[256,512]{1,0:T(8,128)(2,1)S(1)} %get-tuple-element.13), channel_id=1, source_target_pairs={{0,1},{1,0},{2,3},{3,2},{4,5},{5,4},{6,7},{7,6},{8,9},{9,8},{10,11... | collective-permute-start | bytes 786440 | tf_op jit(solution)/shard_map/ppermute | solution.py:62
  10.1 0.6 copy-done.5
  10.7 0.1 copy.17
  10.8 0.1 reshape_squeeze.13
  10.9 0.1 pad_add_fusion.2
  11.1 0.1 pad_add_fusion.8.index_ref
  11.2 0.1 pad_add_fusion.3.index_ref
  11.2 0.1 pad_add_fusion.4.order_ref
  11.5 0.1 pad_add_fusion.7.index_ref
  11.8 1.5 %collective-permute-done.10.refs_1_ = bf16[512,128]{1,0:T(8,128)(2,1)S(1)} collective-permute-done((bf16[512,128]{1,0:T(8,128)(2,1)S(1)}, bf16[512,128]{1,0:T(8,128)(2,1)S(1)}, u32[]{:S(2)}, u32[]{:S(2)}) %collective-permute-start.10) | collective-permute-done | bytes 131104 | tf_op jit(solution)/shard_map/ppermute | solution.py:35
  13.3 1.5 %collective-permute-start = (s16[8,144,128]{2,1,0:T(8,128)(2,1)S(1)}, s16[8,144,128]{2,1,0:T(8,128)(2,1)S(1)}, u32[]{:S(2)}, u32[]{:S(2)}) collective-permute-start(s16[8,144,128]{2,1,0:T(8,128)(2,1)S(1)} %pad_add_fusion.1), channel_id=1, source_target_pairs={{0,1},{1,0},{2,3},{3,2},{4,5},{5,4},{6,7},{7,6},{8,9},{9,8},{10,11... | collective-permute-start | bytes 884744 | tf_op jit(solution)/shard_map/ppermute | solution.py:62
  14.9 0.1 pad_add_fusion.6.index_ref
  15.2 0.1 pad_add_fusion.5.index_ref
  15.3 0.5 collective-permute-start.11
  15.8 1.5 %collective-permute-start.14 = (bf16[512,128]{1,0:T(8,128)(2,1)S(1)}, bf16[512,128]{1,0:T(8,128)(2,1)S(1)}, u32[]{:S(2)}, u32[]{:S(2)}) collective-permute-start(bf16[512,128]{1,0:T(8,128)(2,1)S(1)} %collective-permute-done.13.refs_2_), channel_id=1, source_target_pairs={{0,4},{2,6},{8,0},{10,2},{16,8},{18,10},{24,16},{26,18},{28,24},{3... | collective-permute-start | bytes 393224 | tf_op jit(solution)/shard_map/ppermute | solution.py:35
  17.3 0.5 collective-permute-start.3
  17.9 1.5 %collective-permute-start.7 = (bf16[512,128]{1,0:T(8,128)(2,1)S(1)}, bf16[512,128]{1,0:T(8,128)(2,1)S(1)}, u32[]{:S(2)}, u32[]{:S(2)}) collective-permute-start(bf16[512,128]{1,0:T(8,128)(2,1)S(1)} %collective-permute-done.6.refs_3_), channel_id=1, source_target_pairs={{0,4},{2,6},{8,0},{10,2},{16,8},{18,10},{24,16},{26,18},{28,24},{3... | collective-permute-start | bytes 393224 | tf_op jit(solution)/shard_map/ppermute | solution.py:35
  19.4 0.1 pad_maximum_fusion.own_features
  19.4 2.2 %collective-permute-done = s16[8,144,128]{2,1,0:T(8,128)(2,1)S(1)} collective-permute-done((s16[8,144,128]{2,1,0:T(8,128)(2,1)S(1)}, s16[8,144,128]{2,1,0:T(8,128)(2,1)S(1)}, u32[]{:S(2)}, u32[]{:S(2)}) %collective-permute-start) | collective-permute-done | bytes 294944 | tf_op jit(solution)/shard_map/ppermute | solution.py:62
  21.7 0.8 %fusion.12 = (s16[2,4,1,144,128]{4,3,2,1,0:T(8,128)(2,1)}, s16[2,4,1,144,128]{4,3,2,1,0:T(8,128)(2,1)S(1)}) fusion(s16[2,4,2,144,128]{4,3,2,1,0:T(8,128)(2,1)S(1)} %pad_add_fusion), kind=kLoop, calls=%fused_computation.47 | loop fusion | bytes 1179648 | tf_op jit(solution)/shard_map/slice | solution.py:177
  22.5 0.6 collective-permute-start.17
  23.0 1.7 %collective-permute-start.4 = (bf16[512,128]{1,0:T(8,128)(2,1)S(1)}, bf16[512,128]{1,0:T(8,128)(2,1)S(1)}, u32[]{:S(2)}, u32[]{:S(2)}) collective-permute-start(bf16[512,128]{1,0:T(8,128)(2,1)S(1)} %collective-permute-done.3.refs_0_), channel_id=1, source_target_pairs={{0,8},{2,10},{8,16},{10,18},{16,24},{18,26},{24,28},{26,30},{28,20... | collective-permute-start | bytes 393224 | tf_op jit(solution)/shard_map/ppermute | solution.py:35
  24.7 0.3 collective-permute-start.8
  25.1 0.1 reshape.75.fact_a
  25.2 1.7 %collective-permute-start.12 = (bf16[512,128]{1,0:T(8,128)(2,1)S(1)}, bf16[512,128]{1,0:T(8,128)(2,1)}, u32[]{:S(2)}, u32[]{:S(2)}) collective-permute-start(bf16[512,128]{1,0:T(8,128)(2,1)S(1)} %collective-permute-done.11.refs_1_), channel_id=1, source_target_pairs={{0,8},{2,10},{8,16},{10,18},{16,24},{18,26},{24,28},{26,30},{28,20... | collective-permute-start | bytes 393224 | tf_op jit(solution)/shard_map/ppermute | solution.py:35
  26.9 2.5 %collective-permute-done.4.refs_0_ = bf16[512,128]{1,0:T(8,128)(2,1)S(1)} collective-permute-done((bf16[512,128]{1,0:T(8,128)(2,1)S(1)}, bf16[512,128]{1,0:T(8,128)(2,1)S(1)}, u32[]{:S(2)}, u32[]{:S(2)}) %collective-permute-start.4) | collective-permute-done | bytes 131104 | tf_op jit(solution)/shard_map/ppermute | solution.py:35
  29.4 1.6 %collective-permute-start.15 = (bf16[512,128]{1,0:T(8,128)(2,1)S(1)}, bf16[512,128]{1,0:T(8,128)(2,1)}, u32[]{:S(2)}, u32[]{:S(2)}) collective-permute-start(bf16[512,128]{1,0:T(8,128)(2,1)S(1)} %collective-permute-done.14.refs_2_), channel_id=1, source_target_pairs={{0,4},{2,6},{8,0},{10,2},{16,8},{18,10},{24,16},{26,18},{28,24},{3... | collective-permute-start | bytes 393224 | tf_op jit(solution)/shard_map/ppermute | solution.py:35
  31.0 0.5 collective-permute-start.5
  31.5 1.5 %collective-permute-start.9 = (bf16[512,128]{1,0:T(8,128)(2,1)S(1)}, bf16[512,128]{1,0:T(8,128)(2,1)}, u32[]{:S(2)}, u32[]{:S(2)}) collective-permute-start(bf16[512,128]{1,0:T(8,128)(2,1)S(1)} %collective-permute-done.8.refs_3_), channel_id=1, source_target_pairs={{0,4},{2,6},{8,0},{10,2},{16,8},{18,10},{24,16},{26,18},{28,24},{3... | collective-permute-start | bytes 393224 | tf_op jit(solution)/shard_map/ppermute | solution.py:35
  33.0 0.1 reshape.77.fact_b
  33.1 1.0 %add_step.4.refs_4_ = f32[2,1024,128]{2,1,0:T(8,128)S(1)} custom-call(s32[2]{0:T(128)S(1)} %pad_add_fusion.8.index_ref, s32[136]{0:T(256)S(1)} %reshape.75.fact_a, s32[136]{0:T(256)S(1)} %reshape.77.fact_b, s16[8,144,128]{2,1,0:T(8,128)(2,1)S(1)} %bitcast.47, s16[8,144,128]{2,1,0:T(8,128)(2,1)S(1)} %collective-permute-done.1.words_b, ...), custom_call_target="tpu_custom_call" | custom-call | flops 67108864 | bytes 4194304 | tf_op jit(solution)/shard_map/add_step/pallas_call | solution.py:219
  34.2 1.4 %add_step.5.refs_4_ = f32[2,1024,128]{2,1,0:T(8,128)S(1)} custom-call(s32[4]{0:T(128)S(1)} %pad_add_fusion.7.index_ref, s32[136]{0:T(256)S(1)} %reshape.75.fact_a, s32[136]{0:T(256)S(1)} %reshape.77.fact_b, s16[8,144,128]{2,1,0:T(8,128)(2,1)S(1)} %bitcast.48, s16[8,144,128]{2,1,0:T(8,128)(2,1)S(1)} %collective-permute-done.1.words_b, ...), custom_call_target="tpu_custom_call", output_to_operand_aliasing={{}: (9, {})} | custom-call | flops 134217728 | bytes 4194304 | tf_op jit(solution)/shard_map/add_step/pallas_call | solution.py:219
  35.6 1.4 %add_step.6.refs_4_ = f32[2,1024,128]{2,1,0:T(8,128)S(1)} custom-call(s32[4]{0:T(128)S(1)} %pad_add_fusion.6.index_ref, s32[136]{0:T(256)S(1)} %reshape.75.fact_a, s32[136]{0:T(256)S(1)} %reshape.77.fact_b, s16[8,144,128]{2,1,0:T(8,128)(2,1)S(1)} %bitcast.49, s16[8,144,128]{2,1,0:T(8,128)(2,1)S(1)} %collective-permute-done.1.words_b, ...), custom_call_target="tpu_custom_call", output_to_operand_aliasing={{}: (9, {})} | custom-call | flops 134217728 | bytes 4194304 | tf_op jit(solution)/shard_map/add_step/pallas_call | solution.py:219
  37.1 1.8 %add_step.7.sums_in = f32[2,1024,128]{2,1,0:T(8,128)S(1)} custom-call(s32[4]{0:T(128)S(1)} %pad_add_fusion.5.index_ref, s32[136]{0:T(256)S(1)} %reshape.75.fact_a, s32[136]{0:T(256)S(1)} %reshape.77.fact_b, s16[8,144,128]{2,1,0:T(8,128)(2,1)S(1)} %bitcast.50, s16[8,144,128]{2,1,0:T(8,128)(2,1)S(1)} %collective-permute-done.1.words_b, ...), custom_call_target="tpu_custom_call", output_to_operand_aliasing={{}: (9, {})} | custom-call | flops 134217728 | bytes 4194304 | tf_op jit(solution)/shard_map/add_step/pallas_call | solution.py:219
  38.9 1.8 %last_step.1 = (f32[1024,128]{1,0:T(8,128)S(1)}, f32[1024,128]{1,0:T(8,128)S(1)}, f32[128,128]{1,0:T(8,128)S(1)}, f32[128,128]{1,0:T(8,128)S(1)}) custom-call(s32[2]{0:T(128)S(1)} %pad_add_fusion.3.index_ref, s32[3]{0:T(128)S(1)} %pad_add_fusion.4.order_ref, s32[136]{0:T(256)S(1)} %reshape.75.fact_a, s32[136]{0:T(256)S(1)} %reshape.77.fact_b, ...), custom_call_target="tpu_custom_call" | custom-call | tf_op jit(solution)/shard_map/last_step/pallas_call | solution.py:247
  40.8 0.1 collective-permute-start.20
  40.9 1.2 %collective-permute-done.20 = f32[128,128]{1,0:T(8,128)S(1)} collective-permute-done((f32[128,128]{1,0:T(8,128)S(1)}, f32[128,128]{1,0:T(8,128)S(1)}, u32[]{:S(2)}, u32[]{:S(2)}) %collective-permute-start.20) | collective-permute-done | bytes 65568 | tf_op jit(solution)/shard_map/ppermute | solution.py:57
  42.1 0.6 collective-permute-start.21
  42.7 3.4 %collective-permute-done.21 = bf16[128,128]{1,0:T(8,128)(2,1)S(1)} collective-permute-done((bf16[128,128]{1,0:T(8,128)(2,1)S(1)}, bf16[128,128]{1,0:T(8,128)(2,1)S(1)}, u32[]{:S(2)}, u32[]{:S(2)}) %collective-permute-start.21) | collective-permute-done | bytes 32800 | tf_op jit(solution)/shard_map/ppermute | solution.py:43
  46.1 1.6 %collective-permute-start.22 = (bf16[128,128]{1,0:T(8,128)(2,1)S(1)}, bf16[128,128]{1,0:T(8,128)(2,1)S(1)}, u32[]{:S(2)}, u32[]{:S(2)}) collective-permute-start(bf16[128,128]{1,0:T(8,128)(2,1)S(1)} %add_convert_fusion.1), channel_id=1, source_target_pairs={{0,16},{2,18},{4,20},{6,22},{8,24},{10,26},{12,28},{14,30},{16,0},... | collective-permute-start | bytes 98312 | tf_op jit(solution)/shard_map/ppermute | solution.py:43
  47.7 3.6 %collective-permute-done.22 = bf16[128,128]{1,0:T(8,128)(2,1)S(1)} collective-permute-done((bf16[128,128]{1,0:T(8,128)(2,1)S(1)}, bf16[128,128]{1,0:T(8,128)(2,1)S(1)}, u32[]{:S(2)}, u32[]{:S(2)}) %collective-permute-start.22) | collective-permute-done | bytes 32800 | tf_op jit(solution)/shard_map/ppermute | solution.py:43
  51.3 1.4 %collective-permute-start.23 = (bf16[128,128]{1,0:T(8,128)(2,1)S(1)}, bf16[128,128]{1,0:T(8,128)(2,1)S(1)}, u32[]{:S(2)}, u32[]{:S(2)}) collective-permute-start(bf16[128,128]{1,0:T(8,128)(2,1)S(1)} %add_convert_fusion), channel_id=1, source_target_pairs={{0,4},{2,6},{4,0},{6,2},{8,12},{10,14},{12,8},{14,10},{16,20},{18,... | collective-permute-start | bytes 98312 | tf_op jit(solution)/shard_map/ppermute | solution.py:50
  52.7 1.5 %collective-permute-start.24 = (bf16[128,128]{1,0:T(8,128)(2,1)S(1)}, bf16[128,128]{1,0:T(8,128)(2,1)S(1)}, u32[]{:S(2)}, u32[]{:S(2)}) collective-permute-start(bf16[128,128]{1,0:T(8,128)(2,1)S(1)} %add_convert_fusion), channel_id=1, source_target_pairs={{0,1},{1,0},{2,3},{3,2},{4,5},{5,4},{6,7},{7,6},{8,9},{9,8},{10,11... | collective-permute-start | bytes 98312 | tf_op jit(solution)/shard_map/ppermute | solution.py:62
  54.2 0.7 %collective-permute-start.25 = (bf16[128,128]{1,0:T(8,128)(2,1)S(1)}, bf16[128,128]{1,0:T(8,128)(2,1)S(1)}, u32[]{:S(2)}, u32[]{:S(2)}) collective-permute-start(bf16[128,128]{1,0:T(8,128)(2,1)S(1)} %add_convert_fusion), channel_id=1, source_target_pairs={{0,5},{1,4},{2,7},{3,6},{4,1},{5,0},{6,3},{7,2},{8,13},{9,12},{10,... | collective-permute-start | bytes 98312 | tf_op jit(solution)/shard_map/ppermute | solution.py:72
  54.9 0.4 collective-permute-done.23
  55.3 1.3 %collective-permute-done.24 = bf16[128,128]{1,0:T(8,128)(2,1)S(1)} collective-permute-done((bf16[128,128]{1,0:T(8,128)(2,1)S(1)}, bf16[128,128]{1,0:T(8,128)(2,1)S(1)}, u32[]{:S(2)}, u32[]{:S(2)}) %collective-permute-start.24) | collective-permute-done | bytes 32800 | tf_op jit(solution)/shard_map/ppermute | solution.py:62
  56.6 2.4 %collective-permute-done.25 = bf16[128,128]{1,0:T(8,128)(2,1)S(1)} collective-permute-done((bf16[128,128]{1,0:T(8,128)(2,1)S(1)}, bf16[128,128]{1,0:T(8,128)(2,1)S(1)}, u32[]{:S(2)}, u32[]{:S(2)}) %collective-permute-start.25) | collective-permute-done | bytes 32800 | tf_op jit(solution)/shard_map/ppermute | solution.py:72
  59.0 0.1 collective-permute-start.26
  59.1 0.2 multiply_convert_fusion
  59.4 0.6 collective-permute-start.19
  59.9 0.5 collective-permute-done.26
  60.5 0.7 %pad_maximum_fusion.1 = f32[256,256]{1,0:T(8,128)} fusion(f32[128,256]{1,0:T(8,128)S(1)} %get-tuple-element.15, f32[128,256]{1,0:T(8,128)S(1)} %get-tuple-element.14), kind=kLoop, calls=%fused_computation.8 | loop fusion | flops 65536 | bytes 524288 | tf_op jit(solution)/shard_map/concatenate | solution.py:281
  61.2 4.1 %collective-permute-done.19 = bf16[512,128]{1,0:T(8,128)(2,1)S(1)} collective-permute-done((bf16[512,128]{1,0:T(8,128)(2,1)S(1)}, bf16[512,128]{1,0:T(8,128)(2,1)S(1)}, u32[]{:S(2)}, u32[]{:S(2)}) %collective-permute-start.19) | collective-permute-done | bytes 131104 | tf_op jit(solution)/shard_map/ppermute | solution.py:62
  65.3 0.2 fusion.4
  65.5 0.9 %fusion = bf16[512,256]{1,0:T(8,128)(2,1)} fusion(f32[512,256]{1,0:T(8,128)S(1)} %fusion.4, bf16[1024,128]{1,0:T(8,128)(2,1)S(1)} %multiply_convert_fusion, s32[]{:T(128)S(6)} %select_n.482, bf16[256,256]{1,0:T(8,128)(2,1)S(1)} %copy-done, s32[]{:T(128)S(6)} %select_n.483), kind=kOutput, calls=%fused_computation.1 | convolution fusion | flops 33816576 | bytes 983048 | tf_op jit(solution)/shard_map/dot_general | solution.py:295
  (52 shorter events, 0.4 us)
Async XLA Ops:
  0.6 64.7 %copy-start = (bf16[256,256]{1,0:T(8,128)(2,1)S(1)}, bf16[256,256]{1,0:T(8,128)(2,1)}, u32[]{:S(2)}) copy-start(bf16[256,256]{1,0:T(8,128)(2,1)} %param.9) | copy-start | bytes 393220
  0.7 0.7 %copy-start.4 = (s32[1024]{0:T(1024)S(1)}, s32[1024]{0:T(1024)}, u32[]{:S(2)}) copy-start(s32[1024]{0:T(1024)} %param.13) | copy-start | bytes 12292
  2.5 5.3 %copy-start.2 = (bf16[512,256]{1,0:T(8,128)(2,1)S(1)}, bf16[512,256]{1,0:T(8,128)(2,1)}, u32[]{:S(2)}) copy-start(bf16[512,256]{1,0:T(8,128)(2,1)} %param.7) | copy-start | bytes 786436
  2.6 12.7 %collective-permute-start.13 = (bf16[512,128]{1,0:T(8,128)(2,1)S(1)}, bf16[512,128]{1,0:T(8,128)(2,1)S(1)}, u32[]{:S(2)}, u32[]{:S(2)}) collective-permute-start(bf16[512,128]{1,0:T(8,128)(2,1)S(1)} %get-tuple-element.17.refs_0_), channel_id=1, source_target_pairs={{0,4},{2,6},{8,0},{10,2},{16,8},{18,10},{24,16},{26,18},{28,24},{3... | collective-permute-start | bytes 393224 | tf_op jit(solution)/shard_map/ppermute | solution.py:35
  5.6 10.3 %collective-permute-start.2 = (bf16[512,128]{1,0:T(8,128)(2,1)S(1)}, bf16[512,128]{1,0:T(8,128)(2,1)S(1)}, u32[]{:S(2)}, u32[]{:S(2)}) collective-permute-start(bf16[512,128]{1,0:T(8,128)(2,1)S(1)} %get-tuple-element.17.refs_0_), channel_id=1, source_target_pairs={{0,8},{2,10},{8,16},{10,18},{16,24},{18,26},{24,28},{26,30},{28,20... | collective-permute-start | bytes 393224 | tf_op jit(solution)/shard_map/ppermute | solution.py:35
  5.7 7.6 %collective-permute-start.10 = (bf16[512,128]{1,0:T(8,128)(2,1)S(1)}, bf16[512,128]{1,0:T(8,128)(2,1)S(1)}, u32[]{:S(2)}, u32[]{:S(2)}) collective-permute-start(bf16[512,128]{1,0:T(8,128)(2,1)S(1)} %get-tuple-element.16.refs_1_), channel_id=1, source_target_pairs={{0,8},{2,10},{8,16},{10,18},{16,24},{18,26},{24,28},{26,30},{28,20... | collective-permute-start | bytes 393224 | tf_op jit(solution)/shard_map/ppermute | solution.py:35
  7.7 9.7 %collective-permute-start.6 = (bf16[512,128]{1,0:T(8,128)(2,1)S(1)}, bf16[512,128]{1,0:T(8,128)(2,1)S(1)}, u32[]{:S(2)}, u32[]{:S(2)}) collective-permute-start(bf16[512,128]{1,0:T(8,128)(2,1)S(1)} %get-tuple-element.16.refs_1_), channel_id=1, source_target_pairs={{0,4},{2,6},{8,0},{10,2},{16,8},{18,10},{24,16},{26,18},{28,24},{3... | collective-permute-start | bytes 393224 | tf_op jit(solution)/shard_map/ppermute | solution.py:35
  8.0 2.1 %copy-start.1 = (s32[1,8,8,16,128]{4,3,2,1,0:T(8,128)S(1)}, s32[1,8,8,16,128]{4,3,2,1,0:T(8,128)}, u32[]{:S(2)}) copy-start(s32[1,8,8,16,128]{4,3,2,1,0:T(8,128)} %param.10) | copy-start | bytes 1572868
  8.0 9.8 %collective-permute-start.16 = (bf16[256,512]{1,0:T(8,128)(2,1)S(1)}, bf16[256,512]{1,0:T(8,128)(2,1)S(1)}, u32[]{:S(2)}, u32[]{:S(2)}) collective-permute-start(bf16[256,512]{1,0:T(8,128)(2,1)S(1)} %get-tuple-element.13), channel_id=1, source_target_pairs={{0,1},{1,0},{2,3},{3,2},{4,5},{5,4},{6,7},{7,6},{8,9},{9,8},{10,11... | collective-permute-start | bytes 786440 | tf_op jit(solution)/shard_map/ppermute | solution.py:62
  10.0 0.8 %copy-start.3 = (s32[1,8,2,8]{3,2,1,0:T(2,128)S(1)}, s32[1,8,2,8]{3,2,1,0:T(2,128)}, u32[]{:S(2)}) copy-start(s32[1,8,2,8]{3,2,1,0:T(2,128)} %param.11) | copy-start | bytes 1540
  10.1 0.7 copy-start.5
  13.3 8.3 %collective-permute-start = (s16[8,144,128]{2,1,0:T(8,128)(2,1)S(1)}, s16[8,144,128]{2,1,0:T(8,128)(2,1)S(1)}, u32[]{:S(2)}, u32[]{:S(2)}) collective-permute-start(s16[8,144,128]{2,1,0:T(8,128)(2,1)S(1)} %pad_add_fusion.1), channel_id=1, source_target_pairs={{0,1},{1,0},{2,3},{3,2},{4,5},{5,4},{6,7},{7,6},{8,9},{9,8},{10,11... | collective-permute-start | bytes 884744 | tf_op jit(solution)/shard_map/ppermute | solution.py:62
  15.3 7.1 %collective-permute-start.11 = (bf16[512,128]{1,0:T(8,128)(2,1)S(1)}, bf16[512,128]{1,0:T(8,128)(2,1)S(1)}, u32[]{:S(2)}, u32[]{:S(2)}) collective-permute-start(bf16[512,128]{1,0:T(8,128)(2,1)S(1)} %collective-permute-done.10.refs_1_), channel_id=1, source_target_pairs={{0,8},{2,10},{8,16},{10,18},{16,24},{18,26},{24,28},{26,30},{28,20... | collective-permute-start | bytes 393224 | tf_op jit(solution)/shard_map/ppermute | solution.py:35
  15.8 9.3 %collective-permute-start.14 = (bf16[512,128]{1,0:T(8,128)(2,1)S(1)}, bf16[512,128]{1,0:T(8,128)(2,1)S(1)}, u32[]{:S(2)}, u32[]{:S(2)}) collective-permute-start(bf16[512,128]{1,0:T(8,128)(2,1)S(1)} %collective-permute-done.13.refs_2_), channel_id=1, source_target_pairs={{0,4},{2,6},{8,0},{10,2},{16,8},{18,10},{24,16},{26,18},{28,24},{3... | collective-permute-start | bytes 393224 | tf_op jit(solution)/shard_map/ppermute | solution.py:35
  17.3 5.7 %collective-permute-start.3 = (bf16[512,128]{1,0:T(8,128)(2,1)S(1)}, bf16[512,128]{1,0:T(8,128)(2,1)S(1)}, u32[]{:S(2)}, u32[]{:S(2)}) collective-permute-start(bf16[512,128]{1,0:T(8,128)(2,1)S(1)} %collective-permute-done.2.refs_0_), channel_id=1, source_target_pairs={{0,8},{2,10},{8,16},{10,18},{16,24},{18,26},{24,28},{26,30},{28,20... | collective-permute-start | bytes 393224 | tf_op jit(solution)/shard_map/ppermute | solution.py:35
  17.9 6.8 %collective-permute-start.7 = (bf16[512,128]{1,0:T(8,128)(2,1)S(1)}, bf16[512,128]{1,0:T(8,128)(2,1)S(1)}, u32[]{:S(2)}, u32[]{:S(2)}) collective-permute-start(bf16[512,128]{1,0:T(8,128)(2,1)S(1)} %collective-permute-done.6.refs_3_), channel_id=1, source_target_pairs={{0,4},{2,6},{8,0},{10,2},{16,8},{18,10},{24,16},{26,18},{28,24},{3... | collective-permute-start | bytes 393224 | tf_op jit(solution)/shard_map/ppermute | solution.py:35
  22.4 9.1 %collective-permute-start.1 = (s16[8,144,128]{2,1,0:T(8,128)(2,1)}, s16[8,144,128]{2,1,0:T(8,128)(2,1)S(1)}, u32[]{:S(2)}, u32[]{:S(2)}) collective-permute-start(s16[8,144,128]{2,1,0:T(8,128)(2,1)} %bitcast.9), channel_id=1, source_target_pairs={{0,2},{2,0},{4,6},{6,4},{8,10},{10,8},{12,14},{14,12},{16,18},{18,... | collective-permute-start | bytes 884744 | tf_op jit(solution)/shard_map/ppermute | solution.py:57
  22.5 16.5 %collective-permute-start.17 = (bf16[2,256,512]{2,1,0:T(8,128)(2,1)S(1)}, bf16[2,256,512]{2,1,0:T(8,128)(2,1)S(1)}, u32[]{:S(2)}, u32[]{:S(2)}) collective-permute-start(bf16[2,256,512]{2,1,0:T(8,128)(2,1)S(1)} %pad_maximum_fusion.own_features), channel_id=1, source_target_pairs={{0,2},{2,0},{4,6},{6,4},{8,10},{10,8},{12,14},{14,12},{16,18},{18,... | collective-permute-start | bytes 1572872 | tf_op jit(solution)/shard_map/ppermute | solution.py:57
  23.0 6.4 %collective-permute-start.4 = (bf16[512,128]{1,0:T(8,128)(2,1)S(1)}, bf16[512,128]{1,0:T(8,128)(2,1)S(1)}, u32[]{:S(2)}, u32[]{:S(2)}) collective-permute-start(bf16[512,128]{1,0:T(8,128)(2,1)S(1)} %collective-permute-done.3.refs_0_), channel_id=1, source_target_pairs={{0,8},{2,10},{8,16},{10,18},{16,24},{18,26},{24,28},{26,30},{28,20... | collective-permute-start | bytes 393224 | tf_op jit(solution)/shard_map/ppermute | solution.py:35
  24.7 6.3 %collective-permute-start.8 = (bf16[512,128]{1,0:T(8,128)(2,1)S(1)}, bf16[512,128]{1,0:T(8,128)(2,1)S(1)}, u32[]{:S(2)}, u32[]{:S(2)}) collective-permute-start(bf16[512,128]{1,0:T(8,128)(2,1)S(1)} %collective-permute-done.7.refs_3_), channel_id=1, source_target_pairs={{0,4},{2,6},{8,0},{10,2},{16,8},{18,10},{24,16},{26,18},{28,24},{3... | collective-permute-start | bytes 393224 | tf_op jit(solution)/shard_map/ppermute | solution.py:35
  25.2 11.9 %collective-permute-start.12 = (bf16[512,128]{1,0:T(8,128)(2,1)S(1)}, bf16[512,128]{1,0:T(8,128)(2,1)}, u32[]{:S(2)}, u32[]{:S(2)}) collective-permute-start(bf16[512,128]{1,0:T(8,128)(2,1)S(1)} %collective-permute-done.11.refs_1_), channel_id=1, source_target_pairs={{0,8},{2,10},{8,16},{10,18},{16,24},{18,26},{24,28},{26,30},{28,20... | collective-permute-start | bytes 393224 | tf_op jit(solution)/shard_map/ppermute | solution.py:35
  29.4 7.7 %collective-permute-start.15 = (bf16[512,128]{1,0:T(8,128)(2,1)S(1)}, bf16[512,128]{1,0:T(8,128)(2,1)}, u32[]{:S(2)}, u32[]{:S(2)}) collective-permute-start(bf16[512,128]{1,0:T(8,128)(2,1)S(1)} %collective-permute-done.14.refs_2_), channel_id=1, source_target_pairs={{0,4},{2,6},{8,0},{10,2},{16,8},{18,10},{24,16},{26,18},{28,24},{3... | collective-permute-start | bytes 393224 | tf_op jit(solution)/shard_map/ppermute | solution.py:35
  31.0 7.9 %collective-permute-start.5 = (bf16[512,128]{1,0:T(8,128)(2,1)S(1)}, bf16[512,128]{1,0:T(8,128)(2,1)S(1)}, u32[]{:S(2)}, u32[]{:S(2)}) collective-permute-start(bf16[512,128]{1,0:T(8,128)(2,1)S(1)} %collective-permute-done.4.refs_0_), channel_id=1, source_target_pairs={{0,8},{2,10},{8,16},{10,18},{16,24},{18,26},{24,28},{26,30},{28,20... | collective-permute-start | bytes 393224 | tf_op jit(solution)/shard_map/ppermute | solution.py:35
  31.5 7.4 %collective-permute-start.9 = (bf16[512,128]{1,0:T(8,128)(2,1)S(1)}, bf16[512,128]{1,0:T(8,128)(2,1)}, u32[]{:S(2)}, u32[]{:S(2)}) collective-permute-start(bf16[512,128]{1,0:T(8,128)(2,1)S(1)} %collective-permute-done.8.refs_3_), channel_id=1, source_target_pairs={{0,4},{2,6},{8,0},{10,2},{16,8},{18,10},{24,16},{26,18},{28,24},{3... | collective-permute-start | bytes 393224 | tf_op jit(solution)/shard_map/ppermute | solution.py:35
  40.8 1.3 %collective-permute-start.20 = (f32[128,128]{1,0:T(8,128)S(1)}, f32[128,128]{1,0:T(8,128)S(1)}, u32[]{:S(2)}, u32[]{:S(2)}) collective-permute-start(f32[128,128]{1,0:T(8,128)S(1)} %get-tuple-element.9), channel_id=1, source_target_pairs={{0,2},{2,0},{4,6},{6,4},{8,10},{10,8},{12,14},{14,12},{16,18},{18,... | collective-permute-start | bytes 196616 | tf_op jit(solution)/shard_map/ppermute | solution.py:57
  42.1 4.0 %collective-permute-start.21 = (bf16[128,128]{1,0:T(8,128)(2,1)S(1)}, bf16[128,128]{1,0:T(8,128)(2,1)S(1)}, u32[]{:S(2)}, u32[]{:S(2)}) collective-permute-start(bf16[128,128]{1,0:T(8,128)(2,1)S(1)} %add_convert_fusion.2), channel_id=1, source_target_pairs={{0,8},{2,10},{4,12},{6,14},{8,0},{10,2},{12,4},{14,6},{16,24},{18,... | collective-permute-start | bytes 98312 | tf_op jit(solution)/shard_map/ppermute | solution.py:43
  46.1 5.2 %collective-permute-start.22 = (bf16[128,128]{1,0:T(8,128)(2,1)S(1)}, bf16[128,128]{1,0:T(8,128)(2,1)S(1)}, u32[]{:S(2)}, u32[]{:S(2)}) collective-permute-start(bf16[128,128]{1,0:T(8,128)(2,1)S(1)} %add_convert_fusion.1), channel_id=1, source_target_pairs={{0,16},{2,18},{4,20},{6,22},{8,24},{10,26},{12,28},{14,30},{16,0},... | collective-permute-start | bytes 98312 | tf_op jit(solution)/shard_map/ppermute | solution.py:43
  51.3 4.0 %collective-permute-start.23 = (bf16[128,128]{1,0:T(8,128)(2,1)S(1)}, bf16[128,128]{1,0:T(8,128)(2,1)S(1)}, u32[]{:S(2)}, u32[]{:S(2)}) collective-permute-start(bf16[128,128]{1,0:T(8,128)(2,1)S(1)} %add_convert_fusion), channel_id=1, source_target_pairs={{0,4},{2,6},{4,0},{6,2},{8,12},{10,14},{12,8},{14,10},{16,20},{18,... | collective-permute-start | bytes 98312 | tf_op jit(solution)/shard_map/ppermute | solution.py:50
  52.7 6.5 %collective-permute-start.18 = (f32[1024,128]{1,0:T(8,128)S(1)}, f32[1024,128]{1,0:T(8,128)S(1)}, u32[]{:S(2)}, u32[]{:S(2)}) collective-permute-start(f32[1024,128]{1,0:T(8,128)S(1)} %get-tuple-element.7), channel_id=1, source_target_pairs={{0,2},{2,0},{4,6},{6,4},{8,10},{10,8},{12,14},{14,12},{16,18},{18,... | collective-permute-start | bytes 1572872 | tf_op jit(solution)/shard_map/ppermute | solution.py:57
  52.7 3.9 %collective-permute-start.24 = (bf16[128,128]{1,0:T(8,128)(2,1)S(1)}, bf16[128,128]{1,0:T(8,128)(2,1)S(1)}, u32[]{:S(2)}, u32[]{:S(2)}) collective-permute-start(bf16[128,128]{1,0:T(8,128)(2,1)S(1)} %add_convert_fusion), channel_id=1, source_target_pairs={{0,1},{1,0},{2,3},{3,2},{4,5},{5,4},{6,7},{7,6},{8,9},{9,8},{10,11... | collective-permute-start | bytes 98312 | tf_op jit(solution)/shard_map/ppermute | solution.py:62
  54.2 4.8 %collective-permute-start.25 = (bf16[128,128]{1,0:T(8,128)(2,1)S(1)}, bf16[128,128]{1,0:T(8,128)(2,1)S(1)}, u32[]{:S(2)}, u32[]{:S(2)}) collective-permute-start(bf16[128,128]{1,0:T(8,128)(2,1)S(1)} %add_convert_fusion), channel_id=1, source_target_pairs={{0,5},{1,4},{2,7},{3,6},{4,1},{5,0},{6,3},{7,2},{8,13},{9,12},{10,... | collective-permute-start | bytes 98312 | tf_op jit(solution)/shard_map/ppermute | solution.py:72
  59.0 1.4 %collective-permute-start.26 = (f32[128,256]{1,0:T(8,128)S(1)}, f32[128,256]{1,0:T(8,128)S(1)}, u32[]{:S(2)}, u32[]{:S(2)}) collective-permute-start(f32[128,256]{1,0:T(8,128)S(1)} %broadcast_multiply_fusion), channel_id=1, source_target_pairs={{0,2},{2,0},{4,6},{6,4},{8,10},{10,8},{12,14},{14,12},{16,18},{18,... | collective-permute-start | bytes 393224 | tf_op jit(solution)/shard_map/ppermute | solution.py:57
  59.4 6.0 %collective-permute-start.19 = (bf16[512,128]{1,0:T(8,128)(2,1)S(1)}, bf16[512,128]{1,0:T(8,128)(2,1)S(1)}, u32[]{:S(2)}, u32[]{:S(2)}) collective-permute-start(bf16[512,128]{1,0:T(8,128)(2,1)S(1)} %constant_dynamic-slice_fusion), channel_id=1, source_target_pairs={{0,1},{1,0},{2,3},{3,2},{4,5},{5,4},{6,7},{7,6},{8,9},{9,8},{10,11... | collective-permute-start | bytes 393224 | tf_op jit(solution)/shard_map/ppermute | solution.py:62

commit v3 on v2

--- a/solution.py
+++ b/solution.py
@@ -55,6 +55,11 @@
         (device_of(z, x, c), device_of(z, x, 1 - c)) for z, x, c in places(lax.axis_size("blk"))
     ]
     return lax.ppermute(block, "blk", route)
+
+
+def along_rep(block, distance):
+    size = lax.axis_size("rep")
+    return lax.ppermute(block, "rep", [(i, (i + distance) % size) for i in range(size)])
 
 
 def along_rep(block, distance):
@@ -99,32 +104,22 @@
                 )
 
 
-def fill(slab_buffer, halves):
-    half = slab_buffer.shape[1] // 2
-    for slab_id in range(len(halves) // 2):
-        slab_buffer[slab_id, :half, :] = halves[2 * slab_id][...]
-        slab_buffer[slab_id, half:, :] = halves[2 * slab_id + 1][...]
-    return [slab_buffer.at[slab_id] for slab_id in range(len(halves) // 2)]
-
-
-def step_kernel(half_total, slot_total, first, index_ref, fact_a, fact_b, words_a, words_b, *refs):
-    halves, sums_ref, slab_buffer = refs[:half_total], refs[-2], refs[-1]
+def step_kernel(slab_total, slot_total, first, index_ref, fact_a, fact_b, words_a, words_b, *refs):
+    slabs, sums_ref = refs[:slab_total], refs[-1]
     if first:
         sums_ref[...] = jnp.zeros_like(sums_ref)
     else:
-        sums_ref[...] = refs[half_total][...]
-    slabs = fill(slab_buffer, halves)
+        sums_ref[...] = refs[slab_total][...]
     add_pairs(index_ref, (fact_a, fact_b), (words_a, words_b), slabs, sums_ref, slot_total)
 
 
 def last_kernel(
-    slot_total, rep_size, index_ref, order_ref, fact_a, fact_b, words_a, words_b, low_ref, high_ref,
+    slot_total, rep_size, index_ref, order_ref, fact_a, fact_b, words_a, words_b, slab_ref,
     sums_in, own_features, other_features, own_ref, other_ref, keep_ref, send_ref,
-    sums_ref, term_ref, slab_buffer,
+    sums_ref, term_ref,
 ):
     sums_ref[...] = sums_in[...]
-    slabs = fill(slab_buffer, [low_ref, high_ref])
-    add_pairs(index_ref, (fact_a, fact_b), (words_a, words_b), slabs, sums_ref, slot_total)
+    add_pairs(index_ref, (fact_a, fact_b), (words_a, words_b), [slab_ref], sums_ref, slot_total)
     own_ref[...] = sums_ref[0]
     other_ref[...] = sums_ref[1]
     share = sums_ref.shape[1] // rep_size
@@ -143,7 +138,7 @@
 
 SMEM = pl.BlockSpec(memory_space=pltpu.SMEM)
 VMEM = pl.BlockSpec(memory_space=pltpu.VMEM)
-PARAMS = pltpu.CompilerParams(vmem_limit_bytes=48 * 1024 * 1024)
+PARAMS = pltpu.CompilerParams(vmem_limit_bytes=24 * 1024 * 1024)
 
 
 def per_device(features, out_grad, weight, block_words, block_coords, block_counts, degrees):
@@ -165,6 +160,8 @@
     own_columns = lax.dynamic_slice_in_dim(out_grad, rep_index * share_width, share_width, 1)
     scaled = (own_columns.astype(jnp.float32) * inverse_root[:, None]).astype(jnp.bfloat16)
 
+    forward, backward = along_ring(scaled, 1), along_ring(scaled, -1)
+
     step_total = 2 * half_steps
     facts = jnp.concatenate(
         [block_counts[0][:, None], block_coords[0].reshape(step_total, 2 * slot_total)], axis=1
@@ -206,39 +203,42 @@
     pair_cost = 2 * slot_total * 128 * 128 * share_width * 2
     sums_shape = jax.ShapeDtypeStruct((2, slab_rows, share_width), jnp.float32)
 
-    def add_step(distances, halves, sums):
+    def add_slabs(distances, slabs, sums):
         first = sums is None
-        operands = [pair_indices(distances), fact_a, fact_b, words_a, words_b, *halves]
-        specs = [SMEM] * 3 + [VMEM] * (2 + len(halves))
+        operands = [pair_indices(distances), fact_a, fact_b, words_a, words_b, *slabs]
+        specs = [SMEM] * 3 + [VMEM] * (2 + len(slabs))
         aliases = {}
         if not first:
             aliases = {len(operands): 0}
             operands.append(sums)
             specs.append(VMEM)
-        slab_total = len(halves) // 2
         return pl.pallas_call(
-            functools.partial(step_kernel, len(halves), slot_total, first),
+            functools.partial(step_kernel, len(slabs), slot_total, first),
             out_shape=sums_shape,
             in_specs=specs,
             out_specs=VMEM,
             input_output_aliases=aliases,
-            scratch_shapes=[pltpu.VMEM((slab_total, slab_rows, share_width), jnp.bfloat16)],
             compiler_params=PARAMS,
             cost_estimate=pl.CostEstimate(
-                flops=pair_cost * slab_total, bytes_accessed=4 << 20, transcendentals=0
+                flops=pair_cost * len(slabs), bytes_accessed=4 << 20, transcendentals=0
             ),
-            name="add_step",
+            name="add_slabs",
         )(*operands)
 
-    low, high = scaled[: slab_rows // 2], scaled[slab_rows // 2 :]
-    sums = add_step([0], [low, high], None)
-    low_up = low_down = low
-    high_up = high_down = high
+    sums = None
+    distances, slabs = [0], [scaled]
     for step in range(1, chips // 2):
-        low_up, high_down = along_ring(low_up, 1), along_ring(high_down, -1)
-        high_up, low_down = along_ring(high_up, 1), along_ring(low_down, -1)
-        sums = add_step([-step, step], [low_up, high_up, low_down, high_down], sums)
-    low_up, high_down = along_ring(low_up, 1), along_ring(high_down, -1)
+        distances += [-step, step]
+        slabs += [forward, backward]
+        if step + 1 < chips // 2:
+            if len(slabs) > 4:
+                sums = add_slabs(distances, slabs, sums)
+                distances, slabs = [], []
+            forward, backward = along_ring(forward, 1), along_ring(backward, -1)
+        else:
+            forward, sums = lax.optimization_barrier((forward, sums))
+            forward = along_ring(forward, 1)
+    sums = add_slabs(distances, slabs, sums)
 
     order = (rep_index - jnp.arange(rep_size, dtype=jnp.int32)) % rep_size
     order = jnp.concatenate([order, core[None]]).astype(jnp.int32)
@@ -247,55 +247,59 @@
     own_sums, other_sums, keep, send = pl.pallas_call(
         functools.partial(last_kernel, slot_total, rep_size),
         out_shape=(slab_shape, slab_shape, half_term, half_term),
-        in_specs=[SMEM] * 4 + [VMEM] * 7,
+        in_specs=[SMEM] * 4 + [VMEM] * 6,
         out_specs=(VMEM,) * 4,
         scratch_shapes=[
             pltpu.VMEM(sums_shape.shape, jnp.float32),
             pltpu.VMEM((width, share_width), jnp.float32),
-            pltpu.VMEM((1, slab_rows, share_width), jnp.bfloat16),
         ],
         compiler_params=PARAMS,
         name="last_step",
     )(
-        pair_indices([chips // 2]), order, fact_a, fact_b, words_a, words_b, low_up, high_down, sums,
+        pair_indices([chips // 2]), order, fact_a, fact_b, words_a, words_b, forward, sums,
         own_features, other_features,
     )
 
+    def add_across_rows(total, distance):
+        total = total.astype(jnp.bfloat16)
+        return total.astype(jnp.float32) + across_rows(total, distance).astype(jnp.float32)
+
     total = keep + across_cores(send)
-    distance = 1
-    while distance < rows_of_chips:
-        total = total.astype(jnp.bfloat16)
-        total = total.astype(jnp.float32) + across_rows(total, distance).astype(jnp.float32)
-        distance *= 2
-    total = total.astype(jnp.bfloat16)
-    weight_half = jnp.zeros((width // 2, width), jnp.float32)
-    for d in range(rep_size):
-        near, far = total, across_columns(total)
-        if d:
-            near, far = along_rep(total, d), across_columns_and_rep(total, d)
-        columns = near.astype(jnp.float32) + far.astype(jnp.float32)
-        at = ((rep_index - d) % rep_size) * share_width
-        weight_half = lax.dynamic_update_slice_in_dim(weight_half, columns, at, 1)
-    weight_half = weight_half * (1.0 / math.sqrt(slab_rows * blk_size))
-    other_half = across_cores(weight_half)
-    weight_grad = jnp.concatenate(
-        [jnp.where(core == 0, weight_half, other_half), jnp.where(core == 0, other_half, weight_half)]
-    )
-
     own_sums = own_sums + across_cores(other_sums)
     aggregated = (own_sums * inverse_root[:, None]).astype(jnp.bfloat16)
-    result = jnp.zeros((share_rows, width), jnp.float32)
+    total = add_across_rows(total, 1)
+    total, aggregated = lax.optimization_barrier((total, aggregated))
+    parts = []
     for d in range(rep_size):
         rows_to = ((rep_index + d) % rep_size) * share_rows
         part = lax.dynamic_slice_in_dim(aggregated, rows_to, share_rows, 0)
-        if d:
-            part = along_rep(part, d)
+        parts.append(along_rep(part, d) if d else part)
+    distance = 2
+    while distance < rows_of_chips:
+        total = add_across_rows(total, distance)
+        distance *= 2
+    total = total.astype(jnp.bfloat16)
+    total = total.astype(jnp.float32) + across_columns(total).astype(jnp.float32)
+    total, parts = lax.optimization_barrier((total, parts))
+    result = jnp.zeros((share_rows, width), jnp.float32)
+    for d, part in enumerate(parts):
         columns_at = ((rep_index - d) % rep_size) * share_width
         side = lax.dynamic_slice_in_dim(weight, columns_at, share_width, 1)
         result = result + lax.dot_general(
             part, side, (((1,), (1,)), ((), ())), preferred_element_type=jnp.float32
         )
-    return (result.astype(jnp.bfloat16), weight_grad)
+    input_grad = result.astype(jnp.bfloat16)
+    weight_half = jnp.zeros((width // 2, width), jnp.float32)
+    for d, columns in enumerate(from_all_reps(total)):
+        at = ((rep_index - d) % rep_size) * share_width
+        weight_half = lax.dynamic_update_slice_in_dim(weight_half, columns, at, 1)
+    weight_half = weight_half * (1.0 / math.sqrt(slab_rows * blk_size))
+    weight_half, input_grad = lax.optimization_barrier((weight_half, input_grad))
+    other_half = across_cores(weight_half)
+    weight_grad = jnp.concatenate(
+        [jnp.where(core == 0, weight_half, other_half), jnp.where(core == 0, other_half, weight_half)]
+    )
+    return (input_grad, weight_grad)
 
 
 def solution(mesh):

time: 66.7 us -> 68.7 us (1.030)
  waiting for transfers between devices: 23.2 us -> 31.4 us
  starting transfers between devices: 27.1 us -> 22.5 us
  Pallas kernels: 7.56 us -> 5.88 us
  local copies, waits for them, and re-layouts: 2.78 us -> 3.77 us
  between operations: 1.71 us -> 0.91 us
    ppermute x14 -> x7, starting transfers between devices: 16.6 us -> 7.98 us  [along_ring(): return lax.ppermute(block, 'blk', route)]
    ppermute x4, waiting for transfers between devices: 7.59 us -> 14.1 us  [along_rep(): lax.ppermute(block, 'rep', [(i, (i + distance) % size) for i in range(siz...]
    ppermute x14 -> x7, waiting for transfers between devices: 4.06 us -> 10.5 us  [along_ring(): return lax.ppermute(block, 'blk', route)]
    ppermute x2, waiting for transfers between devices: 6.96 us -> 4.12 us  [across_rows(): return lax.ppermute(block, 'blk', route)]
    ppermute x2, starting transfers between devices: 2.19 us -> 4.74 us  [across_rows(): return lax.ppermute(block, 'blk', route)]
    ppermute x1 -> x0, waiting for transfers between devices: 2.42 us -> none  [across_columns_and_rep(): return lax.ppermute(block, ('blk', 'rep'), route)]
    unnamed x18 -> x26, local copies, waits for them, and re-layouts: 1.57 us -> 3.19 us
    ppermute x4, starting transfers between devices: 5.58 us -> 7.04 us  [along_rep(): lax.ppermute(block, 'rep', [(i, (i + distance) % size) for i in range(siz...]
  transfers between devices with their start and end apart: 27 -> 19, of which waited for: 11 -> 11; matrix products, arithmetic and copies ran while one was open for 5% -> 3% of each run, Pallas kernels for 9% -> 6%
where the time goes in v3:
time: 68.7 us; the launch traced here: 68.4 us
  waiting for transfers between devices  31.4 us (46%)
  starting transfers between devices  22.5 us (33%)
  Pallas kernels  5.88 us (9%)
  local copies, waits for them, and re-layouts  3.77 us (5%)
  other arithmetic  2.83 us (4%)
  matrix products  1.17 us (2%)
  between operations  0.91 us (1%)
    ppermute x4, waiting for transfers between devices, along_rep(): lax.ppermute(block, 'rep', [(i, (i + distance) % size) for i in range(siz...  14.1 us
    ppermute x7, waiting for transfers between devices, along_ring(): return lax.ppermute(block, 'blk', route)  10.5 us
    ppermute x7, starting transfers between devices, along_ring(): return lax.ppermute(block, 'blk', route)  7.98 us
    ppermute x4, starting transfers between devices, along_rep(): lax.ppermute(block, 'rep', [(i, (i + distance) % size) for i in range(siz...  7.04 us
    ppermute x2, starting transfers between devices, across_rows(): return lax.ppermute(block, 'blk', route)  4.74 us
    pallas_call x2, Pallas kernels, add_slabs(): pl.pallas_call(functools.partial(step_kernel, len(slabs), slot_total, fir...  4.41 us
    ppermute x2, waiting for transfers between devices, across_rows(): return lax.ppermute(block, 'blk', route)  4.12 us
    unnamed x26, local copies, waits for them, and re-layouts  3.19 us
  transfers between devices with their start and end apart: 19, of which 11 were waited for; matrix products, arithmetic and copies ran while one was open for 3% of the time, Pallas kernels for 6%

profile of v3, /device:TPU:0, one launch (start us, length us, event | category | flops | bytes accessed | tf_op | source)
XLA Modules:
  0.0 68.4 jit_solution(18307633435911606641)
XLA Ops:
  0.6 0.0 copy-start
  0.7 1.1 %convert.14 = s16[1,8,8,16,128]{4,3,2,1,0:T(8,128)(2,1)S(1)} convert(s32[1,8,8,16,128]{4,3,2,1,0:T(8,128)} %param.10) | non-fusion elementwise | flops 131072 | bytes 786432 | tf_op jit(solution)/shard_map/convert.9
  1.8 0.0 copy-start.9
  1.8 0.6 copy-done.9
  2.4 0.1 copy.15
  2.5 0.1 reshape_squeeze.13
  2.6 0.1 pad_add_fusion.2
  2.7 0.0 copy-start.5
  2.7 0.0 copy-start.8
  2.8 3.0 %collective-permute-start = (s16[8,144,128]{2,1,0:T(8,128)(2,1)S(1)}, s16[8,144,128]{2,1,0:T(8,128)(2,1)S(1)}, u32[]{:S(2)}, u32[]{:S(2)}) collective-permute-start(s16[8,144,128]{2,1,0:T(8,128)(2,1)S(1)} %pad_add_fusion.1), channel_id=1, source_target_pairs={{0,1},{1,0},{2,3},{3,2},{4,5},{5,4},{6,7},{7,6},{8,9},{9,8},{10,11... | collective-permute-start | bytes 884744 | tf_op jit(solution)/shard_map/ppermute | solution.py:67
  5.8 0.1 copy.17
  6.0 0.0 copy-start.6
  6.0 0.1 dynamic_slice.19
  6.0 0.1 fusion.1
  6.1 0.9 %collective-permute-start.9 = (bf16[256,512]{1,0:T(8,128)(2,1)S(1)}, bf16[256,512]{1,0:T(8,128)(2,1)S(1)}, u32[]{:S(2)}, u32[]{:S(2)}) collective-permute-start(bf16[256,512]{1,0:T(8,128)(2,1)S(1)} %get-tuple-element.31), channel_id=1, source_target_pairs={{0,1},{1,0},{2,3},{3,2},{4,5},{5,4},{6,7},{7,6},{8,9},{9,8},{10,11... | collective-permute-start | bytes 786440 | tf_op jit(solution)/shard_map/ppermute | solution.py:67
  7.0 0.2 multiply_convert_fusion.2.refs_0_
  7.2 1.6 %collective-permute-start.2 = (bf16[1024,128]{1,0:T(8,128)(2,1)S(1)}, bf16[1024,128]{1,0:T(8,128)(2,1)S(1)}, u32[]{:S(2)}, u32[]{:S(2)}) collective-permute-start(bf16[1024,128]{1,0:T(8,128)(2,1)S(1)} %multiply_convert_fusion.2.refs_0_), channel_id=1, source_target_pairs={{0,8},{2,10},{8,16},{10,18},{16,24},{18,26},{24,28},{26,30},{28,20... | collective-permute-start | bytes 786440 | tf_op jit(solution)/shard_map/ppermute | solution.py:35
  8.8 0.4 collective-permute-start.5
  9.3 0.1 stack.88.index_ref
  9.4 9.0 %collective-permute-done.9 = bf16[256,512]{1,0:T(8,128)(2,1)S(1)} collective-permute-done((bf16[256,512]{1,0:T(8,128)(2,1)S(1)}, bf16[256,512]{1,0:T(8,128)(2,1)S(1)}, u32[]{:S(2)}, u32[]{:S(2)}) %collective-permute-start.9) | collective-permute-done | bytes 262176 | tf_op jit(solution)/shard_map/ppermute | solution.py:67
  18.4 0.1 pad_maximum_fusion.own_features
  18.5 0.1 collective-permute-start.10
  18.5 0.0 collective-permute-done.2.refs_1_
  18.6 0.0 copy-start.1
  18.6 1.8 %collective-permute-start.3 = (bf16[1024,128]{1,0:T(8,128)(2,1)S(1)}, bf16[1024,128]{1,0:T(8,128)(2,1)}, u32[]{:S(2)}, u32[]{:S(2)}) collective-permute-start(bf16[1024,128]{1,0:T(8,128)(2,1)S(1)} %collective-permute-done.2.refs_1_), channel_id=1, source_target_pairs={{0,8},{2,10},{8,16},{10,18},{16,24},{18,26},{24,28},{26,30},{28,20... | collective-permute-start | bytes 786440 | tf_op jit(solution)/shard_map/ppermute | solution.py:35
  20.4 0.0 collective-permute-done.5.refs_2_
  20.4 0.2 collective-permute-start.6
  20.7 0.4 copy-done.3
  21.2 0.2 collective-permute-start.1
  21.4 0.1 reshape.75.fact_a
  21.5 5.9 %collective-permute-done.3.refs_3_ = bf16[1024,128]{1,0:T(8,128)(2,1)} collective-permute-done((bf16[1024,128]{1,0:T(8,128)(2,1)S(1)}, bf16[1024,128]{1,0:T(8,128)(2,1)}, u32[]{:S(2)}, u32[]{:S(2)}) %collective-permute-start.3) | collective-permute-done | bytes 262176 | tf_op jit(solution)/shard_map/ppermute | solution.py:35
  27.4 1.8 %collective-permute-start.4 = (bf16[1024,128]{1,0:T(8,128)(2,1)}, bf16[1024,128]{1,0:T(8,128)(2,1)S(1)}, u32[]{:S(2)}, u32[]{:S(2)}) collective-permute-start(bf16[1024,128]{1,0:T(8,128)(2,1)} %collective-permute-done.3.refs_3_), channel_id=1, source_target_pairs={{0,8},{2,10},{8,16},{10,18},{16,24},{18,26},{24,28},{26,30},{28,20... | collective-permute-start | bytes 786440 | tf_op jit(solution)/shard_map/ppermute | solution.py:35
  29.2 0.2 collective-permute-start.8
  29.4 0.1 reshape.77.fact_b
  29.5 1.0 %copy-done.2 = bf16[1024,128]{1,0:T(8,128)(2,1)S(1)} copy-done((bf16[1024,128]{1,0:T(8,128)(2,1)S(1)}, bf16[1024,128]{1,0:T(8,128)(2,1)}, u32[]{:S(2)}) %copy-start.2) | copy-done | bytes 262168
  30.5 0.9 %copy-done.4 = bf16[1024,128]{1,0:T(8,128)(2,1)S(1)} copy-done((bf16[1024,128]{1,0:T(8,128)(2,1)S(1)}, bf16[1024,128]{1,0:T(8,128)(2,1)}, u32[]{:S(2)}) %copy-start.4) | copy-done | bytes 262168
  31.4 2.6 %add_slabs.2.refs_2_ = f32[2,1024,128]{2,1,0:T(8,128)S(1)} custom-call(s32[10]{0:T(128)S(1)} %stack.88.index_ref, s32[136]{0:T(256)S(1)} %reshape.75.fact_a, s32[136]{0:T(256)S(1)} %reshape.77.fact_b, s16[8,144,128]{2,1,0:T(8,128)(2,1)S(1)} %bitcast.48, s16[8,144,128]{2,1,0:T(8,128)(2,1)S(1)} %collective-permute-done.1.words_b, ...), custom_call_target="tpu_custom_call" | custom-call | flops 335544320 | bytes 4194304 | tf_op jit(solution)/shard_map/add_slabs/pallas_call | solution.py:215
  34.0 1.4 %collective-permute-done.4.refs_0_ = bf16[1024,128]{1,0:T(8,128)(2,1)S(1)} collective-permute-done((bf16[1024,128]{1,0:T(8,128)(2,1)}, bf16[1024,128]{1,0:T(8,128)(2,1)S(1)}, u32[]{:S(2)}, u32[]{:S(2)}) %collective-permute-start.4) | collective-permute-done | bytes 262176 | tf_op jit(solution)/shard_map/ppermute | solution.py:35
  35.5 1.8 %collective-permute-start.7 = (bf16[1024,128]{1,0:T(8,128)(2,1)S(1)}, bf16[1024,128]{1,0:T(8,128)(2,1)S(1)}, u32[]{:S(2)}, u32[]{:S(2)}) collective-permute-start(bf16[1024,128]{1,0:T(8,128)(2,1)S(1)} %collective-permute-done.4.refs_0_), channel_id=1, source_target_pairs={{0,8},{2,10},{8,16},{10,18},{16,24},{18,26},{24,28},{26,30},{28,20... | collective-permute-start | bytes 786440 | tf_op jit(solution)/shard_map/ppermute | solution.py:35
  37.3 0.1 pad_add_fusion.3.index_ref
  37.3 0.1 pad_add_fusion.4.order_ref
  37.4 0.1 pad_add_fusion.5.index_ref
  37.5 1.8 %add_slabs.3.sums_in = f32[2,1024,128]{2,1,0:T(8,128)S(1)} custom-call(s32[4]{0:T(128)S(1)} %pad_add_fusion.5.index_ref, s32[136]{0:T(256)S(1)} %reshape.75.fact_a, s32[136]{0:T(256)S(1)} %reshape.77.fact_b, s16[8,144,128]{2,1,0:T(8,128)(2,1)S(1)} %bitcast.49, ...), custom_call_target="tpu_custom_call", output_to_operand_aliasing={{}: (7, {})} | custom-call | flops 134217728 | bytes 4194304 | tf_op jit(solution)/shard_map/add_slabs/pallas_call | solution.py:215
  39.3 3.2 %collective-permute-done.7.slab_ref = bf16[1024,128]{1,0:T(8,128)(2,1)S(1)} collective-permute-done((bf16[1024,128]{1,0:T(8,128)(2,1)S(1)}, bf16[1024,128]{1,0:T(8,128)(2,1)S(1)}, u32[]{:S(2)}, u32[]{:S(2)}) %collective-permute-start.7) | collective-permute-done | bytes 262176 | tf_op jit(solution)/shard_map/ppermute | solution.py:35
  42.5 1.5 %last_step.1 = (f32[1024,128]{1,0:T(8,128)S(1)}, f32[1024,128]{1,0:T(8,128)S(1)}, f32[128,128]{1,0:T(8,128)S(1)}, f32[128,128]{1,0:T(8,128)S(1)}) custom-call(s32[2]{0:T(128)S(1)} %pad_add_fusion.3.index_ref, s32[3]{0:T(128)S(1)} %pad_add_fusion.4.order_ref, s32[136]{0:T(256)S(1)} %reshape.75.fact_a, s32[136]{0:T(256)S(1)} %reshape.77.fact_b, ...), custom_call_target="tpu_custom_call" | custom-call | tf_op jit(solution)/shard_map/last_step/pallas_call | solution.py:247
  44.0 0.1 collective-permute-start.11
  44.1 0.5 collective-permute-start.13
  44.6 0.7 %collective-permute-done.11 = f32[128,128]{1,0:T(8,128)S(1)} collective-permute-done((f32[128,128]{1,0:T(8,128)S(1)}, f32[128,128]{1,0:T(8,128)S(1)}, u32[]{:S(2)}, u32[]{:S(2)}) %collective-permute-start.11) | collective-permute-done | bytes 65568 | tf_op jit(solution)/shard_map/ppermute | solution.py:57
  45.3 1.9 %collective-permute-start.12 = (bf16[128,128]{1,0:T(8,128)(2,1)S(1)}, bf16[128,128]{1,0:T(8,128)(2,1)S(1)}, u32[]{:S(2)}, u32[]{:S(2)}) collective-permute-start(bf16[128,128]{1,0:T(8,128)(2,1)S(1)} %add_convert_fusion.1), channel_id=1, source_target_pairs={{0,8},{2,10},{4,12},{6,14},{8,0},{10,2},{12,4},{14,6},{16,24},{18,... | collective-permute-start | bytes 98312 | tf_op jit(solution)/shard_map/ppermute | solution.py:43
  47.2 2.1 %collective-permute-done.12 = bf16[128,128]{1,0:T(8,128)(2,1)S(1)} collective-permute-done((bf16[128,128]{1,0:T(8,128)(2,1)S(1)}, bf16[128,128]{1,0:T(8,128)(2,1)S(1)}, u32[]{:S(2)}, u32[]{:S(2)}) %collective-permute-start.12) | collective-permute-done | bytes 32800 | tf_op jit(solution)/shard_map/ppermute | solution.py:43
  49.3 0.2 multiply_convert_fusion
  49.6 2.9 %collective-permute-start.14 = (bf16[128,128]{1,0:T(8,128)(2,1)S(1)}, bf16[128,128]{1,0:T(8,128)(2,1)S(1)}, u32[]{:S(2)}, u32[]{:S(2)}) collective-permute-start(bf16[128,128]{1,0:T(8,128)(2,1)S(1)} %convert_add_fusion.1), channel_id=1, source_target_pairs={{0,16},{2,18},{4,20},{6,22},{8,24},{10,26},{12,28},{14,30},{16,0},... | collective-permute-start | bytes 98312 | tf_op jit(solution)/shard_map/ppermute | solution.py:43
  52.4 2.0 %collective-permute-done.14 = bf16[128,128]{1,0:T(8,128)(2,1)S(1)} collective-permute-done((bf16[128,128]{1,0:T(8,128)(2,1)S(1)}, bf16[128,128]{1,0:T(8,128)(2,1)S(1)}, u32[]{:S(2)}, u32[]{:S(2)}) %collective-permute-start.14) | collective-permute-done | bytes 32800 | tf_op jit(solution)/shard_map/ppermute | solution.py:43
  54.5 1.8 %collective-permute-start.15 = (bf16[128,128]{1,0:T(8,128)(2,1)S(1)}, bf16[128,128]{1,0:T(8,128)(2,1)S(1)}, u32[]{:S(2)}, u32[]{:S(2)}) collective-permute-start(bf16[128,128]{1,0:T(8,128)(2,1)S(1)} %add_convert_fusion), channel_id=1, source_target_pairs={{0,4},{2,6},{4,0},{6,2},{8,12},{10,14},{12,8},{14,10},{16,20},{18,... | collective-permute-start | bytes 98312 | tf_op jit(solution)/shard_map/ppermute | solution.py:50
  56.3 1.6 %collective-permute-start.16 = (bf16[512,128]{1,0:T(8,128)(2,1)S(1)}, bf16[512,128]{1,0:T(8,128)(2,1)S(1)}, u32[]{:S(2)}, u32[]{:S(2)}) collective-permute-start(bf16[512,128]{1,0:T(8,128)(2,1)S(1)} %get-tuple-element.34), channel_id=1, source_target_pairs={{0,1},{1,0},{2,3},{3,2},{4,5},{5,4},{6,7},{7,6},{8,9},{9,8},{10,11... | collective-permute-start | bytes 393224 | tf_op jit(solution)/shard_map/ppermute | solution.py:67
  57.8 0.6 collective-permute-done.15
  58.5 3.5 %collective-permute-done.16 = bf16[512,128]{1,0:T(8,128)(2,1)S(1)} collective-permute-done((bf16[512,128]{1,0:T(8,128)(2,1)S(1)}, bf16[512,128]{1,0:T(8,128)(2,1)S(1)}, u32[]{:S(2)}, u32[]{:S(2)}) %collective-permute-start.16) | collective-permute-done | bytes 131104 | tf_op jit(solution)/shard_map/ppermute | solution.py:67
  62.0 1.5 %collective-permute-start.17 = (f32[128,128]{1,0:T(8,128)S(1)}, f32[128,128]{1,0:T(8,128)S(1)}, u32[]{:S(2)}, u32[]{:S(2)}) collective-permute-start(f32[128,128]{1,0:T(8,128)S(1)} %convert_add_fusion), channel_id=1, source_target_pairs={{0,1},{1,0},{2,3},{3,2},{4,5},{5,4},{6,7},{7,6},{8,9},{9,8},{10,11... | collective-permute-start | bytes 196616 | tf_op jit(solution)/shard_map/ppermute | solution.py:67
  63.5 0.2 fusion.3
  63.7 0.9 %fusion = bf16[512,256]{1,0:T(8,128)(2,1)} fusion(f32[512,256]{1,0:T(8,128)S(1)} %fusion.3, bf16[512,128]{1,0:T(8,128)(2,1)S(1)} %get-tuple-element.24, bf16[256,256]{1,0:T(8,128)(2,1)S(1)} %copy-done, s32[]{:T(128)S(6)} %select_n.485), kind=kOutput, calls=%fused_computation.1 | convolution fusion | flops 33816576 | bytes 983044 | tf_op jit(solution)/shard_map/dot_general | solution.py:288
  64.7 1.5 %collective-permute-done.17 = f32[128,128]{1,0:T(8,128)S(1)} collective-permute-done((f32[128,128]{1,0:T(8,128)S(1)}, f32[128,128]{1,0:T(8,128)S(1)}, u32[]{:S(2)}, u32[]{:S(2)}) %collective-permute-start.17) | collective-permute-done | bytes 65568 | tf_op jit(solution)/shard_map/ppermute | solution.py:67
  66.3 0.1 collective-permute-start.18
  66.4 1.3 %collective-permute-done.18 = f32[128,256]{1,0:T(8,128)S(1)} collective-permute-done((f32[128,256]{1,0:T(8,128)S(1)}, f32[128,256]{1,0:T(8,128)S(1)}, u32[]{:S(2)}, u32[]{:S(2)}) %collective-permute-start.18) | collective-permute-done | bytes 131104 | tf_op jit(solution)/shard_map/ppermute | solution.py:57
  67.7 0.7 %pad_maximum_fusion.1 = f32[256,256]{1,0:T(8,128)} fusion(f32[128,256]{1,0:T(8,128)S(1)} %get-tuple-element.33, f32[128,256]{1,0:T(8,128)S(1)} %get-tuple-element.32), kind=kLoop, calls=%fused_computation.8 | loop fusion | flops 65536 | bytes 524288 | tf_op jit(solution)/shard_map/concatenate | solution.py:299
  (40 shorter events, 0.3 us)
Async XLA Ops:
  0.6 62.9 %copy-start = (bf16[256,256]{1,0:T(8,128)(2,1)S(1)}, bf16[256,256]{1,0:T(8,128)(2,1)}, u32[]{:S(2)}) copy-start(bf16[256,256]{1,0:T(8,128)(2,1)} %param.9) | copy-start | bytes 393220
  0.6 1.9 %copy-start.7 = (s32[1,8,2,8]{3,2,1,0:T(2,128)S(1)}, s32[1,8,2,8]{3,2,1,0:T(2,128)}, u32[]{:S(2)}) copy-start(s32[1,8,2,8]{3,2,1,0:T(2,128)} %param.11) | copy-start | bytes 1540
  1.8 0.7 copy-start.9
  2.7 3.1 %copy-start.5 = (bf16[512,256]{1,0:T(8,128)(2,1)S(1)}, bf16[512,256]{1,0:T(8,128)(2,1)}, u32[]{:S(2)}) copy-start(bf16[512,256]{1,0:T(8,128)(2,1)} %param.7) | copy-start | bytes 786436
  2.7 3.0 %copy-start.8 = (s32[1024]{0:T(1024)S(1)}, s32[1024]{0:T(1024)}, u32[]{:S(2)}) copy-start(s32[1024]{0:T(1024)} %param.13) | copy-start | bytes 12292
  2.8 17.9 %collective-permute-start = (s16[8,144,128]{2,1,0:T(8,128)(2,1)S(1)}, s16[8,144,128]{2,1,0:T(8,128)(2,1)S(1)}, u32[]{:S(2)}, u32[]{:S(2)}) collective-permute-start(s16[8,144,128]{2,1,0:T(8,128)(2,1)S(1)} %pad_add_fusion.1), channel_id=1, source_target_pairs={{0,1},{1,0},{2,3},{3,2},{4,5},{5,4},{6,7},{7,6},{8,9},{9,8},{10,11... | collective-permute-start | bytes 884744 | tf_op jit(solution)/shard_map/ppermute | solution.py:67
  6.0 1.1 %copy-start.6 = (bf16[1024,256]{1,0:T(8,128)(2,1)S(1)}, bf16[1024,256]{1,0:T(8,128)(2,1)}, u32[]{:S(2)}) copy-start(bf16[1024,256]{1,0:T(8,128)(2,1)} %param.8) | copy-start | bytes 1572868
  6.1 12.3 %collective-permute-start.9 = (bf16[256,512]{1,0:T(8,128)(2,1)S(1)}, bf16[256,512]{1,0:T(8,128)(2,1)S(1)}, u32[]{:S(2)}, u32[]{:S(2)}) collective-permute-start(bf16[256,512]{1,0:T(8,128)(2,1)S(1)} %get-tuple-element.31), channel_id=1, source_target_pairs={{0,1},{1,0},{2,3},{3,2},{4,5},{5,4},{6,7},{7,6},{8,9},{9,8},{10,11... | collective-permute-start | bytes 786440 | tf_op jit(solution)/shard_map/ppermute | solution.py:67
  7.2 11.3 %collective-permute-start.2 = (bf16[1024,128]{1,0:T(8,128)(2,1)S(1)}, bf16[1024,128]{1,0:T(8,128)(2,1)S(1)}, u32[]{:S(2)}, u32[]{:S(2)}) collective-permute-start(bf16[1024,128]{1,0:T(8,128)(2,1)S(1)} %multiply_convert_fusion.2.refs_0_), channel_id=1, source_target_pairs={{0,8},{2,10},{8,16},{10,18},{16,24},{18,26},{24,28},{26,30},{28,20... | collective-permute-start | bytes 786440 | tf_op jit(solution)/shard_map/ppermute | solution.py:35
  8.8 11.6 %collective-permute-start.5 = (bf16[1024,128]{1,0:T(8,128)(2,1)S(1)}, bf16[1024,128]{1,0:T(8,128)(2,1)S(1)}, u32[]{:S(2)}, u32[]{:S(2)}) collective-permute-start(bf16[1024,128]{1,0:T(8,128)(2,1)S(1)} %multiply_convert_fusion.2.refs_0_), channel_id=1, source_target_pairs={{0,4},{2,6},{8,0},{10,2},{16,8},{18,10},{24,16},{26,18},{28,24},{3... | collective-permute-start | bytes 786440 | tf_op jit(solution)/shard_map/ppermute | solution.py:35
  18.5 20.8 %collective-permute-start.10 = (bf16[2,256,512]{2,1,0:T(8,128)(2,1)S(1)}, bf16[2,256,512]{2,1,0:T(8,128)(2,1)S(1)}, u32[]{:S(2)}, u32[]{:S(2)}) collective-permute-start(bf16[2,256,512]{2,1,0:T(8,128)(2,1)S(1)} %pad_maximum_fusion.own_features), channel_id=1, source_target_pairs={{0,2},{2,0},{4,6},{6,4},{8,10},{10,8},{12,14},{14,12},{16,18},{18,... | collective-permute-start | bytes 1572872 | tf_op jit(solution)/shard_map/ppermute | solution.py:57
  18.6 2.1 %copy-start.1 = (bf16[1024,128]{1,0:T(8,128)(2,1)}, bf16[1024,128]{1,0:T(8,128)(2,1)S(1)}, u32[]{:S(2)}) copy-start(bf16[1024,128]{1,0:T(8,128)(2,1)S(1)} %collective-permute-done.2.refs_1_) | copy-start | bytes 786436
  18.6 8.8 %collective-permute-start.3 = (bf16[1024,128]{1,0:T(8,128)(2,1)S(1)}, bf16[1024,128]{1,0:T(8,128)(2,1)}, u32[]{:S(2)}, u32[]{:S(2)}) collective-permute-start(bf16[1024,128]{1,0:T(8,128)(2,1)S(1)} %collective-permute-done.2.refs_1_), channel_id=1, source_target_pairs={{0,8},{2,10},{8,16},{10,18},{16,24},{18,26},{24,28},{26,30},{28,20... | collective-permute-start | bytes 786440 | tf_op jit(solution)/shard_map/ppermute | solution.py:35
  20.4 0.7 %copy-start.3 = (bf16[1024,128]{1,0:T(8,128)(2,1)}, bf16[1024,128]{1,0:T(8,128)(2,1)S(1)}, u32[]{:S(2)}) copy-start(bf16[1024,128]{1,0:T(8,128)(2,1)S(1)} %collective-permute-done.5.refs_2_) | copy-start | bytes 786436
  20.4 8.8 %collective-permute-start.6 = (bf16[1024,128]{1,0:T(8,128)(2,1)S(1)}, bf16[1024,128]{1,0:T(8,128)(2,1)}, u32[]{:S(2)}, u32[]{:S(2)}) collective-permute-start(bf16[1024,128]{1,0:T(8,128)(2,1)S(1)} %collective-permute-done.5.refs_2_), channel_id=1, source_target_pairs={{0,4},{2,6},{8,0},{10,2},{16,8},{18,10},{24,16},{26,18},{28,24},{3... | collective-permute-start | bytes 786440 | tf_op jit(solution)/shard_map/ppermute | solution.py:35
  21.2 8.2 %collective-permute-start.1 = (s16[8,144,128]{2,1,0:T(8,128)(2,1)S(1)}, s16[8,144,128]{2,1,0:T(8,128)(2,1)S(1)}, u32[]{:S(2)}, u32[]{:S(2)}) collective-permute-start(s16[8,144,128]{2,1,0:T(8,128)(2,1)S(1)} %bitcast.54), channel_id=1, source_target_pairs={{0,2},{2,0},{4,6},{6,4},{8,10},{10,8},{12,14},{14,12},{16,18},{18,... | collective-permute-start | bytes 884744 | tf_op jit(solution)/shard_map/ppermute | solution.py:57
  27.4 8.1 %collective-permute-start.4 = (bf16[1024,128]{1,0:T(8,128)(2,1)}, bf16[1024,128]{1,0:T(8,128)(2,1)S(1)}, u32[]{:S(2)}, u32[]{:S(2)}) collective-permute-start(bf16[1024,128]{1,0:T(8,128)(2,1)} %collective-permute-done.3.refs_3_), channel_id=1, source_target_pairs={{0,8},{2,10},{8,16},{10,18},{16,24},{18,26},{24,28},{26,30},{28,20... | collective-permute-start | bytes 786440 | tf_op jit(solution)/shard_map/ppermute | solution.py:35
  29.2 8.3 %collective-permute-start.8 = (bf16[1024,128]{1,0:T(8,128)(2,1)}, bf16[1024,128]{1,0:T(8,128)(2,1)}, u32[]{:S(2)}, u32[]{:S(2)}) collective-permute-start(bf16[1024,128]{1,0:T(8,128)(2,1)} %collective-permute-done.6.refs_4_), channel_id=1, source_target_pairs={{0,4},{2,6},{8,0},{10,2},{16,8},{18,10},{24,16},{26,18},{28,24},{3... | collective-permute-start | bytes 786440 | tf_op jit(solution)/shard_map/ppermute | solution.py:35
  29.5 1.0 %copy-start.2 = (bf16[1024,128]{1,0:T(8,128)(2,1)S(1)}, bf16[1024,128]{1,0:T(8,128)(2,1)}, u32[]{:S(2)}) copy-start(bf16[1024,128]{1,0:T(8,128)(2,1)} %copy-done.1) | copy-start | bytes 786436
  30.5 0.9 %copy-start.4 = (bf16[1024,128]{1,0:T(8,128)(2,1)S(1)}, bf16[1024,128]{1,0:T(8,128)(2,1)}, u32[]{:S(2)}) copy-start(bf16[1024,128]{1,0:T(8,128)(2,1)} %copy-done.3) | copy-start | bytes 786436
  35.5 7.1 %collective-permute-start.7 = (bf16[1024,128]{1,0:T(8,128)(2,1)S(1)}, bf16[1024,128]{1,0:T(8,128)(2,1)S(1)}, u32[]{:S(2)}, u32[]{:S(2)}) collective-permute-start(bf16[1024,128]{1,0:T(8,128)(2,1)S(1)} %collective-permute-done.4.refs_0_), channel_id=1, source_target_pairs={{0,8},{2,10},{8,16},{10,18},{16,24},{18,26},{24,28},{26,30},{28,20... | collective-permute-start | bytes 786440 | tf_op jit(solution)/shard_map/ppermute | solution.py:35
  44.0 1.3 %collective-permute-start.11 = (f32[128,128]{1,0:T(8,128)S(1)}, f32[128,128]{1,0:T(8,128)S(1)}, u32[]{:S(2)}, u32[]{:S(2)}) collective-permute-start(f32[128,128]{1,0:T(8,128)S(1)} %get-tuple-element.18), channel_id=1, source_target_pairs={{0,2},{2,0},{4,6},{6,4},{8,10},{10,8},{12,14},{14,12},{16,18},{18,... | collective-permute-start | bytes 196616 | tf_op jit(solution)/shard_map/ppermute | solution.py:57
  44.1 5.3 %collective-permute-start.13 = (f32[1024,128]{1,0:T(8,128)S(1)}, f32[1024,128]{1,0:T(8,128)S(1)}, u32[]{:S(2)}, u32[]{:S(2)}) collective-permute-start(f32[1024,128]{1,0:T(8,128)S(1)} %get-tuple-element.20), channel_id=1, source_target_pairs={{0,2},{2,0},{4,6},{6,4},{8,10},{10,8},{12,14},{14,12},{16,18},{18,... | collective-permute-start | bytes 1572872 | tf_op jit(solution)/shard_map/ppermute | solution.py:57
  45.3 4.0 %collective-permute-start.12 = (bf16[128,128]{1,0:T(8,128)(2,1)S(1)}, bf16[128,128]{1,0:T(8,128)(2,1)S(1)}, u32[]{:S(2)}, u32[]{:S(2)}) collective-permute-start(bf16[128,128]{1,0:T(8,128)(2,1)S(1)} %add_convert_fusion.1), channel_id=1, source_target_pairs={{0,8},{2,10},{4,12},{6,14},{8,0},{10,2},{12,4},{14,6},{16,24},{18,... | collective-permute-start | bytes 98312 | tf_op jit(solution)/shard_map/ppermute | solution.py:43
  49.6 4.9 %collective-permute-start.14 = (bf16[128,128]{1,0:T(8,128)(2,1)S(1)}, bf16[128,128]{1,0:T(8,128)(2,1)S(1)}, u32[]{:S(2)}, u32[]{:S(2)}) collective-permute-start(bf16[128,128]{1,0:T(8,128)(2,1)S(1)} %convert_add_fusion.1), channel_id=1, source_target_pairs={{0,16},{2,18},{4,20},{6,22},{8,24},{10,26},{12,28},{14,30},{16,0},... | collective-permute-start | bytes 98312 | tf_op jit(solution)/shard_map/ppermute | solution.py:43
  54.5 4.0 %collective-permute-start.15 = (bf16[128,128]{1,0:T(8,128)(2,1)S(1)}, bf16[128,128]{1,0:T(8,128)(2,1)S(1)}, u32[]{:S(2)}, u32[]{:S(2)}) collective-permute-start(bf16[128,128]{1,0:T(8,128)(2,1)S(1)} %add_convert_fusion), channel_id=1, source_target_pairs={{0,4},{2,6},{4,0},{6,2},{8,12},{10,14},{12,8},{14,10},{16,20},{18,... | collective-permute-start | bytes 98312 | tf_op jit(solution)/shard_map/ppermute | solution.py:50
  56.3 5.7 %collective-permute-start.16 = (bf16[512,128]{1,0:T(8,128)(2,1)S(1)}, bf16[512,128]{1,0:T(8,128)(2,1)S(1)}, u32[]{:S(2)}, u32[]{:S(2)}) collective-permute-start(bf16[512,128]{1,0:T(8,128)(2,1)S(1)} %get-tuple-element.34), channel_id=1, source_target_pairs={{0,1},{1,0},{2,3},{3,2},{4,5},{5,4},{6,7},{7,6},{8,9},{9,8},{10,11... | collective-permute-start | bytes 393224 | tf_op jit(solution)/shard_map/ppermute | solution.py:67
  62.0 4.3 %collective-permute-start.17 = (f32[128,128]{1,0:T(8,128)S(1)}, f32[128,128]{1,0:T(8,128)S(1)}, u32[]{:S(2)}, u32[]{:S(2)}) collective-permute-start(f32[128,128]{1,0:T(8,128)S(1)} %convert_add_fusion), channel_id=1, source_target_pairs={{0,1},{1,0},{2,3},{3,2},{4,5},{5,4},{6,7},{7,6},{8,9},{9,8},{10,11... | collective-permute-start | bytes 196616 | tf_op jit(solution)/shard_map/ppermute | solution.py:67
  66.3 1.4 %collective-permute-start.18 = (f32[128,256]{1,0:T(8,128)S(1)}, f32[128,256]{1,0:T(8,128)S(1)}, u32[]{:S(2)}, u32[]{:S(2)}) collective-permute-start(f32[128,256]{1,0:T(8,128)S(1)} %broadcast_multiply_fusion), channel_id=1, source_target_pairs={{0,2},{2,0},{4,6},{6,4},{8,10},{10,8},{12,14},{14,12},{16,18},{18,... | collective-permute-start | bytes 393224 | tf_op jit(solution)/shard_map/ppermute | solution.py:57

commit v4 on v3

v4 whole, which is shorter than its diff:
```python
import functools
import math

import jax
import jax.numpy as jnp
from jax import lax
from jax.experimental import pallas as pl
from jax.experimental.pallas import tpu as pltpu
from jax.sharding import PartitionSpec as P

CORES = 2
COLUMNS = 2


def device_of(row, column, core):
    return (row * COLUMNS + column) * CORES + core


def places(blk_size):
    rows = blk_size // (COLUMNS * CORES)
    return [(z, x, c) for z in range(rows) for x in range(COLUMNS) for c in range(CORES)]


def ring_order(rows):
    return [(z, 0) for z in range(rows)] + [(z, 1) for z in reversed(range(rows))]


def along_ring(block, distance):
    rows = lax.axis_size("blk") // (COLUMNS * CORES)
    order = ring_order(rows)
    route = []
    for place, (z, x) in enumerate(order):
        to_z, to_x = order[(place + distance) % len(order)]
        route += [(device_of(z, x, c), device_of(to_z, to_x, c)) for c in range(CORES)]
    return lax.ppermute(block, "blk", route)


def across_rows(block, distance):
    route = [
        (device_of(z, x, c), device_of(z ^ distance, x, c))
        for z, x, c in places(lax.axis_size("blk"))
    ]
    return lax.ppermute(block, "blk", route)


def across_columns(block):
    route = [
        (device_of(z, x, c), device_of(z, 1 - x, c)) for z, x, c in places(lax.axis_size("blk"))
    ]
    return lax.ppermute(block, "blk", route)


def across_cores(block):
    route = [
        (device_of(z, x, c), device_of(z, x, 1 - c)) for z, x, c in places(lax.axis_size("blk"))
    ]
    return lax.ppermute(block, "blk", route)


def along_rep(block, distance):
    size = lax.axis_size("rep")
    return lax.ppermute(block, "rep", [(i, (i + distance) % size) for i in range(size)])


def along_rep(block, distance):
    size = lax.axis_size("rep")
    return lax.ppermute(block, "rep", [(i, (i + distance) % size) for i in range(size)])


def across_columns_and_rep(block, distance):
    size = lax.axis_size("rep")
    route = [
        (device_of(z, x, c) * size + r, device_of(z, 1 - x, c) * size + (r + distance) % size)
        for z, x, c in places(lax.axis_size("blk"))
        for r in range(size)
    ]
    return lax.ppermute(block, ("blk", "rep"), route)


def from_all_reps(block):
    return [block] + [along_rep(block, d) for d in range(1, lax.axis_size("rep"))]


def add_pairs(plan, table_ref, first_slab, own_pieces, other_pieces, slabs, sums_ref):
    bit_ids = lax.broadcasted_iota(jnp.int32, (16, 8, 128), 1)
    for slab_id, slab_ref in enumerate(slabs):
        for target, pieces in enumerate((own_pieces, other_pieces)):
            at = plan.facts_size + 2 * (2 * (first_slab + slab_id) + target)
            piece, pair = table_ref[at], table_ref[at + 1]
            base = ((piece * 2 + target) * plan.pairs + pair) * plan.facts
            live_count = table_ref[base]
            for slot in range(plan.slots):
                row_block = table_ref[base + 1 + slot]
                column_block = table_ref[base + 1 + plan.slots + slot]
                word_rows = pl.ds(pl.multiple_of(pair * plan.pair_rows + slot * 16, 16), 16)
                slot_words = jnp.zeros((16, 128), jnp.float32)
                for piece_id, piece_ref in enumerate(pieces):
                    chosen = jnp.logical_and(piece == piece_id, slot < live_count)
                    scale = jnp.where(chosen, 1.0, 0.0)
                    slot_words += piece_ref[word_rows, :].astype(jnp.float32) * scale
                slot_words = slot_words.astype(jnp.int32)
                bits = jnp.bitwise_and(jnp.right_shift(slot_words[:, None, :], bit_ids), 1)
                transposed = bits.reshape(128, 128).astype(jnp.float32).astype(jnp.bfloat16)
                rows = pl.ds(pl.multiple_of(row_block * 128, 128), 128)
                columns = pl.ds(pl.multiple_of(column_block * 128, 128), 128)
                sums_ref[target, columns, :] += jnp.dot(
                    transposed, slab_ref[rows, :], preferred_element_type=jnp.float32
                )


def first_kernel(plan, slab_total, table_ref, *refs):
    pieces, slabs, sums_ref = refs[: 2 * plan.reps], refs[2 * plan.reps : -1], refs[-1]
    sums_ref[...] = jnp.zeros_like(sums_ref)
    add_pairs(plan, table_ref, 0, pieces[: plan.reps], pieces[plan.reps :], slabs, sums_ref)


def last_kernel(plan, last_slab, table_ref, *refs):
    own_pieces, other_pieces = refs[: plan.reps], refs[plan.reps : 2 * plan.reps]
    own_features, other_features = refs[2 * plan.reps : 3 * plan.reps], refs[3 * plan.reps : 4 * plan.reps]
    slab_ref, sums_in, own_ref, other_ref, keep_ref, send_ref, sums_ref, term_ref = refs[4 * plan.reps :]
    sums_ref[...] = sums_in[...]
    add_pairs(plan, table_ref, last_slab, own_pieces, other_pieces, [slab_ref], sums_ref)
    own_ref[...] = sums_ref[0]
    other_ref[...] = sums_ref[1]
    share = sums_ref.shape[1] // plan.reps
    width = term_ref.shape[0]
    order_at = plan.facts_size + 4 * (last_slab + 1)
    term = jnp.zeros(term_ref.shape, jnp.float32)
    for target, pieces in enumerate((own_features, other_features)):
        for piece_id, piece_ref in enumerate(pieces):
            start = pl.multiple_of(table_ref[order_at + piece_id] * share, share)
            for block in range(share // 128):
                rows = pl.ds(pl.multiple_of(start + block * 128, 128), 128)
                part = sums_ref[target, rows, :].astype(jnp.bfloat16)
                features = piece_ref[block * width : (block + 1) * width, :]
                term += jnp.dot(features, part, preferred_element_type=jnp.float32)
    term_ref[...] = term
    half = width // 2
    core = table_ref[order_at + plan.reps]
    keep_ref[...] = term_ref[pl.ds(pl.multiple_of(core * half, half), half), :]
    send_ref[...] = term_ref[pl.ds(pl.multiple_of((1 - core) * half, half), half), :]


class Plan:
    def __init__(self, reps, slots, pairs):
        self.reps, self.slots, self.pairs = reps, slots, pairs
        self.pair_rows = slots * 16 + 16
        self.facts = 1 + 2 * slots
        self.facts_size = reps * 2 * pairs * self.facts


def scale_kernel(share_width, degrees_hbm, gradient_hbm, scaled_ref, degrees_ref, rows_ref, semaphores):
    start = pl.multiple_of(lax.axis_index("rep") * share_width, share_width)
    chunks = semaphores.shape[0] - 1
    chunk_rows = rows_ref.shape[0] // chunks
    degrees_copy = pltpu.make_async_copy(degrees_hbm, degrees_ref, semaphores.at[chunks])
    degrees_copy.start()
    copies = []
    for chunk in range(chunks):
        rows = pl.ds(chunk * chunk_rows, chunk_rows)
        copies.append(
            pltpu.make_async_copy(gradient_hbm.at[rows], rows_ref.at[rows], semaphores.at[chunk])
        )
        copies[-1].start()
    degrees_copy.wait()
    roots = lax.rsqrt(degrees_ref[...].astype(jnp.float32))
    for chunk in range(chunks):
        copies[chunk].wait()
        for at in range(chunk * chunk_rows, (chunk + 1) * chunk_rows, 128):
            row = at // 128
            by_row = jnp.broadcast_to(roots[row : row + 1, :], (128, 128)).T
            for column in range(0, share_width, 128):
                own = pl.ds(pl.multiple_of(start + column, 128), 128)
                part = rows_ref[at : at + 128, own].astype(jnp.float32) * by_row
                scaled_ref[at : at + 128, column : column + 128] = part.astype(scaled_ref.dtype)


def payload_kernel(plan, facts_ref, words_ref, features_ref, roots_ref, pairs_ref, turned_ref):
    word_rows = plan.slots * 16
    for step in range(2 * plan.pairs):
        start = ((step % 2) * plan.pairs + step // 2) * plan.pair_rows
        words = words_ref[step].astype(jnp.float32).astype(pairs_ref.dtype)
        pairs_ref[start : start + word_rows, :] = words
        facts = jnp.broadcast_to(facts_ref[step : step + 1, :].astype(jnp.float32), (16, 128))
        pairs_ref[start + word_rows : start + plan.pair_rows, :] = facts.astype(pairs_ref.dtype)
    rows, width = features_ref.shape
    for block in range(rows // 128):
        part = features_ref[block * 128 : (block + 1) * 128, :].astype(jnp.float32).T
        part = part * roots_ref[:, block * 128 : (block + 1) * 128]
        turned_ref[block * width : (block + 1) * width, :] = part.astype(turned_ref.dtype)


SMEM = pl.BlockSpec(memory_space=pltpu.SMEM)
VMEM = pl.BlockSpec(memory_space=pltpu.VMEM)
PARAMS = pltpu.CompilerParams(vmem_limit_bytes=12 * 1024 * 1024)


def per_device(features, out_grad, weight, block_words, block_coords, block_counts, degrees):
    slab_rows, width = out_grad.shape
    rep_size = lax.axis_size("rep")
    blk_size = lax.axis_size("blk")
    chips = blk_size // CORES
    rows_of_chips = chips // COLUMNS
    rep_index = lax.axis_index("rep")
    blk_index = lax.axis_index("blk")
    core = blk_index % CORES
    chip = blk_index // CORES
    share_width = width // rep_size
    share_rows = slab_rows // rep_size
    slot_total = block_words.shape[2]
    half_steps = block_words.shape[1] // 2

    inverse_root = lax.rsqrt(degrees.astype(jnp.float32))
    if share_width % 128 == 0 and slab_rows % 1024 == 0:
        scaled = pl.pallas_call(
            functools.partial(scale_kernel, share_width),
            out_shape=jax.ShapeDtypeStruct((slab_rows, share_width), jnp.bfloat16),
            in_specs=[pl.BlockSpec(memory_space=pltpu.HBM)] * 2,
            out_specs=VMEM,
            scratch_shapes=[
                pltpu.VMEM((slab_rows // 128, 128), jnp.int32),
                pltpu.VMEM((slab_rows, width), jnp.bfloat16),
                pltpu.SemaphoreType.DMA((5,)),
            ],
            compiler_params=pltpu.CompilerParams(vmem_limit_bytes=60 * 1024 * 1024),
            name="scale",
        )(degrees.reshape(slab_rows // 128, 128), out_grad)
    else:
        own_columns = lax.dynamic_slice_in_dim(out_grad, rep_index * share_width, share_width, 1)
        scaled = (own_columns.astype(jnp.float32) * inverse_root[:, None]).astype(jnp.bfloat16)

    forward, backward = along_ring(scaled, 1), along_ring(scaled, -1)

    block_words, features, _ = lax.optimization_barrier((block_words, features, scaled))
    plan = Plan(rep_size, slot_total, half_steps)
    facts = jnp.concatenate(
        [block_counts[0][:, None], block_coords[0].reshape(2 * half_steps, 2 * slot_total)], axis=1
    )
    facts = jnp.pad(facts, ((0, 0), (0, 128 - plan.facts)))
    words_rows = half_steps * plan.pair_rows
    share_root = lax.dynamic_slice_in_dim(inverse_root, rep_index * share_rows, share_rows, 0)
    pairs, turned = pl.pallas_call(
        functools.partial(payload_kernel, plan),
        out_shape=(
            jax.ShapeDtypeStruct((2 * words_rows, 128), jnp.bfloat16),
            jax.ShapeDtypeStruct((share_rows // 128 * width, 128), jnp.bfloat16),
        ),
        in_specs=[VMEM] * 4,
        out_specs=(VMEM, VMEM),
        compiler_params=PARAMS,
        name="payload",
    )(facts, block_words[0].reshape(2 * half_steps, slot_total * 16, 128), features, share_root[None])
    own_pieces = from_all_reps(pairs)
    other_pieces = [across_cores(piece[words_rows:]) for piece in own_pieces]
    own_features = from_all_reps(turned)
    other_features = [across_cores(piece) for piece in own_features]

    def facts_of(piece):
        rows = piece[:words_rows].reshape(half_steps, plan.pair_rows, 128)[:, slot_total * 16]
        return rows[:, : plan.facts].astype(jnp.int32).reshape(-1)

    ring_row = chip // COLUMNS
    place = jnp.where(chip % COLUMNS == 0, ring_row, chips - 1 - ring_row)
    distances = [0]
    for step in range(1, chips // 2):
        distances += [-step, step]
    distances.append(chips // 2)
    entries = []
    for distance in distances:
        at = (place + distance) % chips
        source = jnp.where(at < rows_of_chips, at * COLUMNS, (chips - 1 - at) * COLUMNS + 1)
        for target in range(2):
            offset = (source - chip - jnp.where(core == 0, target, 0)) % chips
            entries += [(rep_index - offset // half_steps) % rep_size, offset % half_steps]
    entries += [(rep_index - d) % rep_size for d in range(rep_size)] + [core]
    table = [facts_of(piece) for pair in zip(own_pieces, other_pieces) for piece in pair]
    table = jnp.concatenate(table + [jnp.stack(entries).astype(jnp.int32)])

    slabs = [scaled]
    for step in range(1, chips // 2):
        slabs += [forward, backward]
        forward, backward = along_ring(forward, 1), along_ring(backward, -1)
    del backward

    slab_shape = jax.ShapeDtypeStruct((slab_rows, share_width), jnp.float32)
    half_term = jax.ShapeDtypeStruct((width // 2, share_width), jnp.float32)
    sums_shape = jax.ShapeDtypeStruct((2, slab_rows, share_width), jnp.float32)
    pair_flops = 2 * slot_total * 128 * 128 * share_width * 2
    sums = pl.pallas_call(
        functools.partial(first_kernel, plan, len(slabs)),
        out_shape=sums_shape,
        in_specs=[SMEM] + [VMEM] * (2 * rep_size + len(slabs)),
        out_specs=VMEM,
        compiler_params=PARAMS,
        cost_estimate=pl.CostEstimate(flops=1, bytes_accessed=1, transcendentals=0),
        name="first_slabs",
    )(table, *own_pieces, *other_pieces, *slabs)
    own_sums, other_sums, keep, send = pl.pallas_call(
        functools.partial(last_kernel, plan, len(slabs)),
        out_shape=(slab_shape, slab_shape, half_term, half_term),
        in_specs=[SMEM] + [VMEM] * (4 * rep_size + 2),
        out_specs=(VMEM,) * 4,
        scratch_shapes=[
            pltpu.VMEM(sums_shape.shape, jnp.float32),
            pltpu.VMEM((width, share_width), jnp.float32),
        ],
        compiler_params=PARAMS,
        name="last_slab",
    )(table, *own_pieces, *other_pieces, *own_features, *other_features, forward, sums)

    def add_across_rows(total, distance):
        total = total.astype(jnp.bfloat16)
        return total.astype(jnp.float32) + across_rows(total, distance).astype(jnp.float32)

    total = keep + across_cores(send)
    own_sums = own_sums + across_cores(other_sums)
    aggregated = (own_sums * inverse_root[:, None]).astype(jnp.bfloat16)
    distance = 1
    while distance < rows_of_chips:
        total = add_across_rows(total, distance)
        distance *= 2
    total, aggregated = lax.optimization_barrier((total, aggregated))
    total = total.astype(jnp.bfloat16)
    total = total.astype(jnp.float32) + across_columns(total).astype(jnp.float32)

    total = total.astype(jnp.bfloat16)
    result = jnp.zeros((share_rows, width), jnp.float32)
    weight_half = jnp.zeros((width // 2, width), jnp.float32)
    for d in range(rep_size):
        rows_to = ((rep_index + d) % rep_size) * share_rows
        part = lax.dynamic_slice_in_dim(aggregated, rows_to, share_rows, 0)
        columns = total
        if d:
            both = along_rep(jnp.concatenate([part, total]), d)
            part, columns = both[:share_rows], both[share_rows:]
        columns_at = ((rep_index - d) % rep_size) * share_width
        side = lax.dynamic_slice_in_dim(weight, columns_at, share_width, 1)
        result = result + lax.dot_general(
            part, side, (((1,), (1,)), ((), ())), preferred_element_type=jnp.float32
        )
        weight_half = lax.dynamic_update_slice_in_dim(
            weight_half, columns.astype(jnp.float32), columns_at, 1
        )
    input_grad = result.astype(jnp.bfloat16)
    weight_half = weight_half * (1.0 / math.sqrt(slab_rows * blk_size))
    other_half = across_cores(weight_half)
    weight_grad = jnp.concatenate(
        [jnp.where(core == 0, weight_half, other_half), jnp.where(core == 0, other_half, weight_half)]
    )
    return (input_grad, weight_grad)


def solution(mesh):
    return jax.shard_map(
        per_device,
        mesh=mesh,
        in_specs=(
            P(("blk", "rep"), None),
            P("blk", None),
            P(),
            P("blk", "rep", None, None, None),
            P("blk", "rep", None, None),
            P("blk", "rep"),
            P("blk"),
        ),
        out_specs=(P(("blk", "rep"), None), P()),
        check_vma=False,
    )
```

time: 68.7 us -> 58.3 us (0.85)
  starting transfers between devices: 22.5 us -> 18.5 us
  waiting for transfers between devices: 31.4 us -> 27.6 us
  local copies, waits for them, and re-layouts: 3.77 us -> 1.49 us
  other arithmetic: 2.83 us -> 1.13 us
  Pallas kernels: 5.88 us -> 7.12 us
    ppermute x4 -> x3, waiting for transfers between devices: 14.1 us -> 3.57 us  [along_rep(): lax.ppermute(block, 'rep', [(i, (i + distance) % size) for i in range(siz...]
    ppermute x7, waiting for transfers between devices: 10.5 us -> 15.1 us  [along_ring(): return lax.ppermute(block, 'blk', route)]
    ppermute x4 -> x3, starting transfers between devices: 7.04 us -> 3.74 us  [along_rep(): lax.ppermute(block, 'rep', [(i, (i + distance) % size) for i in range(siz...]
    ppermute x1, waiting for transfers between devices: 0.6 us -> 3.32 us  [across_columns(): return lax.ppermute(block, 'blk', route)]
    unnamed x26 -> x18, local copies, waits for them, and re-layouts: 3.19 us -> 0.71 us
    another operation x6 -> x0, other arithmetic: 1.41 us -> none
    pallas_call x3 -> x4, Pallas kernels: 5.88 us -> 7.12 us  [the longest x1 2.77 us: per_device(): pl.pallas_call(functools.partial(first_kernel, plan, len(slabs)), out_sha...]
    ppermute x1, starting transfers between devices: 1.77 us -> 0.65 us  [across_columns(): return lax.ppermute(block, 'blk', route)]
  transfers between devices with their start and end apart: 19 -> 20, of which waited for: 11 -> 11; matrix products, arithmetic and copies ran while one was open for 3% -> 4% of each run, Pallas kernels for 6% -> 5%
where the time goes in v4:
time: 58.3 us; the launch traced here: 58.1 us
  waiting for transfers between devices  27.6 us (47%)
  starting transfers between devices  18.5 us (32%)
  Pallas kernels  7.12 us (12%)
  local copies, waits for them, and re-layouts  1.49 us (3%)
  matrix products  1.16 us (2%)
  other arithmetic  1.13 us (2%)
  between operations  1.13 us (2%)
    ppermute x7, waiting for transfers between devices, along_ring(): return lax.ppermute(block, 'blk', route)  15.1 us
    ppermute x7, starting transfers between devices, along_ring(): return lax.ppermute(block, 'blk', route)  8.41 us
    ppermute x2, waiting for transfers between devices, across_rows(): return lax.ppermute(block, 'blk', route)  4.56 us
    ppermute x2, starting transfers between devices, across_rows(): return lax.ppermute(block, 'blk', route)  4.3 us
    ppermute x3, starting transfers between devices, along_rep(): lax.ppermute(block, 'rep', [(i, (i + distance) % size) for i in range(siz...  3.74 us
    ppermute x3, waiting for transfers between devices, along_rep(): lax.ppermute(block, 'rep', [(i, (i + distance) % size) for i in range(siz...  3.57 us
    ppermute x1, waiting for transfers between devices, across_columns(): return lax.ppermute(block, 'blk', route)  3.32 us
    pallas_call x1, Pallas kernels, per_device(): pl.pallas_call(functools.partial(first_kernel, plan, len(slabs)), out_sha...  2.77 us
  transfers between devices with their start and end apart: 20, of which 11 were waited for; matrix products, arithmetic and copies ran while one was open for 4% of the time, Pallas kernels for 5%

profile of v4, /device:TPU:0, one launch (start us, length us, event | category | flops | bytes accessed | tf_op | source)
XLA Modules:
  0.0 58.1 jit_solution(1950632050651220065)
XLA Ops:
  0.6 0.0 copy-start
  0.6 0.0 copy-start.2
  0.7 0.0 copy-start.4
  0.7 0.0 copy-start.3
  0.7 2.2 %scale.1.refs_4_ = bf16[1024,128]{1,0:T(8,128)(2,1)} custom-call(s32[8,128]{1,0:T(8,128)} %bitcast.61, bf16[1024,256]{1,0:T(8,128)(2,1)} %gradient_hbm.1), custom_call_target="tpu_custom_call" | custom-call | tf_op jit(solution)/shard_map/scale/pallas_call | solution.py:215
  2.8 0.0 copy-start.5
  2.8 3.1 %collective-permute-start.6 = (bf16[1024,128]{1,0:T(8,128)(2,1)}, bf16[1024,128]{1,0:T(8,128)(2,1)S(1)}, u32[]{:S(2)}, u32[]{:S(2)}) collective-permute-start(bf16[1024,128]{1,0:T(8,128)(2,1)} %scale.1.refs_4_), channel_id=1, source_target_pairs={{0,8},{2,10},{8,16},{10,18},{16,24},{18,26},{24,28},{26,30},{28,20... | collective-permute-start | bytes 786440 | tf_op jit(solution)/shard_map/ppermute | solution.py:35
  5.9 0.0 collective-permute-start.10
  5.9 0.0 copy-start.6
  5.9 0.6 %copy-done.6 = s32[1,8]{1,0:T(1,128)S(1)} copy-done((s32[1,8]{1,0:T(1,128)S(1)}, s32[1,8]{1,0:T(1,128)}, u32[]{:S(2)}) %copy-start.6) | copy-done | bytes 56
  6.6 0.1 copy.9
  6.7 0.1 reshape_squeeze.6
  6.8 0.1 pad_add_fusion
  6.8 0.1 dynamic_slice.15
  6.9 0.2 payload.1
  7.1 2.0 %collective-permute-start.1 = (bf16[1152,128]{1,0:T(8,128)(2,1)S(1)}, bf16[1152,128]{1,0:T(8,128)(2,1)S(1)}, u32[]{:S(2)}, u32[]{:S(2)}) collective-permute-start(bf16[1152,128]{1,0:T(8,128)(2,1)S(1)} %get-tuple-element.14.refs_0_), channel_id=1, source_target_pairs={{0,1},{1,0},{2,3},{3,2},{4,5},{5,4},{6,7},{7,6},{8,9},{9,8},{10,11... | collective-permute-start | bytes 884744 | tf_op jit(solution)/shard_map/ppermute | solution.py:67
  9.1 0.1 collective-permute-start
  9.2 0.1 collective-permute-start.3
  9.4 3.0 %collective-permute-done.6.refs_5_ = bf16[1024,128]{1,0:T(8,128)(2,1)S(1)} collective-permute-done((bf16[1024,128]{1,0:T(8,128)(2,1)}, bf16[1024,128]{1,0:T(8,128)(2,1)S(1)}, u32[]{:S(2)}, u32[]{:S(2)}) %collective-permute-start.6) | collective-permute-done | bytes 262176 | tf_op jit(solution)/shard_map/ppermute | solution.py:35
  12.4 1.8 %collective-permute-start.7 = (bf16[1024,128]{1,0:T(8,128)(2,1)S(1)}, bf16[1024,128]{1,0:T(8,128)(2,1)S(1)}, u32[]{:S(2)}, u32[]{:S(2)}) collective-permute-start(bf16[1024,128]{1,0:T(8,128)(2,1)S(1)} %collective-permute-done.6.refs_5_), channel_id=1, source_target_pairs={{0,8},{2,10},{8,16},{10,18},{16,24},{18,26},{24,28},{26,30},{28,20... | collective-permute-start | bytes 786440 | tf_op jit(solution)/shard_map/ppermute | solution.py:35
  14.2 0.1 reshape.58
  14.5 0.0 collective-permute-done.refs_2_
  14.5 0.1 collective-permute-start.4
  14.6 0.0 collective-permute-done.10.refs_6_
  14.6 0.3 collective-permute-start.11
  14.8 5.0 %collective-permute-done.7.refs_7_ = bf16[1024,128]{1,0:T(8,128)(2,1)S(1)} collective-permute-done((bf16[1024,128]{1,0:T(8,128)(2,1)S(1)}, bf16[1024,128]{1,0:T(8,128)(2,1)S(1)}, u32[]{:S(2)}, u32[]{:S(2)}) %collective-permute-start.7) | collective-permute-done | bytes 262176 | tf_op jit(solution)/shard_map/ppermute | solution.py:35
  19.8 1.5 %collective-permute-start.8 = (bf16[1024,128]{1,0:T(8,128)(2,1)S(1)}, bf16[1024,128]{1,0:T(8,128)(2,1)S(1)}, u32[]{:S(2)}, u32[]{:S(2)}) collective-permute-start(bf16[1024,128]{1,0:T(8,128)(2,1)S(1)} %collective-permute-done.7.refs_7_), channel_id=1, source_target_pairs={{0,8},{2,10},{8,16},{10,18},{16,24},{18,26},{24,28},{26,30},{28,20... | collective-permute-start | bytes 786440 | tf_op jit(solution)/shard_map/ppermute | solution.py:35
  21.4 0.1 reshape.60
  21.4 0.0 collective-permute-done.3.refs_5_
  21.5 0.0 collective-permute-start.5
  21.5 0.0 collective-permute-done.1.refs_1_
  21.5 0.5 collective-permute-start.2
  22.1 1.2 %collective-permute-done.11.refs_8_ = bf16[1024,128]{1,0:T(8,128)(2,1)S(1)} collective-permute-done((bf16[1024,128]{1,0:T(8,128)(2,1)S(1)}, bf16[1024,128]{1,0:T(8,128)(2,1)S(1)}, u32[]{:S(2)}, u32[]{:S(2)}) %collective-permute-start.11) | collective-permute-done | bytes 262176 | tf_op jit(solution)/shard_map/ppermute | solution.py:35
  23.3 0.3 collective-permute-start.12
  23.6 2.8 %collective-permute-done.8.refs_9_ = bf16[1024,128]{1,0:T(8,128)(2,1)S(1)} collective-permute-done((bf16[1024,128]{1,0:T(8,128)(2,1)S(1)}, bf16[1024,128]{1,0:T(8,128)(2,1)S(1)}, u32[]{:S(2)}, u32[]{:S(2)}) %collective-permute-start.8) | collective-permute-done | bytes 262176 | tf_op jit(solution)/shard_map/ppermute | solution.py:35
  26.4 1.5 %collective-permute-start.9 = (bf16[1024,128]{1,0:T(8,128)(2,1)S(1)}, bf16[1024,128]{1,0:T(8,128)(2,1)}, u32[]{:S(2)}, u32[]{:S(2)}) collective-permute-start(bf16[1024,128]{1,0:T(8,128)(2,1)S(1)} %collective-permute-done.8.refs_9_), channel_id=1, source_target_pairs={{0,8},{2,10},{8,16},{10,18},{16,24},{18,26},{24,28},{26,30},{28,20... | collective-permute-start | bytes 786440 | tf_op jit(solution)/shard_map/ppermute | solution.py:35
  27.9 0.1 reshape.62
  28.0 0.0 collective-permute-done.2.refs_3_
  28.0 0.1 reshape.64
  28.1 0.1 concatenate.13.table_ref
  28.2 3.0 %collective-permute-done.12.refs_10_ = bf16[1024,128]{1,0:T(8,128)(2,1)S(1)} collective-permute-done((bf16[1024,128]{1,0:T(8,128)(2,1)S(1)}, bf16[1024,128]{1,0:T(8,128)(2,1)S(1)}, u32[]{:S(2)}, u32[]{:S(2)}) %collective-permute-start.12) | collective-permute-done | bytes 262176 | tf_op jit(solution)/shard_map/ppermute | solution.py:35
  31.2 2.8 %first_slabs.1.refs_9_ = f32[2,1024,128]{2,1,0:T(8,128)S(1)} custom-call(s32[307]{0:T(512)S(1)} %concatenate.13.table_ref, bf16[1152,128]{1,0:T(8,128)(2,1)S(1)} %get-tuple-element.14.refs_0_, bf16[1152,128]{1,0:T(8,128)(2,1)S(1)} %collective-permute-done.1.refs_1_, bf16[576,128]{1,0:T(8,128)(2,1)S(1)} %collective-permute-done.refs_2_, ...), custom_call_target="tpu_custom_call" | custom-call | flops 1 | bytes 1 | tf_op jit(solution)/shard_map/first_slabs/pallas_call | solution.py:289
  34.0 0.0 collective-permute-done.4.refs_6_
  34.0 0.0 collective-permute-done.5.refs_7_
  34.0 0.0 collective-permute-done.9.refs_8_
  34.0 2.0 %last_slab.1 = (f32[1024,128]{1,0:T(8,128)S(1)}, f32[1024,128]{1,0:T(8,128)S(1)}, f32[128,128]{1,0:T(8,128)S(1)}, f32[128,128]{1,0:T(8,128)S(1)}) custom-call(s32[307]{0:T(512)S(1)} %concatenate.13.table_ref, bf16[1152,128]{1,0:T(8,128)(2,1)S(1)} %get-tuple-element.14.refs_0_, bf16[1152,128]{1,0:T(8,128)(2,1)S(1)} %collective-permute-done.1.refs_1_, ...), custom_call_target="tpu_custom_call" | custom-call | tf_op jit(solution)/shard_map/last_slab/pallas_call | solution.py:298
  36.1 0.1 collective-permute-start.13
  36.2 0.5 collective-permute-start.16
  36.7 0.7 %collective-permute-done.13 = f32[128,128]{1,0:T(8,128)S(1)} collective-permute-done((f32[128,128]{1,0:T(8,128)S(1)}, f32[128,128]{1,0:T(8,128)S(1)}, u32[]{:S(2)}, u32[]{:S(2)}) %collective-permute-start.13) | collective-permute-done | bytes 65568 | tf_op jit(solution)/shard_map/ppermute | solution.py:57
  37.4 1.6 %collective-permute-start.14 = (bf16[128,128]{1,0:T(8,128)(2,1)S(1)}, bf16[128,128]{1,0:T(8,128)(2,1)S(1)}, u32[]{:S(2)}, u32[]{:S(2)}) collective-permute-start(bf16[128,128]{1,0:T(8,128)(2,1)S(1)} %add_convert_fusion.2), channel_id=1, source_target_pairs={{0,8},{2,10},{4,12},{6,14},{8,0},{10,2},{12,4},{14,6},{16,24},{18,... | collective-permute-start | bytes 98312 | tf_op jit(solution)/shard_map/ppermute | solution.py:43
  39.1 2.3 %collective-permute-done.14 = bf16[128,128]{1,0:T(8,128)(2,1)S(1)} collective-permute-done((bf16[128,128]{1,0:T(8,128)(2,1)S(1)}, bf16[128,128]{1,0:T(8,128)(2,1)S(1)}, u32[]{:S(2)}, u32[]{:S(2)}) %collective-permute-start.14) | collective-permute-done | bytes 32800 | tf_op jit(solution)/shard_map/ppermute | solution.py:43
  41.4 2.7 %collective-permute-start.15 = (bf16[128,128]{1,0:T(8,128)(2,1)S(1)}, bf16[128,128]{1,0:T(8,128)(2,1)S(1)}, u32[]{:S(2)}, u32[]{:S(2)}) collective-permute-start(bf16[128,128]{1,0:T(8,128)(2,1)S(1)} %add_convert_fusion.1), channel_id=1, source_target_pairs={{0,16},{2,18},{4,20},{6,22},{8,24},{10,26},{12,28},{14,30},{16,0},... | collective-permute-start | bytes 98312 | tf_op jit(solution)/shard_map/ppermute | solution.py:43
  44.1 2.2 %collective-permute-done.15 = bf16[128,128]{1,0:T(8,128)(2,1)S(1)} collective-permute-done((bf16[128,128]{1,0:T(8,128)(2,1)S(1)}, bf16[128,128]{1,0:T(8,128)(2,1)S(1)}, u32[]{:S(2)}, u32[]{:S(2)}) %collective-permute-start.15) | collective-permute-done | bytes 32800 | tf_op jit(solution)/shard_map/ppermute | solution.py:43
  46.3 0.0 collective-permute-done.16
  46.3 0.2 multiply_convert_fusion
  46.5 0.6 %collective-permute-start.17 = (bf16[128,128]{1,0:T(8,128)(2,1)S(1)}, bf16[128,128]{1,0:T(8,128)(2,1)S(1)}, u32[]{:S(2)}, u32[]{:S(2)}) collective-permute-start(bf16[128,128]{1,0:T(8,128)(2,1)S(1)} %convert_add_fusion), channel_id=1, source_target_pairs={{0,4},{2,6},{4,0},{6,2},{8,12},{10,14},{12,8},{14,10},{16,20},{18,... | collective-permute-start | bytes 98312 | tf_op jit(solution)/shard_map/ppermute | solution.py:50
  47.2 3.3 %collective-permute-done.17 = bf16[128,128]{1,0:T(8,128)(2,1)S(1)} collective-permute-done((bf16[128,128]{1,0:T(8,128)(2,1)S(1)}, bf16[128,128]{1,0:T(8,128)(2,1)S(1)}, u32[]{:S(2)}, u32[]{:S(2)}) %collective-permute-start.17) | collective-permute-done | bytes 32800 | tf_op jit(solution)/shard_map/ppermute | solution.py:50
  50.6 1.6 %collective-permute-start.18 = (bf16[640,128]{1,0:T(8,128)(2,1)S(1)}, bf16[640,128]{1,0:T(8,128)(2,1)S(1)}, u32[]{:S(2)}, u32[]{:S(2)}) collective-permute-start(bf16[640,128]{1,0:T(8,128)(2,1)S(1)} %pad_maximum_fusion.1), channel_id=1, source_target_pairs={{0,1},{1,0},{2,3},{3,2},{4,5},{5,4},{6,7},{7,6},{8,9},{9,8},{10,11... | collective-permute-start | bytes 491528 | tf_op jit(solution)/shard_map/ppermute | solution.py:67
  52.2 0.2 fusion.2
  52.4 3.6 %collective-permute-done.18 = bf16[640,128]{1,0:T(8,128)(2,1)S(1)} collective-permute-done((bf16[640,128]{1,0:T(8,128)(2,1)S(1)}, bf16[640,128]{1,0:T(8,128)(2,1)S(1)}, u32[]{:S(2)}, u32[]{:S(2)}) %collective-permute-start.18) | collective-permute-done | bytes 163872 | tf_op jit(solution)/shard_map/ppermute | solution.py:67
  56.0 0.1 collective-permute-start.19
  56.1 0.9 %fusion = bf16[512,256]{1,0:T(8,128)(2,1)} fusion(f32[512,256]{1,0:T(8,128)S(1)} %fusion.2, bf16[640,128]{1,0:T(8,128)(2,1)S(1)} %collective-permute-done.18, bf16[256,256]{1,0:T(8,128)(2,1)S(1)} %copy-done, s32[]{:T(128)S(6)} %select_n.476), kind=kOutput, calls=%fused_computation.1 | convolution fusion | flops 33816576 | bytes 983044 | tf_op jit(solution)/shard_map/dot_general | solution.py:338
  57.0 0.4 collective-permute-done.19
  57.4 0.7 %pad_maximum_fusion = f32[256,256]{1,0:T(8,128)} fusion(f32[128,256]{1,0:T(8,128)S(1)} %get-tuple-element.29, f32[128,256]{1,0:T(8,128)S(1)} %get-tuple-element.28), kind=kLoop, calls=%fused_computation.3 | loop fusion | flops 65536 | bytes 524288 | tf_op jit(solution)/shard_map/concatenate | solution.py:347
  (33 shorter events, 0.3 us)
Async XLA Ops:
  0.6 51.5 %copy-start = (bf16[256,256]{1,0:T(8,128)(2,1)S(1)}, bf16[256,256]{1,0:T(8,128)(2,1)}, u32[]{:S(2)}) copy-start(bf16[256,256]{1,0:T(8,128)(2,1)} %param.9) | copy-start | bytes 393220
  0.6 6.3 %copy-start.2 = (s32[1,8,8,16,128]{4,3,2,1,0:T(8,128)S(1)}, s32[1,8,8,16,128]{4,3,2,1,0:T(8,128)}, u32[]{:S(2)}) copy-start(s32[1,8,8,16,128]{4,3,2,1,0:T(8,128)} %param.10) | copy-start | bytes 1572868
  0.7 5.3 %copy-start.4 = (s32[1024]{0:T(1024)S(1)}, s32[1024]{0:T(1024)}, u32[]{:S(2)}) copy-start(s32[1024]{0:T(1024)} %param.13) | copy-start | bytes 12292
  0.7 6.3 %copy-start.3 = (bf16[512,256]{1,0:T(8,128)(2,1)S(1)}, bf16[512,256]{1,0:T(8,128)(2,1)}, u32[]{:S(2)}) copy-start(bf16[512,256]{1,0:T(8,128)(2,1)} %features_ref) | copy-start | bytes 786436
  2.8 3.8 %copy-start.5 = (s32[1,8,2,8]{3,2,1,0:T(2,128)S(1)}, s32[1,8,2,8]{3,2,1,0:T(2,128)}, u32[]{:S(2)}) copy-start(s32[1,8,2,8]{3,2,1,0:T(2,128)} %param.11) | copy-start | bytes 1540
  2.8 9.5 %collective-permute-start.6 = (bf16[1024,128]{1,0:T(8,128)(2,1)}, bf16[1024,128]{1,0:T(8,128)(2,1)S(1)}, u32[]{:S(2)}, u32[]{:S(2)}) collective-permute-start(bf16[1024,128]{1,0:T(8,128)(2,1)} %scale.1.refs_4_), channel_id=1, source_target_pairs={{0,8},{2,10},{8,16},{10,18},{16,24},{18,26},{24,28},{26,30},{28,20... | collective-permute-start | bytes 786440 | tf_op jit(solution)/shard_map/ppermute | solution.py:35
  5.9 8.7 %collective-permute-start.10 = (bf16[1024,128]{1,0:T(8,128)(2,1)}, bf16[1024,128]{1,0:T(8,128)(2,1)S(1)}, u32[]{:S(2)}, u32[]{:S(2)}) collective-permute-start(bf16[1024,128]{1,0:T(8,128)(2,1)} %scale.1.refs_4_), channel_id=1, source_target_pairs={{0,4},{2,6},{8,0},{10,2},{16,8},{18,10},{24,16},{26,18},{28,24},{3... | collective-permute-start | bytes 786440 | tf_op jit(solution)/shard_map/ppermute | solution.py:35
  5.9 0.7 %copy-start.6 = (s32[1,8]{1,0:T(1,128)S(1)}, s32[1,8]{1,0:T(1,128)}, u32[]{:S(2)}) copy-start(s32[1,8]{1,0:T(1,128)} %param.12) | copy-start | bytes 100
  7.1 14.4 %collective-permute-start.1 = (bf16[1152,128]{1,0:T(8,128)(2,1)S(1)}, bf16[1152,128]{1,0:T(8,128)(2,1)S(1)}, u32[]{:S(2)}, u32[]{:S(2)}) collective-permute-start(bf16[1152,128]{1,0:T(8,128)(2,1)S(1)} %get-tuple-element.14.refs_0_), channel_id=1, source_target_pairs={{0,1},{1,0},{2,3},{3,2},{4,5},{5,4},{6,7},{7,6},{8,9},{9,8},{10,11... | collective-permute-start | bytes 884744 | tf_op jit(solution)/shard_map/ppermute | solution.py:67
  9.1 5.3 %collective-permute-start = (bf16[576,128]{1,0:T(8,128)(2,1)S(1)}, bf16[576,128]{1,0:T(8,128)(2,1)S(1)}, u32[]{:S(2)}, u32[]{:S(2)}) collective-permute-start(bf16[576,128]{1,0:T(8,128)(2,1)S(1)} %get-tuple-element.26), channel_id=1, source_target_pairs={{0,2},{2,0},{4,6},{6,4},{8,10},{10,8},{12,14},{14,12},{16,18},{18,... | collective-permute-start | bytes 442376 | tf_op jit(solution)/shard_map/ppermute | solution.py:57
  9.2 12.2 %collective-permute-start.3 = (bf16[1024,128]{1,0:T(8,128)(2,1)S(1)}, bf16[1024,128]{1,0:T(8,128)(2,1)S(1)}, u32[]{:S(2)}, u32[]{:S(2)}) collective-permute-start(bf16[1024,128]{1,0:T(8,128)(2,1)S(1)} %get-tuple-element.15.refs_4_), channel_id=1, source_target_pairs={{0,1},{1,0},{2,3},{3,2},{4,5},{5,4},{6,7},{7,6},{8,9},{9,8},{10,11... | collective-permute-start | bytes 786440 | tf_op jit(solution)/shard_map/ppermute | solution.py:67
  12.4 7.5 %collective-permute-start.7 = (bf16[1024,128]{1,0:T(8,128)(2,1)S(1)}, bf16[1024,128]{1,0:T(8,128)(2,1)S(1)}, u32[]{:S(2)}, u32[]{:S(2)}) collective-permute-start(bf16[1024,128]{1,0:T(8,128)(2,1)S(1)} %collective-permute-done.6.refs_5_), channel_id=1, source_target_pairs={{0,8},{2,10},{8,16},{10,18},{16,24},{18,26},{24,28},{26,30},{28,20... | collective-permute-start | bytes 786440 | tf_op jit(solution)/shard_map/ppermute | solution.py:35
  14.5 19.5 %collective-permute-start.4 = (bf16[1024,128]{1,0:T(8,128)(2,1)S(1)}, bf16[1024,128]{1,0:T(8,128)(2,1)}, u32[]{:S(2)}, u32[]{:S(2)}) collective-permute-start(bf16[1024,128]{1,0:T(8,128)(2,1)S(1)} %get-tuple-element.15.refs_4_), channel_id=1, source_target_pairs={{0,2},{2,0},{4,6},{6,4},{8,10},{10,8},{12,14},{14,12},{16,18},{18,... | collective-permute-start | bytes 786440 | tf_op jit(solution)/shard_map/ppermute | solution.py:57
  14.6 8.7 %collective-permute-start.11 = (bf16[1024,128]{1,0:T(8,128)(2,1)S(1)}, bf16[1024,128]{1,0:T(8,128)(2,1)S(1)}, u32[]{:S(2)}, u32[]{:S(2)}) collective-permute-start(bf16[1024,128]{1,0:T(8,128)(2,1)S(1)} %collective-permute-done.10.refs_6_), channel_id=1, source_target_pairs={{0,4},{2,6},{8,0},{10,2},{16,8},{18,10},{24,16},{26,18},{28,24},{3... | collective-permute-start | bytes 786440 | tf_op jit(solution)/shard_map/ppermute | solution.py:35
  19.8 6.6 %collective-permute-start.8 = (bf16[1024,128]{1,0:T(8,128)(2,1)S(1)}, bf16[1024,128]{1,0:T(8,128)(2,1)S(1)}, u32[]{:S(2)}, u32[]{:S(2)}) collective-permute-start(bf16[1024,128]{1,0:T(8,128)(2,1)S(1)} %collective-permute-done.7.refs_7_), channel_id=1, source_target_pairs={{0,8},{2,10},{8,16},{10,18},{16,24},{18,26},{24,28},{26,30},{28,20... | collective-permute-start | bytes 786440 | tf_op jit(solution)/shard_map/ppermute | solution.py:35
  21.4 9.8 %copy-start.1 = (bf16[1024,128]{1,0:T(8,128)(2,1)S(1)}, bf16[1024,128]{1,0:T(8,128)(2,1)}, u32[]{:S(2)}) copy-start(bf16[1024,128]{1,0:T(8,128)(2,1)} %scale.1.refs_4_) | copy-start | bytes 786436
  21.5 12.6 %collective-permute-start.5 = (bf16[1024,128]{1,0:T(8,128)(2,1)S(1)}, bf16[1024,128]{1,0:T(8,128)(2,1)}, u32[]{:S(2)}, u32[]{:S(2)}) collective-permute-start(bf16[1024,128]{1,0:T(8,128)(2,1)S(1)} %collective-permute-done.3.refs_5_), channel_id=1, source_target_pairs={{0,2},{2,0},{4,6},{6,4},{8,10},{10,8},{12,14},{14,12},{16,18},{18,... | collective-permute-start | bytes 786440 | tf_op jit(solution)/shard_map/ppermute | solution.py:57
  21.5 6.4 %collective-permute-start.2 = (bf16[576,128]{1,0:T(8,128)(2,1)S(1)}, bf16[576,128]{1,0:T(8,128)(2,1)S(1)}, u32[]{:S(2)}, u32[]{:S(2)}) collective-permute-start(bf16[576,128]{1,0:T(8,128)(2,1)S(1)} %get-tuple-element.24), channel_id=1, source_target_pairs={{0,2},{2,0},{4,6},{6,4},{8,10},{10,8},{12,14},{14,12},{16,18},{18,... | collective-permute-start | bytes 442376 | tf_op jit(solution)/shard_map/ppermute | solution.py:57
  23.3 7.9 %collective-permute-start.12 = (bf16[1024,128]{1,0:T(8,128)(2,1)S(1)}, bf16[1024,128]{1,0:T(8,128)(2,1)S(1)}, u32[]{:S(2)}, u32[]{:S(2)}) collective-permute-start(bf16[1024,128]{1,0:T(8,128)(2,1)S(1)} %collective-permute-done.11.refs_8_), channel_id=1, source_target_pairs={{0,4},{2,6},{8,0},{10,2},{16,8},{18,10},{24,16},{26,18},{28,24},{3... | collective-permute-start | bytes 786440 | tf_op jit(solution)/shard_map/ppermute | solution.py:35
  26.4 7.6 %collective-permute-start.9 = (bf16[1024,128]{1,0:T(8,128)(2,1)S(1)}, bf16[1024,128]{1,0:T(8,128)(2,1)}, u32[]{:S(2)}, u32[]{:S(2)}) collective-permute-start(bf16[1024,128]{1,0:T(8,128)(2,1)S(1)} %collective-permute-done.8.refs_9_), channel_id=1, source_target_pairs={{0,8},{2,10},{8,16},{10,18},{16,24},{18,26},{24,28},{26,30},{28,20... | collective-permute-start | bytes 786440 | tf_op jit(solution)/shard_map/ppermute | solution.py:35
  36.1 1.3 %collective-permute-start.13 = (f32[128,128]{1,0:T(8,128)S(1)}, f32[128,128]{1,0:T(8,128)S(1)}, u32[]{:S(2)}, u32[]{:S(2)}) collective-permute-start(f32[128,128]{1,0:T(8,128)S(1)} %get-tuple-element.17), channel_id=1, source_target_pairs={{0,2},{2,0},{4,6},{6,4},{8,10},{10,8},{12,14},{14,12},{16,18},{18,... | collective-permute-start | bytes 196616 | tf_op jit(solution)/shard_map/ppermute | solution.py:57
  36.2 10.2 %collective-permute-start.16 = (f32[1024,128]{1,0:T(8,128)S(1)}, f32[1024,128]{1,0:T(8,128)S(1)}, u32[]{:S(2)}, u32[]{:S(2)}) collective-permute-start(f32[1024,128]{1,0:T(8,128)S(1)} %get-tuple-element.19), channel_id=1, source_target_pairs={{0,2},{2,0},{4,6},{6,4},{8,10},{10,8},{12,14},{14,12},{16,18},{18,... | collective-permute-start | bytes 1572872 | tf_op jit(solution)/shard_map/ppermute | solution.py:57
  37.4 4.0 %collective-permute-start.14 = (bf16[128,128]{1,0:T(8,128)(2,1)S(1)}, bf16[128,128]{1,0:T(8,128)(2,1)S(1)}, u32[]{:S(2)}, u32[]{:S(2)}) collective-permute-start(bf16[128,128]{1,0:T(8,128)(2,1)S(1)} %add_convert_fusion.2), channel_id=1, source_target_pairs={{0,8},{2,10},{4,12},{6,14},{8,0},{10,2},{12,4},{14,6},{16,24},{18,... | collective-permute-start | bytes 98312 | tf_op jit(solution)/shard_map/ppermute | solution.py:43
  41.4 4.9 %collective-permute-start.15 = (bf16[128,128]{1,0:T(8,128)(2,1)S(1)}, bf16[128,128]{1,0:T(8,128)(2,1)S(1)}, u32[]{:S(2)}, u32[]{:S(2)}) collective-permute-start(bf16[128,128]{1,0:T(8,128)(2,1)S(1)} %add_convert_fusion.1), channel_id=1, source_target_pairs={{0,16},{2,18},{4,20},{6,22},{8,24},{10,26},{12,28},{14,30},{16,0},... | collective-permute-start | bytes 98312 | tf_op jit(solution)/shard_map/ppermute | solution.py:43
  46.5 4.0 %collective-permute-start.17 = (bf16[128,128]{1,0:T(8,128)(2,1)S(1)}, bf16[128,128]{1,0:T(8,128)(2,1)S(1)}, u32[]{:S(2)}, u32[]{:S(2)}) collective-permute-start(bf16[128,128]{1,0:T(8,128)(2,1)S(1)} %convert_add_fusion), channel_id=1, source_target_pairs={{0,4},{2,6},{4,0},{6,2},{8,12},{10,14},{12,8},{14,10},{16,20},{18,... | collective-permute-start | bytes 98312 | tf_op jit(solution)/shard_map/ppermute | solution.py:50
  50.6 5.4 %collective-permute-start.18 = (bf16[640,128]{1,0:T(8,128)(2,1)S(1)}, bf16[640,128]{1,0:T(8,128)(2,1)S(1)}, u32[]{:S(2)}, u32[]{:S(2)}) collective-permute-start(bf16[640,128]{1,0:T(8,128)(2,1)S(1)} %pad_maximum_fusion.1), channel_id=1, source_target_pairs={{0,1},{1,0},{2,3},{3,2},{4,5},{5,4},{6,7},{7,6},{8,9},{9,8},{10,11... | collective-permute-start | bytes 491528 | tf_op jit(solution)/shard_map/ppermute | solution.py:67
  56.0 1.4 %collective-permute-start.19 = (f32[128,256]{1,0:T(8,128)S(1)}, f32[128,256]{1,0:T(8,128)S(1)}, u32[]{:S(2)}, u32[]{:S(2)}) collective-permute-start(f32[128,256]{1,0:T(8,128)S(1)} %broadcast_multiply_fusion), channel_id=1, source_target_pairs={{0,2},{2,0},{4,6},{6,4},{8,10},{10,8},{12,14},{14,12},{16,18},{18,... | collective-permute-start | bytes 393224 | tf_op jit(solution)/shard_map/ppermute | solution.py:57

commit v5 on v4

--- a/solution.py
+++ b/solution.py
@@ -35,19 +35,16 @@
     return lax.ppermute(block, "blk", route)
 
 
-def across_rows(block, distance):
+def across(block, rows=0, columns=0, reps=0):
+    size = lax.axis_size("rep")
     route = [
-        (device_of(z, x, c), device_of(z ^ distance, x, c))
+        (device_of(z, x, c), device_of(z ^ rows, x ^ columns, c))
         for z, x, c in places(lax.axis_size("blk"))
     ]
-    return lax.ppermute(block, "blk", route)
-
-
-def across_columns(block):
-    route = [
-        (device_of(z, x, c), device_of(z, 1 - x, c)) for z, x, c in places(lax.axis_size("blk"))
-    ]
-    return lax.ppermute(block, "blk", route)
+    if not reps:
+        return lax.ppermute(block, "blk", route)
+    route = [(a * size + r, b * size + (r + reps) % size) for a, b in route for r in range(size)]
+    return lax.ppermute(block, ("blk", "rep"), route)
 
 
 def across_cores(block):
@@ -308,28 +305,27 @@
         name="last_slab",
     )(table, *own_pieces, *other_pieces, *own_features, *other_features, forward, sums)
 
-    def add_across_rows(total, distance):
-        total = total.astype(jnp.bfloat16)
-        return total.astype(jnp.float32) + across_rows(total, distance).astype(jnp.float32)
-
-    total = keep + across_cores(send)
+    def wide(values):
+        return values.astype(jnp.float32)
+
+    total = (keep + across_cores(send)).astype(jnp.bfloat16)
     own_sums = own_sums + across_cores(other_sums)
     aggregated = (own_sums * inverse_root[:, None]).astype(jnp.bfloat16)
-    distance = 1
-    while distance < rows_of_chips:
-        total = add_across_rows(total, distance)
-        distance *= 2
+    row_bits = [1 << bit for bit in range(rows_of_chips.bit_length() - 1)]
+    total = (wide(total) + wide(across(total, rows=row_bits[0]))) + (
+        wide(across(total, columns=1)) + wide(across(total, rows=row_bits[0], columns=1))
+    )
+    total = total.astype(jnp.bfloat16)
+    for bit in row_bits[1:-1]:
+        total = (wide(total) + wide(across(total, rows=bit))).astype(jnp.bfloat16)
     total, aggregated = lax.optimization_barrier((total, aggregated))
-    total = total.astype(jnp.bfloat16)
-    total = total.astype(jnp.float32) + across_columns(total).astype(jnp.float32)
-
-    total = total.astype(jnp.bfloat16)
     result = jnp.zeros((share_rows, width), jnp.float32)
     weight_half = jnp.zeros((width // 2, width), jnp.float32)
     for d in range(rep_size):
         rows_to = ((rep_index + d) % rep_size) * share_rows
         part = lax.dynamic_slice_in_dim(aggregated, rows_to, share_rows, 0)
         columns = total
+        far = across(total, rows=row_bits[-1], reps=d)
         if d:
             both = along_rep(jnp.concatenate([part, total]), d)
             part, columns = both[:share_rows], both[share_rows:]
@@ -339,7 +335,7 @@
             part, side, (((1,), (1,)), ((), ())), preferred_element_type=jnp.float32
         )
         weight_half = lax.dynamic_update_slice_in_dim(
-            weight_half, columns.astype(jnp.float32), columns_at, 1
+            weight_half, wide(columns) + wide(far), columns_at, 1
         )
     input_grad = result.astype(jnp.bfloat16)
     weight_half = weight_half * (1.0 / math.sqrt(slab_rows * blk_size))

time: 58.3 us -> 56.8 us (0.974)
  waiting for transfers between devices: 27.6 us -> 24.6 us
  starting transfers between devices: 18.5 us -> 20 us
    ppermute x3, waiting for transfers between devices: 3.57 us -> 1.01 us  [along_rep(): lax.ppermute(block, 'rep', [(i, (i + distance) % size) for i in range(siz...]
    ppermute x3 -> x5, starting transfers between devices: 4.95 us -> 7.5 us  [the longest x4 6.21 us: across(): return lax.ppermute(block, 'blk', route)]
    ppermute x3, starting transfers between devices: 3.74 us -> 2.73 us  [along_rep(): lax.ppermute(block, 'rep', [(i, (i + distance) % size) for i in range(siz...]
    ppermute x3 -> x5, waiting for transfers between devices: 7.87 us -> 7.38 us  [the longest x4 3.82 us: across(): return lax.ppermute(block, 'blk', route)]
  transfers between devices with their start and end apart: 20 -> 22, of which waited for: 11 -> 13; matrix products, arithmetic and copies ran while one was open for 4% -> 4% of each run, Pallas kernels for 5% -> 5%
where the time goes in v5:
time: 56.8 us; the launch traced here: 56.6 us
  waiting for transfers between devices  24.6 us (43%)
  starting transfers between devices  20 us (35%)
  Pallas kernels  7.12 us (13%)
  local copies, waits for them, and re-layouts  1.49 us (3%)
  matrix products  1.16 us (2%)
  between operations  1.13 us (2%)
  other arithmetic  1.12 us (2%)
    ppermute x7, waiting for transfers between devices, along_ring(): return lax.ppermute(block, 'blk', route)  15.1 us
    ppermute x7, starting transfers between devices, along_ring(): return lax.ppermute(block, 'blk', route)  8.41 us
    ppermute x4, starting transfers between devices, across(): return lax.ppermute(block, 'blk', route)  6.21 us
    ppermute x4, waiting for transfers between devices, across(): return lax.ppermute(block, 'blk', route)  3.82 us
    ppermute x1, waiting for transfers between devices, across(): return lax.ppermute(block, ('blk', 'rep'), route)  3.56 us
    pallas_call x1, Pallas kernels, per_device(): pl.pallas_call(functools.partial(first_kernel, plan, len(slabs)), out_sha...  2.77 us
    ppermute x3, starting transfers between devices, along_rep(): lax.ppermute(block, 'rep', [(i, (i + distance) % size) for i in range(siz...  2.73 us
    pallas_call x1, Pallas kernels, per_device(): pl.pallas_call(functools.partial(scale_kernel, share_width), out_shape=ja...  2.15 us
  transfers between devices with their start and end apart: 22, of which 13 were waited for; matrix products, arithmetic and copies ran while one was open for 4% of the time, Pallas kernels for 5%

profile of v5, /device:TPU:0, one launch (start us, length us, event | category | flops | bytes accessed | tf_op | source)
XLA Modules:
  0.0 56.6 jit_solution(8173675160212951259)
XLA Ops:
  0.6 0.0 copy-start
  0.7 2.2 %scale.1.refs_4_ = bf16[1024,128]{1,0:T(8,128)(2,1)} custom-call(s32[8,128]{1,0:T(8,128)} %bitcast.61, bf16[1024,256]{1,0:T(8,128)(2,1)} %gradient_hbm.1), custom_call_target="tpu_custom_call" | custom-call | tf_op jit(solution)/shard_map/scale/pallas_call | solution.py:212
  2.8 0.0 copy-start.5
  2.8 3.1 %collective-permute-start.6 = (bf16[1024,128]{1,0:T(8,128)(2,1)}, bf16[1024,128]{1,0:T(8,128)(2,1)S(1)}, u32[]{:S(2)}, u32[]{:S(2)}) collective-permute-start(bf16[1024,128]{1,0:T(8,128)(2,1)} %scale.1.refs_4_), channel_id=1, source_target_pairs={{0,8},{2,10},{8,16},{10,18},{16,24},{18,26},{24,28},{26,30},{28,20... | collective-permute-start | bytes 786440 | tf_op jit(solution)/shard_map/ppermute | solution.py:35
  5.9 0.0 collective-permute-start.10
  5.9 0.0 copy-start.6
  5.9 0.6 %copy-done.6 = s32[1,8]{1,0:T(1,128)S(1)} copy-done((s32[1,8]{1,0:T(1,128)S(1)}, s32[1,8]{1,0:T(1,128)}, u32[]{:S(2)}) %copy-start.6) | copy-done | bytes 56
  6.6 0.1 copy.9
  6.7 0.1 reshape_squeeze.6
  6.8 0.1 pad_add_fusion
  6.8 0.1 dynamic_slice.15
  6.9 0.2 payload.1
  7.1 2.0 %collective-permute-start.1 = (bf16[1152,128]{1,0:T(8,128)(2,1)S(1)}, bf16[1152,128]{1,0:T(8,128)(2,1)S(1)}, u32[]{:S(2)}, u32[]{:S(2)}) collective-permute-start(bf16[1152,128]{1,0:T(8,128)(2,1)S(1)} %get-tuple-element.14.refs_0_), channel_id=1, source_target_pairs={{0,1},{1,0},{2,3},{3,2},{4,5},{5,4},{6,7},{7,6},{8,9},{9,8},{10,11... | collective-permute-start | bytes 884744 | tf_op jit(solution)/shard_map/ppermute | solution.py:64
  9.1 0.1 collective-permute-start
  9.2 0.1 collective-permute-start.3
  9.4 3.0 %collective-permute-done.6.refs_5_ = bf16[1024,128]{1,0:T(8,128)(2,1)S(1)} collective-permute-done((bf16[1024,128]{1,0:T(8,128)(2,1)}, bf16[1024,128]{1,0:T(8,128)(2,1)S(1)}, u32[]{:S(2)}, u32[]{:S(2)}) %collective-permute-start.6) | collective-permute-done | bytes 262176 | tf_op jit(solution)/shard_map/ppermute | solution.py:35
  12.4 1.8 %collective-permute-start.7 = (bf16[1024,128]{1,0:T(8,128)(2,1)S(1)}, bf16[1024,128]{1,0:T(8,128)(2,1)S(1)}, u32[]{:S(2)}, u32[]{:S(2)}) collective-permute-start(bf16[1024,128]{1,0:T(8,128)(2,1)S(1)} %collective-permute-done.6.refs_5_), channel_id=1, source_target_pairs={{0,8},{2,10},{8,16},{10,18},{16,24},{18,26},{24,28},{26,30},{28,20... | collective-permute-start | bytes 786440 | tf_op jit(solution)/shard_map/ppermute | solution.py:35
  14.2 0.1 reshape.58
  14.5 0.0 collective-permute-done.refs_2_
  14.5 0.1 collective-permute-start.4
  14.6 0.0 collective-permute-done.10.refs_6_
  14.6 0.3 collective-permute-start.11
  14.8 5.0 %collective-permute-done.7.refs_7_ = bf16[1024,128]{1,0:T(8,128)(2,1)S(1)} collective-permute-done((bf16[1024,128]{1,0:T(8,128)(2,1)S(1)}, bf16[1024,128]{1,0:T(8,128)(2,1)S(1)}, u32[]{:S(2)}, u32[]{:S(2)}) %collective-permute-start.7) | collective-permute-done | bytes 262176 | tf_op jit(solution)/shard_map/ppermute | solution.py:35
  19.8 1.5 %collective-permute-start.8 = (bf16[1024,128]{1,0:T(8,128)(2,1)S(1)}, bf16[1024,128]{1,0:T(8,128)(2,1)S(1)}, u32[]{:S(2)}, u32[]{:S(2)}) collective-permute-start(bf16[1024,128]{1,0:T(8,128)(2,1)S(1)} %collective-permute-done.7.refs_7_), channel_id=1, source_target_pairs={{0,8},{2,10},{8,16},{10,18},{16,24},{18,26},{24,28},{26,30},{28,20... | collective-permute-start | bytes 786440 | tf_op jit(solution)/shard_map/ppermute | solution.py:35
  21.4 0.1 reshape.60
  21.4 0.0 collective-permute-done.3.refs_5_
  21.5 0.0 collective-permute-start.5
  21.5 0.0 collective-permute-done.1.refs_1_
  21.5 0.5 collective-permute-start.2
  22.1 1.2 %collective-permute-done.11.refs_8_ = bf16[1024,128]{1,0:T(8,128)(2,1)S(1)} collective-permute-done((bf16[1024,128]{1,0:T(8,128)(2,1)S(1)}, bf16[1024,128]{1,0:T(8,128)(2,1)S(1)}, u32[]{:S(2)}, u32[]{:S(2)}) %collective-permute-start.11) | collective-permute-done | bytes 262176 | tf_op jit(solution)/shard_map/ppermute | solution.py:35
  23.3 0.3 collective-permute-start.12
  23.6 2.8 %collective-permute-done.8.refs_9_ = bf16[1024,128]{1,0:T(8,128)(2,1)S(1)} collective-permute-done((bf16[1024,128]{1,0:T(8,128)(2,1)S(1)}, bf16[1024,128]{1,0:T(8,128)(2,1)S(1)}, u32[]{:S(2)}, u32[]{:S(2)}) %collective-permute-start.8) | collective-permute-done | bytes 262176 | tf_op jit(solution)/shard_map/ppermute | solution.py:35
  26.4 1.5 %collective-permute-start.9 = (bf16[1024,128]{1,0:T(8,128)(2,1)S(1)}, bf16[1024,128]{1,0:T(8,128)(2,1)}, u32[]{:S(2)}, u32[]{:S(2)}) collective-permute-start(bf16[1024,128]{1,0:T(8,128)(2,1)S(1)} %collective-permute-done.8.refs_9_), channel_id=1, source_target_pairs={{0,8},{2,10},{8,16},{10,18},{16,24},{18,26},{24,28},{26,30},{28,20... | collective-permute-start | bytes 786440 | tf_op jit(solution)/shard_map/ppermute | solution.py:35
  27.9 0.1 reshape.62
  28.0 0.0 collective-permute-done.2.refs_3_
  28.0 0.1 reshape.64
  28.1 0.1 concatenate.13.table_ref
  28.2 3.0 %collective-permute-done.12.refs_10_ = bf16[1024,128]{1,0:T(8,128)(2,1)S(1)} collective-permute-done((bf16[1024,128]{1,0:T(8,128)(2,1)S(1)}, bf16[1024,128]{1,0:T(8,128)(2,1)S(1)}, u32[]{:S(2)}, u32[]{:S(2)}) %collective-permute-start.12) | collective-permute-done | bytes 262176 | tf_op jit(solution)/shard_map/ppermute | solution.py:35
  31.2 2.8 %first_slabs.1.refs_9_ = f32[2,1024,128]{2,1,0:T(8,128)S(1)} custom-call(s32[307]{0:T(512)S(1)} %concatenate.13.table_ref, bf16[1152,128]{1,0:T(8,128)(2,1)S(1)} %get-tuple-element.14.refs_0_, bf16[1152,128]{1,0:T(8,128)(2,1)S(1)} %collective-permute-done.1.refs_1_, bf16[576,128]{1,0:T(8,128)(2,1)S(1)} %collective-permute-done.refs_2_, ...), custom_call_target="tpu_custom_call" | custom-call | flops 1 | bytes 1 | tf_op jit(solution)/shard_map/first_slabs/pallas_call | solution.py:286
  34.0 0.0 collective-permute-done.4.refs_6_
  34.0 0.0 collective-permute-done.5.refs_7_
  34.0 0.0 collective-permute-done.9.refs_8_
  34.0 2.0 %last_slab.1 = (f32[1024,128]{1,0:T(8,128)S(1)}, f32[1024,128]{1,0:T(8,128)S(1)}, f32[128,128]{1,0:T(8,128)S(1)}, f32[128,128]{1,0:T(8,128)S(1)}) custom-call(s32[307]{0:T(512)S(1)} %concatenate.13.table_ref, bf16[1152,128]{1,0:T(8,128)(2,1)S(1)} %get-tuple-element.14.refs_0_, bf16[1152,128]{1,0:T(8,128)(2,1)S(1)} %collective-permute-done.1.refs_1_, ...), custom_call_target="tpu_custom_call" | custom-call | tf_op jit(solution)/shard_map/last_slab/pallas_call | solution.py:295
  36.1 0.1 collective-permute-start.13
  36.2 0.5 collective-permute-start.17
  36.7 0.7 %collective-permute-done.13 = f32[128,128]{1,0:T(8,128)S(1)} collective-permute-done((f32[128,128]{1,0:T(8,128)S(1)}, f32[128,128]{1,0:T(8,128)S(1)}, u32[]{:S(2)}, u32[]{:S(2)}) %collective-permute-start.13) | collective-permute-done | bytes 65568 | tf_op jit(solution)/shard_map/ppermute | solution.py:54
  37.4 1.6 %collective-permute-start.14 = (bf16[128,128]{1,0:T(8,128)(2,1)S(1)}, bf16[128,128]{1,0:T(8,128)(2,1)S(1)}, u32[]{:S(2)}, u32[]{:S(2)}) collective-permute-start(bf16[128,128]{1,0:T(8,128)(2,1)S(1)} %add_convert_fusion.1), channel_id=1, source_target_pairs={{0,8},{2,10},{4,12},{6,14},{8,0},{10,2},{12,4},{14,6},{16,24},{18,... | collective-permute-start | bytes 98312 | tf_op jit(solution)/shard_map/ppermute | solution.py:45
  39.1 0.6 %collective-permute-start.15 = (bf16[128,128]{1,0:T(8,128)(2,1)S(1)}, bf16[128,128]{1,0:T(8,128)(2,1)S(1)}, u32[]{:S(2)}, u32[]{:S(2)}) collective-permute-start(bf16[128,128]{1,0:T(8,128)(2,1)S(1)} %add_convert_fusion.1), channel_id=1, source_target_pairs={{0,4},{2,6},{4,0},{6,2},{8,12},{10,14},{12,8},{14,10},{16,20},{18,... | collective-permute-start | bytes 98312 | tf_op jit(solution)/shard_map/ppermute | solution.py:45
  39.6 1.3 %collective-permute-start.16 = (bf16[128,128]{1,0:T(8,128)(2,1)S(1)}, bf16[128,128]{1,0:T(8,128)(2,1)S(1)}, u32[]{:S(2)}, u32[]{:S(2)}) collective-permute-start(bf16[128,128]{1,0:T(8,128)(2,1)S(1)} %add_convert_fusion.1), channel_id=1, source_target_pairs={{0,12},{2,14},{4,8},{6,10},{8,4},{10,6},{12,0},{14,2},{16,28},{18,... | collective-permute-start | bytes 98312 | tf_op jit(solution)/shard_map/ppermute | solution.py:45
  41.0 0.4 collective-permute-done.14
  41.4 1.9 %collective-permute-done.15 = bf16[128,128]{1,0:T(8,128)(2,1)S(1)} collective-permute-done((bf16[128,128]{1,0:T(8,128)(2,1)S(1)}, bf16[128,128]{1,0:T(8,128)(2,1)S(1)}, u32[]{:S(2)}, u32[]{:S(2)}) %collective-permute-start.15) | collective-permute-done | bytes 32800 | tf_op jit(solution)/shard_map/ppermute | solution.py:45
  43.3 1.1 %collective-permute-done.16 = bf16[128,128]{1,0:T(8,128)(2,1)S(1)} collective-permute-done((bf16[128,128]{1,0:T(8,128)(2,1)S(1)}, bf16[128,128]{1,0:T(8,128)(2,1)S(1)}, u32[]{:S(2)}, u32[]{:S(2)}) %collective-permute-start.16) | collective-permute-done | bytes 32800 | tf_op jit(solution)/shard_map/ppermute | solution.py:45
  44.5 0.2 multiply_convert_fusion
  44.7 2.7 %collective-permute-start.19 = (bf16[128,128]{1,0:T(8,128)(2,1)S(1)}, bf16[128,128]{1,0:T(8,128)(2,1)S(1)}, u32[]{:S(2)}, u32[]{:S(2)}) collective-permute-start(bf16[128,128]{1,0:T(8,128)(2,1)S(1)} %add_convert_fusion), channel_id=1, source_target_pairs={{0,16},{2,18},{4,20},{6,22},{8,24},{10,26},{12,28},{14,30},{16,0},... | collective-permute-start | bytes 98312 | tf_op jit(solution)/shard_map/ppermute | solution.py:45
  47.4 1.3 %collective-permute-start.20 = (bf16[128,128]{1,0:T(8,128)(2,1)S(1)}, bf16[128,128]{1,0:T(8,128)(2,1)S(1)}, u32[]{:S(2)}, u32[]{:S(2)}) collective-permute-start(bf16[128,128]{1,0:T(8,128)(2,1)S(1)} %add_convert_fusion), channel_id=1, source_target_pairs={{0,17},{1,16},{2,19},{3,18},{4,21},{5,20},{6,23},{7,22},{8,25},{9,... | collective-permute-start | bytes 98312 | tf_op jit(solution)/shard_map/ppermute | solution.py:47
  48.7 0.6 %collective-permute-start.18 = (bf16[640,128]{1,0:T(8,128)(2,1)S(1)}, bf16[640,128]{1,0:T(8,128)(2,1)S(1)}, u32[]{:S(2)}, u32[]{:S(2)}) collective-permute-start(bf16[640,128]{1,0:T(8,128)(2,1)S(1)} %pad_maximum_fusion.1), channel_id=1, source_target_pairs={{0,1},{1,0},{2,3},{3,2},{4,5},{5,4},{6,7},{7,6},{8,9},{9,8},{10,11... | collective-permute-start | bytes 491528 | tf_op jit(solution)/shard_map/ppermute | solution.py:64
  49.3 0.2 fusion.2
  49.5 0.3 collective-permute-done.19
  49.9 3.6 %collective-permute-done.20 = bf16[128,128]{1,0:T(8,128)(2,1)S(1)} collective-permute-done((bf16[128,128]{1,0:T(8,128)(2,1)S(1)}, bf16[128,128]{1,0:T(8,128)(2,1)S(1)}, u32[]{:S(2)}, u32[]{:S(2)}) %collective-permute-start.20) | collective-permute-done | bytes 32800 | tf_op jit(solution)/shard_map/ppermute | solution.py:47
  53.4 1.0 %collective-permute-done.18 = bf16[640,128]{1,0:T(8,128)(2,1)S(1)} collective-permute-done((bf16[640,128]{1,0:T(8,128)(2,1)S(1)}, bf16[640,128]{1,0:T(8,128)(2,1)S(1)}, u32[]{:S(2)}, u32[]{:S(2)}) %collective-permute-start.18) | collective-permute-done | bytes 163872 | tf_op jit(solution)/shard_map/ppermute | solution.py:64
  54.5 0.1 collective-permute-start.21
  54.5 0.9 %fusion = bf16[512,256]{1,0:T(8,128)(2,1)} fusion(f32[512,256]{1,0:T(8,128)S(1)} %fusion.2, bf16[640,128]{1,0:T(8,128)(2,1)S(1)} %collective-permute-done.18, bf16[256,256]{1,0:T(8,128)(2,1)S(1)} %copy-done, s32[]{:T(128)S(6)} %select_n.476), kind=kOutput, calls=%fused_computation.1 | convolution fusion | flops 33816576 | bytes 983044 | tf_op jit(solution)/shard_map/dot_general | solution.py:334
  55.5 0.4 collective-permute-done.21
  55.9 0.7 %pad_maximum_fusion = f32[256,256]{1,0:T(8,128)} fusion(f32[128,256]{1,0:T(8,128)S(1)} %get-tuple-element.27, f32[128,256]{1,0:T(8,128)S(1)} %get-tuple-element.26), kind=kLoop, calls=%fused_computation.3 | loop fusion | flops 65536 | bytes 524288 | tf_op jit(solution)/shard_map/concatenate | solution.py:343
  (36 shorter events, 0.3 us)
Async XLA Ops:
  0.6 48.6 %copy-start = (bf16[256,256]{1,0:T(8,128)(2,1)S(1)}, bf16[256,256]{1,0:T(8,128)(2,1)}, u32[]{:S(2)}) copy-start(bf16[256,256]{1,0:T(8,128)(2,1)} %param.9) | copy-start | bytes 393220
  0.6 6.3 %copy-start.2 = (s32[1,8,8,16,128]{4,3,2,1,0:T(8,128)S(1)}, s32[1,8,8,16,128]{4,3,2,1,0:T(8,128)}, u32[]{:S(2)}) copy-start(s32[1,8,8,16,128]{4,3,2,1,0:T(8,128)} %param.10) | copy-start | bytes 1572868
  0.7 5.3 %copy-start.4 = (s32[1024]{0:T(1024)S(1)}, s32[1024]{0:T(1024)}, u32[]{:S(2)}) copy-start(s32[1024]{0:T(1024)} %param.13) | copy-start | bytes 12292
  0.7 6.3 %copy-start.3 = (bf16[512,256]{1,0:T(8,128)(2,1)S(1)}, bf16[512,256]{1,0:T(8,128)(2,1)}, u32[]{:S(2)}) copy-start(bf16[512,256]{1,0:T(8,128)(2,1)} %features_ref) | copy-start | bytes 786436
  2.8 3.8 %copy-start.5 = (s32[1,8,2,8]{3,2,1,0:T(2,128)S(1)}, s32[1,8,2,8]{3,2,1,0:T(2,128)}, u32[]{:S(2)}) copy-start(s32[1,8,2,8]{3,2,1,0:T(2,128)} %param.11) | copy-start | bytes 1540
  2.8 9.5 %collective-permute-start.6 = (bf16[1024,128]{1,0:T(8,128)(2,1)}, bf16[1024,128]{1,0:T(8,128)(2,1)S(1)}, u32[]{:S(2)}, u32[]{:S(2)}) collective-permute-start(bf16[1024,128]{1,0:T(8,128)(2,1)} %scale.1.refs_4_), channel_id=1, source_target_pairs={{0,8},{2,10},{8,16},{10,18},{16,24},{18,26},{24,28},{26,30},{28,20... | collective-permute-start | bytes 786440 | tf_op jit(solution)/shard_map/ppermute | solution.py:35
  5.9 8.7 %collective-permute-start.10 = (bf16[1024,128]{1,0:T(8,128)(2,1)}, bf16[1024,128]{1,0:T(8,128)(2,1)S(1)}, u32[]{:S(2)}, u32[]{:S(2)}) collective-permute-start(bf16[1024,128]{1,0:T(8,128)(2,1)} %scale.1.refs_4_), channel_id=1, source_target_pairs={{0,4},{2,6},{8,0},{10,2},{16,8},{18,10},{24,16},{26,18},{28,24},{3... | collective-permute-start | bytes 786440 | tf_op jit(solution)/shard_map/ppermute | solution.py:35
  5.9 0.7 %copy-start.6 = (s32[1,8]{1,0:T(1,128)S(1)}, s32[1,8]{1,0:T(1,128)}, u32[]{:S(2)}) copy-start(s32[1,8]{1,0:T(1,128)} %param.12) | copy-start | bytes 100
  7.1 14.4 %collective-permute-start.1 = (bf16[1152,128]{1,0:T(8,128)(2,1)S(1)}, bf16[1152,128]{1,0:T(8,128)(2,1)S(1)}, u32[]{:S(2)}, u32[]{:S(2)}) collective-permute-start(bf16[1152,128]{1,0:T(8,128)(2,1)S(1)} %get-tuple-element.14.refs_0_), channel_id=1, source_target_pairs={{0,1},{1,0},{2,3},{3,2},{4,5},{5,4},{6,7},{7,6},{8,9},{9,8},{10,11... | collective-permute-start | bytes 884744 | tf_op jit(solution)/shard_map/ppermute | solution.py:64
  9.1 5.3 %collective-permute-start = (bf16[576,128]{1,0:T(8,128)(2,1)S(1)}, bf16[576,128]{1,0:T(8,128)(2,1)S(1)}, u32[]{:S(2)}, u32[]{:S(2)}) collective-permute-start(bf16[576,128]{1,0:T(8,128)(2,1)S(1)} %get-tuple-element.24), channel_id=1, source_target_pairs={{0,2},{2,0},{4,6},{6,4},{8,10},{10,8},{12,14},{14,12},{16,18},{18,... | collective-permute-start | bytes 442376 | tf_op jit(solution)/shard_map/ppermute | solution.py:54
  9.2 12.2 %collective-permute-start.3 = (bf16[1024,128]{1,0:T(8,128)(2,1)S(1)}, bf16[1024,128]{1,0:T(8,128)(2,1)S(1)}, u32[]{:S(2)}, u32[]{:S(2)}) collective-permute-start(bf16[1024,128]{1,0:T(8,128)(2,1)S(1)} %get-tuple-element.15.refs_4_), channel_id=1, source_target_pairs={{0,1},{1,0},{2,3},{3,2},{4,5},{5,4},{6,7},{7,6},{8,9},{9,8},{10,11... | collective-permute-start | bytes 786440 | tf_op jit(solution)/shard_map/ppermute | solution.py:64
  12.4 7.5 %collective-permute-start.7 = (bf16[1024,128]{1,0:T(8,128)(2,1)S(1)}, bf16[1024,128]{1,0:T(8,128)(2,1)S(1)}, u32[]{:S(2)}, u32[]{:S(2)}) collective-permute-start(bf16[1024,128]{1,0:T(8,128)(2,1)S(1)} %collective-permute-done.6.refs_5_), channel_id=1, source_target_pairs={{0,8},{2,10},{8,16},{10,18},{16,24},{18,26},{24,28},{26,30},{28,20... | collective-permute-start | bytes 786440 | tf_op jit(solution)/shard_map/ppermute | solution.py:35
  14.5 19.5 %collective-permute-start.4 = (bf16[1024,128]{1,0:T(8,128)(2,1)S(1)}, bf16[1024,128]{1,0:T(8,128)(2,1)}, u32[]{:S(2)}, u32[]{:S(2)}) collective-permute-start(bf16[1024,128]{1,0:T(8,128)(2,1)S(1)} %get-tuple-element.15.refs_4_), channel_id=1, source_target_pairs={{0,2},{2,0},{4,6},{6,4},{8,10},{10,8},{12,14},{14,12},{16,18},{18,... | collective-permute-start | bytes 786440 | tf_op jit(solution)/shard_map/ppermute | solution.py:54
  14.6 8.7 %collective-permute-start.11 = (bf16[1024,128]{1,0:T(8,128)(2,1)S(1)}, bf16[1024,128]{1,0:T(8,128)(2,1)S(1)}, u32[]{:S(2)}, u32[]{:S(2)}) collective-permute-start(bf16[1024,128]{1,0:T(8,128)(2,1)S(1)} %collective-permute-done.10.refs_6_), channel_id=1, source_target_pairs={{0,4},{2,6},{8,0},{10,2},{16,8},{18,10},{24,16},{26,18},{28,24},{3... | collective-permute-start | bytes 786440 | tf_op jit(solution)/shard_map/ppermute | solution.py:35
  19.8 6.6 %collective-permute-start.8 = (bf16[1024,128]{1,0:T(8,128)(2,1)S(1)}, bf16[1024,128]{1,0:T(8,128)(2,1)S(1)}, u32[]{:S(2)}, u32[]{:S(2)}) collective-permute-start(bf16[1024,128]{1,0:T(8,128)(2,1)S(1)} %collective-permute-done.7.refs_7_), channel_id=1, source_target_pairs={{0,8},{2,10},{8,16},{10,18},{16,24},{18,26},{24,28},{26,30},{28,20... | collective-permute-start | bytes 786440 | tf_op jit(solution)/shard_map/ppermute | solution.py:35
  21.4 9.8 %copy-start.1 = (bf16[1024,128]{1,0:T(8,128)(2,1)S(1)}, bf16[1024,128]{1,0:T(8,128)(2,1)}, u32[]{:S(2)}) copy-start(bf16[1024,128]{1,0:T(8,128)(2,1)} %scale.1.refs_4_) | copy-start | bytes 786436
  21.5 12.6 %collective-permute-start.5 = (bf16[1024,128]{1,0:T(8,128)(2,1)S(1)}, bf16[1024,128]{1,0:T(8,128)(2,1)}, u32[]{:S(2)}, u32[]{:S(2)}) collective-permute-start(bf16[1024,128]{1,0:T(8,128)(2,1)S(1)} %collective-permute-done.3.refs_5_), channel_id=1, source_target_pairs={{0,2},{2,0},{4,6},{6,4},{8,10},{10,8},{12,14},{14,12},{16,18},{18,... | collective-permute-start | bytes 786440 | tf_op jit(solution)/shard_map/ppermute | solution.py:54
  21.5 6.4 %collective-permute-start.2 = (bf16[576,128]{1,0:T(8,128)(2,1)S(1)}, bf16[576,128]{1,0:T(8,128)(2,1)S(1)}, u32[]{:S(2)}, u32[]{:S(2)}) collective-permute-start(bf16[576,128]{1,0:T(8,128)(2,1)S(1)} %get-tuple-element.22), channel_id=1, source_target_pairs={{0,2},{2,0},{4,6},{6,4},{8,10},{10,8},{12,14},{14,12},{16,18},{18,... | collective-permute-start | bytes 442376 | tf_op jit(solution)/shard_map/ppermute | solution.py:54
  23.3 7.9 %collective-permute-start.12 = (bf16[1024,128]{1,0:T(8,128)(2,1)S(1)}, bf16[1024,128]{1,0:T(8,128)(2,1)S(1)}, u32[]{:S(2)}, u32[]{:S(2)}) collective-permute-start(bf16[1024,128]{1,0:T(8,128)(2,1)S(1)} %collective-permute-done.11.refs_8_), channel_id=1, source_target_pairs={{0,4},{2,6},{8,0},{10,2},{16,8},{18,10},{24,16},{26,18},{28,24},{3... | collective-permute-start | bytes 786440 | tf_op jit(solution)/shard_map/ppermute | solution.py:35
  26.4 7.6 %collective-permute-start.9 = (bf16[1024,128]{1,0:T(8,128)(2,1)S(1)}, bf16[1024,128]{1,0:T(8,128)(2,1)}, u32[]{:S(2)}, u32[]{:S(2)}) collective-permute-start(bf16[1024,128]{1,0:T(8,128)(2,1)S(1)} %collective-permute-done.8.refs_9_), channel_id=1, source_target_pairs={{0,8},{2,10},{8,16},{10,18},{16,24},{18,26},{24,28},{26,30},{28,20... | collective-permute-start | bytes 786440 | tf_op jit(solution)/shard_map/ppermute | solution.py:35
  36.1 1.3 %collective-permute-start.13 = (f32[128,128]{1,0:T(8,128)S(1)}, f32[128,128]{1,0:T(8,128)S(1)}, u32[]{:S(2)}, u32[]{:S(2)}) collective-permute-start(f32[128,128]{1,0:T(8,128)S(1)} %get-tuple-element.17), channel_id=1, source_target_pairs={{0,2},{2,0},{4,6},{6,4},{8,10},{10,8},{12,14},{14,12},{16,18},{18,... | collective-permute-start | bytes 196616 | tf_op jit(solution)/shard_map/ppermute | solution.py:54
  36.2 8.3 %collective-permute-start.17 = (f32[1024,128]{1,0:T(8,128)S(1)}, f32[1024,128]{1,0:T(8,128)S(1)}, u32[]{:S(2)}, u32[]{:S(2)}) collective-permute-start(f32[1024,128]{1,0:T(8,128)S(1)} %get-tuple-element.19), channel_id=1, source_target_pairs={{0,2},{2,0},{4,6},{6,4},{8,10},{10,8},{12,14},{14,12},{16,18},{18,... | collective-permute-start | bytes 1572872 | tf_op jit(solution)/shard_map/ppermute | solution.py:54
  37.4 4.0 %collective-permute-start.14 = (bf16[128,128]{1,0:T(8,128)(2,1)S(1)}, bf16[128,128]{1,0:T(8,128)(2,1)S(1)}, u32[]{:S(2)}, u32[]{:S(2)}) collective-permute-start(bf16[128,128]{1,0:T(8,128)(2,1)S(1)} %add_convert_fusion.1), channel_id=1, source_target_pairs={{0,8},{2,10},{4,12},{6,14},{8,0},{10,2},{12,4},{14,6},{16,24},{18,... | collective-permute-start | bytes 98312 | tf_op jit(solution)/shard_map/ppermute | solution.py:45
  39.1 4.3 %collective-permute-start.15 = (bf16[128,128]{1,0:T(8,128)(2,1)S(1)}, bf16[128,128]{1,0:T(8,128)(2,1)S(1)}, u32[]{:S(2)}, u32[]{:S(2)}) collective-permute-start(bf16[128,128]{1,0:T(8,128)(2,1)S(1)} %add_convert_fusion.1), channel_id=1, source_target_pairs={{0,4},{2,6},{4,0},{6,2},{8,12},{10,14},{12,8},{14,10},{16,20},{18,... | collective-permute-start | bytes 98312 | tf_op jit(solution)/shard_map/ppermute | solution.py:45
  39.6 4.8 %collective-permute-start.16 = (bf16[128,128]{1,0:T(8,128)(2,1)S(1)}, bf16[128,128]{1,0:T(8,128)(2,1)S(1)}, u32[]{:S(2)}, u32[]{:S(2)}) collective-permute-start(bf16[128,128]{1,0:T(8,128)(2,1)S(1)} %add_convert_fusion.1), channel_id=1, source_target_pairs={{0,12},{2,14},{4,8},{6,10},{8,4},{10,6},{12,0},{14,2},{16,28},{18,... | collective-permute-start | bytes 98312 | tf_op jit(solution)/shard_map/ppermute | solution.py:45
  44.7 5.1 %collective-permute-start.19 = (bf16[128,128]{1,0:T(8,128)(2,1)S(1)}, bf16[128,128]{1,0:T(8,128)(2,1)S(1)}, u32[]{:S(2)}, u32[]{:S(2)}) collective-permute-start(bf16[128,128]{1,0:T(8,128)(2,1)S(1)} %add_convert_fusion), channel_id=1, source_target_pairs={{0,16},{2,18},{4,20},{6,22},{8,24},{10,26},{12,28},{14,30},{16,0},... | collective-permute-start | bytes 98312 | tf_op jit(solution)/shard_map/ppermute | solution.py:45
  47.4 6.1 %collective-permute-start.20 = (bf16[128,128]{1,0:T(8,128)(2,1)S(1)}, bf16[128,128]{1,0:T(8,128)(2,1)S(1)}, u32[]{:S(2)}, u32[]{:S(2)}) collective-permute-start(bf16[128,128]{1,0:T(8,128)(2,1)S(1)} %add_convert_fusion), channel_id=1, source_target_pairs={{0,17},{1,16},{2,19},{3,18},{4,21},{5,20},{6,23},{7,22},{8,25},{9,... | collective-permute-start | bytes 98312 | tf_op jit(solution)/shard_map/ppermute | solution.py:47
  48.7 5.7 %collective-permute-start.18 = (bf16[640,128]{1,0:T(8,128)(2,1)S(1)}, bf16[640,128]{1,0:T(8,128)(2,1)S(1)}, u32[]{:S(2)}, u32[]{:S(2)}) collective-permute-start(bf16[640,128]{1,0:T(8,128)(2,1)S(1)} %pad_maximum_fusion.1), channel_id=1, source_target_pairs={{0,1},{1,0},{2,3},{3,2},{4,5},{5,4},{6,7},{7,6},{8,9},{9,8},{10,11... | collective-permute-start | bytes 491528 | tf_op jit(solution)/shard_map/ppermute | solution.py:64
  54.5 1.4 %collective-permute-start.21 = (f32[128,256]{1,0:T(8,128)S(1)}, f32[128,256]{1,0:T(8,128)S(1)}, u32[]{:S(2)}, u32[]{:S(2)}) collective-permute-start(f32[128,256]{1,0:T(8,128)S(1)} %broadcast_multiply_fusion), channel_id=1, source_target_pairs={{0,2},{2,0},{4,6},{6,4},{8,10},{10,8},{12,14},{14,12},{16,18},{18,... | collective-permute-start | bytes 393224 | tf_op jit(solution)/shard_map/ppermute | solution.py:54

commit v6 on v5

--- a/solution.py
+++ b/solution.py
@@ -35,15 +35,14 @@
     return lax.ppermute(block, "blk", route)
 
 
-def across(block, rows=0, columns=0, reps=0):
+def across(block, *moves):
     size = lax.axis_size("rep")
-    route = [
-        (device_of(z, x, c), device_of(z ^ rows, x ^ columns, c))
-        for z, x, c in places(lax.axis_size("blk"))
-    ]
-    if not reps:
-        return lax.ppermute(block, "blk", route)
-    route = [(a * size + r, b * size + (r + reps) % size) for a, b in route for r in range(size)]
+    route = []
+    for z, x, c in places(lax.axis_size("blk")):
+        if moves[c] is not None:
+            rows, columns, reps = moves[c]
+            start, end = device_of(z, x, c), device_of(z ^ rows, x ^ columns, c)
+            route += [(start * size + r, end * size + (r + reps) % size) for r in range(size)]
     return lax.ppermute(block, ("blk", "rep"), route)
 
 
@@ -78,7 +77,7 @@
     return [block] + [along_rep(block, d) for d in range(1, lax.axis_size("rep"))]
 
 
-def add_pairs(plan, table_ref, first_slab, own_pieces, other_pieces, slabs, sums_ref):
+def add_pairs(plan, table_ref, first_slab, own_pieces, other_pieces, slabs, sums):
     bit_ids = lax.broadcasted_iota(jnp.int32, (16, 8, 128), 1)
     for slab_id, slab_ref in enumerate(slabs):
         for target, pieces in enumerate((own_pieces, other_pieces)):
@@ -100,42 +99,36 @@
                 transposed = bits.reshape(128, 128).astype(jnp.float32).astype(jnp.bfloat16)
                 rows = pl.ds(pl.multiple_of(row_block * 128, 128), 128)
                 columns = pl.ds(pl.multiple_of(column_block * 128, 128), 128)
-                sums_ref[target, columns, :] += jnp.dot(
+                sums[target][columns, :] += jnp.dot(
                     transposed, slab_ref[rows, :], preferred_element_type=jnp.float32
                 )
 
 
-def first_kernel(plan, slab_total, table_ref, *refs):
-    pieces, slabs, sums_ref = refs[: 2 * plan.reps], refs[2 * plan.reps : -1], refs[-1]
-    sums_ref[...] = jnp.zeros_like(sums_ref)
-    add_pairs(plan, table_ref, 0, pieces[: plan.reps], pieces[plan.reps :], slabs, sums_ref)
+def adding_kernel(plan, first_slab, slab_total, table_ref, *refs):
+    own_pieces, other_pieces = refs[: plan.reps], refs[plan.reps : 2 * plan.reps]
+    slabs, sums_in, sums = refs[2 * plan.reps :][:slab_total], refs[2 * plan.reps + slab_total : -2], refs[-2:]
+    for target, sums_ref in enumerate(sums):
+        sums_ref[...] = sums_in[target][...] if sums_in else jnp.zeros_like(sums_ref)
+    add_pairs(plan, table_ref, first_slab, own_pieces, other_pieces, slabs, sums)
 
 
 def last_kernel(plan, last_slab, table_ref, *refs):
     own_pieces, other_pieces = refs[: plan.reps], refs[plan.reps : 2 * plan.reps]
     own_features, other_features = refs[2 * plan.reps : 3 * plan.reps], refs[3 * plan.reps : 4 * plan.reps]
-    slab_ref, sums_in, own_ref, other_ref, keep_ref, send_ref, sums_ref, term_ref = refs[4 * plan.reps :]
-    sums_ref[...] = sums_in[...]
-    add_pairs(plan, table_ref, last_slab, own_pieces, other_pieces, [slab_ref], sums_ref)
-    own_ref[...] = sums_ref[0]
-    other_ref[...] = sums_ref[1]
-    share = sums_ref.shape[1] // plan.reps
-    width = term_ref.shape[0]
+    slab_ref, own_in, other_in, own_ref, other_ref, term_ref = refs[4 * plan.reps :]
+    own_ref[...] = own_in[...]
+    other_ref[...] = other_in[...]
+    sums = (own_ref, other_ref)
+    add_pairs(plan, table_ref, last_slab, own_pieces, other_pieces, [slab_ref], sums)
+    share = own_ref.shape[0] // plan.reps
     order_at = plan.facts_size + 4 * (last_slab + 1)
     term = jnp.zeros(term_ref.shape, jnp.float32)
-    for target, pieces in enumerate((own_features, other_features)):
+    for sums_ref, pieces in zip(sums, (own_features, other_features)):
         for piece_id, piece_ref in enumerate(pieces):
-            start = pl.multiple_of(table_ref[order_at + piece_id] * share, share)
-            for block in range(share // 128):
-                rows = pl.ds(pl.multiple_of(start + block * 128, 128), 128)
-                part = sums_ref[target, rows, :].astype(jnp.bfloat16)
-                features = piece_ref[block * width : (block + 1) * width, :]
-                term += jnp.dot(features, part, preferred_element_type=jnp.float32)
-    term_ref[...] = term
-    half = width // 2
-    core = table_ref[order_at + plan.reps]
-    keep_ref[...] = term_ref[pl.ds(pl.multiple_of(core * half, half), half), :]
-    send_ref[...] = term_ref[pl.ds(pl.multiple_of((1 - core) * half, half), half), :]
+            rows = pl.ds(pl.multiple_of(table_ref[order_at + piece_id] * share, share), share)
+            part = sums_ref[rows, :].astype(jnp.bfloat16)
+            term += jnp.dot(piece_ref[...], part, preferred_element_type=jnp.float32)
+    term_ref[...] = term.astype(term_ref.dtype)
 
 
 class Plan:
@@ -180,16 +173,19 @@
         pairs_ref[start : start + word_rows, :] = words
         facts = jnp.broadcast_to(facts_ref[step : step + 1, :].astype(jnp.float32), (16, 128))
         pairs_ref[start + word_rows : start + plan.pair_rows, :] = facts.astype(pairs_ref.dtype)
-    rows, width = features_ref.shape
-    for block in range(rows // 128):
-        part = features_ref[block * 128 : (block + 1) * 128, :].astype(jnp.float32).T
-        part = part * roots_ref[:, block * 128 : (block + 1) * 128]
-        turned_ref[block * width : (block + 1) * width, :] = part.astype(turned_ref.dtype)
+    for at in range(0, features_ref.shape[0], 128):
+        part = features_ref[at : at + 128, :].astype(jnp.float32).T * roots_ref[:, at : at + 128]
+        turned_ref[:, at : at + 128] = part.astype(turned_ref.dtype)
 
 
 SMEM = pl.BlockSpec(memory_space=pltpu.SMEM)
 VMEM = pl.BlockSpec(memory_space=pltpu.VMEM)
+COST = pl.CostEstimate(flops=1, bytes_accessed=1, transcendentals=0)
 PARAMS = pltpu.CompilerParams(vmem_limit_bytes=12 * 1024 * 1024)
+
+
+def in_hbm(block):
+    return pltpu.with_memory_space_constraint(block, pltpu.HBM)
 
 
 def per_device(features, out_grad, weight, block_words, block_coords, block_counts, degrees):
@@ -211,7 +207,7 @@
     if share_width % 128 == 0 and slab_rows % 1024 == 0:
         scaled = pl.pallas_call(
             functools.partial(scale_kernel, share_width),
-            out_shape=jax.ShapeDtypeStruct((slab_rows, share_width), jnp.bfloat16),
+            out_shape=pltpu.VMEM((slab_rows, share_width), jnp.bfloat16),
             in_specs=[pl.BlockSpec(memory_space=pltpu.HBM)] * 2,
             out_specs=VMEM,
             scratch_shapes=[
@@ -219,9 +215,9 @@
                 pltpu.VMEM((slab_rows, width), jnp.bfloat16),
                 pltpu.SemaphoreType.DMA((5,)),
             ],
-            compiler_params=pltpu.CompilerParams(vmem_limit_bytes=60 * 1024 * 1024),
+            compiler_params=PARAMS,
             name="scale",
-        )(degrees.reshape(slab_rows // 128, 128), out_grad)
+        )(in_hbm(degrees.reshape(slab_rows // 128, 128)), in_hbm(out_grad))
     else:
         own_columns = lax.dynamic_slice_in_dim(out_grad, rep_index * share_width, share_width, 1)
         scaled = (own_columns.astype(jnp.float32) * inverse_root[:, None]).astype(jnp.bfloat16)
@@ -240,11 +236,12 @@
         functools.partial(payload_kernel, plan),
         out_shape=(
             jax.ShapeDtypeStruct((2 * words_rows, 128), jnp.bfloat16),
-            jax.ShapeDtypeStruct((share_rows // 128 * width, 128), jnp.bfloat16),
+            jax.ShapeDtypeStruct((width, share_rows), jnp.bfloat16),
         ),
         in_specs=[VMEM] * 4,
         out_specs=(VMEM, VMEM),
         compiler_params=PARAMS,
+        cost_estimate=COST,
         name="payload",
     )(facts, block_words[0].reshape(2 * half_steps, slot_total * 16, 128), features, share_root[None])
     own_pieces = from_all_reps(pairs)
@@ -269,7 +266,7 @@
         for target in range(2):
             offset = (source - chip - jnp.where(core == 0, target, 0)) % chips
             entries += [(rep_index - offset // half_steps) % rep_size, offset % half_steps]
-    entries += [(rep_index - d) % rep_size for d in range(rep_size)] + [core]
+    entries += [(rep_index - d) % rep_size for d in range(rep_size)]
     table = [facts_of(piece) for pair in zip(own_pieces, other_pieces) for piece in pair]
     table = jnp.concatenate(table + [jnp.stack(entries).astype(jnp.int32)])
 
@@ -280,69 +277,79 @@
     del backward
 
     slab_shape = jax.ShapeDtypeStruct((slab_rows, share_width), jnp.float32)
-    half_term = jax.ShapeDtypeStruct((width // 2, share_width), jnp.float32)
-    sums_shape = jax.ShapeDtypeStruct((2, slab_rows, share_width), jnp.float32)
-    pair_flops = 2 * slot_total * 128 * 128 * share_width * 2
-    sums = pl.pallas_call(
-        functools.partial(first_kernel, plan, len(slabs)),
-        out_shape=sums_shape,
-        in_specs=[SMEM] + [VMEM] * (2 * rep_size + len(slabs)),
-        out_specs=VMEM,
+    term_shape = jax.ShapeDtypeStruct((width, share_width), jnp.bfloat16)
+    def add_slabs(first_slab, slabs, sums):
+        operands = own_pieces + other_pieces + slabs
+        aliases = {1 + len(operands) + target: target for target in range(len(sums))}
+        operands = operands + sums
+        return pl.pallas_call(
+            functools.partial(adding_kernel, plan, first_slab, len(slabs)),
+            out_shape=(slab_shape, slab_shape),
+            in_specs=[SMEM] + [VMEM] * len(operands),
+            out_specs=(VMEM, VMEM),
+            input_output_aliases=aliases,
+            compiler_params=PARAMS,
+            cost_estimate=COST,
+            name="add_slabs",
+        )(table, *operands)
+
+    early = len(slabs) - 4
+    sums = add_slabs(0, slabs[:early], [])
+    for at in range(early, len(slabs), 2):
+        sums = add_slabs(at, slabs[at : at + 2], list(sums))
+    own_sums, other_sums, term = pl.pallas_call(
+        functools.partial(last_kernel, plan, len(slabs)),
+        out_shape=(slab_shape, slab_shape, term_shape),
+        in_specs=[SMEM] + [VMEM] * (4 * rep_size + 3),
+        out_specs=(VMEM,) * 3,
         compiler_params=PARAMS,
-        cost_estimate=pl.CostEstimate(flops=1, bytes_accessed=1, transcendentals=0),
-        name="first_slabs",
-    )(table, *own_pieces, *other_pieces, *slabs)
-    own_sums, other_sums, keep, send = pl.pallas_call(
-        functools.partial(last_kernel, plan, len(slabs)),
-        out_shape=(slab_shape, slab_shape, half_term, half_term),
-        in_specs=[SMEM] + [VMEM] * (4 * rep_size + 2),
-        out_specs=(VMEM,) * 4,
-        scratch_shapes=[
-            pltpu.VMEM(sums_shape.shape, jnp.float32),
-            pltpu.VMEM((width, share_width), jnp.float32),
-        ],
-        compiler_params=PARAMS,
+        cost_estimate=COST,
         name="last_slab",
-    )(table, *own_pieces, *other_pieces, *own_features, *other_features, forward, sums)
+    )(table, *own_pieces, *other_pieces, *own_features, *other_features, forward, *sums)
 
     def wide(values):
         return values.astype(jnp.float32)
 
-    total = (keep + across_cores(send)).astype(jnp.bfloat16)
+    total = (wide(term) + wide(across_cores(term))).astype(jnp.bfloat16)
     own_sums = own_sums + across_cores(other_sums)
     aggregated = (own_sums * inverse_root[:, None]).astype(jnp.bfloat16)
     row_bits = [1 << bit for bit in range(rows_of_chips.bit_length() - 1)]
-    total = (wide(total) + wide(across(total, rows=row_bits[0]))) + (
-        wide(across(total, columns=1)) + wide(across(total, rows=row_bits[0], columns=1))
-    )
+    first_bit, last_bit = row_bits[0], row_bits[-1]
+    one = across(total, (first_bit, 1, 0), (first_bit, 0, 0))
+    two = across(total, None, (0, 1, 0))
+    part = wide(one) + wide(jnp.where(core == 0, total, two))
+    total = part + across_cores(part)
+    for bit in row_bits[1:-1]:
+        total = total.astype(jnp.bfloat16)
+        total = wide(total) + wide(across(total, (bit, 0, 0), (bit, 0, 0)))
+    total, aggregated = lax.optimization_barrier((total, aggregated))
     total = total.astype(jnp.bfloat16)
-    for bit in row_bits[1:-1]:
-        total = (wide(total) + wide(across(total, rows=bit))).astype(jnp.bfloat16)
-    total, aggregated = lax.optimization_barrier((total, aggregated))
     result = jnp.zeros((share_rows, width), jnp.float32)
-    weight_half = jnp.zeros((width // 2, width), jnp.float32)
+    shares = []
     for d in range(rep_size):
         rows_to = ((rep_index + d) % rep_size) * share_rows
         part = lax.dynamic_slice_in_dim(aggregated, rows_to, share_rows, 0)
-        columns = total
-        far = across(total, rows=row_bits[-1], reps=d)
         if d:
+            far = across(total, (last_bit, 0, 0), (last_bit, 0, d))
             both = along_rep(jnp.concatenate([part, total]), d)
-            part, columns = both[:share_rows], both[share_rows:]
+            part, near = both[:share_rows], both[share_rows:]
+            shares.append(wide(jnp.where(core == 0, total, near)) + wide(far))
         columns_at = ((rep_index - d) % rep_size) * share_width
         side = lax.dynamic_slice_in_dim(weight, columns_at, share_width, 1)
         result = result + lax.dot_general(
             part, side, (((1,), (1,)), ((), ())), preferred_element_type=jnp.float32
         )
-        weight_half = lax.dynamic_update_slice_in_dim(
-            weight_half, wide(columns) + wide(far), columns_at, 1
-        )
     input_grad = result.astype(jnp.bfloat16)
-    weight_half = weight_half * (1.0 / math.sqrt(slab_rows * blk_size))
-    other_half = across_cores(weight_half)
-    weight_grad = jnp.concatenate(
-        [jnp.where(core == 0, weight_half, other_half), jnp.where(core == 0, other_half, weight_half)]
-    )
+    shares = jnp.stack(shares)
+    others = across_cores(shares)
+    own_share = jnp.where(core == 0, shares[0], others[0])
+    other_shares = jnp.where(core == 0, others, shares)
+    weight_grad = jnp.zeros((width, width), jnp.float32)
+    for d in range(rep_size):
+        columns_at = ((rep_index - d) % rep_size) * share_width
+        share = other_shares[d - 1] if d else own_share
+        weight_grad = lax.dynamic_update_slice_in_dim(weight_grad, share, columns_at, 1)
+    weight_grad = weight_grad * (1.0 / math.sqrt(slab_rows * blk_size))
     return (input_grad, weight_grad)
 
 

time: 56.8 us -> 54.6 us (0.961)
  waiting for transfers between devices: 24.6 us -> 19.1 us
  Pallas kernels: 7.12 us -> 8.74 us
  starting transfers between devices: 20 us -> 21.5 us
    ppermute x4 -> x0, starting transfers between devices: 6.21 us -> none  [across(): return lax.ppermute(block, 'blk', route)]
    ppermute x1 -> x3, starting transfers between devices: 1.29 us -> 5.91 us  [across(): return lax.ppermute(block, ('blk', 'rep'), route)]
    ppermute x4 -> x0, waiting for transfers between devices: 3.82 us -> none  [across(): return lax.ppermute(block, 'blk', route)]
    ppermute x7, waiting for transfers between devices: 15.1 us -> 11.9 us  [along_ring(): return lax.ppermute(block, 'blk', route)]
    ppermute x7 -> x8, starting transfers between devices: 1.38 us -> 3.48 us  [across_cores(): return lax.ppermute(block, 'blk', route)]
    pallas_call x2 -> x4, Pallas kernels: 4.92 us -> 6.82 us  [the longest x3 5.37 us: add_slabs(): pl.pallas_call(functools.partial(adding_kernel, plan, first_slab, len(sla...]
    ppermute x1 -> x3, waiting for transfers between devices: 3.56 us -> 5.42 us  [across(): return lax.ppermute(block, ('blk', 'rep'), route)]
    ppermute x3, starting transfers between devices: 2.73 us -> 3.76 us  [along_rep(): lax.ppermute(block, 'rep', [(i, (i + distance) % size) for i in range(siz...]
  transfers between devices with their start and end apart: 22 -> 21, of which waited for: 13 -> 9; matrix products, arithmetic and copies ran while one was open for 4% -> 4% of each run, Pallas kernels for 5% -> 10%
where the time goes in v6:
time: 54.6 us; the launch traced here: 54.3 us
  starting transfers between devices  21.5 us (39%)
  waiting for transfers between devices  19.1 us (35%)
  Pallas kernels  8.74 us (16%)
  local copies, waits for them, and re-layouts  1.5 us (3%)
  other arithmetic  1.19 us (2%)
  matrix products  1.15 us (2%)
  between operations  1.13 us (2%)
    ppermute x7, waiting for transfers between devices, along_ring(): return lax.ppermute(block, 'blk', route)  11.9 us
    ppermute x7, starting transfers between devices, along_ring(): return lax.ppermute(block, 'blk', route)  8.36 us
    ppermute x3, starting transfers between devices, across(): return lax.ppermute(block, ('blk', 'rep'), route)  5.91 us
    ppermute x3, waiting for transfers between devices, across(): return lax.ppermute(block, ('blk', 'rep'), route)  5.42 us
    pallas_call x3, Pallas kernels, add_slabs(): pl.pallas_call(functools.partial(adding_kernel, plan, first_slab, len(sla...  5.37 us
    ppermute x3, starting transfers between devices, along_rep(): lax.ppermute(block, 'rep', [(i, (i + distance) % size) for i in range(siz...  3.76 us
    ppermute x8, starting transfers between devices, across_cores(): return lax.ppermute(block, 'blk', route)  3.48 us
    ppermute x8, waiting for transfers between devices, across_cores(): return lax.ppermute(block, 'blk', route)  1.79 us
  transfers between devices with their start and end apart: 21, of which 9 were waited for; matrix products, arithmetic and copies ran while one was open for 4% of the time, Pallas kernels for 10%

profile of v6, /device:TPU:0, one launch (start us, length us, event | category | flops | bytes accessed | tf_op | source)
XLA Modules:
  0.0 54.3 jit_solution(13800071068955868463)
XLA Ops:
  0.6 0.0 copy-start
  0.7 1.5 %scale.1.refs_4_ = bf16[1024,128]{1,0:T(8,128)(2,1)S(1)} custom-call(s32[8,128]{1,0:T(8,128)} %bitcast.68, bf16[1024,256]{1,0:T(8,128)(2,1)} %gradient_hbm.1), custom_call_target="tpu_custom_call" | custom-call | tf_op jit(solution)/shard_map/scale/pallas_call | solution.py:208
  2.1 0.0 copy-start.4
  2.1 3.0 %collective-permute-start.10 = (bf16[1024,128]{1,0:T(8,128)(2,1)S(1)}, bf16[1024,128]{1,0:T(8,128)(2,1)S(1)}, u32[]{:S(2)}, u32[]{:S(2)}) collective-permute-start(bf16[1024,128]{1,0:T(8,128)(2,1)S(1)} %scale.1.refs_4_), channel_id=1, source_target_pairs={{0,4},{2,6},{8,0},{10,2},{16,8},{18,10},{24,16},{26,18},{28,24},{3... | collective-permute-start | bytes 786440 | tf_op jit(solution)/shard_map/ppermute | solution.py:35
  5.1 0.2 collective-permute-start.6
  5.3 0.7 %copy-done.5 = s32[1,8]{1,0:T(1,128)S(1)} copy-done((s32[1,8]{1,0:T(1,128)S(1)}, s32[1,8]{1,0:T(1,128)}, u32[]{:S(2)}) %copy-start.5) | copy-done | bytes 56
  6.0 0.1 copy.13
  6.0 0.1 reshape_squeeze.6
  6.1 0.1 pad_add_fusion
  6.2 0.1 dynamic_slice.15
  6.3 0.2 payload.1
  6.5 2.0 %collective-permute-start.1 = (bf16[1152,128]{1,0:T(8,128)(2,1)S(1)}, bf16[1152,128]{1,0:T(8,128)(2,1)S(1)}, u32[]{:S(2)}, u32[]{:S(2)}) collective-permute-start(bf16[1152,128]{1,0:T(8,128)(2,1)S(1)} %get-tuple-element.19.refs_0_), channel_id=1, source_target_pairs={{0,1},{1,0},{2,3},{3,2},{4,5},{5,4},{6,7},{7,6},{8,9},{9,8},{10,11... | collective-permute-start | bytes 884744 | tf_op jit(solution)/shard_map/ppermute | solution.py:63
  8.4 0.1 collective-permute-start
  8.5 0.2 collective-permute-start.3
  8.7 4.2 %collective-permute-done.6.refs_5_ = bf16[1024,128]{1,0:T(8,128)(2,1)S(1)} collective-permute-done((bf16[1024,128]{1,0:T(8,128)(2,1)S(1)}, bf16[1024,128]{1,0:T(8,128)(2,1)S(1)}, u32[]{:S(2)}, u32[]{:S(2)}) %collective-permute-start.6) | collective-permute-done | bytes 262176 | tf_op jit(solution)/shard_map/ppermute | solution.py:35
  12.9 0.4 collective-permute-start.7
  13.3 0.1 reshape.58
  13.6 0.0 collective-permute-done.refs_2_
  13.6 0.1 collective-permute-start.4
  13.7 0.0 collective-permute-done.10.refs_6_
  13.7 1.6 %collective-permute-start.11 = (bf16[1024,128]{1,0:T(8,128)(2,1)S(1)}, bf16[1024,128]{1,0:T(8,128)(2,1)}, u32[]{:S(2)}, u32[]{:S(2)}) collective-permute-start(bf16[1024,128]{1,0:T(8,128)(2,1)S(1)} %collective-permute-done.10.refs_6_), channel_id=1, source_target_pairs={{0,4},{2,6},{8,0},{10,2},{16,8},{18,10},{24,16},{26,18},{28,24},{3... | collective-permute-start | bytes 786440 | tf_op jit(solution)/shard_map/ppermute | solution.py:35
  15.4 4.4 %collective-permute-done.7.refs_4_ = bf16[1024,128]{1,0:T(8,128)(2,1)S(1)} collective-permute-done((bf16[1024,128]{1,0:T(8,128)(2,1)S(1)}, bf16[1024,128]{1,0:T(8,128)(2,1)S(1)}, u32[]{:S(2)}, u32[]{:S(2)}) %collective-permute-start.7) | collective-permute-done | bytes 262176 | tf_op jit(solution)/shard_map/ppermute | solution.py:35
  19.8 0.7 %collective-permute-start.8 = (bf16[1024,128]{1,0:T(8,128)(2,1)S(1)}, bf16[1024,128]{1,0:T(8,128)(2,1)S(1)}, u32[]{:S(2)}, u32[]{:S(2)}) collective-permute-start(bf16[1024,128]{1,0:T(8,128)(2,1)S(1)} %collective-permute-done.7.refs_4_), channel_id=1, source_target_pairs={{0,8},{2,10},{8,16},{10,18},{16,24},{18,26},{24,28},{26,30},{28,20... | collective-permute-start | bytes 786440 | tf_op jit(solution)/shard_map/ppermute | solution.py:35
  20.5 0.1 reshape.60
  20.6 0.0 collective-permute-done.3.refs_5_
  20.6 0.0 collective-permute-start.5
  20.6 0.0 collective-permute-done.1.refs_1_
  20.7 0.6 %collective-permute-start.2 = (bf16[576,128]{1,0:T(8,128)(2,1)S(1)}, bf16[576,128]{1,0:T(8,128)(2,1)S(1)}, u32[]{:S(2)}, u32[]{:S(2)}) collective-permute-start(bf16[576,128]{1,0:T(8,128)(2,1)S(1)} %get-tuple-element.32), channel_id=1, source_target_pairs={{0,2},{2,0},{4,6},{6,4},{8,10},{10,8},{12,14},{14,12},{16,18},{18,... | collective-permute-start | bytes 442376 | tf_op jit(solution)/shard_map/ppermute | solution.py:53
  21.2 1.4 %collective-permute-done.11.refs_5_ = bf16[1024,128]{1,0:T(8,128)(2,1)} collective-permute-done((bf16[1024,128]{1,0:T(8,128)(2,1)S(1)}, bf16[1024,128]{1,0:T(8,128)(2,1)}, u32[]{:S(2)}, u32[]{:S(2)}) %collective-permute-start.11) | collective-permute-done | bytes 262176 | tf_op jit(solution)/shard_map/ppermute | solution.py:35
  22.6 1.6 %collective-permute-start.12 = (bf16[1024,128]{1,0:T(8,128)(2,1)}, bf16[1024,128]{1,0:T(8,128)(2,1)}, u32[]{:S(2)}, u32[]{:S(2)}) collective-permute-start(bf16[1024,128]{1,0:T(8,128)(2,1)} %collective-permute-done.11.refs_5_), channel_id=1, source_target_pairs={{0,4},{2,6},{8,0},{10,2},{16,8},{18,10},{24,16},{26,18},{28,24},{3... | collective-permute-start | bytes 786440 | tf_op jit(solution)/shard_map/ppermute | solution.py:35
  24.2 1.9 %collective-permute-done.8.refs_4_ = bf16[1024,128]{1,0:T(8,128)(2,1)S(1)} collective-permute-done((bf16[1024,128]{1,0:T(8,128)(2,1)S(1)}, bf16[1024,128]{1,0:T(8,128)(2,1)S(1)}, u32[]{:S(2)}, u32[]{:S(2)}) %collective-permute-start.8) | collective-permute-done | bytes 262176 | tf_op jit(solution)/shard_map/ppermute | solution.py:35
  26.1 0.8 %collective-permute-start.9 = (bf16[1024,128]{1,0:T(8,128)(2,1)S(1)}, bf16[1024,128]{1,0:T(8,128)(2,1)}, u32[]{:S(2)}, u32[]{:S(2)}) collective-permute-start(bf16[1024,128]{1,0:T(8,128)(2,1)S(1)} %collective-permute-done.8.refs_4_), channel_id=1, source_target_pairs={{0,8},{2,10},{8,16},{10,18},{16,24},{18,26},{24,28},{26,30},{28,20... | collective-permute-start | bytes 786440 | tf_op jit(solution)/shard_map/ppermute | solution.py:35
  26.9 0.1 reshape.62
  27.0 0.0 collective-permute-done.2.refs_3_
  27.0 0.1 reshape.64
  27.1 0.1 concatenate.10.table_ref
  27.3 1.6 %add_slabs.3 = (f32[1024,128]{1,0:T(8,128)S(1)}, f32[1024,128]{1,0:T(8,128)S(1)}) custom-call(s32[306]{0:T(512)S(1)} %concatenate.10.table_ref, bf16[1152,128]{1,0:T(8,128)(2,1)S(1)} %get-tuple-element.19.refs_0_, bf16[1152,128]{1,0:T(8,128)(2,1)S(1)} %collective-permute-done.1.refs_1_, bf16[576,128]{1,0:T(8,128)(2,1)S(1)} %collective-permute-done.refs_2_, ...), custom_call_target="tpu_custom_call" | custom-call | flops 1 | bytes 1 | tf_op jit(solution)/shard_map/add_slabs/pallas_call | solution.py:285
  28.9 1.9 %add_slabs.4 = (f32[1024,128]{1,0:T(8,128)S(1)}, f32[1024,128]{1,0:T(8,128)S(1)}) custom-call(s32[306]{0:T(512)S(1)} %concatenate.10.table_ref, bf16[1152,128]{1,0:T(8,128)(2,1)S(1)} %get-tuple-element.19.refs_0_, bf16[1152,128]{1,0:T(8,128)(2,1)S(1)} %collective-permute-done.1.refs_1_, ...), custom_call_target="tpu_custom_call", output_to_operand_aliasing={{0}: (7, {}), {1}: (8, {})} | custom-call | flops 1 | bytes 1 | tf_op jit(solution)/shard_map/add_slabs/pallas_call | solution.py:285
  30.8 0.0 collective-permute-done.12.refs_5_
  30.8 1.9 %add_slabs.5 = (f32[1024,128]{1,0:T(8,128)S(1)}, f32[1024,128]{1,0:T(8,128)S(1)}) custom-call(s32[306]{0:T(512)S(1)} %concatenate.10.table_ref, bf16[1152,128]{1,0:T(8,128)(2,1)S(1)} %get-tuple-element.19.refs_0_, bf16[1152,128]{1,0:T(8,128)(2,1)S(1)} %collective-permute-done.1.refs_1_, ...), custom_call_target="tpu_custom_call", output_to_operand_aliasing={{0}: (7, {}), {1}: (8, {})} | custom-call | flops 1 | bytes 1 | tf_op jit(solution)/shard_map/add_slabs/pallas_call | solution.py:285
  32.7 0.0 collective-permute-done.4.refs_6_
  32.7 0.0 collective-permute-done.5.refs_7_
  32.7 0.0 collective-permute-done.9.refs_8_
  32.7 1.8 %last_slab.1 = (f32[1024,128]{1,0:T(8,128)S(1)}, f32[1024,128]{1,0:T(8,128)S(1)}, bf16[256,128]{1,0:T(8,128)(2,1)S(1)}) custom-call(s32[306]{0:T(512)S(1)} %concatenate.10.table_ref, bf16[1152,128]{1,0:T(8,128)(2,1)S(1)} %get-tuple-element.19.refs_0_, bf16[1152,128]{1,0:T(8,128)(2,1)S(1)} %collective-permute-done.1.refs_1_, ...), custom_call_target="tpu_custom_call" | custom-call | flops 1 | bytes 1 | tf_op jit(solution)/shard_map/last_slab/pallas_call | solution.py:300
  34.5 0.1 collective-permute-start.13
  34.5 0.5 collective-permute-start.17
  35.0 0.7 %collective-permute-done.13 = bf16[256,128]{1,0:T(8,128)(2,1)S(1)} collective-permute-done((bf16[256,128]{1,0:T(8,128)(2,1)S(1)}, bf16[256,128]{1,0:T(8,128)(2,1)S(1)}, u32[]{:S(2)}, u32[]{:S(2)}) %collective-permute-start.13) | collective-permute-done | bytes 65568 | tf_op jit(solution)/shard_map/ppermute | solution.py:53
  35.8 2.7 %collective-permute-start.14 = (bf16[256,128]{1,0:T(8,128)(2,1)S(1)}, bf16[256,128]{1,0:T(8,128)(2,1)S(1)}, u32[]{:S(2)}, u32[]{:S(2)}) collective-permute-start(bf16[256,128]{1,0:T(8,128)(2,1)S(1)} %add_convert_fusion), channel_id=1, source_target_pairs={{0,12},{1,13},{2,10},{3,11},{4,8},{5,9},{6,14},{7,15},{8,4},{9,5},... | collective-permute-start | bytes 196616 | tf_op jit(solution)/shard_map/ppermute | solution.py:46
  38.5 0.7 %collective-permute-start.15 = (bf16[256,128]{1,0:T(8,128)(2,1)S(1)}, bf16[256,128]{1,0:T(8,128)(2,1)S(1)}, u32[]{:S(2)}, u32[]{:S(2)}) collective-permute-start(bf16[256,128]{1,0:T(8,128)(2,1)S(1)} %add_convert_fusion), channel_id=1, source_target_pairs={{2,6},{3,7},{6,2},{7,3},{10,14},{11,15},{14,10},{15,11},{18,22},{1... | collective-permute-start | bytes 196616 | tf_op jit(solution)/shard_map/ppermute | solution.py:46
  39.1 1.9 %collective-permute-done.14 = bf16[256,128]{1,0:T(8,128)(2,1)S(1)} collective-permute-done((bf16[256,128]{1,0:T(8,128)(2,1)S(1)}, bf16[256,128]{1,0:T(8,128)(2,1)S(1)}, u32[]{:S(2)}, u32[]{:S(2)}) %collective-permute-start.14) | collective-permute-done | bytes 65568 | tf_op jit(solution)/shard_map/ppermute | solution.py:46
  41.1 0.0 collective-permute-done.15
  41.1 1.4 %collective-permute-start.16 = (f32[256,128]{1,0:T(8,128)S(1)}, f32[256,128]{1,0:T(8,128)S(1)}, u32[]{:S(2)}, u32[]{:S(2)}) collective-permute-start(f32[256,128]{1,0:T(8,128)S(1)} %convert_add_fusion.1), channel_id=1, source_target_pairs={{0,2},{2,0},{4,6},{6,4},{8,10},{10,8},{12,14},{14,12},{16,18},{18,... | collective-permute-start | bytes 393224 | tf_op jit(solution)/shard_map/ppermute | solution.py:53
  42.5 1.0 %collective-permute-done.16 = f32[256,128]{1,0:T(8,128)S(1)} collective-permute-done((f32[256,128]{1,0:T(8,128)S(1)}, f32[256,128]{1,0:T(8,128)S(1)}, u32[]{:S(2)}, u32[]{:S(2)}) %collective-permute-start.16) | collective-permute-done | bytes 131104 | tf_op jit(solution)/shard_map/ppermute | solution.py:53
  43.5 0.0 collective-permute-done.17
  43.5 0.2 multiply_convert_fusion
  43.8 1.6 %collective-permute-start.18 = (bf16[768,128]{1,0:T(8,128)(2,1)S(1)}, bf16[768,128]{1,0:T(8,128)(2,1)S(1)}, u32[]{:S(2)}, u32[]{:S(2)}) collective-permute-start(bf16[768,128]{1,0:T(8,128)(2,1)S(1)} %pad_maximum_fusion), channel_id=1, source_target_pairs={{0,1},{1,0},{2,3},{3,2},{4,5},{5,4},{6,7},{7,6},{8,9},{9,8},{10,11... | collective-permute-start | bytes 589832 | tf_op jit(solution)/shard_map/ppermute | solution.py:63
  45.4 2.6 %collective-permute-start.19 = (bf16[256,128]{1,0:T(8,128)(2,1)S(1)}, bf16[256,128]{1,0:T(8,128)(2,1)S(1)}, u32[]{:S(2)}, u32[]{:S(2)}) collective-permute-start(bf16[256,128]{1,0:T(8,128)(2,1)S(1)} %add.371), channel_id=1, source_target_pairs={{0,16},{1,17},{2,19},{3,18},{4,20},{5,21},{6,23},{7,22},{8,24},{9,... | collective-permute-start | bytes 196616 | tf_op jit(solution)/shard_map/ppermute | solution.py:46
  48.0 0.2 fusion.3
  48.2 3.5 %collective-permute-done.19 = bf16[256,128]{1,0:T(8,128)(2,1)S(1)} collective-permute-done((bf16[256,128]{1,0:T(8,128)(2,1)S(1)}, bf16[256,128]{1,0:T(8,128)(2,1)S(1)}, u32[]{:S(2)}, u32[]{:S(2)}) %collective-permute-start.19) | collective-permute-done | bytes 65568 | tf_op jit(solution)/shard_map/ppermute | solution.py:46
  51.7 0.0 collective-permute-done.18
  51.8 0.8 %collective-permute-start.20 = (f32[1,256,128]{2,1,0:T(8,128)S(1)}, f32[1,256,128]{2,1,0:T(8,128)S(1)}, u32[]{:S(2)}, u32[]{:S(2)}) collective-permute-start(f32[1,256,128]{2,1,0:T(8,128)S(1)} %fusion.5), channel_id=1, source_target_pairs={{0,2},{2,0},{4,6},{6,4},{8,10},{10,8},{12,14},{14,12},{16,18},{18,... | collective-permute-start | bytes 393224 | tf_op jit(solution)/shard_map/ppermute | solution.py:53
  52.5 0.9 %fusion = bf16[512,256]{1,0:T(8,128)(2,1)} fusion(f32[512,256]{1,0:T(8,128)S(1)} %fusion.3, bf16[768,128]{1,0:T(8,128)(2,1)S(1)} %collective-permute-done.18, bf16[256,256]{1,0:T(8,128)(2,1)S(1)} %copy-done, s32[]{:T(128)S(6)} %select_n.496), kind=kOutput, calls=%fused_computation.1 | convolution fusion | flops 33816576 | bytes 983044 | tf_op jit(solution)/shard_map/dot_general | solution.py:339
  53.5 0.1 collective-permute-done.20
  53.6 0.7 %broadcast_multiply_fusion = f32[256,256]{1,0:T(8,128)} fusion(f32[256,256]{1,0:T(8,128)S(1)} %bitcast_dynamic-update-slice_fusion), kind=kLoop, calls=%fused_computation.8 | loop fusion | flops 65536 | bytes 524288 | tf_op jit(solution)/shard_map/mul | solution.py:352
  (34 shorter events, 0.3 us)
Async XLA Ops:
  0.6 47.4 %copy-start = (bf16[256,256]{1,0:T(8,128)(2,1)S(1)}, bf16[256,256]{1,0:T(8,128)(2,1)}, u32[]{:S(2)}) copy-start(bf16[256,256]{1,0:T(8,128)(2,1)} %param.9) | copy-start | bytes 393220
  0.6 5.6 %copy-start.1 = (s32[1,8,8,16,128]{4,3,2,1,0:T(8,128)S(1)}, s32[1,8,8,16,128]{4,3,2,1,0:T(8,128)}, u32[]{:S(2)}) copy-start(s32[1,8,8,16,128]{4,3,2,1,0:T(8,128)} %param.10) | copy-start | bytes 1572868
  0.7 4.6 %copy-start.3 = (s32[1024]{0:T(1024)S(1)}, s32[1024]{0:T(1024)}, u32[]{:S(2)}) copy-start(s32[1024]{0:T(1024)} %param.13) | copy-start | bytes 12292
  0.7 5.6 %copy-start.2 = (bf16[512,256]{1,0:T(8,128)(2,1)S(1)}, bf16[512,256]{1,0:T(8,128)(2,1)}, u32[]{:S(2)}) copy-start(bf16[512,256]{1,0:T(8,128)(2,1)} %features_ref) | copy-start | bytes 786436
  2.1 3.9 %copy-start.4 = (s32[1,8,2,8]{3,2,1,0:T(2,128)S(1)}, s32[1,8,2,8]{3,2,1,0:T(2,128)}, u32[]{:S(2)}) copy-start(s32[1,8,2,8]{3,2,1,0:T(2,128)} %param.11) | copy-start | bytes 1540
  2.1 11.6 %collective-permute-start.10 = (bf16[1024,128]{1,0:T(8,128)(2,1)S(1)}, bf16[1024,128]{1,0:T(8,128)(2,1)S(1)}, u32[]{:S(2)}, u32[]{:S(2)}) collective-permute-start(bf16[1024,128]{1,0:T(8,128)(2,1)S(1)} %scale.1.refs_4_), channel_id=1, source_target_pairs={{0,4},{2,6},{8,0},{10,2},{16,8},{18,10},{24,16},{26,18},{28,24},{3... | collective-permute-start | bytes 786440 | tf_op jit(solution)/shard_map/ppermute | solution.py:35
  5.1 7.8 %collective-permute-start.6 = (bf16[1024,128]{1,0:T(8,128)(2,1)S(1)}, bf16[1024,128]{1,0:T(8,128)(2,1)S(1)}, u32[]{:S(2)}, u32[]{:S(2)}) collective-permute-start(bf16[1024,128]{1,0:T(8,128)(2,1)S(1)} %scale.1.refs_4_), channel_id=1, source_target_pairs={{0,8},{2,10},{8,16},{10,18},{16,24},{18,26},{24,28},{26,30},{28,20... | collective-permute-start | bytes 786440 | tf_op jit(solution)/shard_map/ppermute | solution.py:35
  5.3 0.7 %copy-start.5 = (s32[1,8]{1,0:T(1,128)S(1)}, s32[1,8]{1,0:T(1,128)}, u32[]{:S(2)}) copy-start(s32[1,8]{1,0:T(1,128)} %param.12) | copy-start | bytes 100
  6.5 14.2 %collective-permute-start.1 = (bf16[1152,128]{1,0:T(8,128)(2,1)S(1)}, bf16[1152,128]{1,0:T(8,128)(2,1)S(1)}, u32[]{:S(2)}, u32[]{:S(2)}) collective-permute-start(bf16[1152,128]{1,0:T(8,128)(2,1)S(1)} %get-tuple-element.19.refs_0_), channel_id=1, source_target_pairs={{0,1},{1,0},{2,3},{3,2},{4,5},{5,4},{6,7},{7,6},{8,9},{9,8},{10,11... | collective-permute-start | bytes 884744 | tf_op jit(solution)/shard_map/ppermute | solution.py:63
  8.4 5.2 %collective-permute-start = (bf16[576,128]{1,0:T(8,128)(2,1)S(1)}, bf16[576,128]{1,0:T(8,128)(2,1)S(1)}, u32[]{:S(2)}, u32[]{:S(2)}) collective-permute-start(bf16[576,128]{1,0:T(8,128)(2,1)S(1)} %get-tuple-element.34), channel_id=1, source_target_pairs={{0,2},{2,0},{4,6},{6,4},{8,10},{10,8},{12,14},{14,12},{16,18},{18,... | collective-permute-start | bytes 442376 | tf_op jit(solution)/shard_map/ppermute | solution.py:53
  8.5 12.1 %collective-permute-start.3 = (bf16[256,512]{1,0:T(8,128)(2,1)S(1)}, bf16[256,512]{1,0:T(8,128)(2,1)S(1)}, u32[]{:S(2)}, u32[]{:S(2)}) collective-permute-start(bf16[256,512]{1,0:T(8,128)(2,1)S(1)} %get-tuple-element.20.refs_4_), channel_id=1, source_target_pairs={{0,1},{1,0},{2,3},{3,2},{4,5},{5,4},{6,7},{7,6},{8,9},{9,8},{10,11... | collective-permute-start | bytes 786440 | tf_op jit(solution)/shard_map/ppermute | solution.py:63
  12.9 6.9 %collective-permute-start.7 = (bf16[1024,128]{1,0:T(8,128)(2,1)S(1)}, bf16[1024,128]{1,0:T(8,128)(2,1)S(1)}, u32[]{:S(2)}, u32[]{:S(2)}) collective-permute-start(bf16[1024,128]{1,0:T(8,128)(2,1)S(1)} %collective-permute-done.6.refs_5_), channel_id=1, source_target_pairs={{0,8},{2,10},{8,16},{10,18},{16,24},{18,26},{24,28},{26,30},{28,20... | collective-permute-start | bytes 786440 | tf_op jit(solution)/shard_map/ppermute | solution.py:35
  13.6 19.1 %collective-permute-start.4 = (bf16[256,512]{1,0:T(8,128)(2,1)S(1)}, bf16[256,512]{1,0:T(8,128)(2,1)S(1)}, u32[]{:S(2)}, u32[]{:S(2)}) collective-permute-start(bf16[256,512]{1,0:T(8,128)(2,1)S(1)} %get-tuple-element.20.refs_4_), channel_id=1, source_target_pairs={{0,2},{2,0},{4,6},{6,4},{8,10},{10,8},{12,14},{14,12},{16,18},{18,... | collective-permute-start | bytes 786440 | tf_op jit(solution)/shard_map/ppermute | solution.py:53
  13.7 8.8 %collective-permute-start.11 = (bf16[1024,128]{1,0:T(8,128)(2,1)S(1)}, bf16[1024,128]{1,0:T(8,128)(2,1)}, u32[]{:S(2)}, u32[]{:S(2)}) collective-permute-start(bf16[1024,128]{1,0:T(8,128)(2,1)S(1)} %collective-permute-done.10.refs_6_), channel_id=1, source_target_pairs={{0,4},{2,6},{8,0},{10,2},{16,8},{18,10},{24,16},{26,18},{28,24},{3... | collective-permute-start | bytes 786440 | tf_op jit(solution)/shard_map/ppermute | solution.py:35
  19.8 6.4 %collective-permute-start.8 = (bf16[1024,128]{1,0:T(8,128)(2,1)S(1)}, bf16[1024,128]{1,0:T(8,128)(2,1)S(1)}, u32[]{:S(2)}, u32[]{:S(2)}) collective-permute-start(bf16[1024,128]{1,0:T(8,128)(2,1)S(1)} %collective-permute-done.7.refs_4_), channel_id=1, source_target_pairs={{0,8},{2,10},{8,16},{10,18},{16,24},{18,26},{24,28},{26,30},{28,20... | collective-permute-start | bytes 786440 | tf_op jit(solution)/shard_map/ppermute | solution.py:35
  20.6 12.1 %collective-permute-start.5 = (bf16[256,512]{1,0:T(8,128)(2,1)S(1)}, bf16[256,512]{1,0:T(8,128)(2,1)S(1)}, u32[]{:S(2)}, u32[]{:S(2)}) collective-permute-start(bf16[256,512]{1,0:T(8,128)(2,1)S(1)} %collective-permute-done.3.refs_5_), channel_id=1, source_target_pairs={{0,2},{2,0},{4,6},{6,4},{8,10},{10,8},{12,14},{14,12},{16,18},{18,... | collective-permute-start | bytes 786440 | tf_op jit(solution)/shard_map/ppermute | solution.py:53
  20.7 6.4 %collective-permute-start.2 = (bf16[576,128]{1,0:T(8,128)(2,1)S(1)}, bf16[576,128]{1,0:T(8,128)(2,1)S(1)}, u32[]{:S(2)}, u32[]{:S(2)}) collective-permute-start(bf16[576,128]{1,0:T(8,128)(2,1)S(1)} %get-tuple-element.32), channel_id=1, source_target_pairs={{0,2},{2,0},{4,6},{6,4},{8,10},{10,8},{12,14},{14,12},{16,18},{18,... | collective-permute-start | bytes 442376 | tf_op jit(solution)/shard_map/ppermute | solution.py:53
  22.6 8.2 %collective-permute-start.12 = (bf16[1024,128]{1,0:T(8,128)(2,1)}, bf16[1024,128]{1,0:T(8,128)(2,1)}, u32[]{:S(2)}, u32[]{:S(2)}) collective-permute-start(bf16[1024,128]{1,0:T(8,128)(2,1)} %collective-permute-done.11.refs_5_), channel_id=1, source_target_pairs={{0,4},{2,6},{8,0},{10,2},{16,8},{18,10},{24,16},{26,18},{28,24},{3... | collective-permute-start | bytes 786440 | tf_op jit(solution)/shard_map/ppermute | solution.py:35
  26.1 6.6 %collective-permute-start.9 = (bf16[1024,128]{1,0:T(8,128)(2,1)S(1)}, bf16[1024,128]{1,0:T(8,128)(2,1)}, u32[]{:S(2)}, u32[]{:S(2)}) collective-permute-start(bf16[1024,128]{1,0:T(8,128)(2,1)S(1)} %collective-permute-done.8.refs_4_), channel_id=1, source_target_pairs={{0,8},{2,10},{8,16},{10,18},{16,24},{18,26},{24,28},{26,30},{28,20... | collective-permute-start | bytes 786440 | tf_op jit(solution)/shard_map/ppermute | solution.py:35
  34.5 1.3 %collective-permute-start.13 = (bf16[256,128]{1,0:T(8,128)(2,1)S(1)}, bf16[256,128]{1,0:T(8,128)(2,1)S(1)}, u32[]{:S(2)}, u32[]{:S(2)}) collective-permute-start(bf16[256,128]{1,0:T(8,128)(2,1)S(1)} %get-tuple-element.27), channel_id=1, source_target_pairs={{0,2},{2,0},{4,6},{6,4},{8,10},{10,8},{12,14},{14,12},{16,18},{18,... | collective-permute-start | bytes 196616 | tf_op jit(solution)/shard_map/ppermute | solution.py:53
  34.5 9.0 %collective-permute-start.17 = (f32[1024,128]{1,0:T(8,128)S(1)}, f32[1024,128]{1,0:T(8,128)S(1)}, u32[]{:S(2)}, u32[]{:S(2)}) collective-permute-start(f32[1024,128]{1,0:T(8,128)S(1)} %get-tuple-element.29), channel_id=1, source_target_pairs={{0,2},{2,0},{4,6},{6,4},{8,10},{10,8},{12,14},{14,12},{16,18},{18,... | collective-permute-start | bytes 1572872 | tf_op jit(solution)/shard_map/ppermute | solution.py:53
  35.8 5.3 %collective-permute-start.14 = (bf16[256,128]{1,0:T(8,128)(2,1)S(1)}, bf16[256,128]{1,0:T(8,128)(2,1)S(1)}, u32[]{:S(2)}, u32[]{:S(2)}) collective-permute-start(bf16[256,128]{1,0:T(8,128)(2,1)S(1)} %add_convert_fusion), channel_id=1, source_target_pairs={{0,12},{1,13},{2,10},{3,11},{4,8},{5,9},{6,14},{7,15},{8,4},{9,5},... | collective-permute-start | bytes 196616 | tf_op jit(solution)/shard_map/ppermute | solution.py:46
  38.5 2.6 %collective-permute-start.15 = (bf16[256,128]{1,0:T(8,128)(2,1)S(1)}, bf16[256,128]{1,0:T(8,128)(2,1)S(1)}, u32[]{:S(2)}, u32[]{:S(2)}) collective-permute-start(bf16[256,128]{1,0:T(8,128)(2,1)S(1)} %add_convert_fusion), channel_id=1, source_target_pairs={{2,6},{3,7},{6,2},{7,3},{10,14},{11,15},{14,10},{15,11},{18,22},{1... | collective-permute-start | bytes 196616 | tf_op jit(solution)/shard_map/ppermute | solution.py:46
  41.1 2.4 %collective-permute-start.16 = (f32[256,128]{1,0:T(8,128)S(1)}, f32[256,128]{1,0:T(8,128)S(1)}, u32[]{:S(2)}, u32[]{:S(2)}) collective-permute-start(f32[256,128]{1,0:T(8,128)S(1)} %convert_add_fusion.1), channel_id=1, source_target_pairs={{0,2},{2,0},{4,6},{6,4},{8,10},{10,8},{12,14},{14,12},{16,18},{18,... | collective-permute-start | bytes 393224 | tf_op jit(solution)/shard_map/ppermute | solution.py:53
  43.8 7.9 %collective-permute-start.18 = (bf16[768,128]{1,0:T(8,128)(2,1)S(1)}, bf16[768,128]{1,0:T(8,128)(2,1)S(1)}, u32[]{:S(2)}, u32[]{:S(2)}) collective-permute-start(bf16[768,128]{1,0:T(8,128)(2,1)S(1)} %pad_maximum_fusion), channel_id=1, source_target_pairs={{0,1},{1,0},{2,3},{3,2},{4,5},{5,4},{6,7},{7,6},{8,9},{9,8},{10,11... | collective-permute-start | bytes 589832 | tf_op jit(solution)/shard_map/ppermute | solution.py:63
  45.4 6.3 %collective-permute-start.19 = (bf16[256,128]{1,0:T(8,128)(2,1)S(1)}, bf16[256,128]{1,0:T(8,128)(2,1)S(1)}, u32[]{:S(2)}, u32[]{:S(2)}) collective-permute-start(bf16[256,128]{1,0:T(8,128)(2,1)S(1)} %add.371), channel_id=1, source_target_pairs={{0,16},{1,17},{2,19},{3,18},{4,20},{5,21},{6,23},{7,22},{8,24},{9,... | collective-permute-start | bytes 196616 | tf_op jit(solution)/shard_map/ppermute | solution.py:46
  51.8 1.8 %collective-permute-start.20 = (f32[1,256,128]{2,1,0:T(8,128)S(1)}, f32[1,256,128]{2,1,0:T(8,128)S(1)}, u32[]{:S(2)}, u32[]{:S(2)}) collective-permute-start(f32[1,256,128]{2,1,0:T(8,128)S(1)} %fusion.5), channel_id=1, source_target_pairs={{0,2},{2,0},{4,6},{6,4},{8,10},{10,8},{12,14},{14,12},{16,18},{18,... | collective-permute-start | bytes 393224 | tf_op jit(solution)/shard_map/ppermute | solution.py:53

commit v7 on v6

--- a/solution.py
+++ b/solution.py
@@ -115,11 +115,12 @@
 def last_kernel(plan, last_slab, table_ref, *refs):
     own_pieces, other_pieces = refs[: plan.reps], refs[plan.reps : 2 * plan.reps]
     own_features, other_features = refs[2 * plan.reps : 3 * plan.reps], refs[3 * plan.reps : 4 * plan.reps]
-    slab_ref, own_in, other_in, own_ref, other_ref, term_ref = refs[4 * plan.reps :]
+    slab_ref, own_in, other_in, own_ref, other_ref, term_ref, total_ref = refs[4 * plan.reps :]
     own_ref[...] = own_in[...]
-    other_ref[...] = other_in[...]
-    sums = (own_ref, other_ref)
+    total_ref[...] = other_in[...]
+    sums = (own_ref, total_ref)
     add_pairs(plan, table_ref, last_slab, own_pieces, other_pieces, [slab_ref], sums)
+    other_ref[...] = total_ref[...].astype(other_ref.dtype)
     share = own_ref.shape[0] // plan.reps
     order_at = plan.facts_size + 4 * (last_slab + 1)
     term = jnp.zeros(term_ref.shape, jnp.float32)
@@ -244,8 +245,9 @@
         cost_estimate=COST,
         name="payload",
     )(facts, block_words[0].reshape(2 * half_steps, slot_total * 16, 128), features, share_root[None])
-    own_pieces = from_all_reps(pairs)
-    other_pieces = [across_cores(piece[words_rows:]) for piece in own_pieces]
+    both_pieces = from_all_reps(pairs)
+    other_pieces = [across_cores(piece[words_rows:]) for piece in both_pieces]
+    own_pieces = [piece[:words_rows] for piece in both_pieces]
     own_features = from_all_reps(turned)
     other_features = [across_cores(piece) for piece in own_features]
 
@@ -277,6 +279,7 @@
     del backward
 
     slab_shape = jax.ShapeDtypeStruct((slab_rows, share_width), jnp.float32)
+    sent_shape = jax.ShapeDtypeStruct((slab_rows, share_width), jnp.bfloat16)
     term_shape = jax.ShapeDtypeStruct((width, share_width), jnp.bfloat16)
     def add_slabs(first_slab, slabs, sums):
         operands = own_pieces + other_pieces + slabs
@@ -295,13 +298,14 @@
 
     early = len(slabs) - 4
     sums = add_slabs(0, slabs[:early], [])
-    for at in range(early, len(slabs), 2):
-        sums = add_slabs(at, slabs[at : at + 2], list(sums))
+    sums = add_slabs(early, slabs[early:-1], list(sums))
+    sums = add_slabs(len(slabs) - 1, slabs[-1:], list(sums))
     own_sums, other_sums, term = pl.pallas_call(
         functools.partial(last_kernel, plan, len(slabs)),
-        out_shape=(slab_shape, slab_shape, term_shape),
+        out_shape=(slab_shape, sent_shape, term_shape),
         in_specs=[SMEM] + [VMEM] * (4 * rep_size + 3),
         out_specs=(VMEM,) * 3,
+        scratch_shapes=[pltpu.VMEM((slab_rows, share_width), jnp.float32)],
         compiler_params=PARAMS,
         cost_estimate=COST,
         name="last_slab",
@@ -311,18 +315,18 @@
         return values.astype(jnp.float32)
 
     total = (wide(term) + wide(across_cores(term))).astype(jnp.bfloat16)
-    own_sums = own_sums + across_cores(other_sums)
+    own_sums = own_sums + wide(across_cores(other_sums))
     aggregated = (own_sums * inverse_root[:, None]).astype(jnp.bfloat16)
     row_bits = [1 << bit for bit in range(rows_of_chips.bit_length() - 1)]
     first_bit, last_bit = row_bits[0], row_bits[-1]
     one = across(total, (first_bit, 1, 0), (first_bit, 0, 0))
     two = across(total, None, (0, 1, 0))
     part = wide(one) + wide(jnp.where(core == 0, total, two))
+    part, aggregated = lax.optimization_barrier((part, aggregated))
     total = part + across_cores(part)
     for bit in row_bits[1:-1]:
         total = total.astype(jnp.bfloat16)
         total = wide(total) + wide(across(total, (bit, 0, 0), (bit, 0, 0)))
-    total, aggregated = lax.optimization_barrier((total, aggregated))
     total = total.astype(jnp.bfloat16)
     result = jnp.zeros((share_rows, width), jnp.float32)
     shares = []

time: 54.6 us -> 54.1 us (level)
  local copies, waits for them, and re-layouts: 1.5 us -> 2.48 us
  Pallas kernels: 8.74 us -> 8.01 us
  starting transfers between devices: 21.5 us -> 20.9 us
    ppermute x8, waiting for transfers between devices: 1.79 us -> 2.97 us  [across_cores(): return lax.ppermute(block, 'blk', route)]
    slice x2, local copies, waits for them, and re-layouts: 0.04 us -> 1.02 us  [per_device(): other_pieces = [across_cores(piece[words_rows:]) for piece in both_pieces]]
    ppermute x3, waiting for transfers between devices: 5.42 us -> 4.51 us  [across(): return lax.ppermute(block, ('blk', 'rep'), route)]
    ppermute x3, starting transfers between devices: 5.91 us -> 5.33 us  [across(): return lax.ppermute(block, ('blk', 'rep'), route)]
  transfers between devices with their start and end apart: 21 -> 21, of which waited for: 9 -> 11; matrix products, arithmetic and copies ran while one was open for 4% -> 6% of each run, Pallas kernels for 10% -> 10%
where the time goes in v7:
time: 54.1 us; the launch traced here: 53.9 us
  starting transfers between devices  20.9 us (39%)
  waiting for transfers between devices  19 us (35%)
  Pallas kernels  8.01 us (15%)
  local copies, waits for them, and re-layouts  2.48 us (5%)
  other arithmetic  1.19 us (2%)
  matrix products  1.15 us (2%)
  between operations  1.1 us (2%)
    ppermute x7, waiting for transfers between devices, along_ring(): return lax.ppermute(block, 'blk', route)  11.5 us
    ppermute x7, starting transfers between devices, along_ring(): return lax.ppermute(block, 'blk', route)  8.31 us
    ppermute x3, starting transfers between devices, across(): return lax.ppermute(block, ('blk', 'rep'), route)  5.33 us
    pallas_call x3, Pallas kernels, add_slabs(): pl.pallas_call(functools.partial(adding_kernel, plan, first_slab, len(sla...  5.04 us
    ppermute x3, waiting for transfers between devices, across(): return lax.ppermute(block, ('blk', 'rep'), route)  4.51 us
    ppermute x3, starting transfers between devices, along_rep(): lax.ppermute(block, 'rep', [(i, (i + distance) % size) for i in range(siz...  3.75 us
    ppermute x8, starting transfers between devices, across_cores(): return lax.ppermute(block, 'blk', route)  3.55 us
    ppermute x8, waiting for transfers between devices, across_cores(): return lax.ppermute(block, 'blk', route)  2.97 us
  transfers between devices with their start and end apart: 21, of which 11 were waited for; matrix products, arithmetic and copies ran while one was open for 6% of the time, Pallas kernels for 10%

profile of v7, /device:TPU:0, one launch (start us, length us, event | category | flops | bytes accessed | tf_op | source)
XLA Modules:
  0.0 53.9 jit_solution(4616860390337538860)
XLA Ops:
  0.6 0.0 copy-start
  0.7 1.5 %scale.1.refs_4_ = bf16[1024,128]{1,0:T(8,128)(2,1)S(1)} custom-call(s32[8,128]{1,0:T(8,128)} %bitcast.68, bf16[1024,256]{1,0:T(8,128)(2,1)} %gradient_hbm.1), custom_call_target="tpu_custom_call" | custom-call | tf_op jit(solution)/shard_map/scale/pallas_call | solution.py:209
  2.1 0.0 copy-start.4
  2.1 3.0 %collective-permute-start.10 = (bf16[1024,128]{1,0:T(8,128)(2,1)S(1)}, bf16[1024,128]{1,0:T(8,128)(2,1)S(1)}, u32[]{:S(2)}, u32[]{:S(2)}) collective-permute-start(bf16[1024,128]{1,0:T(8,128)(2,1)S(1)} %scale.1.refs_4_), channel_id=1, source_target_pairs={{0,4},{2,6},{8,0},{10,2},{16,8},{18,10},{24,16},{26,18},{28,24},{3... | collective-permute-start | bytes 786440 | tf_op jit(solution)/shard_map/ppermute | solution.py:35
  5.1 0.2 collective-permute-start.6
  5.3 0.7 %copy-done.5 = s32[1,8]{1,0:T(1,128)S(1)} copy-done((s32[1,8]{1,0:T(1,128)S(1)}, s32[1,8]{1,0:T(1,128)}, u32[]{:S(2)}) %copy-start.5) | copy-done | bytes 56
  6.0 0.1 copy.13
  6.0 0.1 reshape_squeeze.6
  6.1 0.1 pad_add_fusion
  6.2 0.1 dynamic_slice.15
  6.3 0.2 payload.1
  6.5 2.0 %collective-permute-start.1 = (bf16[1152,128]{1,0:T(8,128)(2,1)S(1)}, bf16[1152,128]{1,0:T(8,128)(2,1)}, u32[]{:S(2)}, u32[]{:S(2)}) collective-permute-start(bf16[1152,128]{1,0:T(8,128)(2,1)S(1)} %get-tuple-element.19), channel_id=1, source_target_pairs={{0,1},{1,0},{2,3},{3,2},{4,5},{5,4},{6,7},{7,6},{8,9},{9,8},{10,11... | collective-permute-start | bytes 884744 | tf_op jit(solution)/shard_map/ppermute | solution.py:63
  8.4 0.1 collective-permute-start
  8.5 0.2 collective-permute-start.3
  8.7 4.2 %collective-permute-done.6.refs_5_ = bf16[1024,128]{1,0:T(8,128)(2,1)S(1)} collective-permute-done((bf16[1024,128]{1,0:T(8,128)(2,1)S(1)}, bf16[1024,128]{1,0:T(8,128)(2,1)S(1)}, u32[]{:S(2)}, u32[]{:S(2)}) %collective-permute-start.6) | collective-permute-done | bytes 262176 | tf_op jit(solution)/shard_map/ppermute | solution.py:35
  12.9 0.4 collective-permute-start.7
  13.3 0.1 reshape.58
  13.6 0.0 collective-permute-done.refs_2_
  13.6 0.1 collective-permute-start.4
  13.7 0.0 collective-permute-done.10.refs_6_
  13.7 1.6 %collective-permute-start.11 = (bf16[1024,128]{1,0:T(8,128)(2,1)S(1)}, bf16[1024,128]{1,0:T(8,128)(2,1)}, u32[]{:S(2)}, u32[]{:S(2)}) collective-permute-start(bf16[1024,128]{1,0:T(8,128)(2,1)S(1)} %collective-permute-done.10.refs_6_), channel_id=1, source_target_pairs={{0,4},{2,6},{8,0},{10,2},{16,8},{18,10},{24,16},{26,18},{28,24},{3... | collective-permute-start | bytes 786440 | tf_op jit(solution)/shard_map/ppermute | solution.py:35
  15.4 4.5 %collective-permute-done.7.refs_4_ = bf16[1024,128]{1,0:T(8,128)(2,1)S(1)} collective-permute-done((bf16[1024,128]{1,0:T(8,128)(2,1)S(1)}, bf16[1024,128]{1,0:T(8,128)(2,1)S(1)}, u32[]{:S(2)}, u32[]{:S(2)}) %collective-permute-start.7) | collective-permute-done | bytes 262176 | tf_op jit(solution)/shard_map/ppermute | solution.py:35
  19.9 0.7 %collective-permute-start.8 = (bf16[1024,128]{1,0:T(8,128)(2,1)S(1)}, bf16[1024,128]{1,0:T(8,128)(2,1)}, u32[]{:S(2)}, u32[]{:S(2)}) collective-permute-start(bf16[1024,128]{1,0:T(8,128)(2,1)S(1)} %collective-permute-done.7.refs_4_), channel_id=1, source_target_pairs={{0,8},{2,10},{8,16},{10,18},{16,24},{18,26},{24,28},{26,30},{28,20... | collective-permute-start | bytes 786440 | tf_op jit(solution)/shard_map/ppermute | solution.py:35
  20.6 0.1 reshape.60
  20.7 0.0 collective-permute-done.3.refs_5_
  20.7 0.0 collective-permute-start.5
  20.7 0.0 collective-permute-done.1
  20.7 1.0 %fusion.10 = (bf16[576,128]{1,0:T(8,128)(2,1)S(1)}, bf16[576,128]{1,0:T(8,128)(2,1)S(1)}) fusion(bf16[1152,128]{1,0:T(8,128)(2,1)} %collective-permute-done.1), kind=kLoop, calls=%fused_computation.32 | loop fusion | bytes 589824 | tf_op jit(solution)/shard_map/slice | solution.py:249
  21.7 0.6 %collective-permute-start.2 = (bf16[576,128]{1,0:T(8,128)(2,1)S(1)}, bf16[576,128]{1,0:T(8,128)(2,1)S(1)}, u32[]{:S(2)}, u32[]{:S(2)}) collective-permute-start(bf16[576,128]{1,0:T(8,128)(2,1)S(1)} %get-tuple-element.32), channel_id=1, source_target_pairs={{0,2},{2,0},{4,6},{6,4},{8,10},{10,8},{12,14},{14,12},{16,18},{18,... | collective-permute-start | bytes 442376 | tf_op jit(solution)/shard_map/ppermute | solution.py:53
  22.3 0.3 collective-permute-done.11.refs_5_
  22.6 1.6 %collective-permute-start.12 = (bf16[1024,128]{1,0:T(8,128)(2,1)}, bf16[1024,128]{1,0:T(8,128)(2,1)S(1)}, u32[]{:S(2)}, u32[]{:S(2)}) collective-permute-start(bf16[1024,128]{1,0:T(8,128)(2,1)} %collective-permute-done.11.refs_5_), channel_id=1, source_target_pairs={{0,4},{2,6},{8,0},{10,2},{16,8},{18,10},{24,16},{26,18},{28,24},{3... | collective-permute-start | bytes 786440 | tf_op jit(solution)/shard_map/ppermute | solution.py:35
  24.2 2.2 %collective-permute-done.8.refs_6_ = bf16[1024,128]{1,0:T(8,128)(2,1)} collective-permute-done((bf16[1024,128]{1,0:T(8,128)(2,1)S(1)}, bf16[1024,128]{1,0:T(8,128)(2,1)}, u32[]{:S(2)}, u32[]{:S(2)}) %collective-permute-start.8) | collective-permute-done | bytes 262176 | tf_op jit(solution)/shard_map/ppermute | solution.py:35
  26.3 0.7 %collective-permute-start.9 = (bf16[1024,128]{1,0:T(8,128)(2,1)}, bf16[1024,128]{1,0:T(8,128)(2,1)S(1)}, u32[]{:S(2)}, u32[]{:S(2)}) collective-permute-start(bf16[1024,128]{1,0:T(8,128)(2,1)} %collective-permute-done.8.refs_6_), channel_id=1, source_target_pairs={{0,8},{2,10},{8,16},{10,18},{16,24},{18,26},{24,28},{26,30},{28,20... | collective-permute-start | bytes 786440 | tf_op jit(solution)/shard_map/ppermute | solution.py:35
  27.1 0.1 reshape.62
  27.2 0.0 collective-permute-done.2.refs_3_
  27.2 0.1 reshape.64
  27.3 0.1 concatenate.10.table_ref
  27.4 1.6 %add_slabs.3 = (f32[1024,128]{1,0:T(8,128)S(1)}, f32[1024,128]{1,0:T(8,128)S(1)}) custom-call(s32[306]{0:T(512)S(1)} %concatenate.10.table_ref, bf16[576,128]{1,0:T(8,128)(2,1)S(1)} %get-tuple-element.35.refs_0_, bf16[576,128]{1,0:T(8,128)(2,1)S(1)} %get-tuple-element.33.refs_1_, bf16[576,128]{1,0:T(8,128)(2,1)S(1)} %collective-permute-done.refs_2_, ...), custom_call_target="tpu_custom_call" | custom-call | flops 1 | bytes 1 | tf_op jit(solution)/shard_map/add_slabs/pallas_call | solution.py:288
  29.1 2.3 %add_slabs.4 = (f32[1024,128]{1,0:T(8,128)S(1)}, f32[1024,128]{1,0:T(8,128)S(1)}) custom-call(s32[306]{0:T(512)S(1)} %concatenate.10.table_ref, bf16[576,128]{1,0:T(8,128)(2,1)S(1)} %get-tuple-element.35.refs_0_, bf16[576,128]{1,0:T(8,128)(2,1)S(1)} %get-tuple-element.33.refs_1_, ...), custom_call_target="tpu_custom_call", output_to_operand_aliasing={{0}: (8, {}), {1}: (9, {})} | custom-call | flops 1 | bytes 1 | tf_op jit(solution)/shard_map/add_slabs/pallas_call | solution.py:288
  31.3 0.0 collective-permute-done.12.refs_4_
  31.3 1.1 %add_slabs.5 = (f32[1024,128]{1,0:T(8,128)S(1)}, f32[1024,128]{1,0:T(8,128)S(1)}) custom-call(s32[306]{0:T(512)S(1)} %concatenate.10.table_ref, bf16[576,128]{1,0:T(8,128)(2,1)S(1)} %get-tuple-element.35.refs_0_, bf16[576,128]{1,0:T(8,128)(2,1)S(1)} %get-tuple-element.33.refs_1_, ...), custom_call_target="tpu_custom_call", output_to_operand_aliasing={{0}: (6, {}), {1}: (7, {})} | custom-call | flops 1 | bytes 1 | tf_op jit(solution)/shard_map/add_slabs/pallas_call | solution.py:288
  32.5 0.0 collective-permute-done.4.refs_6_
  32.5 0.0 collective-permute-done.5.refs_7_
  32.5 0.4 collective-permute-done.9.refs_8_
  32.9 1.4 %last_slab.1 = (f32[1024,128]{1,0:T(8,128)S(1)}, bf16[1024,128]{1,0:T(8,128)(2,1)S(1)}, bf16[256,128]{1,0:T(8,128)(2,1)S(1)}) custom-call(s32[306]{0:T(512)S(1)} %concatenate.10.table_ref, bf16[576,128]{1,0:T(8,128)(2,1)S(1)} %get-tuple-element.35.refs_0_, bf16[576,128]{1,0:T(8,128)(2,1)S(1)} %get-tuple-element.33.refs_1_, ...), custom_call_target="tpu_custom_call" | custom-call | flops 1 | bytes 1 | tf_op jit(solution)/shard_map/last_slab/pallas_call | solution.py:303
  34.3 0.1 collective-permute-start.13
  34.4 1.2 %collective-permute-done.13 = bf16[256,128]{1,0:T(8,128)(2,1)S(1)} collective-permute-done((bf16[256,128]{1,0:T(8,128)(2,1)S(1)}, bf16[256,128]{1,0:T(8,128)(2,1)S(1)}, u32[]{:S(2)}, u32[]{:S(2)}) %collective-permute-start.13) | collective-permute-done | bytes 65568 | tf_op jit(solution)/shard_map/ppermute | solution.py:53
  35.6 2.7 %collective-permute-start.14 = (bf16[256,128]{1,0:T(8,128)(2,1)S(1)}, bf16[256,128]{1,0:T(8,128)(2,1)S(1)}, u32[]{:S(2)}, u32[]{:S(2)}) collective-permute-start(bf16[256,128]{1,0:T(8,128)(2,1)S(1)} %add_convert_fusion.1), channel_id=1, source_target_pairs={{0,12},{1,13},{2,10},{3,11},{4,8},{5,9},{6,14},{7,15},{8,4},{9,5},... | collective-permute-start | bytes 196616 | tf_op jit(solution)/shard_map/ppermute | solution.py:46
  38.3 0.7 %collective-permute-start.15 = (bf16[256,128]{1,0:T(8,128)(2,1)S(1)}, bf16[256,128]{1,0:T(8,128)(2,1)S(1)}, u32[]{:S(2)}, u32[]{:S(2)}) collective-permute-start(bf16[256,128]{1,0:T(8,128)(2,1)S(1)} %add_convert_fusion.1), channel_id=1, source_target_pairs={{2,6},{3,7},{6,2},{7,3},{10,14},{11,15},{14,10},{15,11},{18,22},{1... | collective-permute-start | bytes 196616 | tf_op jit(solution)/shard_map/ppermute | solution.py:46
  39.0 1.5 %collective-permute-start.16 = (bf16[1024,128]{1,0:T(8,128)(2,1)S(1)}, bf16[1024,128]{1,0:T(8,128)(2,1)S(1)}, u32[]{:S(2)}, u32[]{:S(2)}) collective-permute-start(bf16[1024,128]{1,0:T(8,128)(2,1)S(1)} %get-tuple-element.29), channel_id=1, source_target_pairs={{0,2},{2,0},{4,6},{6,4},{8,10},{10,8},{12,14},{14,12},{16,18},{18,... | collective-permute-start | bytes 786440 | tf_op jit(solution)/shard_map/ppermute | solution.py:53
  40.4 0.4 collective-permute-done.14
  40.9 0.0 collective-permute-done.15
  40.9 0.7 %collective-permute-done.16 = bf16[1024,128]{1,0:T(8,128)(2,1)S(1)} collective-permute-done((bf16[1024,128]{1,0:T(8,128)(2,1)S(1)}, bf16[1024,128]{1,0:T(8,128)(2,1)S(1)}, u32[]{:S(2)}, u32[]{:S(2)}) %collective-permute-start.16) | collective-permute-done | bytes 262176 | tf_op jit(solution)/shard_map/ppermute | solution.py:53
  41.6 0.2 multiply_convert_fusion
  41.8 0.5 collective-permute-start.17
  42.3 1.0 %collective-permute-done.17 = f32[256,128]{1,0:T(8,128)S(1)} collective-permute-done((f32[256,128]{1,0:T(8,128)S(1)}, f32[256,128]{1,0:T(8,128)S(1)}, u32[]{:S(2)}, u32[]{:S(2)}) %collective-permute-start.17) | collective-permute-done | bytes 131104 | tf_op jit(solution)/shard_map/ppermute | solution.py:53
  43.3 1.6 %collective-permute-start.18 = (bf16[768,128]{1,0:T(8,128)(2,1)S(1)}, bf16[768,128]{1,0:T(8,128)(2,1)S(1)}, u32[]{:S(2)}, u32[]{:S(2)}) collective-permute-start(bf16[768,128]{1,0:T(8,128)(2,1)S(1)} %pad_maximum_fusion), channel_id=1, source_target_pairs={{0,1},{1,0},{2,3},{3,2},{4,5},{5,4},{6,7},{7,6},{8,9},{9,8},{10,11... | collective-permute-start | bytes 589832 | tf_op jit(solution)/shard_map/ppermute | solution.py:63
  44.9 2.0 %collective-permute-start.19 = (bf16[256,128]{1,0:T(8,128)(2,1)S(1)}, bf16[256,128]{1,0:T(8,128)(2,1)S(1)}, u32[]{:S(2)}, u32[]{:S(2)}) collective-permute-start(bf16[256,128]{1,0:T(8,128)(2,1)S(1)} %add_convert_fusion), channel_id=1, source_target_pairs={{0,16},{1,17},{2,19},{3,18},{4,20},{5,21},{6,23},{7,22},{8,24},{9,... | collective-permute-start | bytes 196616 | tf_op jit(solution)/shard_map/ppermute | solution.py:46
  47.0 0.2 fusion.3
  47.2 4.1 %collective-permute-done.19 = bf16[256,128]{1,0:T(8,128)(2,1)S(1)} collective-permute-done((bf16[256,128]{1,0:T(8,128)(2,1)S(1)}, bf16[256,128]{1,0:T(8,128)(2,1)S(1)}, u32[]{:S(2)}, u32[]{:S(2)}) %collective-permute-start.19) | collective-permute-done | bytes 65568 | tf_op jit(solution)/shard_map/ppermute | solution.py:46
  51.3 0.8 %collective-permute-start.20 = (f32[1,256,128]{2,1,0:T(8,128)S(1)}, f32[1,256,128]{2,1,0:T(8,128)S(1)}, u32[]{:S(2)}, u32[]{:S(2)}) collective-permute-start(f32[1,256,128]{2,1,0:T(8,128)S(1)} %fusion.5), channel_id=1, source_target_pairs={{0,2},{2,0},{4,6},{6,4},{8,10},{10,8},{12,14},{14,12},{16,18},{18,... | collective-permute-start | bytes 393224 | tf_op jit(solution)/shard_map/ppermute | solution.py:53
  52.1 0.9 %fusion = bf16[512,256]{1,0:T(8,128)(2,1)} fusion(f32[512,256]{1,0:T(8,128)S(1)} %fusion.3, bf16[768,128]{1,0:T(8,128)(2,1)S(1)} %collective-permute-done.18, bf16[256,256]{1,0:T(8,128)(2,1)S(1)} %copy-done, s32[]{:T(128)S(6)} %select_n.496), kind=kOutput, calls=%fused_computation.1 | convolution fusion | flops 33816576 | bytes 983044 | tf_op jit(solution)/shard_map/dot_general | solution.py:343
  53.0 0.1 collective-permute-done.20
  53.2 0.7 %broadcast_multiply_fusion = f32[256,256]{1,0:T(8,128)} fusion(f32[256,256]{1,0:T(8,128)S(1)} %bitcast_dynamic-update-slice_fusion), kind=kLoop, calls=%fused_computation.8 | loop fusion | flops 65536 | bytes 524288 | tf_op jit(solution)/shard_map/mul | solution.py:356
  (34 shorter events, 0.3 us)
Async XLA Ops:
  0.6 46.3 %copy-start = (bf16[256,256]{1,0:T(8,128)(2,1)S(1)}, bf16[256,256]{1,0:T(8,128)(2,1)}, u32[]{:S(2)}) copy-start(bf16[256,256]{1,0:T(8,128)(2,1)} %param.9) | copy-start | bytes 393220
  0.6 5.6 %copy-start.1 = (s32[1,8,8,16,128]{4,3,2,1,0:T(8,128)S(1)}, s32[1,8,8,16,128]{4,3,2,1,0:T(8,128)}, u32[]{:S(2)}) copy-start(s32[1,8,8,16,128]{4,3,2,1,0:T(8,128)} %param.10) | copy-start | bytes 1572868
  0.7 4.6 %copy-start.3 = (s32[1024]{0:T(1024)S(1)}, s32[1024]{0:T(1024)}, u32[]{:S(2)}) copy-start(s32[1024]{0:T(1024)} %param.13) | copy-start | bytes 12292
  0.7 5.6 %copy-start.2 = (bf16[512,256]{1,0:T(8,128)(2,1)S(1)}, bf16[512,256]{1,0:T(8,128)(2,1)}, u32[]{:S(2)}) copy-start(bf16[512,256]{1,0:T(8,128)(2,1)} %features_ref) | copy-start | bytes 786436
  2.1 3.9 %copy-start.4 = (s32[1,8,2,8]{3,2,1,0:T(2,128)S(1)}, s32[1,8,2,8]{3,2,1,0:T(2,128)}, u32[]{:S(2)}) copy-start(s32[1,8,2,8]{3,2,1,0:T(2,128)} %param.11) | copy-start | bytes 1540
  2.1 11.6 %collective-permute-start.10 = (bf16[1024,128]{1,0:T(8,128)(2,1)S(1)}, bf16[1024,128]{1,0:T(8,128)(2,1)S(1)}, u32[]{:S(2)}, u32[]{:S(2)}) collective-permute-start(bf16[1024,128]{1,0:T(8,128)(2,1)S(1)} %scale.1.refs_4_), channel_id=1, source_target_pairs={{0,4},{2,6},{8,0},{10,2},{16,8},{18,10},{24,16},{26,18},{28,24},{3... | collective-permute-start | bytes 786440 | tf_op jit(solution)/shard_map/ppermute | solution.py:35
  5.1 7.8 %collective-permute-start.6 = (bf16[1024,128]{1,0:T(8,128)(2,1)S(1)}, bf16[1024,128]{1,0:T(8,128)(2,1)S(1)}, u32[]{:S(2)}, u32[]{:S(2)}) collective-permute-start(bf16[1024,128]{1,0:T(8,128)(2,1)S(1)} %scale.1.refs_4_), channel_id=1, source_target_pairs={{0,8},{2,10},{8,16},{10,18},{16,24},{18,26},{24,28},{26,30},{28,20... | collective-permute-start | bytes 786440 | tf_op jit(solution)/shard_map/ppermute | solution.py:35
  5.3 0.7 %copy-start.5 = (s32[1,8]{1,0:T(1,128)S(1)}, s32[1,8]{1,0:T(1,128)}, u32[]{:S(2)}) copy-start(s32[1,8]{1,0:T(1,128)} %param.12) | copy-start | bytes 100
  6.5 14.3 %collective-permute-start.1 = (bf16[1152,128]{1,0:T(8,128)(2,1)S(1)}, bf16[1152,128]{1,0:T(8,128)(2,1)}, u32[]{:S(2)}, u32[]{:S(2)}) collective-permute-start(bf16[1152,128]{1,0:T(8,128)(2,1)S(1)} %get-tuple-element.19), channel_id=1, source_target_pairs={{0,1},{1,0},{2,3},{3,2},{4,5},{5,4},{6,7},{7,6},{8,9},{9,8},{10,11... | collective-permute-start | bytes 884744 | tf_op jit(solution)/shard_map/ppermute | solution.py:63
  8.4 5.2 %collective-permute-start = (bf16[576,128]{1,0:T(8,128)(2,1)S(1)}, bf16[576,128]{1,0:T(8,128)(2,1)S(1)}, u32[]{:S(2)}, u32[]{:S(2)}) collective-permute-start(bf16[576,128]{1,0:T(8,128)(2,1)S(1)} %get-tuple-element.34), channel_id=1, source_target_pairs={{0,2},{2,0},{4,6},{6,4},{8,10},{10,8},{12,14},{14,12},{16,18},{18,... | collective-permute-start | bytes 442376 | tf_op jit(solution)/shard_map/ppermute | solution.py:53
  8.5 12.2 %collective-permute-start.3 = (bf16[256,512]{1,0:T(8,128)(2,1)S(1)}, bf16[256,512]{1,0:T(8,128)(2,1)S(1)}, u32[]{:S(2)}, u32[]{:S(2)}) collective-permute-start(bf16[256,512]{1,0:T(8,128)(2,1)S(1)} %get-tuple-element.20.refs_4_), channel_id=1, source_target_pairs={{0,1},{1,0},{2,3},{3,2},{4,5},{5,4},{6,7},{7,6},{8,9},{9,8},{10,11... | collective-permute-start | bytes 786440 | tf_op jit(solution)/shard_map/ppermute | solution.py:63
  12.9 7.0 %collective-permute-start.7 = (bf16[1024,128]{1,0:T(8,128)(2,1)S(1)}, bf16[1024,128]{1,0:T(8,128)(2,1)S(1)}, u32[]{:S(2)}, u32[]{:S(2)}) collective-permute-start(bf16[1024,128]{1,0:T(8,128)(2,1)S(1)} %collective-permute-done.6.refs_5_), channel_id=1, source_target_pairs={{0,8},{2,10},{8,16},{10,18},{16,24},{18,26},{24,28},{26,30},{28,20... | collective-permute-start | bytes 786440 | tf_op jit(solution)/shard_map/ppermute | solution.py:35
  13.6 18.9 %collective-permute-start.4 = (bf16[256,512]{1,0:T(8,128)(2,1)S(1)}, bf16[256,512]{1,0:T(8,128)(2,1)S(1)}, u32[]{:S(2)}, u32[]{:S(2)}) collective-permute-start(bf16[256,512]{1,0:T(8,128)(2,1)S(1)} %get-tuple-element.20.refs_4_), channel_id=1, source_target_pairs={{0,2},{2,0},{4,6},{6,4},{8,10},{10,8},{12,14},{14,12},{16,18},{18,... | collective-permute-start | bytes 786440 | tf_op jit(solution)/shard_map/ppermute | solution.py:53
  13.7 8.8 %collective-permute-start.11 = (bf16[1024,128]{1,0:T(8,128)(2,1)S(1)}, bf16[1024,128]{1,0:T(8,128)(2,1)}, u32[]{:S(2)}, u32[]{:S(2)}) collective-permute-start(bf16[1024,128]{1,0:T(8,128)(2,1)S(1)} %collective-permute-done.10.refs_6_), channel_id=1, source_target_pairs={{0,4},{2,6},{8,0},{10,2},{16,8},{18,10},{24,16},{26,18},{28,24},{3... | collective-permute-start | bytes 786440 | tf_op jit(solution)/shard_map/ppermute | solution.py:35
  19.9 6.5 %collective-permute-start.8 = (bf16[1024,128]{1,0:T(8,128)(2,1)S(1)}, bf16[1024,128]{1,0:T(8,128)(2,1)}, u32[]{:S(2)}, u32[]{:S(2)}) collective-permute-start(bf16[1024,128]{1,0:T(8,128)(2,1)S(1)} %collective-permute-done.7.refs_4_), channel_id=1, source_target_pairs={{0,8},{2,10},{8,16},{10,18},{16,24},{18,26},{24,28},{26,30},{28,20... | collective-permute-start | bytes 786440 | tf_op jit(solution)/shard_map/ppermute | solution.py:35
  20.7 11.8 %collective-permute-start.5 = (bf16[256,512]{1,0:T(8,128)(2,1)S(1)}, bf16[256,512]{1,0:T(8,128)(2,1)S(1)}, u32[]{:S(2)}, u32[]{:S(2)}) collective-permute-start(bf16[256,512]{1,0:T(8,128)(2,1)S(1)} %collective-permute-done.3.refs_5_), channel_id=1, source_target_pairs={{0,2},{2,0},{4,6},{6,4},{8,10},{10,8},{12,14},{14,12},{16,18},{18,... | collective-permute-start | bytes 786440 | tf_op jit(solution)/shard_map/ppermute | solution.py:53
  21.7 5.5 %collective-permute-start.2 = (bf16[576,128]{1,0:T(8,128)(2,1)S(1)}, bf16[576,128]{1,0:T(8,128)(2,1)S(1)}, u32[]{:S(2)}, u32[]{:S(2)}) collective-permute-start(bf16[576,128]{1,0:T(8,128)(2,1)S(1)} %get-tuple-element.32), channel_id=1, source_target_pairs={{0,2},{2,0},{4,6},{6,4},{8,10},{10,8},{12,14},{14,12},{16,18},{18,... | collective-permute-start | bytes 442376 | tf_op jit(solution)/shard_map/ppermute | solution.py:53
  22.6 8.7 %collective-permute-start.12 = (bf16[1024,128]{1,0:T(8,128)(2,1)}, bf16[1024,128]{1,0:T(8,128)(2,1)S(1)}, u32[]{:S(2)}, u32[]{:S(2)}) collective-permute-start(bf16[1024,128]{1,0:T(8,128)(2,1)} %collective-permute-done.11.refs_5_), channel_id=1, source_target_pairs={{0,4},{2,6},{8,0},{10,2},{16,8},{18,10},{24,16},{26,18},{28,24},{3... | collective-permute-start | bytes 786440 | tf_op jit(solution)/shard_map/ppermute | solution.py:35
  26.3 6.6 %collective-permute-start.9 = (bf16[1024,128]{1,0:T(8,128)(2,1)}, bf16[1024,128]{1,0:T(8,128)(2,1)S(1)}, u32[]{:S(2)}, u32[]{:S(2)}) collective-permute-start(bf16[1024,128]{1,0:T(8,128)(2,1)} %collective-permute-done.8.refs_6_), channel_id=1, source_target_pairs={{0,8},{2,10},{8,16},{10,18},{16,24},{18,26},{24,28},{26,30},{28,20... | collective-permute-start | bytes 786440 | tf_op jit(solution)/shard_map/ppermute | solution.py:35
  34.3 1.3 %collective-permute-start.13 = (bf16[256,128]{1,0:T(8,128)(2,1)S(1)}, bf16[256,128]{1,0:T(8,128)(2,1)S(1)}, u32[]{:S(2)}, u32[]{:S(2)}) collective-permute-start(bf16[256,128]{1,0:T(8,128)(2,1)S(1)} %get-tuple-element.27), channel_id=1, source_target_pairs={{0,2},{2,0},{4,6},{6,4},{8,10},{10,8},{12,14},{14,12},{16,18},{18,... | collective-permute-start | bytes 196616 | tf_op jit(solution)/shard_map/ppermute | solution.py:53
  35.6 5.2 %collective-permute-start.14 = (bf16[256,128]{1,0:T(8,128)(2,1)S(1)}, bf16[256,128]{1,0:T(8,128)(2,1)S(1)}, u32[]{:S(2)}, u32[]{:S(2)}) collective-permute-start(bf16[256,128]{1,0:T(8,128)(2,1)S(1)} %add_convert_fusion.1), channel_id=1, source_target_pairs={{0,12},{1,13},{2,10},{3,11},{4,8},{5,9},{6,14},{7,15},{8,4},{9,5},... | collective-permute-start | bytes 196616 | tf_op jit(solution)/shard_map/ppermute | solution.py:46
  38.3 2.6 %collective-permute-start.15 = (bf16[256,128]{1,0:T(8,128)(2,1)S(1)}, bf16[256,128]{1,0:T(8,128)(2,1)S(1)}, u32[]{:S(2)}, u32[]{:S(2)}) collective-permute-start(bf16[256,128]{1,0:T(8,128)(2,1)S(1)} %add_convert_fusion.1), channel_id=1, source_target_pairs={{2,6},{3,7},{6,2},{7,3},{10,14},{11,15},{14,10},{15,11},{18,22},{1... | collective-permute-start | bytes 196616 | tf_op jit(solution)/shard_map/ppermute | solution.py:46
  39.0 2.6 %collective-permute-start.16 = (bf16[1024,128]{1,0:T(8,128)(2,1)S(1)}, bf16[1024,128]{1,0:T(8,128)(2,1)S(1)}, u32[]{:S(2)}, u32[]{:S(2)}) collective-permute-start(bf16[1024,128]{1,0:T(8,128)(2,1)S(1)} %get-tuple-element.29), channel_id=1, source_target_pairs={{0,2},{2,0},{4,6},{6,4},{8,10},{10,8},{12,14},{14,12},{16,18},{18,... | collective-permute-start | bytes 786440 | tf_op jit(solution)/shard_map/ppermute | solution.py:53
  41.8 1.5 %collective-permute-start.17 = (f32[256,128]{1,0:T(8,128)S(1)}, f32[256,128]{1,0:T(8,128)S(1)}, u32[]{:S(2)}, u32[]{:S(2)}) collective-permute-start(f32[256,128]{1,0:T(8,128)S(1)} %convert_add_fusion.1), channel_id=1, source_target_pairs={{0,2},{2,0},{4,6},{6,4},{8,10},{10,8},{12,14},{14,12},{16,18},{18,... | collective-permute-start | bytes 393224 | tf_op jit(solution)/shard_map/ppermute | solution.py:53
  43.3 7.9 %collective-permute-start.18 = (bf16[768,128]{1,0:T(8,128)(2,1)S(1)}, bf16[768,128]{1,0:T(8,128)(2,1)S(1)}, u32[]{:S(2)}, u32[]{:S(2)}) collective-permute-start(bf16[768,128]{1,0:T(8,128)(2,1)S(1)} %pad_maximum_fusion), channel_id=1, source_target_pairs={{0,1},{1,0},{2,3},{3,2},{4,5},{5,4},{6,7},{7,6},{8,9},{9,8},{10,11... | collective-permute-start | bytes 589832 | tf_op jit(solution)/shard_map/ppermute | solution.py:63
  44.9 6.3 %collective-permute-start.19 = (bf16[256,128]{1,0:T(8,128)(2,1)S(1)}, bf16[256,128]{1,0:T(8,128)(2,1)S(1)}, u32[]{:S(2)}, u32[]{:S(2)}) collective-permute-start(bf16[256,128]{1,0:T(8,128)(2,1)S(1)} %add_convert_fusion), channel_id=1, source_target_pairs={{0,16},{1,17},{2,19},{3,18},{4,20},{5,21},{6,23},{7,22},{8,24},{9,... | collective-permute-start | bytes 196616 | tf_op jit(solution)/shard_map/ppermute | solution.py:46
  51.3 1.8 %collective-permute-start.20 = (f32[1,256,128]{2,1,0:T(8,128)S(1)}, f32[1,256,128]{2,1,0:T(8,128)S(1)}, u32[]{:S(2)}, u32[]{:S(2)}) collective-permute-start(f32[1,256,128]{2,1,0:T(8,128)S(1)} %fusion.5), channel_id=1, source_target_pairs={{0,2},{2,0},{4,6},{6,4},{8,10},{10,8},{12,14},{14,12},{16,18},{18,... | collective-permute-start | bytes 393224 | tf_op jit(solution)/shard_map/ppermute | solution.py:53

commit v8 on v7

--- a/solution.py
+++ b/solution.py
@@ -318,13 +318,12 @@
     own_sums = own_sums + wide(across_cores(other_sums))
     aggregated = (own_sums * inverse_root[:, None]).astype(jnp.bfloat16)
     row_bits = [1 << bit for bit in range(rows_of_chips.bit_length() - 1)]
-    first_bit, last_bit = row_bits[0], row_bits[-1]
-    one = across(total, (first_bit, 1, 0), (first_bit, 0, 0))
-    two = across(total, None, (0, 1, 0))
+    one = across(total, (row_bits[0] | row_bits[1], 0, 0), (row_bits[1], 0, 0))
+    two = across(total, None, (row_bits[0], 0, 0))
     part = wide(one) + wide(jnp.where(core == 0, total, two))
     part, aggregated = lax.optimization_barrier((part, aggregated))
     total = part + across_cores(part)
-    for bit in row_bits[1:-1]:
+    for bit in row_bits[2:]:
         total = total.astype(jnp.bfloat16)
         total = wide(total) + wide(across(total, (bit, 0, 0), (bit, 0, 0)))
     total = total.astype(jnp.bfloat16)
@@ -334,9 +333,8 @@
         rows_to = ((rep_index + d) % rep_size) * share_rows
         part = lax.dynamic_slice_in_dim(aggregated, rows_to, share_rows, 0)
         if d:
-            far = across(total, (last_bit, 0, 0), (last_bit, 0, d))
-            both = along_rep(jnp.concatenate([part, total]), d)
-            part, near = both[:share_rows], both[share_rows:]
+            far = across(total, (0, 1, 0), (0, 1, d))
+            part, near = along_rep(part, d), along_rep(total, d)
             shares.append(wide(jnp.where(core == 0, total, near)) + wide(far))
         columns_at = ((rep_index - d) % rep_size) * share_width
         side = lax.dynamic_slice_in_dim(weight, columns_at, share_width, 1)

time: 54.1 us -> 52.9 us (0.978)
  waiting for transfers between devices: 19 us -> 16.9 us
  starting transfers between devices: 20.9 us -> 21.9 us
    ppermute x3, waiting for transfers between devices: 4.51 us -> 1.16 us  [across(): return lax.ppermute(block, ('blk', 'rep'), route)]
    ppermute x3 -> x4, waiting for transfers between devices: 0.01 us -> 2.54 us  [along_rep(): lax.ppermute(block, 'rep', [(i, (i + distance) % size) for i in range(siz...]
    ppermute x8, waiting for transfers between devices: 2.97 us -> 1.63 us  [across_cores(): return lax.ppermute(block, 'blk', route)]
    ppermute x3 -> x4, starting transfers between devices: 3.75 us -> 4.73 us  [along_rep(): lax.ppermute(block, 'rep', [(i, (i + distance) % size) for i in range(siz...]
    ppermute x8, starting transfers between devices: 3.55 us -> 2.98 us  [across_cores(): return lax.ppermute(block, 'blk', route)]
    ppermute x3, starting transfers between devices: 5.33 us -> 5.88 us  [across(): return lax.ppermute(block, ('blk', 'rep'), route)]
  transfers between devices with their start and end apart: 21 -> 22, of which waited for: 11 -> 9; matrix products, arithmetic and copies ran while one was open for 6% -> 6% of each run, Pallas kernels for 10% -> 10%
where the time goes in v8:
time: 52.9 us; the launch traced here: 52.7 us
  starting transfers between devices  21.9 us (41%)
  waiting for transfers between devices  16.9 us (32%)
  Pallas kernels  8.01 us (15%)
  local copies, waits for them, and re-layouts  2.48 us (5%)
  matrix products  1.17 us (2%)
  other arithmetic  1.16 us (2%)
  between operations  1.12 us (2%)
    ppermute x7, waiting for transfers between devices, along_ring(): return lax.ppermute(block, 'blk', route)  11.5 us
    ppermute x7, starting transfers between devices, along_ring(): return lax.ppermute(block, 'blk', route)  8.31 us
    ppermute x3, starting transfers between devices, across(): return lax.ppermute(block, ('blk', 'rep'), route)  5.88 us
    pallas_call x3, Pallas kernels, add_slabs(): pl.pallas_call(functools.partial(adding_kernel, plan, first_slab, len(sla...  5.04 us
    ppermute x4, starting transfers between devices, along_rep(): lax.ppermute(block, 'rep', [(i, (i + distance) % size) for i in range(siz...  4.73 us
    ppermute x8, starting transfers between devices, across_cores(): return lax.ppermute(block, 'blk', route)  2.98 us
    ppermute x4, waiting for transfers between devices, along_rep(): lax.ppermute(block, 'rep', [(i, (i + distance) % size) for i in range(siz...  2.54 us
    ppermute x8, waiting for transfers between devices, across_cores(): return lax.ppermute(block, 'blk', route)  1.63 us
  transfers between devices with their start and end apart: 22, of which 9 were waited for; matrix products, arithmetic and copies ran while one was open for 6% of the time, Pallas kernels for 10%

profile of v8, /device:TPU:0, one launch (start us, length us, event | category | flops | bytes accessed | tf_op | source)
XLA Modules:
  0.0 52.7 jit_solution(15197985977164460182)
XLA Ops:
  0.6 0.0 copy-start
  0.7 1.5 %scale.1.refs_4_ = bf16[1024,128]{1,0:T(8,128)(2,1)S(1)} custom-call(s32[8,128]{1,0:T(8,128)} %bitcast.69, bf16[1024,256]{1,0:T(8,128)(2,1)} %gradient_hbm.1), custom_call_target="tpu_custom_call" | custom-call | tf_op jit(solution)/shard_map/scale/pallas_call | solution.py:209
  2.1 0.0 copy-start.4
  2.1 3.0 %collective-permute-start.10 = (bf16[1024,128]{1,0:T(8,128)(2,1)S(1)}, bf16[1024,128]{1,0:T(8,128)(2,1)S(1)}, u32[]{:S(2)}, u32[]{:S(2)}) collective-permute-start(bf16[1024,128]{1,0:T(8,128)(2,1)S(1)} %scale.1.refs_4_), channel_id=1, source_target_pairs={{0,4},{2,6},{8,0},{10,2},{16,8},{18,10},{24,16},{26,18},{28,24},{3... | collective-permute-start | bytes 786440 | tf_op jit(solution)/shard_map/ppermute | solution.py:35
  5.1 0.2 collective-permute-start.6
  5.3 0.7 %copy-done.5 = s32[1,8]{1,0:T(1,128)S(1)} copy-done((s32[1,8]{1,0:T(1,128)S(1)}, s32[1,8]{1,0:T(1,128)}, u32[]{:S(2)}) %copy-start.5) | copy-done | bytes 56
  6.0 0.1 copy.13
  6.0 0.1 reshape_squeeze.6
  6.1 0.1 pad_add_fusion
  6.2 0.1 dynamic_slice.15
  6.3 0.2 payload.1
  6.5 2.0 %collective-permute-start.1 = (bf16[1152,128]{1,0:T(8,128)(2,1)S(1)}, bf16[1152,128]{1,0:T(8,128)(2,1)}, u32[]{:S(2)}, u32[]{:S(2)}) collective-permute-start(bf16[1152,128]{1,0:T(8,128)(2,1)S(1)} %get-tuple-element.19), channel_id=1, source_target_pairs={{0,1},{1,0},{2,3},{3,2},{4,5},{5,4},{6,7},{7,6},{8,9},{9,8},{10,11... | collective-permute-start | bytes 884744 | tf_op jit(solution)/shard_map/ppermute | solution.py:63
  8.4 0.1 collective-permute-start
  8.5 0.2 collective-permute-start.3
  8.7 4.2 %collective-permute-done.6.refs_5_ = bf16[1024,128]{1,0:T(8,128)(2,1)S(1)} collective-permute-done((bf16[1024,128]{1,0:T(8,128)(2,1)S(1)}, bf16[1024,128]{1,0:T(8,128)(2,1)S(1)}, u32[]{:S(2)}, u32[]{:S(2)}) %collective-permute-start.6) | collective-permute-done | bytes 262176 | tf_op jit(solution)/shard_map/ppermute | solution.py:35
  12.9 0.4 collective-permute-start.7
  13.3 0.1 reshape.58
  13.6 0.0 collective-permute-done.refs_2_
  13.6 0.1 collective-permute-start.4
  13.7 0.0 collective-permute-done.10.refs_6_
  13.7 1.6 %collective-permute-start.11 = (bf16[1024,128]{1,0:T(8,128)(2,1)S(1)}, bf16[1024,128]{1,0:T(8,128)(2,1)}, u32[]{:S(2)}, u32[]{:S(2)}) collective-permute-start(bf16[1024,128]{1,0:T(8,128)(2,1)S(1)} %collective-permute-done.10.refs_6_), channel_id=1, source_target_pairs={{0,4},{2,6},{8,0},{10,2},{16,8},{18,10},{24,16},{26,18},{28,24},{3... | collective-permute-start | bytes 786440 | tf_op jit(solution)/shard_map/ppermute | solution.py:35
  15.4 4.5 %collective-permute-done.7.refs_4_ = bf16[1024,128]{1,0:T(8,128)(2,1)S(1)} collective-permute-done((bf16[1024,128]{1,0:T(8,128)(2,1)S(1)}, bf16[1024,128]{1,0:T(8,128)(2,1)S(1)}, u32[]{:S(2)}, u32[]{:S(2)}) %collective-permute-start.7) | collective-permute-done | bytes 262176 | tf_op jit(solution)/shard_map/ppermute | solution.py:35
  19.9 0.7 %collective-permute-start.8 = (bf16[1024,128]{1,0:T(8,128)(2,1)S(1)}, bf16[1024,128]{1,0:T(8,128)(2,1)}, u32[]{:S(2)}, u32[]{:S(2)}) collective-permute-start(bf16[1024,128]{1,0:T(8,128)(2,1)S(1)} %collective-permute-done.7.refs_4_), channel_id=1, source_target_pairs={{0,8},{2,10},{8,16},{10,18},{16,24},{18,26},{24,28},{26,30},{28,20... | collective-permute-start | bytes 786440 | tf_op jit(solution)/shard_map/ppermute | solution.py:35
  20.6 0.1 reshape.60
  20.7 0.0 collective-permute-done.3.refs_5_
  20.7 0.0 collective-permute-start.5
  20.7 0.0 collective-permute-done.1
  20.7 1.0 %fusion.9 = (bf16[576,128]{1,0:T(8,128)(2,1)S(1)}, bf16[576,128]{1,0:T(8,128)(2,1)S(1)}) fusion(bf16[1152,128]{1,0:T(8,128)(2,1)} %collective-permute-done.1), kind=kLoop, calls=%fused_computation.30 | loop fusion | bytes 589824 | tf_op jit(solution)/shard_map/slice | solution.py:249
  21.7 0.6 %collective-permute-start.2 = (bf16[576,128]{1,0:T(8,128)(2,1)S(1)}, bf16[576,128]{1,0:T(8,128)(2,1)S(1)}, u32[]{:S(2)}, u32[]{:S(2)}) collective-permute-start(bf16[576,128]{1,0:T(8,128)(2,1)S(1)} %get-tuple-element.32), channel_id=1, source_target_pairs={{0,2},{2,0},{4,6},{6,4},{8,10},{10,8},{12,14},{14,12},{16,18},{18,... | collective-permute-start | bytes 442376 | tf_op jit(solution)/shard_map/ppermute | solution.py:53
  22.3 0.3 collective-permute-done.11.refs_5_
  22.6 1.6 %collective-permute-start.12 = (bf16[1024,128]{1,0:T(8,128)(2,1)}, bf16[1024,128]{1,0:T(8,128)(2,1)S(1)}, u32[]{:S(2)}, u32[]{:S(2)}) collective-permute-start(bf16[1024,128]{1,0:T(8,128)(2,1)} %collective-permute-done.11.refs_5_), channel_id=1, source_target_pairs={{0,4},{2,6},{8,0},{10,2},{16,8},{18,10},{24,16},{26,18},{28,24},{3... | collective-permute-start | bytes 786440 | tf_op jit(solution)/shard_map/ppermute | solution.py:35
  24.2 2.2 %collective-permute-done.8.refs_6_ = bf16[1024,128]{1,0:T(8,128)(2,1)} collective-permute-done((bf16[1024,128]{1,0:T(8,128)(2,1)S(1)}, bf16[1024,128]{1,0:T(8,128)(2,1)}, u32[]{:S(2)}, u32[]{:S(2)}) %collective-permute-start.8) | collective-permute-done | bytes 262176 | tf_op jit(solution)/shard_map/ppermute | solution.py:35
  26.3 0.7 %collective-permute-start.9 = (bf16[1024,128]{1,0:T(8,128)(2,1)}, bf16[1024,128]{1,0:T(8,128)(2,1)S(1)}, u32[]{:S(2)}, u32[]{:S(2)}) collective-permute-start(bf16[1024,128]{1,0:T(8,128)(2,1)} %collective-permute-done.8.refs_6_), channel_id=1, source_target_pairs={{0,8},{2,10},{8,16},{10,18},{16,24},{18,26},{24,28},{26,30},{28,20... | collective-permute-start | bytes 786440 | tf_op jit(solution)/shard_map/ppermute | solution.py:35
  27.1 0.1 reshape.62
  27.2 0.0 collective-permute-done.2.refs_3_
  27.2 0.1 reshape.64
  27.3 0.1 concatenate.7.table_ref
  27.4 1.6 %add_slabs.3 = (f32[1024,128]{1,0:T(8,128)S(1)}, f32[1024,128]{1,0:T(8,128)S(1)}) custom-call(s32[306]{0:T(512)S(1)} %concatenate.7.table_ref, bf16[576,128]{1,0:T(8,128)(2,1)S(1)} %get-tuple-element.35.refs_0_, bf16[576,128]{1,0:T(8,128)(2,1)S(1)} %get-tuple-element.33.refs_1_, bf16[576,128]{1,0:T(8,128)(2,1)S(1)} %collective-permute-done.refs_2_, ...), custom_call_target="tpu_custom_call" | custom-call | flops 1 | bytes 1 | tf_op jit(solution)/shard_map/add_slabs/pallas_call | solution.py:288
  29.1 2.3 %add_slabs.4 = (f32[1024,128]{1,0:T(8,128)S(1)}, f32[1024,128]{1,0:T(8,128)S(1)}) custom-call(s32[306]{0:T(512)S(1)} %concatenate.7.table_ref, bf16[576,128]{1,0:T(8,128)(2,1)S(1)} %get-tuple-element.35.refs_0_, bf16[576,128]{1,0:T(8,128)(2,1)S(1)} %get-tuple-element.33.refs_1_, ...), custom_call_target="tpu_custom_call", output_to_operand_aliasing={{0}: (8, {}), {1}: (9, {})} | custom-call | flops 1 | bytes 1 | tf_op jit(solution)/shard_map/add_slabs/pallas_call | solution.py:288
  31.3 0.0 collective-permute-done.12.refs_4_
  31.3 1.1 %add_slabs.5 = (f32[1024,128]{1,0:T(8,128)S(1)}, f32[1024,128]{1,0:T(8,128)S(1)}) custom-call(s32[306]{0:T(512)S(1)} %concatenate.7.table_ref, bf16[576,128]{1,0:T(8,128)(2,1)S(1)} %get-tuple-element.35.refs_0_, bf16[576,128]{1,0:T(8,128)(2,1)S(1)} %get-tuple-element.33.refs_1_, ...), custom_call_target="tpu_custom_call", output_to_operand_aliasing={{0}: (6, {}), {1}: (7, {})} | custom-call | flops 1 | bytes 1 | tf_op jit(solution)/shard_map/add_slabs/pallas_call | solution.py:288
  32.5 0.0 collective-permute-done.4.refs_6_
  32.5 0.4 collective-permute-done.9.refs_8_
  32.9 1.4 %last_slab.1 = (f32[1024,128]{1,0:T(8,128)S(1)}, bf16[1024,128]{1,0:T(8,128)(2,1)S(1)}, bf16[256,128]{1,0:T(8,128)(2,1)S(1)}) custom-call(s32[306]{0:T(512)S(1)} %concatenate.7.table_ref, bf16[576,128]{1,0:T(8,128)(2,1)S(1)} %get-tuple-element.35.refs_0_, bf16[576,128]{1,0:T(8,128)(2,1)S(1)} %get-tuple-element.33.refs_1_, ...), custom_call_target="tpu_custom_call" | custom-call | flops 1 | bytes 1 | tf_op jit(solution)/shard_map/last_slab/pallas_call | solution.py:303
  34.3 0.1 collective-permute-start.13
  34.4 1.2 %collective-permute-done.13 = bf16[256,128]{1,0:T(8,128)(2,1)S(1)} collective-permute-done((bf16[256,128]{1,0:T(8,128)(2,1)S(1)}, bf16[256,128]{1,0:T(8,128)(2,1)S(1)}, u32[]{:S(2)}, u32[]{:S(2)}) %collective-permute-start.13) | collective-permute-done | bytes 65568 | tf_op jit(solution)/shard_map/ppermute | solution.py:53
  35.6 2.9 %collective-permute-start.14 = (bf16[256,128]{1,0:T(8,128)(2,1)S(1)}, bf16[256,128]{1,0:T(8,128)(2,1)S(1)}, u32[]{:S(2)}, u32[]{:S(2)}) collective-permute-start(bf16[256,128]{1,0:T(8,128)(2,1)S(1)} %add_convert_fusion.1), channel_id=1, source_target_pairs={{0,24},{1,25},{2,18},{3,19},{4,28},{5,29},{6,22},{7,23},{8,16},{9,... | collective-permute-start | bytes 196616 | tf_op jit(solution)/shard_map/ppermute | solution.py:46
  38.6 0.7 %collective-permute-start.15 = (bf16[256,128]{1,0:T(8,128)(2,1)S(1)}, bf16[256,128]{1,0:T(8,128)(2,1)S(1)}, u32[]{:S(2)}, u32[]{:S(2)}) collective-permute-start(bf16[256,128]{1,0:T(8,128)(2,1)S(1)} %add_convert_fusion.1), channel_id=1, source_target_pairs={{2,10},{3,11},{6,14},{7,15},{10,2},{11,3},{14,6},{15,7},{18,26},{1... | collective-permute-start | bytes 196616 | tf_op jit(solution)/shard_map/ppermute | solution.py:46
  39.2 1.5 %collective-permute-start.16 = (bf16[1024,128]{1,0:T(8,128)(2,1)S(1)}, bf16[1024,128]{1,0:T(8,128)(2,1)S(1)}, u32[]{:S(2)}, u32[]{:S(2)}) collective-permute-start(bf16[1024,128]{1,0:T(8,128)(2,1)S(1)} %get-tuple-element.29), channel_id=1, source_target_pairs={{0,2},{2,0},{4,6},{6,4},{8,10},{10,8},{12,14},{14,12},{16,18},{18,... | collective-permute-start | bytes 786440 | tf_op jit(solution)/shard_map/ppermute | solution.py:53
  40.7 1.2 %collective-permute-done.14 = bf16[256,128]{1,0:T(8,128)(2,1)S(1)} collective-permute-done((bf16[256,128]{1,0:T(8,128)(2,1)S(1)}, bf16[256,128]{1,0:T(8,128)(2,1)S(1)}, u32[]{:S(2)}, u32[]{:S(2)}) %collective-permute-start.14) | collective-permute-done | bytes 65568 | tf_op jit(solution)/shard_map/ppermute | solution.py:46
  41.9 0.0 collective-permute-done.15
  41.9 0.2 multiply_convert_fusion
  42.1 0.7 %collective-permute-start.18 = (f32[256,128]{1,0:T(8,128)S(1)}, f32[256,128]{1,0:T(8,128)S(1)}, u32[]{:S(2)}, u32[]{:S(2)}) collective-permute-start(f32[256,128]{1,0:T(8,128)S(1)} %convert_add_fusion.1), channel_id=1, source_target_pairs={{0,2},{2,0},{4,6},{6,4},{8,10},{10,8},{12,14},{14,12},{16,18},{18,... | collective-permute-start | bytes 393224 | tf_op jit(solution)/shard_map/ppermute | solution.py:53
  42.8 1.6 %collective-permute-start.17 = (bf16[512,128]{1,0:T(8,128)(2,1)S(1)}, bf16[512,128]{1,0:T(8,128)(2,1)S(1)}, u32[]{:S(2)}, u32[]{:S(2)}) collective-permute-start(bf16[512,128]{1,0:T(8,128)(2,1)S(1)} %constant_dynamic-slice_fusion), channel_id=1, source_target_pairs={{0,1},{1,0},{2,3},{3,2},{4,5},{5,4},{6,7},{7,6},{8,9},{9,8},{10,11... | collective-permute-start | bytes 393224 | tf_op jit(solution)/shard_map/ppermute | solution.py:63
  44.4 0.0 collective-permute-done.18
  44.4 1.0 %collective-permute-start.19 = (bf16[256,128]{1,0:T(8,128)(2,1)S(1)}, bf16[256,128]{1,0:T(8,128)(2,1)S(1)}, u32[]{:S(2)}, u32[]{:S(2)}) collective-permute-start(bf16[256,128]{1,0:T(8,128)(2,1)S(1)} %add_convert_fusion), channel_id=1, source_target_pairs={{0,1},{1,0},{2,3},{3,2},{4,5},{5,4},{6,7},{7,6},{8,9},{9,8},{10,11... | collective-permute-start | bytes 196616 | tf_op jit(solution)/shard_map/ppermute | solution.py:63
  45.4 2.3 %collective-permute-start.20 = (bf16[256,128]{1,0:T(8,128)(2,1)S(1)}, bf16[256,128]{1,0:T(8,128)(2,1)S(1)}, u32[]{:S(2)}, u32[]{:S(2)}) collective-permute-start(bf16[256,128]{1,0:T(8,128)(2,1)S(1)} %add_convert_fusion), channel_id=1, source_target_pairs={{0,4},{1,5},{2,7},{3,6},{4,0},{5,1},{6,3},{7,2},{8,12},{9,13},{10,... | collective-permute-start | bytes 196616 | tf_op jit(solution)/shard_map/ppermute | solution.py:46
  47.7 0.2 fusion.2
  47.9 2.5 %collective-permute-done.19 = bf16[256,128]{1,0:T(8,128)(2,1)S(1)} collective-permute-done((bf16[256,128]{1,0:T(8,128)(2,1)S(1)}, bf16[256,128]{1,0:T(8,128)(2,1)S(1)}, u32[]{:S(2)}, u32[]{:S(2)}) %collective-permute-start.19) | collective-permute-done | bytes 65568 | tf_op jit(solution)/shard_map/ppermute | solution.py:63
  50.5 0.1 collective-permute-start.21
  50.5 0.0 collective-permute-done.17
  50.5 0.9 %fusion = bf16[512,256]{1,0:T(8,128)(2,1)} fusion(f32[512,256]{1,0:T(8,128)S(1)} %fusion.2, bf16[512,128]{1,0:T(8,128)(2,1)S(1)} %collective-permute-done.17, bf16[256,256]{1,0:T(8,128)(2,1)S(1)} %copy-done, s32[]{:T(128)S(6)} %select_n.496), kind=kOutput, calls=%fused_computation.1 | convolution fusion | flops 33816576 | bytes 983044 | tf_op jit(solution)/shard_map/dot_general | solution.py:341
  51.5 0.4 collective-permute-done.21
  52.0 0.7 %broadcast_multiply_fusion = f32[256,256]{1,0:T(8,128)} fusion(f32[256,256]{1,0:T(8,128)S(1)} %bitcast_dynamic-update-slice_fusion), kind=kLoop, calls=%fused_computation.6 | loop fusion | flops 65536 | bytes 524288 | tf_op jit(solution)/shard_map/mul | solution.py:354
  (35 shorter events, 0.3 us)
Async XLA Ops:
  0.6 47.0 %copy-start = (bf16[256,256]{1,0:T(8,128)(2,1)S(1)}, bf16[256,256]{1,0:T(8,128)(2,1)}, u32[]{:S(2)}) copy-start(bf16[256,256]{1,0:T(8,128)(2,1)} %param.9) | copy-start | bytes 393220
  0.6 5.6 %copy-start.1 = (s32[1,8,8,16,128]{4,3,2,1,0:T(8,128)S(1)}, s32[1,8,8,16,128]{4,3,2,1,0:T(8,128)}, u32[]{:S(2)}) copy-start(s32[1,8,8,16,128]{4,3,2,1,0:T(8,128)} %param.10) | copy-start | bytes 1572868
  0.7 4.6 %copy-start.3 = (s32[1024]{0:T(1024)S(1)}, s32[1024]{0:T(1024)}, u32[]{:S(2)}) copy-start(s32[1024]{0:T(1024)} %param.13) | copy-start | bytes 12292
  0.7 5.6 %copy-start.2 = (bf16[512,256]{1,0:T(8,128)(2,1)S(1)}, bf16[512,256]{1,0:T(8,128)(2,1)}, u32[]{:S(2)}) copy-start(bf16[512,256]{1,0:T(8,128)(2,1)} %features_ref) | copy-start | bytes 786436
  2.1 3.9 %copy-start.4 = (s32[1,8,2,8]{3,2,1,0:T(2,128)S(1)}, s32[1,8,2,8]{3,2,1,0:T(2,128)}, u32[]{:S(2)}) copy-start(s32[1,8,2,8]{3,2,1,0:T(2,128)} %param.11) | copy-start | bytes 1540
  2.1 11.6 %collective-permute-start.10 = (bf16[1024,128]{1,0:T(8,128)(2,1)S(1)}, bf16[1024,128]{1,0:T(8,128)(2,1)S(1)}, u32[]{:S(2)}, u32[]{:S(2)}) collective-permute-start(bf16[1024,128]{1,0:T(8,128)(2,1)S(1)} %scale.1.refs_4_), channel_id=1, source_target_pairs={{0,4},{2,6},{8,0},{10,2},{16,8},{18,10},{24,16},{26,18},{28,24},{3... | collective-permute-start | bytes 786440 | tf_op jit(solution)/shard_map/ppermute | solution.py:35
  5.1 7.8 %collective-permute-start.6 = (bf16[1024,128]{1,0:T(8,128)(2,1)S(1)}, bf16[1024,128]{1,0:T(8,128)(2,1)S(1)}, u32[]{:S(2)}, u32[]{:S(2)}) collective-permute-start(bf16[1024,128]{1,0:T(8,128)(2,1)S(1)} %scale.1.refs_4_), channel_id=1, source_target_pairs={{0,8},{2,10},{8,16},{10,18},{16,24},{18,26},{24,28},{26,30},{28,20... | collective-permute-start | bytes 786440 | tf_op jit(solution)/shard_map/ppermute | solution.py:35
  5.3 0.7 %copy-start.5 = (s32[1,8]{1,0:T(1,128)S(1)}, s32[1,8]{1,0:T(1,128)}, u32[]{:S(2)}) copy-start(s32[1,8]{1,0:T(1,128)} %param.12) | copy-start | bytes 100
  6.5 14.3 %collective-permute-start.1 = (bf16[1152,128]{1,0:T(8,128)(2,1)S(1)}, bf16[1152,128]{1,0:T(8,128)(2,1)}, u32[]{:S(2)}, u32[]{:S(2)}) collective-permute-start(bf16[1152,128]{1,0:T(8,128)(2,1)S(1)} %get-tuple-element.19), channel_id=1, source_target_pairs={{0,1},{1,0},{2,3},{3,2},{4,5},{5,4},{6,7},{7,6},{8,9},{9,8},{10,11... | collective-permute-start | bytes 884744 | tf_op jit(solution)/shard_map/ppermute | solution.py:63
  8.4 5.2 %collective-permute-start = (bf16[576,128]{1,0:T(8,128)(2,1)S(1)}, bf16[576,128]{1,0:T(8,128)(2,1)S(1)}, u32[]{:S(2)}, u32[]{:S(2)}) collective-permute-start(bf16[576,128]{1,0:T(8,128)(2,1)S(1)} %get-tuple-element.34), channel_id=1, source_target_pairs={{0,2},{2,0},{4,6},{6,4},{8,10},{10,8},{12,14},{14,12},{16,18},{18,... | collective-permute-start | bytes 442376 | tf_op jit(solution)/shard_map/ppermute | solution.py:53
  8.5 12.2 %collective-permute-start.3 = (bf16[256,512]{1,0:T(8,128)(2,1)S(1)}, bf16[256,512]{1,0:T(8,128)(2,1)S(1)}, u32[]{:S(2)}, u32[]{:S(2)}) collective-permute-start(bf16[256,512]{1,0:T(8,128)(2,1)S(1)} %get-tuple-element.20.refs_4_), channel_id=1, source_target_pairs={{0,1},{1,0},{2,3},{3,2},{4,5},{5,4},{6,7},{7,6},{8,9},{9,8},{10,11... | collective-permute-start | bytes 786440 | tf_op jit(solution)/shard_map/ppermute | solution.py:63
  12.9 7.0 %collective-permute-start.7 = (bf16[1024,128]{1,0:T(8,128)(2,1)S(1)}, bf16[1024,128]{1,0:T(8,128)(2,1)S(1)}, u32[]{:S(2)}, u32[]{:S(2)}) collective-permute-start(bf16[1024,128]{1,0:T(8,128)(2,1)S(1)} %collective-permute-done.6.refs_5_), channel_id=1, source_target_pairs={{0,8},{2,10},{8,16},{10,18},{16,24},{18,26},{24,28},{26,30},{28,20... | collective-permute-start | bytes 786440 | tf_op jit(solution)/shard_map/ppermute | solution.py:35
  13.6 18.9 %collective-permute-start.4 = (bf16[256,512]{1,0:T(8,128)(2,1)S(1)}, bf16[256,512]{1,0:T(8,128)(2,1)S(1)}, u32[]{:S(2)}, u32[]{:S(2)}) collective-permute-start(bf16[256,512]{1,0:T(8,128)(2,1)S(1)} %get-tuple-element.20.refs_4_), channel_id=1, source_target_pairs={{0,2},{2,0},{4,6},{6,4},{8,10},{10,8},{12,14},{14,12},{16,18},{18,... | collective-permute-start | bytes 786440 | tf_op jit(solution)/shard_map/ppermute | solution.py:53
  13.7 8.8 %collective-permute-start.11 = (bf16[1024,128]{1,0:T(8,128)(2,1)S(1)}, bf16[1024,128]{1,0:T(8,128)(2,1)}, u32[]{:S(2)}, u32[]{:S(2)}) collective-permute-start(bf16[1024,128]{1,0:T(8,128)(2,1)S(1)} %collective-permute-done.10.refs_6_), channel_id=1, source_target_pairs={{0,4},{2,6},{8,0},{10,2},{16,8},{18,10},{24,16},{26,18},{28,24},{3... | collective-permute-start | bytes 786440 | tf_op jit(solution)/shard_map/ppermute | solution.py:35
  19.9 6.5 %collective-permute-start.8 = (bf16[1024,128]{1,0:T(8,128)(2,1)S(1)}, bf16[1024,128]{1,0:T(8,128)(2,1)}, u32[]{:S(2)}, u32[]{:S(2)}) collective-permute-start(bf16[1024,128]{1,0:T(8,128)(2,1)S(1)} %collective-permute-done.7.refs_4_), channel_id=1, source_target_pairs={{0,8},{2,10},{8,16},{10,18},{16,24},{18,26},{24,28},{26,30},{28,20... | collective-permute-start | bytes 786440 | tf_op jit(solution)/shard_map/ppermute | solution.py:35
  20.7 11.8 %collective-permute-start.5 = (bf16[256,512]{1,0:T(8,128)(2,1)S(1)}, bf16[256,512]{1,0:T(8,128)(2,1)S(1)}, u32[]{:S(2)}, u32[]{:S(2)}) collective-permute-start(bf16[256,512]{1,0:T(8,128)(2,1)S(1)} %collective-permute-done.3.refs_5_), channel_id=1, source_target_pairs={{0,2},{2,0},{4,6},{6,4},{8,10},{10,8},{12,14},{14,12},{16,18},{18,... | collective-permute-start | bytes 786440 | tf_op jit(solution)/shard_map/ppermute | solution.py:53
  21.7 5.5 %collective-permute-start.2 = (bf16[576,128]{1,0:T(8,128)(2,1)S(1)}, bf16[576,128]{1,0:T(8,128)(2,1)S(1)}, u32[]{:S(2)}, u32[]{:S(2)}) collective-permute-start(bf16[576,128]{1,0:T(8,128)(2,1)S(1)} %get-tuple-element.32), channel_id=1, source_target_pairs={{0,2},{2,0},{4,6},{6,4},{8,10},{10,8},{12,14},{14,12},{16,18},{18,... | collective-permute-start | bytes 442376 | tf_op jit(solution)/shard_map/ppermute | solution.py:53
  22.6 8.7 %collective-permute-start.12 = (bf16[1024,128]{1,0:T(8,128)(2,1)}, bf16[1024,128]{1,0:T(8,128)(2,1)S(1)}, u32[]{:S(2)}, u32[]{:S(2)}) collective-permute-start(bf16[1024,128]{1,0:T(8,128)(2,1)} %collective-permute-done.11.refs_5_), channel_id=1, source_target_pairs={{0,4},{2,6},{8,0},{10,2},{16,8},{18,10},{24,16},{26,18},{28,24},{3... | collective-permute-start | bytes 786440 | tf_op jit(solution)/shard_map/ppermute | solution.py:35
  26.3 6.6 %collective-permute-start.9 = (bf16[1024,128]{1,0:T(8,128)(2,1)}, bf16[1024,128]{1,0:T(8,128)(2,1)S(1)}, u32[]{:S(2)}, u32[]{:S(2)}) collective-permute-start(bf16[1024,128]{1,0:T(8,128)(2,1)} %collective-permute-done.8.refs_6_), channel_id=1, source_target_pairs={{0,8},{2,10},{8,16},{10,18},{16,24},{18,26},{24,28},{26,30},{28,20... | collective-permute-start | bytes 786440 | tf_op jit(solution)/shard_map/ppermute | solution.py:35
  34.3 1.3 %collective-permute-start.13 = (bf16[256,128]{1,0:T(8,128)(2,1)S(1)}, bf16[256,128]{1,0:T(8,128)(2,1)S(1)}, u32[]{:S(2)}, u32[]{:S(2)}) collective-permute-start(bf16[256,128]{1,0:T(8,128)(2,1)S(1)} %get-tuple-element.27), channel_id=1, source_target_pairs={{0,2},{2,0},{4,6},{6,4},{8,10},{10,8},{12,14},{14,12},{16,18},{18,... | collective-permute-start | bytes 196616 | tf_op jit(solution)/shard_map/ppermute | solution.py:53
  35.6 6.2 %collective-permute-start.14 = (bf16[256,128]{1,0:T(8,128)(2,1)S(1)}, bf16[256,128]{1,0:T(8,128)(2,1)S(1)}, u32[]{:S(2)}, u32[]{:S(2)}) collective-permute-start(bf16[256,128]{1,0:T(8,128)(2,1)S(1)} %add_convert_fusion.1), channel_id=1, source_target_pairs={{0,24},{1,25},{2,18},{3,19},{4,28},{5,29},{6,22},{7,23},{8,16},{9,... | collective-permute-start | bytes 196616 | tf_op jit(solution)/shard_map/ppermute | solution.py:46
  38.6 3.3 %collective-permute-start.15 = (bf16[256,128]{1,0:T(8,128)(2,1)S(1)}, bf16[256,128]{1,0:T(8,128)(2,1)S(1)}, u32[]{:S(2)}, u32[]{:S(2)}) collective-permute-start(bf16[256,128]{1,0:T(8,128)(2,1)S(1)} %add_convert_fusion.1), channel_id=1, source_target_pairs={{2,10},{3,11},{6,14},{7,15},{10,2},{11,3},{14,6},{15,7},{18,26},{1... | collective-permute-start | bytes 196616 | tf_op jit(solution)/shard_map/ppermute | solution.py:46
  39.2 2.7 %collective-permute-start.16 = (bf16[1024,128]{1,0:T(8,128)(2,1)S(1)}, bf16[1024,128]{1,0:T(8,128)(2,1)S(1)}, u32[]{:S(2)}, u32[]{:S(2)}) collective-permute-start(bf16[1024,128]{1,0:T(8,128)(2,1)S(1)} %get-tuple-element.29), channel_id=1, source_target_pairs={{0,2},{2,0},{4,6},{6,4},{8,10},{10,8},{12,14},{14,12},{16,18},{18,... | collective-permute-start | bytes 786440 | tf_op jit(solution)/shard_map/ppermute | solution.py:53
  42.1 2.3 %collective-permute-start.18 = (f32[256,128]{1,0:T(8,128)S(1)}, f32[256,128]{1,0:T(8,128)S(1)}, u32[]{:S(2)}, u32[]{:S(2)}) collective-permute-start(f32[256,128]{1,0:T(8,128)S(1)} %convert_add_fusion.1), channel_id=1, source_target_pairs={{0,2},{2,0},{4,6},{6,4},{8,10},{10,8},{12,14},{14,12},{16,18},{18,... | collective-permute-start | bytes 393224 | tf_op jit(solution)/shard_map/ppermute | solution.py:53
  42.8 7.8 %collective-permute-start.17 = (bf16[512,128]{1,0:T(8,128)(2,1)S(1)}, bf16[512,128]{1,0:T(8,128)(2,1)S(1)}, u32[]{:S(2)}, u32[]{:S(2)}) collective-permute-start(bf16[512,128]{1,0:T(8,128)(2,1)S(1)} %constant_dynamic-slice_fusion), channel_id=1, source_target_pairs={{0,1},{1,0},{2,3},{3,2},{4,5},{5,4},{6,7},{7,6},{8,9},{9,8},{10,11... | collective-permute-start | bytes 393224 | tf_op jit(solution)/shard_map/ppermute | solution.py:63
  44.4 6.0 %collective-permute-start.19 = (bf16[256,128]{1,0:T(8,128)(2,1)S(1)}, bf16[256,128]{1,0:T(8,128)(2,1)S(1)}, u32[]{:S(2)}, u32[]{:S(2)}) collective-permute-start(bf16[256,128]{1,0:T(8,128)(2,1)S(1)} %add_convert_fusion), channel_id=1, source_target_pairs={{0,1},{1,0},{2,3},{3,2},{4,5},{5,4},{6,7},{7,6},{8,9},{9,8},{10,11... | collective-permute-start | bytes 196616 | tf_op jit(solution)/shard_map/ppermute | solution.py:63
  45.4 5.0 %collective-permute-start.20 = (bf16[256,128]{1,0:T(8,128)(2,1)S(1)}, bf16[256,128]{1,0:T(8,128)(2,1)S(1)}, u32[]{:S(2)}, u32[]{:S(2)}) collective-permute-start(bf16[256,128]{1,0:T(8,128)(2,1)S(1)} %add_convert_fusion), channel_id=1, source_target_pairs={{0,4},{1,5},{2,7},{3,6},{4,0},{5,1},{6,3},{7,2},{8,12},{9,13},{10,... | collective-permute-start | bytes 196616 | tf_op jit(solution)/shard_map/ppermute | solution.py:46
  50.5 1.4 %collective-permute-start.21 = (f32[1,256,128]{2,1,0:T(8,128)S(1)}, f32[1,256,128]{2,1,0:T(8,128)S(1)}, u32[]{:S(2)}, u32[]{:S(2)}) collective-permute-start(f32[1,256,128]{2,1,0:T(8,128)S(1)} %fusion.4), channel_id=1, source_target_pairs={{0,2},{2,0},{4,6},{6,4},{8,10},{10,8},{12,14},{14,12},{16,18},{18,... | collective-permute-start | bytes 393224 | tf_op jit(solution)/shard_map/ppermute | solution.py:53

commit v9 on v8

--- a/solution.py
+++ b/solution.py
@@ -149,9 +149,8 @@
     copies = []
     for chunk in range(chunks):
         rows = pl.ds(chunk * chunk_rows, chunk_rows)
-        copies.append(
-            pltpu.make_async_copy(gradient_hbm.at[rows], rows_ref.at[rows], semaphores.at[chunk])
-        )
+        columns = gradient_hbm.at[rows, pl.ds(start, share_width)]
+        copies.append(pltpu.make_async_copy(columns, rows_ref.at[rows], semaphores.at[chunk]))
         copies[-1].start()
     degrees_copy.wait()
     roots = lax.rsqrt(degrees_ref[...].astype(jnp.float32))
@@ -161,8 +160,7 @@
             row = at // 128
             by_row = jnp.broadcast_to(roots[row : row + 1, :], (128, 128)).T
             for column in range(0, share_width, 128):
-                own = pl.ds(pl.multiple_of(start + column, 128), 128)
-                part = rows_ref[at : at + 128, own].astype(jnp.float32) * by_row
+                part = rows_ref[at : at + 128, column : column + 128].astype(jnp.float32) * by_row
                 scaled_ref[at : at + 128, column : column + 128] = part.astype(scaled_ref.dtype)
 
 
@@ -213,8 +211,8 @@
             out_specs=VMEM,
             scratch_shapes=[
                 pltpu.VMEM((slab_rows // 128, 128), jnp.int32),
-                pltpu.VMEM((slab_rows, width), jnp.bfloat16),
-                pltpu.SemaphoreType.DMA((5,)),
+                pltpu.VMEM((slab_rows, share_width), jnp.bfloat16),
+                pltpu.SemaphoreType.DMA((3,)),
             ],
             compiler_params=PARAMS,
             name="scale",
@@ -343,6 +341,7 @@
         )
     input_grad = result.astype(jnp.bfloat16)
     shares = jnp.stack(shares)
+    shares, input_grad = lax.optimization_barrier((shares, input_grad))
     others = across_cores(shares)
     own_share = jnp.where(core == 0, shares[0], others[0])
     other_shares = jnp.where(core == 0, others, shares)

time: 52.9 us -> 52.7 us (level)
    ppermute x8, waiting for transfers between devices: 1.63 us -> 2.59 us  [across_cores(): return lax.ppermute(block, 'blk', route)]
    ppermute x4, waiting for transfers between devices: 2.54 us -> 1.8 us  [along_rep(): lax.ppermute(block, 'rep', [(i, (i + distance) % size) for i in range(siz...]
  transfers between devices with their start and end apart: 22 -> 22, of which waited for: 9 -> 10; matrix products, arithmetic and copies ran while one was open for 6% -> 6% of each run, Pallas kernels for 10% -> 10%
where the time goes in v9:
time: 52.7 us; the launch traced here: 52.5 us
  starting transfers between devices  21.7 us (41%)
  waiting for transfers between devices  17.1 us (32%)
  Pallas kernels  7.83 us (15%)
  local copies, waits for them, and re-layouts  2.48 us (5%)
  other arithmetic  1.16 us (2%)
  matrix products  1.14 us (2%)
  between operations  1.12 us (2%)
    ppermute x7, waiting for transfers between devices, along_ring(): return lax.ppermute(block, 'blk', route)  11.5 us
    ppermute x7, starting transfers between devices, along_ring(): return lax.ppermute(block, 'blk', route)  8.31 us
    ppermute x3, starting transfers between devices, across(): return lax.ppermute(block, ('blk', 'rep'), route)  5.88 us
    pallas_call x3, Pallas kernels, add_slabs(): pl.pallas_call(functools.partial(adding_kernel, plan, first_slab, len(sla...  5.03 us
    ppermute x4, starting transfers between devices, along_rep(): lax.ppermute(block, 'rep', [(i, (i + distance) % size) for i in range(siz...  4.49 us
    ppermute x8, starting transfers between devices, across_cores(): return lax.ppermute(block, 'blk', route)  2.98 us
    ppermute x8, waiting for transfers between devices, across_cores(): return lax.ppermute(block, 'blk', route)  2.59 us
    ppermute x4, waiting for transfers between devices, along_rep(): lax.ppermute(block, 'rep', [(i, (i + distance) % size) for i in range(siz...  1.8 us
  transfers between devices with their start and end apart: 22, of which 10 were waited for; matrix products, arithmetic and copies ran while one was open for 6% of the time, Pallas kernels for 10%

profile of v9, /device:TPU:0, one launch (start us, length us, event | category | flops | bytes accessed | tf_op | source)
XLA Modules:
  0.0 52.5 jit_solution(5069283628368211193)
XLA Ops:
  0.6 0.0 copy-start
  0.7 1.3 %scale.1.refs_4_ = bf16[1024,128]{1,0:T(8,128)(2,1)S(1)} custom-call(s32[8,128]{1,0:T(8,128)} %bitcast.67, bf16[1024,256]{1,0:T(8,128)(2,1)} %gradient_hbm.1), custom_call_target="tpu_custom_call" | custom-call | tf_op jit(solution)/shard_map/scale/pallas_call | solution.py:207
  2.0 0.0 copy-start.4
  2.0 3.0 %collective-permute-start.10 = (bf16[1024,128]{1,0:T(8,128)(2,1)S(1)}, bf16[1024,128]{1,0:T(8,128)(2,1)S(1)}, u32[]{:S(2)}, u32[]{:S(2)}) collective-permute-start(bf16[1024,128]{1,0:T(8,128)(2,1)S(1)} %scale.1.refs_4_), channel_id=1, source_target_pairs={{0,4},{2,6},{8,0},{10,2},{16,8},{18,10},{24,16},{26,18},{28,24},{3... | collective-permute-start | bytes 786440 | tf_op jit(solution)/shard_map/ppermute | solution.py:35
  5.0 0.2 collective-permute-start.6
  5.1 0.7 %copy-done.5 = s32[1,8]{1,0:T(1,128)S(1)} copy-done((s32[1,8]{1,0:T(1,128)S(1)}, s32[1,8]{1,0:T(1,128)}, u32[]{:S(2)}) %copy-start.5) | copy-done | bytes 56
  5.8 0.1 copy.13
  5.9 0.1 reshape_squeeze.6
  6.0 0.1 pad_add_fusion
  6.0 0.1 dynamic_slice.15
  6.1 0.2 payload.1
  6.3 2.0 %collective-permute-start.1 = (bf16[1152,128]{1,0:T(8,128)(2,1)S(1)}, bf16[1152,128]{1,0:T(8,128)(2,1)}, u32[]{:S(2)}, u32[]{:S(2)}) collective-permute-start(bf16[1152,128]{1,0:T(8,128)(2,1)S(1)} %get-tuple-element.21), channel_id=1, source_target_pairs={{0,1},{1,0},{2,3},{3,2},{4,5},{5,4},{6,7},{7,6},{8,9},{9,8},{10,11... | collective-permute-start | bytes 884744 | tf_op jit(solution)/shard_map/ppermute | solution.py:63
  8.3 0.1 collective-permute-start
  8.4 0.2 collective-permute-start.3
  8.6 4.2 %collective-permute-done.6.refs_5_ = bf16[1024,128]{1,0:T(8,128)(2,1)S(1)} collective-permute-done((bf16[1024,128]{1,0:T(8,128)(2,1)S(1)}, bf16[1024,128]{1,0:T(8,128)(2,1)S(1)}, u32[]{:S(2)}, u32[]{:S(2)}) %collective-permute-start.6) | collective-permute-done | bytes 262176 | tf_op jit(solution)/shard_map/ppermute | solution.py:35
  12.7 0.4 collective-permute-start.7
  13.2 0.1 reshape.60
  13.5 0.0 collective-permute-done.refs_2_
  13.5 0.1 collective-permute-start.4
  13.6 0.0 collective-permute-done.10.refs_6_
  13.6 1.6 %collective-permute-start.11 = (bf16[1024,128]{1,0:T(8,128)(2,1)S(1)}, bf16[1024,128]{1,0:T(8,128)(2,1)}, u32[]{:S(2)}, u32[]{:S(2)}) collective-permute-start(bf16[1024,128]{1,0:T(8,128)(2,1)S(1)} %collective-permute-done.10.refs_6_), channel_id=1, source_target_pairs={{0,4},{2,6},{8,0},{10,2},{16,8},{18,10},{24,16},{26,18},{28,24},{3... | collective-permute-start | bytes 786440 | tf_op jit(solution)/shard_map/ppermute | solution.py:35
  15.2 4.5 %collective-permute-done.7.refs_4_ = bf16[1024,128]{1,0:T(8,128)(2,1)S(1)} collective-permute-done((bf16[1024,128]{1,0:T(8,128)(2,1)S(1)}, bf16[1024,128]{1,0:T(8,128)(2,1)S(1)}, u32[]{:S(2)}, u32[]{:S(2)}) %collective-permute-start.7) | collective-permute-done | bytes 262176 | tf_op jit(solution)/shard_map/ppermute | solution.py:35
  19.7 0.7 %collective-permute-start.8 = (bf16[1024,128]{1,0:T(8,128)(2,1)S(1)}, bf16[1024,128]{1,0:T(8,128)(2,1)}, u32[]{:S(2)}, u32[]{:S(2)}) collective-permute-start(bf16[1024,128]{1,0:T(8,128)(2,1)S(1)} %collective-permute-done.7.refs_4_), channel_id=1, source_target_pairs={{0,8},{2,10},{8,16},{10,18},{16,24},{18,26},{24,28},{26,30},{28,20... | collective-permute-start | bytes 786440 | tf_op jit(solution)/shard_map/ppermute | solution.py:35
  20.5 0.1 reshape.62
  20.6 0.0 collective-permute-done.1
  20.6 1.0 %fusion.7 = (bf16[576,128]{1,0:T(8,128)(2,1)S(1)}, bf16[576,128]{1,0:T(8,128)(2,1)S(1)}) fusion(bf16[1152,128]{1,0:T(8,128)(2,1)} %collective-permute-done.1), kind=kLoop, calls=%fused_computation.27 | loop fusion | bytes 589824 | tf_op jit(solution)/shard_map/slice | solution.py:247
  21.6 0.6 %collective-permute-start.2 = (bf16[576,128]{1,0:T(8,128)(2,1)S(1)}, bf16[576,128]{1,0:T(8,128)(2,1)S(1)}, u32[]{:S(2)}, u32[]{:S(2)}) collective-permute-start(bf16[576,128]{1,0:T(8,128)(2,1)S(1)} %get-tuple-element.36), channel_id=1, source_target_pairs={{0,2},{2,0},{4,6},{6,4},{8,10},{10,8},{12,14},{14,12},{16,18},{18,... | collective-permute-start | bytes 442376 | tf_op jit(solution)/shard_map/ppermute | solution.py:53
  22.2 0.3 collective-permute-done.11.refs_5_
  22.4 1.6 %collective-permute-start.12 = (bf16[1024,128]{1,0:T(8,128)(2,1)}, bf16[1024,128]{1,0:T(8,128)(2,1)S(1)}, u32[]{:S(2)}, u32[]{:S(2)}) collective-permute-start(bf16[1024,128]{1,0:T(8,128)(2,1)} %collective-permute-done.11.refs_5_), channel_id=1, source_target_pairs={{0,4},{2,6},{8,0},{10,2},{16,8},{18,10},{24,16},{26,18},{28,24},{3... | collective-permute-start | bytes 786440 | tf_op jit(solution)/shard_map/ppermute | solution.py:35
  24.0 2.2 %collective-permute-done.8.refs_6_ = bf16[1024,128]{1,0:T(8,128)(2,1)} collective-permute-done((bf16[1024,128]{1,0:T(8,128)(2,1)S(1)}, bf16[1024,128]{1,0:T(8,128)(2,1)}, u32[]{:S(2)}, u32[]{:S(2)}) %collective-permute-start.8) | collective-permute-done | bytes 262176 | tf_op jit(solution)/shard_map/ppermute | solution.py:35
  26.2 0.7 %collective-permute-start.9 = (bf16[1024,128]{1,0:T(8,128)(2,1)}, bf16[1024,128]{1,0:T(8,128)(2,1)S(1)}, u32[]{:S(2)}, u32[]{:S(2)}) collective-permute-start(bf16[1024,128]{1,0:T(8,128)(2,1)} %collective-permute-done.8.refs_6_), channel_id=1, source_target_pairs={{0,8},{2,10},{8,16},{10,18},{16,24},{18,26},{24,28},{26,30},{28,20... | collective-permute-start | bytes 786440 | tf_op jit(solution)/shard_map/ppermute | solution.py:35
  26.9 0.1 reshape.64
  27.0 0.0 collective-permute-done.2.refs_3_
  27.1 0.1 reshape.66
  27.1 0.1 concatenate.7.table_ref
  27.3 1.6 %add_slabs.3 = (f32[1024,128]{1,0:T(8,128)S(1)}, f32[1024,128]{1,0:T(8,128)S(1)}) custom-call(s32[306]{0:T(512)S(1)} %concatenate.7.table_ref, bf16[576,128]{1,0:T(8,128)(2,1)S(1)} %get-tuple-element.39.refs_0_, bf16[576,128]{1,0:T(8,128)(2,1)S(1)} %get-tuple-element.37.refs_1_, bf16[576,128]{1,0:T(8,128)(2,1)S(1)} %collective-permute-done.refs_2_, ...), custom_call_target="tpu_custom_call" | custom-call | flops 1 | bytes 1 | tf_op jit(solution)/shard_map/add_slabs/pallas_call | solution.py:286
  28.9 2.3 %add_slabs.4 = (f32[1024,128]{1,0:T(8,128)S(1)}, f32[1024,128]{1,0:T(8,128)S(1)}) custom-call(s32[306]{0:T(512)S(1)} %concatenate.7.table_ref, bf16[576,128]{1,0:T(8,128)(2,1)S(1)} %get-tuple-element.39.refs_0_, bf16[576,128]{1,0:T(8,128)(2,1)S(1)} %get-tuple-element.37.refs_1_, ...), custom_call_target="tpu_custom_call", output_to_operand_aliasing={{0}: (8, {}), {1}: (9, {})} | custom-call | flops 1 | bytes 1 | tf_op jit(solution)/shard_map/add_slabs/pallas_call | solution.py:286
  31.2 0.0 collective-permute-done.12.refs_4_
  31.2 1.1 %add_slabs.5 = (f32[1024,128]{1,0:T(8,128)S(1)}, f32[1024,128]{1,0:T(8,128)S(1)}) custom-call(s32[306]{0:T(512)S(1)} %concatenate.7.table_ref, bf16[576,128]{1,0:T(8,128)(2,1)S(1)} %get-tuple-element.39.refs_0_, bf16[576,128]{1,0:T(8,128)(2,1)S(1)} %get-tuple-element.37.refs_1_, ...), custom_call_target="tpu_custom_call", output_to_operand_aliasing={{0}: (6, {}), {1}: (7, {})} | custom-call | flops 1 | bytes 1 | tf_op jit(solution)/shard_map/add_slabs/pallas_call | solution.py:286
  32.3 0.0 collective-permute-done.4.refs_6_
  32.3 0.0 collective-permute-done.5.refs_7_
  32.3 0.4 collective-permute-done.9.refs_8_
  32.8 1.3 %last_slab.1 = (f32[1024,128]{1,0:T(8,128)S(1)}, bf16[1024,128]{1,0:T(8,128)(2,1)S(1)}, bf16[256,128]{1,0:T(8,128)(2,1)S(1)}) custom-call(s32[306]{0:T(512)S(1)} %concatenate.7.table_ref, bf16[576,128]{1,0:T(8,128)(2,1)S(1)} %get-tuple-element.39.refs_0_, bf16[576,128]{1,0:T(8,128)(2,1)S(1)} %get-tuple-element.37.refs_1_, ...), custom_call_target="tpu_custom_call" | custom-call | flops 1 | bytes 1 | tf_op jit(solution)/shard_map/last_slab/pallas_call | solution.py:301
  34.1 0.1 collective-permute-start.13
  34.2 1.2 %collective-permute-done.13 = bf16[256,128]{1,0:T(8,128)(2,1)S(1)} collective-permute-done((bf16[256,128]{1,0:T(8,128)(2,1)S(1)}, bf16[256,128]{1,0:T(8,128)(2,1)S(1)}, u32[]{:S(2)}, u32[]{:S(2)}) %collective-permute-start.13) | collective-permute-done | bytes 65568 | tf_op jit(solution)/shard_map/ppermute | solution.py:53
  35.5 2.9 %collective-permute-start.14 = (bf16[256,128]{1,0:T(8,128)(2,1)S(1)}, bf16[256,128]{1,0:T(8,128)(2,1)S(1)}, u32[]{:S(2)}, u32[]{:S(2)}) collective-permute-start(bf16[256,128]{1,0:T(8,128)(2,1)S(1)} %add_convert_fusion.1), channel_id=1, source_target_pairs={{0,24},{1,25},{2,18},{3,19},{4,28},{5,29},{6,22},{7,23},{8,16},{9,... | collective-permute-start | bytes 196616 | tf_op jit(solution)/shard_map/ppermute | solution.py:46
  38.4 0.7 %collective-permute-start.15 = (bf16[256,128]{1,0:T(8,128)(2,1)S(1)}, bf16[256,128]{1,0:T(8,128)(2,1)S(1)}, u32[]{:S(2)}, u32[]{:S(2)}) collective-permute-start(bf16[256,128]{1,0:T(8,128)(2,1)S(1)} %add_convert_fusion.1), channel_id=1, source_target_pairs={{2,10},{3,11},{6,14},{7,15},{10,2},{11,3},{14,6},{15,7},{18,26},{1... | collective-permute-start | bytes 196616 | tf_op jit(solution)/shard_map/ppermute | solution.py:46
  39.1 1.5 %collective-permute-start.16 = (bf16[1024,128]{1,0:T(8,128)(2,1)S(1)}, bf16[1024,128]{1,0:T(8,128)(2,1)S(1)}, u32[]{:S(2)}, u32[]{:S(2)}) collective-permute-start(bf16[1024,128]{1,0:T(8,128)(2,1)S(1)} %get-tuple-element.31), channel_id=1, source_target_pairs={{0,2},{2,0},{4,6},{6,4},{8,10},{10,8},{12,14},{14,12},{16,18},{18,... | collective-permute-start | bytes 786440 | tf_op jit(solution)/shard_map/ppermute | solution.py:53
  40.5 1.1 %collective-permute-done.14 = bf16[256,128]{1,0:T(8,128)(2,1)S(1)} collective-permute-done((bf16[256,128]{1,0:T(8,128)(2,1)S(1)}, bf16[256,128]{1,0:T(8,128)(2,1)S(1)}, u32[]{:S(2)}, u32[]{:S(2)}) %collective-permute-start.14) | collective-permute-done | bytes 65568 | tf_op jit(solution)/shard_map/ppermute | solution.py:46
  41.7 0.0 collective-permute-done.16
  41.7 0.2 multiply_convert_fusion
  41.9 0.7 %collective-permute-start.17 = (f32[256,128]{1,0:T(8,128)S(1)}, f32[256,128]{1,0:T(8,128)S(1)}, u32[]{:S(2)}, u32[]{:S(2)}) collective-permute-start(f32[256,128]{1,0:T(8,128)S(1)} %convert_add_fusion), channel_id=1, source_target_pairs={{0,2},{2,0},{4,6},{6,4},{8,10},{10,8},{12,14},{14,12},{16,18},{18,... | collective-permute-start | bytes 393224 | tf_op jit(solution)/shard_map/ppermute | solution.py:53
  42.6 1.6 %collective-permute-start.20 = (bf16[512,128]{1,0:T(8,128)(2,1)S(1)}, bf16[512,128]{1,0:T(8,128)(2,1)S(1)}, u32[]{:S(2)}, u32[]{:S(2)}) collective-permute-start(bf16[512,128]{1,0:T(8,128)(2,1)S(1)} %constant_dynamic-slice_fusion), channel_id=1, source_target_pairs={{0,1},{1,0},{2,3},{3,2},{4,5},{5,4},{6,7},{7,6},{8,9},{9,8},{10,11... | collective-permute-start | bytes 393224 | tf_op jit(solution)/shard_map/ppermute | solution.py:63
  44.2 0.2 fusion.1
  44.4 0.0 collective-permute-done.17
  44.5 0.7 %collective-permute-start.18 = (bf16[256,128]{1,0:T(8,128)(2,1)S(1)}, bf16[256,128]{1,0:T(8,128)(2,1)S(1)}, u32[]{:S(2)}, u32[]{:S(2)}) collective-permute-start(bf16[256,128]{1,0:T(8,128)(2,1)S(1)} %add_convert_fusion), channel_id=1, source_target_pairs={{0,1},{1,0},{2,3},{3,2},{4,5},{5,4},{6,7},{7,6},{8,9},{9,8},{10,11... | collective-permute-start | bytes 196616 | tf_op jit(solution)/shard_map/ppermute | solution.py:63
  45.2 2.3 %collective-permute-start.19 = (bf16[256,128]{1,0:T(8,128)(2,1)S(1)}, bf16[256,128]{1,0:T(8,128)(2,1)S(1)}, u32[]{:S(2)}, u32[]{:S(2)}) collective-permute-start(bf16[256,128]{1,0:T(8,128)(2,1)S(1)} %add_convert_fusion), channel_id=1, source_target_pairs={{0,4},{1,5},{2,7},{3,6},{4,0},{5,1},{6,3},{7,2},{8,12},{9,13},{10,... | collective-permute-start | bytes 196616 | tf_op jit(solution)/shard_map/ppermute | solution.py:46
  47.5 1.3 %collective-permute-done.20 = bf16[512,128]{1,0:T(8,128)(2,1)S(1)} collective-permute-done((bf16[512,128]{1,0:T(8,128)(2,1)S(1)}, bf16[512,128]{1,0:T(8,128)(2,1)S(1)}, u32[]{:S(2)}, u32[]{:S(2)}) %collective-permute-start.20) | collective-permute-done | bytes 131104 | tf_op jit(solution)/shard_map/ppermute | solution.py:63
  48.8 0.9 %fusion = bf16[512,256]{1,0:T(8,128)(2,1)} fusion(f32[512,256]{1,0:T(8,128)S(1)} %fusion.1, bf16[512,128]{1,0:T(8,128)(2,1)S(1)} %collective-permute-done.20, bf16[256,256]{1,0:T(8,128)(2,1)S(1)} %copy-done, s32[]{:T(128)S(6)} %select_n.500), kind=kOutput, calls=%fused_computation.1 | convolution fusion | flops 33816576 | bytes 983044 | tf_op jit(solution)/shard_map/dot_general | solution.py:339
  49.8 0.5 collective-permute-done.18
  50.2 0.0 collective-permute-done.19
  50.2 0.1 collective-permute-start.21
  50.3 1.3 %collective-permute-done.21 = f32[1,256,128]{2,1,0:T(8,128)S(1)} collective-permute-done((f32[1,256,128]{2,1,0:T(8,128)S(1)}, f32[1,256,128]{2,1,0:T(8,128)S(1)}, u32[]{:S(2)}, u32[]{:S(2)}) %collective-permute-start.21) | collective-permute-done | bytes 131104 | tf_op jit(solution)/shard_map/ppermute | solution.py:53
  51.7 0.7 %broadcast_multiply_fusion = f32[256,256]{1,0:T(8,128)} fusion(f32[256,256]{1,0:T(8,128)S(1)} %bitcast_dynamic-update-slice_fusion), kind=kLoop, calls=%fused_computation.5 | loop fusion | flops 65536 | bytes 524288 | tf_op jit(solution)/shard_map/mul | solution.py:353
  (35 shorter events, 0.3 us)
Async XLA Ops:
  0.6 43.6 %copy-start = (bf16[256,256]{1,0:T(8,128)(2,1)S(1)}, bf16[256,256]{1,0:T(8,128)(2,1)}, u32[]{:S(2)}) copy-start(bf16[256,256]{1,0:T(8,128)(2,1)} %param.9) | copy-start | bytes 393220
  0.6 5.5 %copy-start.1 = (s32[1,8,8,16,128]{4,3,2,1,0:T(8,128)S(1)}, s32[1,8,8,16,128]{4,3,2,1,0:T(8,128)}, u32[]{:S(2)}) copy-start(s32[1,8,8,16,128]{4,3,2,1,0:T(8,128)} %param.10) | copy-start | bytes 1572868
  0.7 4.5 %copy-start.3 = (s32[1024]{0:T(1024)S(1)}, s32[1024]{0:T(1024)}, u32[]{:S(2)}) copy-start(s32[1024]{0:T(1024)} %param.13) | copy-start | bytes 12292
  0.7 5.5 %copy-start.2 = (bf16[512,256]{1,0:T(8,128)(2,1)S(1)}, bf16[512,256]{1,0:T(8,128)(2,1)}, u32[]{:S(2)}) copy-start(bf16[512,256]{1,0:T(8,128)(2,1)} %features_ref) | copy-start | bytes 786436
  2.0 3.9 %copy-start.4 = (s32[1,8,2,8]{3,2,1,0:T(2,128)S(1)}, s32[1,8,2,8]{3,2,1,0:T(2,128)}, u32[]{:S(2)}) copy-start(s32[1,8,2,8]{3,2,1,0:T(2,128)} %param.11) | copy-start | bytes 1540
  2.0 11.6 %collective-permute-start.10 = (bf16[1024,128]{1,0:T(8,128)(2,1)S(1)}, bf16[1024,128]{1,0:T(8,128)(2,1)S(1)}, u32[]{:S(2)}, u32[]{:S(2)}) collective-permute-start(bf16[1024,128]{1,0:T(8,128)(2,1)S(1)} %scale.1.refs_4_), channel_id=1, source_target_pairs={{0,4},{2,6},{8,0},{10,2},{16,8},{18,10},{24,16},{26,18},{28,24},{3... | collective-permute-start | bytes 786440 | tf_op jit(solution)/shard_map/ppermute | solution.py:35
  5.0 7.8 %collective-permute-start.6 = (bf16[1024,128]{1,0:T(8,128)(2,1)S(1)}, bf16[1024,128]{1,0:T(8,128)(2,1)S(1)}, u32[]{:S(2)}, u32[]{:S(2)}) collective-permute-start(bf16[1024,128]{1,0:T(8,128)(2,1)S(1)} %scale.1.refs_4_), channel_id=1, source_target_pairs={{0,8},{2,10},{8,16},{10,18},{16,24},{18,26},{24,28},{26,30},{28,20... | collective-permute-start | bytes 786440 | tf_op jit(solution)/shard_map/ppermute | solution.py:35
  5.1 0.7 %copy-start.5 = (s32[1,8]{1,0:T(1,128)S(1)}, s32[1,8]{1,0:T(1,128)}, u32[]{:S(2)}) copy-start(s32[1,8]{1,0:T(1,128)} %param.12) | copy-start | bytes 100
  6.3 14.3 %collective-permute-start.1 = (bf16[1152,128]{1,0:T(8,128)(2,1)S(1)}, bf16[1152,128]{1,0:T(8,128)(2,1)}, u32[]{:S(2)}, u32[]{:S(2)}) collective-permute-start(bf16[1152,128]{1,0:T(8,128)(2,1)S(1)} %get-tuple-element.21), channel_id=1, source_target_pairs={{0,1},{1,0},{2,3},{3,2},{4,5},{5,4},{6,7},{7,6},{8,9},{9,8},{10,11... | collective-permute-start | bytes 884744 | tf_op jit(solution)/shard_map/ppermute | solution.py:63
  8.3 5.2 %collective-permute-start = (bf16[576,128]{1,0:T(8,128)(2,1)S(1)}, bf16[576,128]{1,0:T(8,128)(2,1)S(1)}, u32[]{:S(2)}, u32[]{:S(2)}) collective-permute-start(bf16[576,128]{1,0:T(8,128)(2,1)S(1)} %get-tuple-element.38), channel_id=1, source_target_pairs={{0,2},{2,0},{4,6},{6,4},{8,10},{10,8},{12,14},{14,12},{16,18},{18,... | collective-permute-start | bytes 442376 | tf_op jit(solution)/shard_map/ppermute | solution.py:53
  8.4 12.2 %collective-permute-start.3 = (bf16[256,512]{1,0:T(8,128)(2,1)S(1)}, bf16[256,512]{1,0:T(8,128)(2,1)S(1)}, u32[]{:S(2)}, u32[]{:S(2)}) collective-permute-start(bf16[256,512]{1,0:T(8,128)(2,1)S(1)} %get-tuple-element.22.refs_4_), channel_id=1, source_target_pairs={{0,1},{1,0},{2,3},{3,2},{4,5},{5,4},{6,7},{7,6},{8,9},{9,8},{10,11... | collective-permute-start | bytes 786440 | tf_op jit(solution)/shard_map/ppermute | solution.py:63
  12.7 7.0 %collective-permute-start.7 = (bf16[1024,128]{1,0:T(8,128)(2,1)S(1)}, bf16[1024,128]{1,0:T(8,128)(2,1)S(1)}, u32[]{:S(2)}, u32[]{:S(2)}) collective-permute-start(bf16[1024,128]{1,0:T(8,128)(2,1)S(1)} %collective-permute-done.6.refs_5_), channel_id=1, source_target_pairs={{0,8},{2,10},{8,16},{10,18},{16,24},{18,26},{24,28},{26,30},{28,20... | collective-permute-start | bytes 786440 | tf_op jit(solution)/shard_map/ppermute | solution.py:35
  13.5 18.9 %collective-permute-start.4 = (bf16[256,512]{1,0:T(8,128)(2,1)S(1)}, bf16[256,512]{1,0:T(8,128)(2,1)S(1)}, u32[]{:S(2)}, u32[]{:S(2)}) collective-permute-start(bf16[256,512]{1,0:T(8,128)(2,1)S(1)} %get-tuple-element.22.refs_4_), channel_id=1, source_target_pairs={{0,2},{2,0},{4,6},{6,4},{8,10},{10,8},{12,14},{14,12},{16,18},{18,... | collective-permute-start | bytes 786440 | tf_op jit(solution)/shard_map/ppermute | solution.py:53
  13.6 8.8 %collective-permute-start.11 = (bf16[1024,128]{1,0:T(8,128)(2,1)S(1)}, bf16[1024,128]{1,0:T(8,128)(2,1)}, u32[]{:S(2)}, u32[]{:S(2)}) collective-permute-start(bf16[1024,128]{1,0:T(8,128)(2,1)S(1)} %collective-permute-done.10.refs_6_), channel_id=1, source_target_pairs={{0,4},{2,6},{8,0},{10,2},{16,8},{18,10},{24,16},{26,18},{28,24},{3... | collective-permute-start | bytes 786440 | tf_op jit(solution)/shard_map/ppermute | solution.py:35
  19.7 6.5 %collective-permute-start.8 = (bf16[1024,128]{1,0:T(8,128)(2,1)S(1)}, bf16[1024,128]{1,0:T(8,128)(2,1)}, u32[]{:S(2)}, u32[]{:S(2)}) collective-permute-start(bf16[1024,128]{1,0:T(8,128)(2,1)S(1)} %collective-permute-done.7.refs_4_), channel_id=1, source_target_pairs={{0,8},{2,10},{8,16},{10,18},{16,24},{18,26},{24,28},{26,30},{28,20... | collective-permute-start | bytes 786440 | tf_op jit(solution)/shard_map/ppermute | solution.py:35
  20.6 11.8 %collective-permute-start.5 = (bf16[256,512]{1,0:T(8,128)(2,1)S(1)}, bf16[256,512]{1,0:T(8,128)(2,1)S(1)}, u32[]{:S(2)}, u32[]{:S(2)}) collective-permute-start(bf16[256,512]{1,0:T(8,128)(2,1)S(1)} %collective-permute-done.3.refs_5_), channel_id=1, source_target_pairs={{0,2},{2,0},{4,6},{6,4},{8,10},{10,8},{12,14},{14,12},{16,18},{18,... | collective-permute-start | bytes 786440 | tf_op jit(solution)/shard_map/ppermute | solution.py:53
  21.6 5.5 %collective-permute-start.2 = (bf16[576,128]{1,0:T(8,128)(2,1)S(1)}, bf16[576,128]{1,0:T(8,128)(2,1)S(1)}, u32[]{:S(2)}, u32[]{:S(2)}) collective-permute-start(bf16[576,128]{1,0:T(8,128)(2,1)S(1)} %get-tuple-element.36), channel_id=1, source_target_pairs={{0,2},{2,0},{4,6},{6,4},{8,10},{10,8},{12,14},{14,12},{16,18},{18,... | collective-permute-start | bytes 442376 | tf_op jit(solution)/shard_map/ppermute | solution.py:53
  22.4 8.7 %collective-permute-start.12 = (bf16[1024,128]{1,0:T(8,128)(2,1)}, bf16[1024,128]{1,0:T(8,128)(2,1)S(1)}, u32[]{:S(2)}, u32[]{:S(2)}) collective-permute-start(bf16[1024,128]{1,0:T(8,128)(2,1)} %collective-permute-done.11.refs_5_), channel_id=1, source_target_pairs={{0,4},{2,6},{8,0},{10,2},{16,8},{18,10},{24,16},{26,18},{28,24},{3... | collective-permute-start | bytes 786440 | tf_op jit(solution)/shard_map/ppermute | solution.py:35
  26.2 6.6 %collective-permute-start.9 = (bf16[1024,128]{1,0:T(8,128)(2,1)}, bf16[1024,128]{1,0:T(8,128)(2,1)S(1)}, u32[]{:S(2)}, u32[]{:S(2)}) collective-permute-start(bf16[1024,128]{1,0:T(8,128)(2,1)} %collective-permute-done.8.refs_6_), channel_id=1, source_target_pairs={{0,8},{2,10},{8,16},{10,18},{16,24},{18,26},{24,28},{26,30},{28,20... | collective-permute-start | bytes 786440 | tf_op jit(solution)/shard_map/ppermute | solution.py:35
  34.1 1.3 %collective-permute-start.13 = (bf16[256,128]{1,0:T(8,128)(2,1)S(1)}, bf16[256,128]{1,0:T(8,128)(2,1)S(1)}, u32[]{:S(2)}, u32[]{:S(2)}) collective-permute-start(bf16[256,128]{1,0:T(8,128)(2,1)S(1)} %get-tuple-element.29), channel_id=1, source_target_pairs={{0,2},{2,0},{4,6},{6,4},{8,10},{10,8},{12,14},{14,12},{16,18},{18,... | collective-permute-start | bytes 196616 | tf_op jit(solution)/shard_map/ppermute | solution.py:53
  35.5 6.2 %collective-permute-start.14 = (bf16[256,128]{1,0:T(8,128)(2,1)S(1)}, bf16[256,128]{1,0:T(8,128)(2,1)S(1)}, u32[]{:S(2)}, u32[]{:S(2)}) collective-permute-start(bf16[256,128]{1,0:T(8,128)(2,1)S(1)} %add_convert_fusion.1), channel_id=1, source_target_pairs={{0,24},{1,25},{2,18},{3,19},{4,28},{5,29},{6,22},{7,23},{8,16},{9,... | collective-permute-start | bytes 196616 | tf_op jit(solution)/shard_map/ppermute | solution.py:46
  38.4 3.3 %collective-permute-start.15 = (bf16[256,128]{1,0:T(8,128)(2,1)S(1)}, bf16[256,128]{1,0:T(8,128)(2,1)S(1)}, u32[]{:S(2)}, u32[]{:S(2)}) collective-permute-start(bf16[256,128]{1,0:T(8,128)(2,1)S(1)} %add_convert_fusion.1), channel_id=1, source_target_pairs={{2,10},{3,11},{6,14},{7,15},{10,2},{11,3},{14,6},{15,7},{18,26},{1... | collective-permute-start | bytes 196616 | tf_op jit(solution)/shard_map/ppermute | solution.py:46
  39.1 2.7 %collective-permute-start.16 = (bf16[1024,128]{1,0:T(8,128)(2,1)S(1)}, bf16[1024,128]{1,0:T(8,128)(2,1)S(1)}, u32[]{:S(2)}, u32[]{:S(2)}) collective-permute-start(bf16[1024,128]{1,0:T(8,128)(2,1)S(1)} %get-tuple-element.31), channel_id=1, source_target_pairs={{0,2},{2,0},{4,6},{6,4},{8,10},{10,8},{12,14},{14,12},{16,18},{18,... | collective-permute-start | bytes 786440 | tf_op jit(solution)/shard_map/ppermute | solution.py:53
  41.9 2.5 %collective-permute-start.17 = (f32[256,128]{1,0:T(8,128)S(1)}, f32[256,128]{1,0:T(8,128)S(1)}, u32[]{:S(2)}, u32[]{:S(2)}) collective-permute-start(f32[256,128]{1,0:T(8,128)S(1)} %convert_add_fusion), channel_id=1, source_target_pairs={{0,2},{2,0},{4,6},{6,4},{8,10},{10,8},{12,14},{14,12},{16,18},{18,... | collective-permute-start | bytes 393224 | tf_op jit(solution)/shard_map/ppermute | solution.py:53
  42.6 6.2 %collective-permute-start.20 = (bf16[512,128]{1,0:T(8,128)(2,1)S(1)}, bf16[512,128]{1,0:T(8,128)(2,1)S(1)}, u32[]{:S(2)}, u32[]{:S(2)}) collective-permute-start(bf16[512,128]{1,0:T(8,128)(2,1)S(1)} %constant_dynamic-slice_fusion), channel_id=1, source_target_pairs={{0,1},{1,0},{2,3},{3,2},{4,5},{5,4},{6,7},{7,6},{8,9},{9,8},{10,11... | collective-permute-start | bytes 393224 | tf_op jit(solution)/shard_map/ppermute | solution.py:63
  44.5 5.8 %collective-permute-start.18 = (bf16[256,128]{1,0:T(8,128)(2,1)S(1)}, bf16[256,128]{1,0:T(8,128)(2,1)S(1)}, u32[]{:S(2)}, u32[]{:S(2)}) collective-permute-start(bf16[256,128]{1,0:T(8,128)(2,1)S(1)} %add_convert_fusion), channel_id=1, source_target_pairs={{0,1},{1,0},{2,3},{3,2},{4,5},{5,4},{6,7},{7,6},{8,9},{9,8},{10,11... | collective-permute-start | bytes 196616 | tf_op jit(solution)/shard_map/ppermute | solution.py:63
  45.2 5.0 %collective-permute-start.19 = (bf16[256,128]{1,0:T(8,128)(2,1)S(1)}, bf16[256,128]{1,0:T(8,128)(2,1)S(1)}, u32[]{:S(2)}, u32[]{:S(2)}) collective-permute-start(bf16[256,128]{1,0:T(8,128)(2,1)S(1)} %add_convert_fusion), channel_id=1, source_target_pairs={{0,4},{1,5},{2,7},{3,6},{4,0},{5,1},{6,3},{7,2},{8,12},{9,13},{10,... | collective-permute-start | bytes 196616 | tf_op jit(solution)/shard_map/ppermute | solution.py:46
  50.2 1.4 %collective-permute-start.21 = (f32[1,256,128]{2,1,0:T(8,128)S(1)}, f32[1,256,128]{2,1,0:T(8,128)S(1)}, u32[]{:S(2)}, u32[]{:S(2)}) collective-permute-start(f32[1,256,128]{2,1,0:T(8,128)S(1)} %add_bitcast_fusion), channel_id=1, source_target_pairs={{0,2},{2,0},{4,6},{6,4},{8,10},{10,8},{12,14},{14,12},{16,18},{18,... | collective-permute-start | bytes 393224 | tf_op jit(solution)/shard_map/ppermute | solution.py:53

commit v10 on v9

--- a/solution.py
+++ b/solution.py
@@ -56,21 +56,6 @@
 def along_rep(block, distance):
     size = lax.axis_size("rep")
     return lax.ppermute(block, "rep", [(i, (i + distance) % size) for i in range(size)])
-
-
-def along_rep(block, distance):
-    size = lax.axis_size("rep")
-    return lax.ppermute(block, "rep", [(i, (i + distance) % size) for i in range(size)])
-
-
-def across_columns_and_rep(block, distance):
-    size = lax.axis_size("rep")
-    route = [
-        (device_of(z, x, c) * size + r, device_of(z, 1 - x, c) * size + (r + distance) % size)
-        for z, x, c in places(lax.axis_size("blk"))
-        for r in range(size)
-    ]
-    return lax.ppermute(block, ("blk", "rep"), route)
 
 
 def from_all_reps(block):
@@ -279,6 +264,7 @@
     slab_shape = jax.ShapeDtypeStruct((slab_rows, share_width), jnp.float32)
     sent_shape = jax.ShapeDtypeStruct((slab_rows, share_width), jnp.bfloat16)
     term_shape = jax.ShapeDtypeStruct((width, share_width), jnp.bfloat16)
+
     def add_slabs(first_slab, slabs, sums):
         operands = own_pieces + other_pieces + slabs
         aliases = {1 + len(operands) + target: target for target in range(len(sums))}

time: 52.7 us -> 52.7 us (level)
  no operation moved by 1% of the time
where the time goes in v10:
time: 52.7 us; the launch traced here: 52.5 us
  starting transfers between devices  21.7 us (41%)
  waiting for transfers between devices  17.1 us (32%)
  Pallas kernels  7.83 us (15%)
  local copies, waits for them, and re-layouts  2.48 us (5%)
  other arithmetic  1.16 us (2%)
  matrix products  1.15 us (2%)
  between operations  1.12 us (2%)
    ppermute x7, waiting for transfers between devices, along_ring(): return lax.ppermute(block, 'blk', route)  11.5 us
    ppermute x7, starting transfers between devices, along_ring(): return lax.ppermute(block, 'blk', route)  8.31 us
    ppermute x3, starting transfers between devices, across(): return lax.ppermute(block, ('blk', 'rep'), route)  5.88 us
    pallas_call x3, Pallas kernels, add_slabs(): pl.pallas_call(functools.partial(adding_kernel, plan, first_slab, len(sla...  5.03 us
    ppermute x4, starting transfers between devices, along_rep(): lax.ppermute(block, 'rep', [(i, (i + distance) % size) for i in range(siz...  4.48 us
    ppermute x8, starting transfers between devices, across_cores(): return lax.ppermute(block, 'blk', route)  2.98 us
    ppermute x8, waiting for transfers between devices, across_cores(): return lax.ppermute(block, 'blk', route)  2.59 us
    ppermute x4, waiting for transfers between devices, along_rep(): lax.ppermute(block, 'rep', [(i, (i + distance) % size) for i in range(siz...  1.81 us
  transfers between devices with their start and end apart: 22, of which 10 were waited for; matrix products, arithmetic and copies ran while one was open for 6% of the time, Pallas kernels for 10%

profile of v10, /device:TPU:0, one launch (start us, length us, event | category | flops | bytes accessed | tf_op | source)
XLA Modules:
  0.0 52.5 jit_solution(5069283628368211193)
XLA Ops:
  0.6 0.0 copy-start
  0.7 1.3 %scale.1.refs_4_ = bf16[1024,128]{1,0:T(8,128)(2,1)S(1)} custom-call(s32[8,128]{1,0:T(8,128)} %bitcast.67, bf16[1024,256]{1,0:T(8,128)(2,1)} %gradient_hbm.1), custom_call_target="tpu_custom_call" | custom-call | tf_op jit(solution)/shard_map/scale/pallas_call | solution.py:192
  2.0 0.0 copy-start.4
  2.0 3.0 %collective-permute-start.10 = (bf16[1024,128]{1,0:T(8,128)(2,1)S(1)}, bf16[1024,128]{1,0:T(8,128)(2,1)S(1)}, u32[]{:S(2)}, u32[]{:S(2)}) collective-permute-start(bf16[1024,128]{1,0:T(8,128)(2,1)S(1)} %scale.1.refs_4_), channel_id=1, source_target_pairs={{0,4},{2,6},{8,0},{10,2},{16,8},{18,10},{24,16},{26,18},{28,24},{3... | collective-permute-start | bytes 786440 | tf_op jit(solution)/shard_map/ppermute | solution.py:35
  5.0 0.2 collective-permute-start.6
  5.1 0.7 %copy-done.5 = s32[1,8]{1,0:T(1,128)S(1)} copy-done((s32[1,8]{1,0:T(1,128)S(1)}, s32[1,8]{1,0:T(1,128)}, u32[]{:S(2)}) %copy-start.5) | copy-done | bytes 56
  5.8 0.1 copy.13
  5.9 0.1 reshape_squeeze.6
  6.0 0.1 pad_add_fusion
  6.0 0.1 dynamic_slice.15
  6.1 0.2 payload.1
  6.3 2.0 %collective-permute-start.1 = (bf16[1152,128]{1,0:T(8,128)(2,1)S(1)}, bf16[1152,128]{1,0:T(8,128)(2,1)}, u32[]{:S(2)}, u32[]{:S(2)}) collective-permute-start(bf16[1152,128]{1,0:T(8,128)(2,1)S(1)} %get-tuple-element.21), channel_id=1, source_target_pairs={{0,1},{1,0},{2,3},{3,2},{4,5},{5,4},{6,7},{7,6},{8,9},{9,8},{10,11... | collective-permute-start | bytes 884744 | tf_op jit(solution)/shard_map/ppermute | solution.py:58
  8.3 0.1 collective-permute-start
  8.4 0.2 collective-permute-start.3
  8.6 4.2 %collective-permute-done.6.refs_5_ = bf16[1024,128]{1,0:T(8,128)(2,1)S(1)} collective-permute-done((bf16[1024,128]{1,0:T(8,128)(2,1)S(1)}, bf16[1024,128]{1,0:T(8,128)(2,1)S(1)}, u32[]{:S(2)}, u32[]{:S(2)}) %collective-permute-start.6) | collective-permute-done | bytes 262176 | tf_op jit(solution)/shard_map/ppermute | solution.py:35
  12.7 0.4 collective-permute-start.7
  13.2 0.1 reshape.60
  13.5 0.0 collective-permute-done.refs_2_
  13.5 0.1 collective-permute-start.4
  13.6 0.0 collective-permute-done.10.refs_6_
  13.6 1.6 %collective-permute-start.11 = (bf16[1024,128]{1,0:T(8,128)(2,1)S(1)}, bf16[1024,128]{1,0:T(8,128)(2,1)}, u32[]{:S(2)}, u32[]{:S(2)}) collective-permute-start(bf16[1024,128]{1,0:T(8,128)(2,1)S(1)} %collective-permute-done.10.refs_6_), channel_id=1, source_target_pairs={{0,4},{2,6},{8,0},{10,2},{16,8},{18,10},{24,16},{26,18},{28,24},{3... | collective-permute-start | bytes 786440 | tf_op jit(solution)/shard_map/ppermute | solution.py:35
  15.2 4.5 %collective-permute-done.7.refs_4_ = bf16[1024,128]{1,0:T(8,128)(2,1)S(1)} collective-permute-done((bf16[1024,128]{1,0:T(8,128)(2,1)S(1)}, bf16[1024,128]{1,0:T(8,128)(2,1)S(1)}, u32[]{:S(2)}, u32[]{:S(2)}) %collective-permute-start.7) | collective-permute-done | bytes 262176 | tf_op jit(solution)/shard_map/ppermute | solution.py:35
  19.7 0.7 %collective-permute-start.8 = (bf16[1024,128]{1,0:T(8,128)(2,1)S(1)}, bf16[1024,128]{1,0:T(8,128)(2,1)}, u32[]{:S(2)}, u32[]{:S(2)}) collective-permute-start(bf16[1024,128]{1,0:T(8,128)(2,1)S(1)} %collective-permute-done.7.refs_4_), channel_id=1, source_target_pairs={{0,8},{2,10},{8,16},{10,18},{16,24},{18,26},{24,28},{26,30},{28,20... | collective-permute-start | bytes 786440 | tf_op jit(solution)/shard_map/ppermute | solution.py:35
  20.5 0.1 reshape.62
  20.6 0.0 collective-permute-done.3.refs_5_
  20.6 0.0 collective-permute-start.5
  20.6 0.0 collective-permute-done.1
  20.6 1.0 %fusion.7 = (bf16[576,128]{1,0:T(8,128)(2,1)S(1)}, bf16[576,128]{1,0:T(8,128)(2,1)S(1)}) fusion(bf16[1152,128]{1,0:T(8,128)(2,1)} %collective-permute-done.1), kind=kLoop, calls=%fused_computation.27 | loop fusion | bytes 589824 | tf_op jit(solution)/shard_map/slice | solution.py:232
  21.6 0.6 %collective-permute-start.2 = (bf16[576,128]{1,0:T(8,128)(2,1)S(1)}, bf16[576,128]{1,0:T(8,128)(2,1)S(1)}, u32[]{:S(2)}, u32[]{:S(2)}) collective-permute-start(bf16[576,128]{1,0:T(8,128)(2,1)S(1)} %get-tuple-element.36), channel_id=1, source_target_pairs={{0,2},{2,0},{4,6},{6,4},{8,10},{10,8},{12,14},{14,12},{16,18},{18,... | collective-permute-start | bytes 442376 | tf_op jit(solution)/shard_map/ppermute | solution.py:53
  22.2 0.3 collective-permute-done.11.refs_5_
  22.4 1.6 %collective-permute-start.12 = (bf16[1024,128]{1,0:T(8,128)(2,1)}, bf16[1024,128]{1,0:T(8,128)(2,1)S(1)}, u32[]{:S(2)}, u32[]{:S(2)}) collective-permute-start(bf16[1024,128]{1,0:T(8,128)(2,1)} %collective-permute-done.11.refs_5_), channel_id=1, source_target_pairs={{0,4},{2,6},{8,0},{10,2},{16,8},{18,10},{24,16},{26,18},{28,24},{3... | collective-permute-start | bytes 786440 | tf_op jit(solution)/shard_map/ppermute | solution.py:35
  24.0 2.2 %collective-permute-done.8.refs_6_ = bf16[1024,128]{1,0:T(8,128)(2,1)} collective-permute-done((bf16[1024,128]{1,0:T(8,128)(2,1)S(1)}, bf16[1024,128]{1,0:T(8,128)(2,1)}, u32[]{:S(2)}, u32[]{:S(2)}) %collective-permute-start.8) | collective-permute-done | bytes 262176 | tf_op jit(solution)/shard_map/ppermute | solution.py:35
  26.2 0.7 %collective-permute-start.9 = (bf16[1024,128]{1,0:T(8,128)(2,1)}, bf16[1024,128]{1,0:T(8,128)(2,1)S(1)}, u32[]{:S(2)}, u32[]{:S(2)}) collective-permute-start(bf16[1024,128]{1,0:T(8,128)(2,1)} %collective-permute-done.8.refs_6_), channel_id=1, source_target_pairs={{0,8},{2,10},{8,16},{10,18},{16,24},{18,26},{24,28},{26,30},{28,20... | collective-permute-start | bytes 786440 | tf_op jit(solution)/shard_map/ppermute | solution.py:35
  26.9 0.1 reshape.64
  27.1 0.1 reshape.66
  27.1 0.1 concatenate.7.table_ref
  27.3 1.6 %add_slabs.3 = (f32[1024,128]{1,0:T(8,128)S(1)}, f32[1024,128]{1,0:T(8,128)S(1)}) custom-call(s32[306]{0:T(512)S(1)} %concatenate.7.table_ref, bf16[576,128]{1,0:T(8,128)(2,1)S(1)} %get-tuple-element.39.refs_0_, bf16[576,128]{1,0:T(8,128)(2,1)S(1)} %get-tuple-element.37.refs_1_, bf16[576,128]{1,0:T(8,128)(2,1)S(1)} %collective-permute-done.refs_2_, ...), custom_call_target="tpu_custom_call" | custom-call | flops 1 | bytes 1 | tf_op jit(solution)/shard_map/add_slabs/pallas_call | solution.py:272
  28.9 2.3 %add_slabs.4 = (f32[1024,128]{1,0:T(8,128)S(1)}, f32[1024,128]{1,0:T(8,128)S(1)}) custom-call(s32[306]{0:T(512)S(1)} %concatenate.7.table_ref, bf16[576,128]{1,0:T(8,128)(2,1)S(1)} %get-tuple-element.39.refs_0_, bf16[576,128]{1,0:T(8,128)(2,1)S(1)} %get-tuple-element.37.refs_1_, ...), custom_call_target="tpu_custom_call", output_to_operand_aliasing={{0}: (8, {}), {1}: (9, {})} | custom-call | flops 1 | bytes 1 | tf_op jit(solution)/shard_map/add_slabs/pallas_call | solution.py:272
  31.2 1.1 %add_slabs.5 = (f32[1024,128]{1,0:T(8,128)S(1)}, f32[1024,128]{1,0:T(8,128)S(1)}) custom-call(s32[306]{0:T(512)S(1)} %concatenate.7.table_ref, bf16[576,128]{1,0:T(8,128)(2,1)S(1)} %get-tuple-element.39.refs_0_, bf16[576,128]{1,0:T(8,128)(2,1)S(1)} %get-tuple-element.37.refs_1_, ...), custom_call_target="tpu_custom_call", output_to_operand_aliasing={{0}: (6, {}), {1}: (7, {})} | custom-call | flops 1 | bytes 1 | tf_op jit(solution)/shard_map/add_slabs/pallas_call | solution.py:272
  32.3 0.0 collective-permute-done.5.refs_7_
  32.3 0.4 collective-permute-done.9.refs_8_
  32.8 1.3 %last_slab.1 = (f32[1024,128]{1,0:T(8,128)S(1)}, bf16[1024,128]{1,0:T(8,128)(2,1)S(1)}, bf16[256,128]{1,0:T(8,128)(2,1)S(1)}) custom-call(s32[306]{0:T(512)S(1)} %concatenate.7.table_ref, bf16[576,128]{1,0:T(8,128)(2,1)S(1)} %get-tuple-element.39.refs_0_, bf16[576,128]{1,0:T(8,128)(2,1)S(1)} %get-tuple-element.37.refs_1_, ...), custom_call_target="tpu_custom_call" | custom-call | flops 1 | bytes 1 | tf_op jit(solution)/shard_map/last_slab/pallas_call | solution.py:287
  34.1 0.1 collective-permute-start.13
  34.2 1.2 %collective-permute-done.13 = bf16[256,128]{1,0:T(8,128)(2,1)S(1)} collective-permute-done((bf16[256,128]{1,0:T(8,128)(2,1)S(1)}, bf16[256,128]{1,0:T(8,128)(2,1)S(1)}, u32[]{:S(2)}, u32[]{:S(2)}) %collective-permute-start.13) | collective-permute-done | bytes 65568 | tf_op jit(solution)/shard_map/ppermute | solution.py:53
  35.5 2.9 %collective-permute-start.14 = (bf16[256,128]{1,0:T(8,128)(2,1)S(1)}, bf16[256,128]{1,0:T(8,128)(2,1)S(1)}, u32[]{:S(2)}, u32[]{:S(2)}) collective-permute-start(bf16[256,128]{1,0:T(8,128)(2,1)S(1)} %add_convert_fusion.1), channel_id=1, source_target_pairs={{0,24},{1,25},{2,18},{3,19},{4,28},{5,29},{6,22},{7,23},{8,16},{9,... | collective-permute-start | bytes 196616 | tf_op jit(solution)/shard_map/ppermute | solution.py:46
  38.4 0.7 %collective-permute-start.15 = (bf16[256,128]{1,0:T(8,128)(2,1)S(1)}, bf16[256,128]{1,0:T(8,128)(2,1)S(1)}, u32[]{:S(2)}, u32[]{:S(2)}) collective-permute-start(bf16[256,128]{1,0:T(8,128)(2,1)S(1)} %add_convert_fusion.1), channel_id=1, source_target_pairs={{2,10},{3,11},{6,14},{7,15},{10,2},{11,3},{14,6},{15,7},{18,26},{1... | collective-permute-start | bytes 196616 | tf_op jit(solution)/shard_map/ppermute | solution.py:46
  39.1 1.5 %collective-permute-start.16 = (bf16[1024,128]{1,0:T(8,128)(2,1)S(1)}, bf16[1024,128]{1,0:T(8,128)(2,1)S(1)}, u32[]{:S(2)}, u32[]{:S(2)}) collective-permute-start(bf16[1024,128]{1,0:T(8,128)(2,1)S(1)} %get-tuple-element.31), channel_id=1, source_target_pairs={{0,2},{2,0},{4,6},{6,4},{8,10},{10,8},{12,14},{14,12},{16,18},{18,... | collective-permute-start | bytes 786440 | tf_op jit(solution)/shard_map/ppermute | solution.py:53
  40.5 1.1 %collective-permute-done.14 = bf16[256,128]{1,0:T(8,128)(2,1)S(1)} collective-permute-done((bf16[256,128]{1,0:T(8,128)(2,1)S(1)}, bf16[256,128]{1,0:T(8,128)(2,1)S(1)}, u32[]{:S(2)}, u32[]{:S(2)}) %collective-permute-start.14) | collective-permute-done | bytes 65568 | tf_op jit(solution)/shard_map/ppermute | solution.py:46
  41.7 0.0 collective-permute-done.15
  41.7 0.0 collective-permute-done.16
  41.7 0.2 multiply_convert_fusion
  41.9 0.7 %collective-permute-start.17 = (f32[256,128]{1,0:T(8,128)S(1)}, f32[256,128]{1,0:T(8,128)S(1)}, u32[]{:S(2)}, u32[]{:S(2)}) collective-permute-start(f32[256,128]{1,0:T(8,128)S(1)} %convert_add_fusion), channel_id=1, source_target_pairs={{0,2},{2,0},{4,6},{6,4},{8,10},{10,8},{12,14},{14,12},{16,18},{18,... | collective-permute-start | bytes 393224 | tf_op jit(solution)/shard_map/ppermute | solution.py:53
  42.6 1.6 %collective-permute-start.20 = (bf16[512,128]{1,0:T(8,128)(2,1)S(1)}, bf16[512,128]{1,0:T(8,128)(2,1)S(1)}, u32[]{:S(2)}, u32[]{:S(2)}) collective-permute-start(bf16[512,128]{1,0:T(8,128)(2,1)S(1)} %constant_dynamic-slice_fusion), channel_id=1, source_target_pairs={{0,1},{1,0},{2,3},{3,2},{4,5},{5,4},{6,7},{7,6},{8,9},{9,8},{10,11... | collective-permute-start | bytes 393224 | tf_op jit(solution)/shard_map/ppermute | solution.py:58
  44.2 0.2 fusion.1
  44.4 0.0 collective-permute-done.17
  44.5 0.7 %collective-permute-start.18 = (bf16[256,128]{1,0:T(8,128)(2,1)S(1)}, bf16[256,128]{1,0:T(8,128)(2,1)S(1)}, u32[]{:S(2)}, u32[]{:S(2)}) collective-permute-start(bf16[256,128]{1,0:T(8,128)(2,1)S(1)} %add_convert_fusion), channel_id=1, source_target_pairs={{0,1},{1,0},{2,3},{3,2},{4,5},{5,4},{6,7},{7,6},{8,9},{9,8},{10,11... | collective-permute-start | bytes 196616 | tf_op jit(solution)/shard_map/ppermute | solution.py:58
  45.2 2.3 %collective-permute-start.19 = (bf16[256,128]{1,0:T(8,128)(2,1)S(1)}, bf16[256,128]{1,0:T(8,128)(2,1)S(1)}, u32[]{:S(2)}, u32[]{:S(2)}) collective-permute-start(bf16[256,128]{1,0:T(8,128)(2,1)S(1)} %add_convert_fusion), channel_id=1, source_target_pairs={{0,4},{1,5},{2,7},{3,6},{4,0},{5,1},{6,3},{7,2},{8,12},{9,13},{10,... | collective-permute-start | bytes 196616 | tf_op jit(solution)/shard_map/ppermute | solution.py:46
  47.5 1.3 %collective-permute-done.20 = bf16[512,128]{1,0:T(8,128)(2,1)S(1)} collective-permute-done((bf16[512,128]{1,0:T(8,128)(2,1)S(1)}, bf16[512,128]{1,0:T(8,128)(2,1)S(1)}, u32[]{:S(2)}, u32[]{:S(2)}) %collective-permute-start.20) | collective-permute-done | bytes 131104 | tf_op jit(solution)/shard_map/ppermute | solution.py:58
  48.8 0.9 %fusion = bf16[512,256]{1,0:T(8,128)(2,1)} fusion(f32[512,256]{1,0:T(8,128)S(1)} %fusion.1, bf16[512,128]{1,0:T(8,128)(2,1)S(1)} %collective-permute-done.20, bf16[256,256]{1,0:T(8,128)(2,1)S(1)} %copy-done, s32[]{:T(128)S(6)} %select_n.500), kind=kOutput, calls=%fused_computation.1 | convolution fusion | flops 33816576 | bytes 983044 | tf_op jit(solution)/shard_map/dot_general | solution.py:325
  49.8 0.5 collective-permute-done.18
  50.2 0.0 collective-permute-done.19
  50.2 0.1 collective-permute-start.21
  50.3 1.3 %collective-permute-done.21 = f32[1,256,128]{2,1,0:T(8,128)S(1)} collective-permute-done((f32[1,256,128]{2,1,0:T(8,128)S(1)}, f32[1,256,128]{2,1,0:T(8,128)S(1)}, u32[]{:S(2)}, u32[]{:S(2)}) %collective-permute-start.21) | collective-permute-done | bytes 131104 | tf_op jit(solution)/shard_map/ppermute | solution.py:53
  51.7 0.7 %broadcast_multiply_fusion = f32[256,256]{1,0:T(8,128)} fusion(f32[256,256]{1,0:T(8,128)S(1)} %bitcast_dynamic-update-slice_fusion), kind=kLoop, calls=%fused_computation.5 | loop fusion | flops 65536 | bytes 524288 | tf_op jit(solution)/shard_map/mul | solution.py:339
  (35 shorter events, 0.3 us)
Async XLA Ops:
  0.6 43.6 %copy-start = (bf16[256,256]{1,0:T(8,128)(2,1)S(1)}, bf16[256,256]{1,0:T(8,128)(2,1)}, u32[]{:S(2)}) copy-start(bf16[256,256]{1,0:T(8,128)(2,1)} %param.9) | copy-start | bytes 393220
  0.6 5.5 %copy-start.1 = (s32[1,8,8,16,128]{4,3,2,1,0:T(8,128)S(1)}, s32[1,8,8,16,128]{4,3,2,1,0:T(8,128)}, u32[]{:S(2)}) copy-start(s32[1,8,8,16,128]{4,3,2,1,0:T(8,128)} %param.10) | copy-start | bytes 1572868
  0.7 4.5 %copy-start.3 = (s32[1024]{0:T(1024)S(1)}, s32[1024]{0:T(1024)}, u32[]{:S(2)}) copy-start(s32[1024]{0:T(1024)} %param.13) | copy-start | bytes 12292
  0.7 5.5 %copy-start.2 = (bf16[512,256]{1,0:T(8,128)(2,1)S(1)}, bf16[512,256]{1,0:T(8,128)(2,1)}, u32[]{:S(2)}) copy-start(bf16[512,256]{1,0:T(8,128)(2,1)} %features_ref) | copy-start | bytes 786436
  2.0 3.9 %copy-start.4 = (s32[1,8,2,8]{3,2,1,0:T(2,128)S(1)}, s32[1,8,2,8]{3,2,1,0:T(2,128)}, u32[]{:S(2)}) copy-start(s32[1,8,2,8]{3,2,1,0:T(2,128)} %param.11) | copy-start | bytes 1540
  2.0 11.6 %collective-permute-start.10 = (bf16[1024,128]{1,0:T(8,128)(2,1)S(1)}, bf16[1024,128]{1,0:T(8,128)(2,1)S(1)}, u32[]{:S(2)}, u32[]{:S(2)}) collective-permute-start(bf16[1024,128]{1,0:T(8,128)(2,1)S(1)} %scale.1.refs_4_), channel_id=1, source_target_pairs={{0,4},{2,6},{8,0},{10,2},{16,8},{18,10},{24,16},{26,18},{28,24},{3... | collective-permute-start | bytes 786440 | tf_op jit(solution)/shard_map/ppermute | solution.py:35
  5.0 7.8 %collective-permute-start.6 = (bf16[1024,128]{1,0:T(8,128)(2,1)S(1)}, bf16[1024,128]{1,0:T(8,128)(2,1)S(1)}, u32[]{:S(2)}, u32[]{:S(2)}) collective-permute-start(bf16[1024,128]{1,0:T(8,128)(2,1)S(1)} %scale.1.refs_4_), channel_id=1, source_target_pairs={{0,8},{2,10},{8,16},{10,18},{16,24},{18,26},{24,28},{26,30},{28,20... | collective-permute-start | bytes 786440 | tf_op jit(solution)/shard_map/ppermute | solution.py:35
  5.1 0.7 %copy-start.5 = (s32[1,8]{1,0:T(1,128)S(1)}, s32[1,8]{1,0:T(1,128)}, u32[]{:S(2)}) copy-start(s32[1,8]{1,0:T(1,128)} %param.12) | copy-start | bytes 100
  6.3 14.3 %collective-permute-start.1 = (bf16[1152,128]{1,0:T(8,128)(2,1)S(1)}, bf16[1152,128]{1,0:T(8,128)(2,1)}, u32[]{:S(2)}, u32[]{:S(2)}) collective-permute-start(bf16[1152,128]{1,0:T(8,128)(2,1)S(1)} %get-tuple-element.21), channel_id=1, source_target_pairs={{0,1},{1,0},{2,3},{3,2},{4,5},{5,4},{6,7},{7,6},{8,9},{9,8},{10,11... | collective-permute-start | bytes 884744 | tf_op jit(solution)/shard_map/ppermute | solution.py:58
  8.3 5.2 %collective-permute-start = (bf16[576,128]{1,0:T(8,128)(2,1)S(1)}, bf16[576,128]{1,0:T(8,128)(2,1)S(1)}, u32[]{:S(2)}, u32[]{:S(2)}) collective-permute-start(bf16[576,128]{1,0:T(8,128)(2,1)S(1)} %get-tuple-element.38), channel_id=1, source_target_pairs={{0,2},{2,0},{4,6},{6,4},{8,10},{10,8},{12,14},{14,12},{16,18},{18,... | collective-permute-start | bytes 442376 | tf_op jit(solution)/shard_map/ppermute | solution.py:53
  8.4 12.2 %collective-permute-start.3 = (bf16[256,512]{1,0:T(8,128)(2,1)S(1)}, bf16[256,512]{1,0:T(8,128)(2,1)S(1)}, u32[]{:S(2)}, u32[]{:S(2)}) collective-permute-start(bf16[256,512]{1,0:T(8,128)(2,1)S(1)} %get-tuple-element.22.refs_4_), channel_id=1, source_target_pairs={{0,1},{1,0},{2,3},{3,2},{4,5},{5,4},{6,7},{7,6},{8,9},{9,8},{10,11... | collective-permute-start | bytes 786440 | tf_op jit(solution)/shard_map/ppermute | solution.py:58
  12.7 7.0 %collective-permute-start.7 = (bf16[1024,128]{1,0:T(8,128)(2,1)S(1)}, bf16[1024,128]{1,0:T(8,128)(2,1)S(1)}, u32[]{:S(2)}, u32[]{:S(2)}) collective-permute-start(bf16[1024,128]{1,0:T(8,128)(2,1)S(1)} %collective-permute-done.6.refs_5_), channel_id=1, source_target_pairs={{0,8},{2,10},{8,16},{10,18},{16,24},{18,26},{24,28},{26,30},{28,20... | collective-permute-start | bytes 786440 | tf_op jit(solution)/shard_map/ppermute | solution.py:35
  13.5 18.9 %collective-permute-start.4 = (bf16[256,512]{1,0:T(8,128)(2,1)S(1)}, bf16[256,512]{1,0:T(8,128)(2,1)S(1)}, u32[]{:S(2)}, u32[]{:S(2)}) collective-permute-start(bf16[256,512]{1,0:T(8,128)(2,1)S(1)} %get-tuple-element.22.refs_4_), channel_id=1, source_target_pairs={{0,2},{2,0},{4,6},{6,4},{8,10},{10,8},{12,14},{14,12},{16,18},{18,... | collective-permute-start | bytes 786440 | tf_op jit(solution)/shard_map/ppermute | solution.py:53
  13.6 8.8 %collective-permute-start.11 = (bf16[1024,128]{1,0:T(8,128)(2,1)S(1)}, bf16[1024,128]{1,0:T(8,128)(2,1)}, u32[]{:S(2)}, u32[]{:S(2)}) collective-permute-start(bf16[1024,128]{1,0:T(8,128)(2,1)S(1)} %collective-permute-done.10.refs_6_), channel_id=1, source_target_pairs={{0,4},{2,6},{8,0},{10,2},{16,8},{18,10},{24,16},{26,18},{28,24},{3... | collective-permute-start | bytes 786440 | tf_op jit(solution)/shard_map/ppermute | solution.py:35
  19.7 6.5 %collective-permute-start.8 = (bf16[1024,128]{1,0:T(8,128)(2,1)S(1)}, bf16[1024,128]{1,0:T(8,128)(2,1)}, u32[]{:S(2)}, u32[]{:S(2)}) collective-permute-start(bf16[1024,128]{1,0:T(8,128)(2,1)S(1)} %collective-permute-done.7.refs_4_), channel_id=1, source_target_pairs={{0,8},{2,10},{8,16},{10,18},{16,24},{18,26},{24,28},{26,30},{28,20... | collective-permute-start | bytes 786440 | tf_op jit(solution)/shard_map/ppermute | solution.py:35
  20.6 11.8 %collective-permute-start.5 = (bf16[256,512]{1,0:T(8,128)(2,1)S(1)}, bf16[256,512]{1,0:T(8,128)(2,1)S(1)}, u32[]{:S(2)}, u32[]{:S(2)}) collective-permute-start(bf16[256,512]{1,0:T(8,128)(2,1)S(1)} %collective-permute-done.3.refs_5_), channel_id=1, source_target_pairs={{0,2},{2,0},{4,6},{6,4},{8,10},{10,8},{12,14},{14,12},{16,18},{18,... | collective-permute-start | bytes 786440 | tf_op jit(solution)/shard_map/ppermute | solution.py:53
  21.6 5.5 %collective-permute-start.2 = (bf16[576,128]{1,0:T(8,128)(2,1)S(1)}, bf16[576,128]{1,0:T(8,128)(2,1)S(1)}, u32[]{:S(2)}, u32[]{:S(2)}) collective-permute-start(bf16[576,128]{1,0:T(8,128)(2,1)S(1)} %get-tuple-element.36), channel_id=1, source_target_pairs={{0,2},{2,0},{4,6},{6,4},{8,10},{10,8},{12,14},{14,12},{16,18},{18,... | collective-permute-start | bytes 442376 | tf_op jit(solution)/shard_map/ppermute | solution.py:53
  22.4 8.7 %collective-permute-start.12 = (bf16[1024,128]{1,0:T(8,128)(2,1)}, bf16[1024,128]{1,0:T(8,128)(2,1)S(1)}, u32[]{:S(2)}, u32[]{:S(2)}) collective-permute-start(bf16[1024,128]{1,0:T(8,128)(2,1)} %collective-permute-done.11.refs_5_), channel_id=1, source_target_pairs={{0,4},{2,6},{8,0},{10,2},{16,8},{18,10},{24,16},{26,18},{28,24},{3... | collective-permute-start | bytes 786440 | tf_op jit(solution)/shard_map/ppermute | solution.py:35
  26.2 6.6 %collective-permute-start.9 = (bf16[1024,128]{1,0:T(8,128)(2,1)}, bf16[1024,128]{1,0:T(8,128)(2,1)S(1)}, u32[]{:S(2)}, u32[]{:S(2)}) collective-permute-start(bf16[1024,128]{1,0:T(8,128)(2,1)} %collective-permute-done.8.refs_6_), channel_id=1, source_target_pairs={{0,8},{2,10},{8,16},{10,18},{16,24},{18,26},{24,28},{26,30},{28,20... | collective-permute-start | bytes 786440 | tf_op jit(solution)/shard_map/ppermute | solution.py:35
  34.1 1.3 %collective-permute-start.13 = (bf16[256,128]{1,0:T(8,128)(2,1)S(1)}, bf16[256,128]{1,0:T(8,128)(2,1)S(1)}, u32[]{:S(2)}, u32[]{:S(2)}) collective-permute-start(bf16[256,128]{1,0:T(8,128)(2,1)S(1)} %get-tuple-element.29), channel_id=1, source_target_pairs={{0,2},{2,0},{4,6},{6,4},{8,10},{10,8},{12,14},{14,12},{16,18},{18,... | collective-permute-start | bytes 196616 | tf_op jit(solution)/shard_map/ppermute | solution.py:53
  35.5 6.2 %collective-permute-start.14 = (bf16[256,128]{1,0:T(8,128)(2,1)S(1)}, bf16[256,128]{1,0:T(8,128)(2,1)S(1)}, u32[]{:S(2)}, u32[]{:S(2)}) collective-permute-start(bf16[256,128]{1,0:T(8,128)(2,1)S(1)} %add_convert_fusion.1), channel_id=1, source_target_pairs={{0,24},{1,25},{2,18},{3,19},{4,28},{5,29},{6,22},{7,23},{8,16},{9,... | collective-permute-start | bytes 196616 | tf_op jit(solution)/shard_map/ppermute | solution.py:46
  38.4 3.3 %collective-permute-start.15 = (bf16[256,128]{1,0:T(8,128)(2,1)S(1)}, bf16[256,128]{1,0:T(8,128)(2,1)S(1)}, u32[]{:S(2)}, u32[]{:S(2)}) collective-permute-start(bf16[256,128]{1,0:T(8,128)(2,1)S(1)} %add_convert_fusion.1), channel_id=1, source_target_pairs={{2,10},{3,11},{6,14},{7,15},{10,2},{11,3},{14,6},{15,7},{18,26},{1... | collective-permute-start | bytes 196616 | tf_op jit(solution)/shard_map/ppermute | solution.py:46
  39.1 2.7 %collective-permute-start.16 = (bf16[1024,128]{1,0:T(8,128)(2,1)S(1)}, bf16[1024,128]{1,0:T(8,128)(2,1)S(1)}, u32[]{:S(2)}, u32[]{:S(2)}) collective-permute-start(bf16[1024,128]{1,0:T(8,128)(2,1)S(1)} %get-tuple-element.31), channel_id=1, source_target_pairs={{0,2},{2,0},{4,6},{6,4},{8,10},{10,8},{12,14},{14,12},{16,18},{18,... | collective-permute-start | bytes 786440 | tf_op jit(solution)/shard_map/ppermute | solution.py:53
  41.9 2.5 %collective-permute-start.17 = (f32[256,128]{1,0:T(8,128)S(1)}, f32[256,128]{1,0:T(8,128)S(1)}, u32[]{:S(2)}, u32[]{:S(2)}) collective-permute-start(f32[256,128]{1,0:T(8,128)S(1)} %convert_add_fusion), channel_id=1, source_target_pairs={{0,2},{2,0},{4,6},{6,4},{8,10},{10,8},{12,14},{14,12},{16,18},{18,... | collective-permute-start | bytes 393224 | tf_op jit(solution)/shard_map/ppermute | solution.py:53
  42.6 6.2 %collective-permute-start.20 = (bf16[512,128]{1,0:T(8,128)(2,1)S(1)}, bf16[512,128]{1,0:T(8,128)(2,1)S(1)}, u32[]{:S(2)}, u32[]{:S(2)}) collective-permute-start(bf16[512,128]{1,0:T(8,128)(2,1)S(1)} %constant_dynamic-slice_fusion), channel_id=1, source_target_pairs={{0,1},{1,0},{2,3},{3,2},{4,5},{5,4},{6,7},{7,6},{8,9},{9,8},{10,11... | collective-permute-start | bytes 393224 | tf_op jit(solution)/shard_map/ppermute | solution.py:58
  44.5 5.8 %collective-permute-start.18 = (bf16[256,128]{1,0:T(8,128)(2,1)S(1)}, bf16[256,128]{1,0:T(8,128)(2,1)S(1)}, u32[]{:S(2)}, u32[]{:S(2)}) collective-permute-start(bf16[256,128]{1,0:T(8,128)(2,1)S(1)} %add_convert_fusion), channel_id=1, source_target_pairs={{0,1},{1,0},{2,3},{3,2},{4,5},{5,4},{6,7},{7,6},{8,9},{9,8},{10,11... | collective-permute-start | bytes 196616 | tf_op jit(solution)/shard_map/ppermute | solution.py:58
  45.2 5.0 %collective-permute-start.19 = (bf16[256,128]{1,0:T(8,128)(2,1)S(1)}, bf16[256,128]{1,0:T(8,128)(2,1)S(1)}, u32[]{:S(2)}, u32[]{:S(2)}) collective-permute-start(bf16[256,128]{1,0:T(8,128)(2,1)S(1)} %add_convert_fusion), channel_id=1, source_target_pairs={{0,4},{1,5},{2,7},{3,6},{4,0},{5,1},{6,3},{7,2},{8,12},{9,13},{10,... | collective-permute-start | bytes 196616 | tf_op jit(solution)/shard_map/ppermute | solution.py:46
  50.2 1.4 %collective-permute-start.21 = (f32[1,256,128]{2,1,0:T(8,128)S(1)}, f32[1,256,128]{2,1,0:T(8,128)S(1)}, u32[]{:S(2)}, u32[]{:S(2)}) collective-permute-start(f32[1,256,128]{2,1,0:T(8,128)S(1)} %add_bitcast_fusion), channel_id=1, source_target_pairs={{0,2},{2,0},{4,6},{6,4},{8,10},{10,8},{12,14},{14,12},{16,18},{18,... | collective-permute-start | bytes 393224 | tf_op jit(solution)/shard_map/ppermute | solution.py:53

commit v11 on v10

--- a/solution.py
+++ b/solution.py
@@ -326,7 +326,7 @@
             part, side, (((1,), (1,)), ((), ())), preferred_element_type=jnp.float32
         )
     input_grad = result.astype(jnp.bfloat16)
-    shares = jnp.stack(shares)
+    shares = jnp.stack(shares).astype(jnp.bfloat16)
     shares, input_grad = lax.optimization_barrier((shares, input_grad))
     others = across_cores(shares)
     own_share = jnp.where(core == 0, shares[0], others[0])
@@ -335,7 +335,7 @@
     for d in range(rep_size):
         columns_at = ((rep_index - d) % rep_size) * share_width
         share = other_shares[d - 1] if d else own_share
-        weight_grad = lax.dynamic_update_slice_in_dim(weight_grad, share, columns_at, 1)
+        weight_grad = lax.dynamic_update_slice_in_dim(weight_grad, wide(share), columns_at, 1)
     weight_grad = weight_grad * (1.0 / math.sqrt(slab_rows * blk_size))
     return (input_grad, weight_grad)
 

time: 52.7 us -> 52.6 us (level)
  no operation moved by 1% of the time
where the time goes in v11:
time: 52.6 us; the launch traced here: 52.4 us
  starting transfers between devices  21.7 us (41%)
  waiting for transfers between devices  17 us (32%)
  Pallas kernels  7.83 us (15%)
  local copies, waits for them, and re-layouts  2.48 us (5%)
  other arithmetic  1.16 us (2%)
  matrix products  1.14 us (2%)
  between operations  1.12 us (2%)
    ppermute x7, waiting for transfers between devices, along_ring(): return lax.ppermute(block, 'blk', route)  11.5 us
    ppermute x7, starting transfers between devices, along_ring(): return lax.ppermute(block, 'blk', route)  8.31 us
    ppermute x3, starting transfers between devices, across(): return lax.ppermute(block, ('blk', 'rep'), route)  5.89 us
    pallas_call x3, Pallas kernels, add_slabs(): pl.pallas_call(functools.partial(adding_kernel, plan, first_slab, len(sla...  5.03 us
    ppermute x4, starting transfers between devices, along_rep(): lax.ppermute(block, 'rep', [(i, (i + distance) % size) for i in range(siz...  4.49 us
    ppermute x8, starting transfers between devices, across_cores(): return lax.ppermute(block, 'blk', route)  2.98 us
    ppermute x8, waiting for transfers between devices, across_cores(): return lax.ppermute(block, 'blk', route)  2.5 us
    ppermute x4, waiting for transfers between devices, along_rep(): lax.ppermute(block, 'rep', [(i, (i + distance) % size) for i in range(siz...  1.8 us
  transfers between devices with their start and end apart: 22, of which 10 were waited for; matrix products, arithmetic and copies ran while one was open for 6% of the time, Pallas kernels for 10%

profile of v11, /device:TPU:0, one launch (start us, length us, event | category | flops | bytes accessed | tf_op | source)
XLA Modules:
  0.0 52.4 jit_solution(1719824680129751693)
XLA Ops:
  0.6 0.0 copy-start
  0.7 1.3 %scale.1.refs_4_ = bf16[1024,128]{1,0:T(8,128)(2,1)S(1)} custom-call(s32[8,128]{1,0:T(8,128)} %bitcast.69, bf16[1024,256]{1,0:T(8,128)(2,1)} %gradient_hbm.1), custom_call_target="tpu_custom_call" | custom-call | tf_op jit(solution)/shard_map/scale/pallas_call | solution.py:192
  2.0 0.0 copy-start.4
  2.0 3.0 %collective-permute-start.10 = (bf16[1024,128]{1,0:T(8,128)(2,1)S(1)}, bf16[1024,128]{1,0:T(8,128)(2,1)S(1)}, u32[]{:S(2)}, u32[]{:S(2)}) collective-permute-start(bf16[1024,128]{1,0:T(8,128)(2,1)S(1)} %scale.1.refs_4_), channel_id=1, source_target_pairs={{0,4},{2,6},{8,0},{10,2},{16,8},{18,10},{24,16},{26,18},{28,24},{3... | collective-permute-start | bytes 786440 | tf_op jit(solution)/shard_map/ppermute | solution.py:35
  5.0 0.2 collective-permute-start.6
  5.1 0.7 %copy-done.5 = s32[1,8]{1,0:T(1,128)S(1)} copy-done((s32[1,8]{1,0:T(1,128)S(1)}, s32[1,8]{1,0:T(1,128)}, u32[]{:S(2)}) %copy-start.5) | copy-done | bytes 56
  5.8 0.1 copy.13
  5.9 0.1 reshape_squeeze.6
  6.0 0.1 pad_add_fusion
  6.0 0.1 dynamic_slice.15
  6.1 0.2 payload.1
  6.3 2.0 %collective-permute-start.1 = (bf16[1152,128]{1,0:T(8,128)(2,1)S(1)}, bf16[1152,128]{1,0:T(8,128)(2,1)}, u32[]{:S(2)}, u32[]{:S(2)}) collective-permute-start(bf16[1152,128]{1,0:T(8,128)(2,1)S(1)} %get-tuple-element.21), channel_id=1, source_target_pairs={{0,1},{1,0},{2,3},{3,2},{4,5},{5,4},{6,7},{7,6},{8,9},{9,8},{10,11... | collective-permute-start | bytes 884744 | tf_op jit(solution)/shard_map/ppermute | solution.py:58
  8.3 0.1 collective-permute-start
  8.4 0.2 collective-permute-start.3
  8.6 4.2 %collective-permute-done.6.refs_5_ = bf16[1024,128]{1,0:T(8,128)(2,1)S(1)} collective-permute-done((bf16[1024,128]{1,0:T(8,128)(2,1)S(1)}, bf16[1024,128]{1,0:T(8,128)(2,1)S(1)}, u32[]{:S(2)}, u32[]{:S(2)}) %collective-permute-start.6) | collective-permute-done | bytes 262176 | tf_op jit(solution)/shard_map/ppermute | solution.py:35
  12.7 0.4 collective-permute-start.7
  13.2 0.1 reshape.65
  13.5 0.0 collective-permute-done.refs_2_
  13.5 0.1 collective-permute-start.4
  13.6 0.0 collective-permute-done.10.refs_6_
  13.6 1.6 %collective-permute-start.11 = (bf16[1024,128]{1,0:T(8,128)(2,1)S(1)}, bf16[1024,128]{1,0:T(8,128)(2,1)}, u32[]{:S(2)}, u32[]{:S(2)}) collective-permute-start(bf16[1024,128]{1,0:T(8,128)(2,1)S(1)} %collective-permute-done.10.refs_6_), channel_id=1, source_target_pairs={{0,4},{2,6},{8,0},{10,2},{16,8},{18,10},{24,16},{26,18},{28,24},{3... | collective-permute-start | bytes 786440 | tf_op jit(solution)/shard_map/ppermute | solution.py:35
  15.2 4.5 %collective-permute-done.7.refs_4_ = bf16[1024,128]{1,0:T(8,128)(2,1)S(1)} collective-permute-done((bf16[1024,128]{1,0:T(8,128)(2,1)S(1)}, bf16[1024,128]{1,0:T(8,128)(2,1)S(1)}, u32[]{:S(2)}, u32[]{:S(2)}) %collective-permute-start.7) | collective-permute-done | bytes 262176 | tf_op jit(solution)/shard_map/ppermute | solution.py:35
  19.7 0.7 %collective-permute-start.8 = (bf16[1024,128]{1,0:T(8,128)(2,1)S(1)}, bf16[1024,128]{1,0:T(8,128)(2,1)}, u32[]{:S(2)}, u32[]{:S(2)}) collective-permute-start(bf16[1024,128]{1,0:T(8,128)(2,1)S(1)} %collective-permute-done.7.refs_4_), channel_id=1, source_target_pairs={{0,8},{2,10},{8,16},{10,18},{16,24},{18,26},{24,28},{26,30},{28,20... | collective-permute-start | bytes 786440 | tf_op jit(solution)/shard_map/ppermute | solution.py:35
  20.5 0.1 reshape.67
  20.6 0.0 collective-permute-done.3.refs_5_
  20.6 0.0 collective-permute-done.1
  20.6 1.0 %fusion.8 = (bf16[576,128]{1,0:T(8,128)(2,1)S(1)}, bf16[576,128]{1,0:T(8,128)(2,1)S(1)}) fusion(bf16[1152,128]{1,0:T(8,128)(2,1)} %collective-permute-done.1), kind=kLoop, calls=%fused_computation.28 | loop fusion | bytes 589824 | tf_op jit(solution)/shard_map/slice | solution.py:232
  21.6 0.6 %collective-permute-start.2 = (bf16[576,128]{1,0:T(8,128)(2,1)S(1)}, bf16[576,128]{1,0:T(8,128)(2,1)S(1)}, u32[]{:S(2)}, u32[]{:S(2)}) collective-permute-start(bf16[576,128]{1,0:T(8,128)(2,1)S(1)} %get-tuple-element.36), channel_id=1, source_target_pairs={{0,2},{2,0},{4,6},{6,4},{8,10},{10,8},{12,14},{14,12},{16,18},{18,... | collective-permute-start | bytes 442376 | tf_op jit(solution)/shard_map/ppermute | solution.py:53
  22.2 0.3 collective-permute-done.11.refs_5_
  22.4 1.6 %collective-permute-start.12 = (bf16[1024,128]{1,0:T(8,128)(2,1)}, bf16[1024,128]{1,0:T(8,128)(2,1)S(1)}, u32[]{:S(2)}, u32[]{:S(2)}) collective-permute-start(bf16[1024,128]{1,0:T(8,128)(2,1)} %collective-permute-done.11.refs_5_), channel_id=1, source_target_pairs={{0,4},{2,6},{8,0},{10,2},{16,8},{18,10},{24,16},{26,18},{28,24},{3... | collective-permute-start | bytes 786440 | tf_op jit(solution)/shard_map/ppermute | solution.py:35
  24.0 2.2 %collective-permute-done.8.refs_6_ = bf16[1024,128]{1,0:T(8,128)(2,1)} collective-permute-done((bf16[1024,128]{1,0:T(8,128)(2,1)S(1)}, bf16[1024,128]{1,0:T(8,128)(2,1)}, u32[]{:S(2)}, u32[]{:S(2)}) %collective-permute-start.8) | collective-permute-done | bytes 262176 | tf_op jit(solution)/shard_map/ppermute | solution.py:35
  26.2 0.7 %collective-permute-start.9 = (bf16[1024,128]{1,0:T(8,128)(2,1)}, bf16[1024,128]{1,0:T(8,128)(2,1)S(1)}, u32[]{:S(2)}, u32[]{:S(2)}) collective-permute-start(bf16[1024,128]{1,0:T(8,128)(2,1)} %collective-permute-done.8.refs_6_), channel_id=1, source_target_pairs={{0,8},{2,10},{8,16},{10,18},{16,24},{18,26},{24,28},{26,30},{28,20... | collective-permute-start | bytes 786440 | tf_op jit(solution)/shard_map/ppermute | solution.py:35
  26.9 0.1 reshape.69
  27.0 0.0 collective-permute-done.2.refs_3_
  27.1 0.1 reshape.71
  27.1 0.1 concatenate.7.table_ref
  27.3 1.6 %add_slabs.3 = (f32[1024,128]{1,0:T(8,128)S(1)}, f32[1024,128]{1,0:T(8,128)S(1)}) custom-call(s32[306]{0:T(512)S(1)} %concatenate.7.table_ref, bf16[576,128]{1,0:T(8,128)(2,1)S(1)} %get-tuple-element.39.refs_0_, bf16[576,128]{1,0:T(8,128)(2,1)S(1)} %get-tuple-element.37.refs_1_, bf16[576,128]{1,0:T(8,128)(2,1)S(1)} %collective-permute-done.refs_2_, ...), custom_call_target="tpu_custom_call" | custom-call | flops 1 | bytes 1 | tf_op jit(solution)/shard_map/add_slabs/pallas_call | solution.py:272
  28.9 2.3 %add_slabs.4 = (f32[1024,128]{1,0:T(8,128)S(1)}, f32[1024,128]{1,0:T(8,128)S(1)}) custom-call(s32[306]{0:T(512)S(1)} %concatenate.7.table_ref, bf16[576,128]{1,0:T(8,128)(2,1)S(1)} %get-tuple-element.39.refs_0_, bf16[576,128]{1,0:T(8,128)(2,1)S(1)} %get-tuple-element.37.refs_1_, ...), custom_call_target="tpu_custom_call", output_to_operand_aliasing={{0}: (8, {}), {1}: (9, {})} | custom-call | flops 1 | bytes 1 | tf_op jit(solution)/shard_map/add_slabs/pallas_call | solution.py:272
  31.2 0.0 collective-permute-done.12.refs_4_
  31.2 1.1 %add_slabs.5 = (f32[1024,128]{1,0:T(8,128)S(1)}, f32[1024,128]{1,0:T(8,128)S(1)}) custom-call(s32[306]{0:T(512)S(1)} %concatenate.7.table_ref, bf16[576,128]{1,0:T(8,128)(2,1)S(1)} %get-tuple-element.39.refs_0_, bf16[576,128]{1,0:T(8,128)(2,1)S(1)} %get-tuple-element.37.refs_1_, ...), custom_call_target="tpu_custom_call", output_to_operand_aliasing={{0}: (6, {}), {1}: (7, {})} | custom-call | flops 1 | bytes 1 | tf_op jit(solution)/shard_map/add_slabs/pallas_call | solution.py:272
  32.3 0.0 collective-permute-done.4.refs_6_
  32.3 0.0 collective-permute-done.5.refs_7_
  32.3 0.4 collective-permute-done.9.refs_8_
  32.8 1.3 %last_slab.1 = (f32[1024,128]{1,0:T(8,128)S(1)}, bf16[1024,128]{1,0:T(8,128)(2,1)S(1)}, bf16[256,128]{1,0:T(8,128)(2,1)S(1)}) custom-call(s32[306]{0:T(512)S(1)} %concatenate.7.table_ref, bf16[576,128]{1,0:T(8,128)(2,1)S(1)} %get-tuple-element.39.refs_0_, bf16[576,128]{1,0:T(8,128)(2,1)S(1)} %get-tuple-element.37.refs_1_, ...), custom_call_target="tpu_custom_call" | custom-call | flops 1 | bytes 1 | tf_op jit(solution)/shard_map/last_slab/pallas_call | solution.py:287
  34.1 0.1 collective-permute-start.13
  34.2 1.2 %collective-permute-done.13 = bf16[256,128]{1,0:T(8,128)(2,1)S(1)} collective-permute-done((bf16[256,128]{1,0:T(8,128)(2,1)S(1)}, bf16[256,128]{1,0:T(8,128)(2,1)S(1)}, u32[]{:S(2)}, u32[]{:S(2)}) %collective-permute-start.13) | collective-permute-done | bytes 65568 | tf_op jit(solution)/shard_map/ppermute | solution.py:53
  35.5 3.0 %collective-permute-start.14 = (bf16[256,128]{1,0:T(8,128)(2,1)S(1)}, bf16[256,128]{1,0:T(8,128)(2,1)S(1)}, u32[]{:S(2)}, u32[]{:S(2)}) collective-permute-start(bf16[256,128]{1,0:T(8,128)(2,1)S(1)} %add_convert_fusion.2), channel_id=1, source_target_pairs={{0,24},{1,25},{2,18},{3,19},{4,28},{5,29},{6,22},{7,23},{8,16},{9,... | collective-permute-start | bytes 196616 | tf_op jit(solution)/shard_map/ppermute | solution.py:46
  38.4 0.7 %collective-permute-start.15 = (bf16[256,128]{1,0:T(8,128)(2,1)S(1)}, bf16[256,128]{1,0:T(8,128)(2,1)S(1)}, u32[]{:S(2)}, u32[]{:S(2)}) collective-permute-start(bf16[256,128]{1,0:T(8,128)(2,1)S(1)} %add_convert_fusion.2), channel_id=1, source_target_pairs={{2,10},{3,11},{6,14},{7,15},{10,2},{11,3},{14,6},{15,7},{18,26},{1... | collective-permute-start | bytes 196616 | tf_op jit(solution)/shard_map/ppermute | solution.py:46
  39.1 1.5 %collective-permute-start.16 = (bf16[1024,128]{1,0:T(8,128)(2,1)S(1)}, bf16[1024,128]{1,0:T(8,128)(2,1)S(1)}, u32[]{:S(2)}, u32[]{:S(2)}) collective-permute-start(bf16[1024,128]{1,0:T(8,128)(2,1)S(1)} %get-tuple-element.31), channel_id=1, source_target_pairs={{0,2},{2,0},{4,6},{6,4},{8,10},{10,8},{12,14},{14,12},{16,18},{18,... | collective-permute-start | bytes 786440 | tf_op jit(solution)/shard_map/ppermute | solution.py:53
  40.5 1.1 %collective-permute-done.14 = bf16[256,128]{1,0:T(8,128)(2,1)S(1)} collective-permute-done((bf16[256,128]{1,0:T(8,128)(2,1)S(1)}, bf16[256,128]{1,0:T(8,128)(2,1)S(1)}, u32[]{:S(2)}, u32[]{:S(2)}) %collective-permute-start.14) | collective-permute-done | bytes 65568 | tf_op jit(solution)/shard_map/ppermute | solution.py:46
  41.7 0.0 collective-permute-done.16
  41.7 0.2 multiply_convert_fusion
  41.9 0.7 %collective-permute-start.17 = (f32[256,128]{1,0:T(8,128)S(1)}, f32[256,128]{1,0:T(8,128)S(1)}, u32[]{:S(2)}, u32[]{:S(2)}) collective-permute-start(f32[256,128]{1,0:T(8,128)S(1)} %convert_add_fusion), channel_id=1, source_target_pairs={{0,2},{2,0},{4,6},{6,4},{8,10},{10,8},{12,14},{14,12},{16,18},{18,... | collective-permute-start | bytes 393224 | tf_op jit(solution)/shard_map/ppermute | solution.py:53
  42.6 1.6 %collective-permute-start.20 = (bf16[512,128]{1,0:T(8,128)(2,1)S(1)}, bf16[512,128]{1,0:T(8,128)(2,1)S(1)}, u32[]{:S(2)}, u32[]{:S(2)}) collective-permute-start(bf16[512,128]{1,0:T(8,128)(2,1)S(1)} %constant_dynamic-slice_fusion), channel_id=1, source_target_pairs={{0,1},{1,0},{2,3},{3,2},{4,5},{5,4},{6,7},{7,6},{8,9},{9,8},{10,11... | collective-permute-start | bytes 393224 | tf_op jit(solution)/shard_map/ppermute | solution.py:58
  44.2 0.2 fusion.1
  44.4 0.0 collective-permute-done.17
  44.5 0.7 %collective-permute-start.18 = (bf16[256,128]{1,0:T(8,128)(2,1)S(1)}, bf16[256,128]{1,0:T(8,128)(2,1)S(1)}, u32[]{:S(2)}, u32[]{:S(2)}) collective-permute-start(bf16[256,128]{1,0:T(8,128)(2,1)S(1)} %add_convert_fusion.1), channel_id=1, source_target_pairs={{0,1},{1,0},{2,3},{3,2},{4,5},{5,4},{6,7},{7,6},{8,9},{9,8},{10,11... | collective-permute-start | bytes 196616 | tf_op jit(solution)/shard_map/ppermute | solution.py:58
  45.2 2.3 %collective-permute-start.19 = (bf16[256,128]{1,0:T(8,128)(2,1)S(1)}, bf16[256,128]{1,0:T(8,128)(2,1)S(1)}, u32[]{:S(2)}, u32[]{:S(2)}) collective-permute-start(bf16[256,128]{1,0:T(8,128)(2,1)S(1)} %add_convert_fusion.1), channel_id=1, source_target_pairs={{0,4},{1,5},{2,7},{3,6},{4,0},{5,1},{6,3},{7,2},{8,12},{9,13},{10,... | collective-permute-start | bytes 196616 | tf_op jit(solution)/shard_map/ppermute | solution.py:46
  47.5 1.3 %collective-permute-done.20 = bf16[512,128]{1,0:T(8,128)(2,1)S(1)} collective-permute-done((bf16[512,128]{1,0:T(8,128)(2,1)S(1)}, bf16[512,128]{1,0:T(8,128)(2,1)S(1)}, u32[]{:S(2)}, u32[]{:S(2)}) %collective-permute-start.20) | collective-permute-done | bytes 131104 | tf_op jit(solution)/shard_map/ppermute | solution.py:58
  48.8 0.9 %fusion = bf16[512,256]{1,0:T(8,128)(2,1)} fusion(f32[512,256]{1,0:T(8,128)S(1)} %fusion.1, bf16[512,128]{1,0:T(8,128)(2,1)S(1)} %collective-permute-done.20, bf16[256,256]{1,0:T(8,128)(2,1)S(1)} %copy-done, s32[]{:T(128)S(6)} %select_n.496), kind=kOutput, calls=%fused_computation.1 | convolution fusion | flops 33816576 | bytes 983044 | tf_op jit(solution)/shard_map/dot_general | solution.py:325
  49.8 0.5 collective-permute-done.18
  50.3 0.1 collective-permute-start.21
  50.3 1.2 %collective-permute-done.21 = bf16[1,256,128]{2,1,0:T(8,128)(2,1)S(1)} collective-permute-done((bf16[1,256,128]{2,1,0:T(8,128)(2,1)S(1)}, bf16[1,256,128]{2,1,0:T(8,128)(2,1)S(1)}, u32[]{:S(2)}, u32[]{:S(2)}) %collective-permute-start.21) | collective-permute-done | bytes 65568 | tf_op jit(solution)/shard_map/ppermute | solution.py:53
  51.6 0.7 %broadcast_multiply_fusion = f32[256,256]{1,0:T(8,128)} fusion(f32[256,256]{1,0:T(8,128)S(1)} %convert_dynamic-update-slice_fusion), kind=kLoop, calls=%fused_computation.5 | loop fusion | flops 65536 | bytes 524288 | tf_op jit(solution)/shard_map/mul | solution.py:339
  (35 shorter events, 0.3 us)
Async XLA Ops:
  0.6 43.6 %copy-start = (bf16[256,256]{1,0:T(8,128)(2,1)S(1)}, bf16[256,256]{1,0:T(8,128)(2,1)}, u32[]{:S(2)}) copy-start(bf16[256,256]{1,0:T(8,128)(2,1)} %param.9) | copy-start | bytes 393220
  0.6 5.5 %copy-start.1 = (s32[1,8,8,16,128]{4,3,2,1,0:T(8,128)S(1)}, s32[1,8,8,16,128]{4,3,2,1,0:T(8,128)}, u32[]{:S(2)}) copy-start(s32[1,8,8,16,128]{4,3,2,1,0:T(8,128)} %param.10) | copy-start | bytes 1572868
  0.7 4.5 %copy-start.3 = (s32[1024]{0:T(1024)S(1)}, s32[1024]{0:T(1024)}, u32[]{:S(2)}) copy-start(s32[1024]{0:T(1024)} %param.13) | copy-start | bytes 12292
  0.7 5.5 %copy-start.2 = (bf16[512,256]{1,0:T(8,128)(2,1)S(1)}, bf16[512,256]{1,0:T(8,128)(2,1)}, u32[]{:S(2)}) copy-start(bf16[512,256]{1,0:T(8,128)(2,1)} %features_ref) | copy-start | bytes 786436
  2.0 3.9 %copy-start.4 = (s32[1,8,2,8]{3,2,1,0:T(2,128)S(1)}, s32[1,8,2,8]{3,2,1,0:T(2,128)}, u32[]{:S(2)}) copy-start(s32[1,8,2,8]{3,2,1,0:T(2,128)} %param.11) | copy-start | bytes 1540
  2.0 11.6 %collective-permute-start.10 = (bf16[1024,128]{1,0:T(8,128)(2,1)S(1)}, bf16[1024,128]{1,0:T(8,128)(2,1)S(1)}, u32[]{:S(2)}, u32[]{:S(2)}) collective-permute-start(bf16[1024,128]{1,0:T(8,128)(2,1)S(1)} %scale.1.refs_4_), channel_id=1, source_target_pairs={{0,4},{2,6},{8,0},{10,2},{16,8},{18,10},{24,16},{26,18},{28,24},{3... | collective-permute-start | bytes 786440 | tf_op jit(solution)/shard_map/ppermute | solution.py:35
  5.0 7.8 %collective-permute-start.6 = (bf16[1024,128]{1,0:T(8,128)(2,1)S(1)}, bf16[1024,128]{1,0:T(8,128)(2,1)S(1)}, u32[]{:S(2)}, u32[]{:S(2)}) collective-permute-start(bf16[1024,128]{1,0:T(8,128)(2,1)S(1)} %scale.1.refs_4_), channel_id=1, source_target_pairs={{0,8},{2,10},{8,16},{10,18},{16,24},{18,26},{24,28},{26,30},{28,20... | collective-permute-start | bytes 786440 | tf_op jit(solution)/shard_map/ppermute | solution.py:35
  5.1 0.7 %copy-start.5 = (s32[1,8]{1,0:T(1,128)S(1)}, s32[1,8]{1,0:T(1,128)}, u32[]{:S(2)}) copy-start(s32[1,8]{1,0:T(1,128)} %param.12) | copy-start | bytes 100
  6.3 14.3 %collective-permute-start.1 = (bf16[1152,128]{1,0:T(8,128)(2,1)S(1)}, bf16[1152,128]{1,0:T(8,128)(2,1)}, u32[]{:S(2)}, u32[]{:S(2)}) collective-permute-start(bf16[1152,128]{1,0:T(8,128)(2,1)S(1)} %get-tuple-element.21), channel_id=1, source_target_pairs={{0,1},{1,0},{2,3},{3,2},{4,5},{5,4},{6,7},{7,6},{8,9},{9,8},{10,11... | collective-permute-start | bytes 884744 | tf_op jit(solution)/shard_map/ppermute | solution.py:58
  8.3 5.2 %collective-permute-start = (bf16[576,128]{1,0:T(8,128)(2,1)S(1)}, bf16[576,128]{1,0:T(8,128)(2,1)S(1)}, u32[]{:S(2)}, u32[]{:S(2)}) collective-permute-start(bf16[576,128]{1,0:T(8,128)(2,1)S(1)} %get-tuple-element.38), channel_id=1, source_target_pairs={{0,2},{2,0},{4,6},{6,4},{8,10},{10,8},{12,14},{14,12},{16,18},{18,... | collective-permute-start | bytes 442376 | tf_op jit(solution)/shard_map/ppermute | solution.py:53
  8.4 12.2 %collective-permute-start.3 = (bf16[256,512]{1,0:T(8,128)(2,1)S(1)}, bf16[256,512]{1,0:T(8,128)(2,1)S(1)}, u32[]{:S(2)}, u32[]{:S(2)}) collective-permute-start(bf16[256,512]{1,0:T(8,128)(2,1)S(1)} %get-tuple-element.22.refs_4_), channel_id=1, source_target_pairs={{0,1},{1,0},{2,3},{3,2},{4,5},{5,4},{6,7},{7,6},{8,9},{9,8},{10,11... | collective-permute-start | bytes 786440 | tf_op jit(solution)/shard_map/ppermute | solution.py:58
  12.7 7.0 %collective-permute-start.7 = (bf16[1024,128]{1,0:T(8,128)(2,1)S(1)}, bf16[1024,128]{1,0:T(8,128)(2,1)S(1)}, u32[]{:S(2)}, u32[]{:S(2)}) collective-permute-start(bf16[1024,128]{1,0:T(8,128)(2,1)S(1)} %collective-permute-done.6.refs_5_), channel_id=1, source_target_pairs={{0,8},{2,10},{8,16},{10,18},{16,24},{18,26},{24,28},{26,30},{28,20... | collective-permute-start | bytes 786440 | tf_op jit(solution)/shard_map/ppermute | solution.py:35
  13.5 18.9 %collective-permute-start.4 = (bf16[256,512]{1,0:T(8,128)(2,1)S(1)}, bf16[256,512]{1,0:T(8,128)(2,1)S(1)}, u32[]{:S(2)}, u32[]{:S(2)}) collective-permute-start(bf16[256,512]{1,0:T(8,128)(2,1)S(1)} %get-tuple-element.22.refs_4_), channel_id=1, source_target_pairs={{0,2},{2,0},{4,6},{6,4},{8,10},{10,8},{12,14},{14,12},{16,18},{18,... | collective-permute-start | bytes 786440 | tf_op jit(solution)/shard_map/ppermute | solution.py:53
  13.6 8.8 %collective-permute-start.11 = (bf16[1024,128]{1,0:T(8,128)(2,1)S(1)}, bf16[1024,128]{1,0:T(8,128)(2,1)}, u32[]{:S(2)}, u32[]{:S(2)}) collective-permute-start(bf16[1024,128]{1,0:T(8,128)(2,1)S(1)} %collective-permute-done.10.refs_6_), channel_id=1, source_target_pairs={{0,4},{2,6},{8,0},{10,2},{16,8},{18,10},{24,16},{26,18},{28,24},{3... | collective-permute-start | bytes 786440 | tf_op jit(solution)/shard_map/ppermute | solution.py:35
  19.7 6.5 %collective-permute-start.8 = (bf16[1024,128]{1,0:T(8,128)(2,1)S(1)}, bf16[1024,128]{1,0:T(8,128)(2,1)}, u32[]{:S(2)}, u32[]{:S(2)}) collective-permute-start(bf16[1024,128]{1,0:T(8,128)(2,1)S(1)} %collective-permute-done.7.refs_4_), channel_id=1, source_target_pairs={{0,8},{2,10},{8,16},{10,18},{16,24},{18,26},{24,28},{26,30},{28,20... | collective-permute-start | bytes 786440 | tf_op jit(solution)/shard_map/ppermute | solution.py:35
  20.6 11.8 %collective-permute-start.5 = (bf16[256,512]{1,0:T(8,128)(2,1)S(1)}, bf16[256,512]{1,0:T(8,128)(2,1)S(1)}, u32[]{:S(2)}, u32[]{:S(2)}) collective-permute-start(bf16[256,512]{1,0:T(8,128)(2,1)S(1)} %collective-permute-done.3.refs_5_), channel_id=1, source_target_pairs={{0,2},{2,0},{4,6},{6,4},{8,10},{10,8},{12,14},{14,12},{16,18},{18,... | collective-permute-start | bytes 786440 | tf_op jit(solution)/shard_map/ppermute | solution.py:53
  21.6 5.5 %collective-permute-start.2 = (bf16[576,128]{1,0:T(8,128)(2,1)S(1)}, bf16[576,128]{1,0:T(8,128)(2,1)S(1)}, u32[]{:S(2)}, u32[]{:S(2)}) collective-permute-start(bf16[576,128]{1,0:T(8,128)(2,1)S(1)} %get-tuple-element.36), channel_id=1, source_target_pairs={{0,2},{2,0},{4,6},{6,4},{8,10},{10,8},{12,14},{14,12},{16,18},{18,... | collective-permute-start | bytes 442376 | tf_op jit(solution)/shard_map/ppermute | solution.py:53
  22.4 8.7 %collective-permute-start.12 = (bf16[1024,128]{1,0:T(8,128)(2,1)}, bf16[1024,128]{1,0:T(8,128)(2,1)S(1)}, u32[]{:S(2)}, u32[]{:S(2)}) collective-permute-start(bf16[1024,128]{1,0:T(8,128)(2,1)} %collective-permute-done.11.refs_5_), channel_id=1, source_target_pairs={{0,4},{2,6},{8,0},{10,2},{16,8},{18,10},{24,16},{26,18},{28,24},{3... | collective-permute-start | bytes 786440 | tf_op jit(solution)/shard_map/ppermute | solution.py:35
  26.2 6.6 %collective-permute-start.9 = (bf16[1024,128]{1,0:T(8,128)(2,1)}, bf16[1024,128]{1,0:T(8,128)(2,1)S(1)}, u32[]{:S(2)}, u32[]{:S(2)}) collective-permute-start(bf16[1024,128]{1,0:T(8,128)(2,1)} %collective-permute-done.8.refs_6_), channel_id=1, source_target_pairs={{0,8},{2,10},{8,16},{10,18},{16,24},{18,26},{24,28},{26,30},{28,20... | collective-permute-start | bytes 786440 | tf_op jit(solution)/shard_map/ppermute | solution.py:35
  34.1 1.3 %collective-permute-start.13 = (bf16[256,128]{1,0:T(8,128)(2,1)S(1)}, bf16[256,128]{1,0:T(8,128)(2,1)S(1)}, u32[]{:S(2)}, u32[]{:S(2)}) collective-permute-start(bf16[256,128]{1,0:T(8,128)(2,1)S(1)} %get-tuple-element.29), channel_id=1, source_target_pairs={{0,2},{2,0},{4,6},{6,4},{8,10},{10,8},{12,14},{14,12},{16,18},{18,... | collective-permute-start | bytes 196616 | tf_op jit(solution)/shard_map/ppermute | solution.py:53
  35.5 6.2 %collective-permute-start.14 = (bf16[256,128]{1,0:T(8,128)(2,1)S(1)}, bf16[256,128]{1,0:T(8,128)(2,1)S(1)}, u32[]{:S(2)}, u32[]{:S(2)}) collective-permute-start(bf16[256,128]{1,0:T(8,128)(2,1)S(1)} %add_convert_fusion.2), channel_id=1, source_target_pairs={{0,24},{1,25},{2,18},{3,19},{4,28},{5,29},{6,22},{7,23},{8,16},{9,... | collective-permute-start | bytes 196616 | tf_op jit(solution)/shard_map/ppermute | solution.py:46
  38.4 3.3 %collective-permute-start.15 = (bf16[256,128]{1,0:T(8,128)(2,1)S(1)}, bf16[256,128]{1,0:T(8,128)(2,1)S(1)}, u32[]{:S(2)}, u32[]{:S(2)}) collective-permute-start(bf16[256,128]{1,0:T(8,128)(2,1)S(1)} %add_convert_fusion.2), channel_id=1, source_target_pairs={{2,10},{3,11},{6,14},{7,15},{10,2},{11,3},{14,6},{15,7},{18,26},{1... | collective-permute-start | bytes 196616 | tf_op jit(solution)/shard_map/ppermute | solution.py:46
  39.1 2.6 %collective-permute-start.16 = (bf16[1024,128]{1,0:T(8,128)(2,1)S(1)}, bf16[1024,128]{1,0:T(8,128)(2,1)S(1)}, u32[]{:S(2)}, u32[]{:S(2)}) collective-permute-start(bf16[1024,128]{1,0:T(8,128)(2,1)S(1)} %get-tuple-element.31), channel_id=1, source_target_pairs={{0,2},{2,0},{4,6},{6,4},{8,10},{10,8},{12,14},{14,12},{16,18},{18,... | collective-permute-start | bytes 786440 | tf_op jit(solution)/shard_map/ppermute | solution.py:53
  41.9 2.5 %collective-permute-start.17 = (f32[256,128]{1,0:T(8,128)S(1)}, f32[256,128]{1,0:T(8,128)S(1)}, u32[]{:S(2)}, u32[]{:S(2)}) collective-permute-start(f32[256,128]{1,0:T(8,128)S(1)} %convert_add_fusion), channel_id=1, source_target_pairs={{0,2},{2,0},{4,6},{6,4},{8,10},{10,8},{12,14},{14,12},{16,18},{18,... | collective-permute-start | bytes 393224 | tf_op jit(solution)/shard_map/ppermute | solution.py:53
  42.6 6.2 %collective-permute-start.20 = (bf16[512,128]{1,0:T(8,128)(2,1)S(1)}, bf16[512,128]{1,0:T(8,128)(2,1)S(1)}, u32[]{:S(2)}, u32[]{:S(2)}) collective-permute-start(bf16[512,128]{1,0:T(8,128)(2,1)S(1)} %constant_dynamic-slice_fusion), channel_id=1, source_target_pairs={{0,1},{1,0},{2,3},{3,2},{4,5},{5,4},{6,7},{7,6},{8,9},{9,8},{10,11... | collective-permute-start | bytes 393224 | tf_op jit(solution)/shard_map/ppermute | solution.py:58
  44.5 5.8 %collective-permute-start.18 = (bf16[256,128]{1,0:T(8,128)(2,1)S(1)}, bf16[256,128]{1,0:T(8,128)(2,1)S(1)}, u32[]{:S(2)}, u32[]{:S(2)}) collective-permute-start(bf16[256,128]{1,0:T(8,128)(2,1)S(1)} %add_convert_fusion.1), channel_id=1, source_target_pairs={{0,1},{1,0},{2,3},{3,2},{4,5},{5,4},{6,7},{7,6},{8,9},{9,8},{10,11... | collective-permute-start | bytes 196616 | tf_op jit(solution)/shard_map/ppermute | solution.py:58
  45.2 5.0 %collective-permute-start.19 = (bf16[256,128]{1,0:T(8,128)(2,1)S(1)}, bf16[256,128]{1,0:T(8,128)(2,1)S(1)}, u32[]{:S(2)}, u32[]{:S(2)}) collective-permute-start(bf16[256,128]{1,0:T(8,128)(2,1)S(1)} %add_convert_fusion.1), channel_id=1, source_target_pairs={{0,4},{1,5},{2,7},{3,6},{4,0},{5,1},{6,3},{7,2},{8,12},{9,13},{10,... | collective-permute-start | bytes 196616 | tf_op jit(solution)/shard_map/ppermute | solution.py:46
  50.3 1.3 %collective-permute-start.21 = (bf16[1,256,128]{2,1,0:T(8,128)(2,1)S(1)}, bf16[1,256,128]{2,1,0:T(8,128)(2,1)S(1)}, u32[]{:S(2)}, u32[]{:S(2)}) collective-permute-start(bf16[1,256,128]{2,1,0:T(8,128)(2,1)S(1)} %fusion.3), channel_id=1, source_target_pairs={{0,2},{2,0},{4,6},{6,4},{8,10},{10,8},{12,14},{14,12},{16,18},{18,... | collective-permute-start | bytes 196616 | tf_op jit(solution)/shard_map/ppermute | solution.py:53
